TPU v7x, 32 devices: a whole 2x2x4 slice. The times are simulated.
32 devices in a mesh: grp: 4 (over x, core), ep: 8 (over z, y).
Axes of the slice: x: 2, y: 2, z: 4, core: 2. Of those that a mesh axis runs over, the one named last changes fastest.
Arguments:
- tokens: bfloat16 [1024, 3584], P('ep', 'grp'), may hold values from -6 to 6
- routes: int32 [1024, 1], P('ep'), may hold values from 0 to 7; in each aligned block of 128 rows (0 to 127, 128 to 255, ...) at most 32 rows name the same one
- route_weights: float32 [1024, 1], P('ep'), may hold values from 0.2 to 1
- hot_experts: int32 [4], replicated, may hold values from 0 to 3, as said below
- w_gate: bfloat16 [4, 3584, 2048], P(None, 'ep', 'grp'), may hold values from -0.09375 to 0.09375
- w_up: bfloat16 [4, 3584, 2048], P(None, 'ep', 'grp'), may hold values from -0.09375 to 0.09375
- w_down: bfloat16 [4, 2048, 3584], P(None, 'grp', 'ep'), may hold values from -0.125 to 0.125
- cotangent: bfloat16 [1024, 3584], P('ep', 'grp'), may hold values from -3 to 3
Outputs:
- layer_output: bfloat16 [1024, 3584], P('ep', 'grp')
- grad_tokens: bfloat16 [1024, 3584], P('ep', 'grp')
- grad_gate: bfloat16 [4, 3584, 2048], P(None, 'ep', 'grp')
- grad_up: bfloat16 [4, 3584, 2048], P(None, 'ep', 'grp')
- grad_down: bfloat16 [4, 2048, 3584], P(None, 'grp', 'ep')
Inputs may be any that keep to these rules, and one draw needn't show every extreme that they name: `routes`: each row names one slot. Among the rows of one device (aligned blocks of 128 rows) no slot is named by more than 32 rows. `hot_experts`: entry j is the expert held by slot 4 + j; an expert may appear several times.
All inputs are finite; a program needn't handle non-finite values.
Results may differ from a plain program's by a relative error of at most 0.02.
Values may be sent and summed in bfloat16 or wider, within the bound.
No kernel may reach another device: no remote copies, remote signals or barrier semaphores. Data moves between devices by JAX's collectives and lax.ppermute only.
A program may use at most 128 MiB of HBM per device.

v0:
```python
import jax
import jax.numpy as jnp
from jax import lax
from jax.sharding import PartitionSpec as P


def shards(tokens, routes, route_weights, hot_experts, w_gate, w_up, w_down, cotangent):
    ep_size = lax.axis_size("ep")
    tok_count = tokens.shape[0]
    top_count = routes.shape[1]
    flat_count = tok_count * top_count
    capacity = 2 * flat_count // ep_size
    pad_rows = ep_size * capacity
    expert_count = w_gate.shape[0]
    hidden = w_gate.shape[2]
    stored = w_gate.shape[1]
    width = stored * ep_size
    slot_host = jnp.concatenate([jnp.arange(expert_count, dtype=jnp.int32), hot_experts])
    flat_slot = routes.reshape(-1)
    onehot = (flat_slot[:, None] == jnp.arange(ep_size, dtype=jnp.int32)[None, :]).astype(jnp.int32)
    before = jnp.cumsum(onehot, axis=0) - onehot
    position = jnp.sum(before * onehot, axis=1)
    dest = flat_slot * capacity + position
    source = (
        jnp.full((pad_rows,), flat_count, jnp.int32)
        .at[dest]
        .set(jnp.arange(flat_count, dtype=jnp.int32))
    )
    token_of = source // top_count
    flat_weights = route_weights.reshape(-1)
    weight_of = jnp.take(jnp.concatenate([flat_weights, jnp.zeros((1,), jnp.float32)]), source)
    sel_gate = jnp.take(w_gate, slot_host, axis=0)
    sel_up = jnp.take(w_up, slot_host, axis=0)
    sel_down = jnp.swapaxes(jnp.take(w_down, slot_host, axis=0), 1, 2)
    packed = jnp.concatenate([sel_gate, sel_up, sel_down], axis=2)
    received = lax.all_to_all(packed, "ep", split_axis=0, concat_axis=0, tiled=True)
    slot_weights = received.reshape(width, 3 * hidden)
    gate_up_w = slot_weights[:, : 2 * hidden]
    down_t = slot_weights[:, 2 * hidden :]

    def pick_rows(source_table, route_scale):
        extended = jnp.concatenate(
            [source_table, jnp.zeros((1, source_table.shape[1]), source_table.dtype)], axis=0
        )
        picked = jnp.take(extended, token_of, axis=0)
        if route_scale is not None:
            picked = (picked.astype(jnp.float32) * route_scale[:, None]).astype(jnp.bfloat16)
        return picked

    def deliver(source_table, route_scale):
        send_rows = pick_rows(source_table, route_scale)
        moved = lax.all_to_all(
            send_rows.reshape(ep_size, capacity, -1), "ep", split_axis=0, concat_axis=0, tiled=True
        )
        return lax.all_gather(moved.reshape(pad_rows, -1), "grp", axis=1, tiled=True)

    def combine(part_rows, weighted):
        block_sum = lax.psum_scatter(
            part_rows.astype(jnp.float32).astype(jnp.bfloat16),
            "grp",
            scatter_dimension=1,
            tiled=True,
        ).astype(jnp.float32)
        returned = lax.all_to_all(
            block_sum.reshape(ep_size, capacity, -1).astype(jnp.bfloat16),
            "ep",
            split_axis=0,
            concat_axis=0,
            tiled=True,
        ).astype(jnp.float32)
        route_rows = jnp.take(returned.reshape(pad_rows, -1), dest, axis=0)
        if weighted:
            route_rows = route_rows * flat_weights[:, None]
        return jnp.sum(route_rows.reshape(tok_count, top_count, -1), axis=1)

    contract_last = (((1,), (1,)), ((), ()))
    contract_first = (((0,), (0,)), ((), ()))
    x_rows = deliver(tokens, None)
    gate_up = jnp.dot(x_rows, gate_up_w, preferred_element_type=jnp.float32)
    gate_pre = gate_up[:, :hidden]
    up_pre = gate_up[:, hidden:]
    sigmoid_gate = jax.nn.sigmoid(gate_pre)
    act = (gate_pre * sigmoid_gate * up_pre).astype(jnp.bfloat16)
    out_parts = lax.dot_general(
        act, down_t, contract_last, preferred_element_type=jnp.float32
    ).astype(jnp.bfloat16)
    layer_output = combine(out_parts, True).astype(jnp.bfloat16)
    dz_rows = deliver(cotangent, weight_of)
    act_grad = jnp.dot(dz_rows, down_t, preferred_element_type=jnp.float32)
    gate_grad = act_grad * up_pre * sigmoid_gate * (1.0 + gate_pre * (1.0 - sigmoid_gate))
    up_grad = act_grad * gate_pre * sigmoid_gate
    pre_grad = jnp.concatenate([gate_grad, up_grad], axis=1).astype(jnp.bfloat16)
    tok_parts = lax.dot_general(
        pre_grad, gate_up_w, contract_last, preferred_element_type=jnp.float32
    ).astype(jnp.bfloat16)
    grad_tokens = combine(tok_parts, False).astype(jnp.bfloat16)
    grad_gate_up = lax.dot_general(
        x_rows, pre_grad, contract_first, preferred_element_type=jnp.float32
    )
    grad_down_t = lax.dot_general(dz_rows, act, contract_first, preferred_element_type=jnp.float32)
    slot_grad = jnp.concatenate([grad_gate_up, grad_down_t], axis=1).astype(jnp.bfloat16)
    owner_pieces = lax.all_to_all(
        slot_grad.reshape(ep_size, stored, 3 * hidden),
        "ep",
        split_axis=0,
        concat_axis=0,
        tiled=True,
    )
    host_onehot = (slot_host[None, :] == jnp.arange(expert_count, dtype=jnp.int32)[:, None]).astype(
        jnp.bfloat16
    )
    totals = jnp.einsum(
        "es,sdh->edh", host_onehot, owner_pieces, preferred_element_type=jnp.float32
    )
    grad_gate = totals[:, :, :hidden].astype(jnp.bfloat16)
    grad_up = totals[:, :, hidden : 2 * hidden].astype(jnp.bfloat16)
    grad_down = jnp.swapaxes(totals[:, :, 2 * hidden :], 1, 2).astype(jnp.bfloat16)
    return (layer_output, grad_tokens, grad_gate, grad_up, grad_down)


def solution(mesh):
    placed = (
        P("ep", "grp"),
        P("ep", None),
        P("ep", None),
        P(),
        P(None, "ep", "grp"),
        P(None, "ep", "grp"),
        P(None, "grp", "ep"),
        P("ep", "grp"),
    )
    return jax.shard_map(
        shards,
        mesh=mesh,
        in_specs=placed,
        out_specs=(
            P("ep", "grp"),
            P("ep", "grp"),
            P(None, "ep", "grp"),
            P(None, "ep", "grp"),
            P(None, "grp", "ep"),
        ),
        check_vma=False,
    )
```

profile of v0, /device:TPU:17, one launch (start us, length us, event | category | flops | bytes accessed | tf_op | source)
XLA Modules:
  0.0 669.8 jit_solution(9967467966650265204)
XLA Ops:
  7.2 0.0 copy-start
  7.2 0.9 fusion.16
  8.1 0.2 reduce_window_sum.11
  8.2 0.8 select_reduce_fusion
  9.1 0.7 fusion.20
  9.7 1.0 scatter_custom_fusion
  10.8 1.0 concatenate.53
  11.7 1.2 gather_fusion.2
  13.0 1.9 gather_fusion.1
  14.9 0.9 broadcast_select_fusion.2
  15.8 5.6 all-to-all-start
  21.4 0.1 fusion.21
  21.5 0.1 compare_select_fusion.2
  21.6 2.6 gather_fusion.3
  24.2 4.2 gather_fusion.4
  28.4 1.2 gather_fusion.6
  29.6 4.1 gather_fusion
  33.7 4.5 select_bitcast_fusion
  38.2 1.0 multiply_convert_fusion
  39.2 0.1 copy-done.3
  39.3 3.7 broadcast_select_fusion.1
  43.0 5.4 all-to-all-start.3
  48.5 9.5 %pad_maximum_fusion = bf16[8,448,1536]{2,1,0:T(8,128)(2,1)} fusion(bf16[8,448,512]{2,1,0:T(8,128)(2,1)} %select_bitcast_fusion, bf16[8,448,512]{2,1,0:T(8,128)(2,1)} %get-tuple-element.36, bf16[8,448,512]{2,1,0:T(8,128)(2,1)} %get-tuple-element.35), kind=kLoop, calls=%fused_computation.9 | loop fusion | flops 33030144 | bytes 22020096 | tf_op jit(solution)/shard_map/concatenate | solution.py:35
  58.0 0.7 all-to-all-done.3
  58.7 0.8 copy-done.7
  59.5 5.9 all-to-all-start.1
  65.4 0.7 all-gather.3.cloned.1.call-update
  66.1 0.0 all-gather.5.cloned.1.call-start
  66.1 0.7 all-gather.5.cloned.1.call-update
  66.8 0.0 reduce-scatter.7.cloned.1.call-start
  66.9 26.6 %all-gather.3.cloned.1.call-done = bf16[256,3584]{1,0:T(8,128)(2,1)} async-done(((bf16[256,896]{1,0:T(8,128)(2,1)}), bf16[256,3584]{1,0:T(8,128)(2,1)}) %all-gather.3.cloned.1.call-update) | async-done | bytes 1835024 | tf_op jit(solution)/shard_map/all_gather | solution.py:55
  93.5 205.1 %all-to-all-done.1 = bf16[8,448,1536]{2,1,0:T(8,128)(2,1)} async-done(((bf16[8,448,1536]{2,1,0:T(8,128)(2,1)}), bf16[8,448,1536]{2,1,0:T(8,128)(2,1)}, u32[]{:S(2)}, u32[]{:S(2)}) %all-to-all-start.1) | async-done | bytes 11010080 | tf_op jit(solution)/shard_map/all_to_all | solution.py:36
  298.6 5.7 fusion.7
  304.3 0.0 all-gather.5.cloned.1.call-done
  304.3 3.9 multiply_convert_fusion.2
  308.2 3.2 convolution_convert_fusion.2
  311.4 2.3 copy.27
  313.7 0.0 reduce-scatter.7.cloned.1.call-update
  313.7 0.2 reduce-scatter.9.cloned.1.call-start
  313.9 6.4 fusion.9
  320.3 3.9 copy.29
  324.3 0.0 reduce-scatter.9.cloned.1.call-update
  324.3 24.6 %reduce-scatter.7.cloned.1.call-done = bf16[896,256]{1,0:T(8,128)(2,1)} async-done(((bf16[3584,256]{1,0:T(8,128)(2,1)}), bf16[896,256]{1,0:T(8,128)(2,1)}) %reduce-scatter.7.cloned.1.call-update) | async-done | bytes 458768
  348.8 2.0 copy.28
  350.8 5.5 all-to-all-start.2
  356.3 3.0 convolution_convert_fusion.1
  359.3 5.1 convolution_convert_fusion
  364.5 17.4 %reduce-scatter.9.cloned.1.call-done = bf16[896,256]{1,0:T(8,128)(2,1)} async-done(((bf16[3584,256]{1,0:T(8,128)(2,1)}), bf16[896,256]{1,0:T(8,128)(2,1)}) %reduce-scatter.9.cloned.1.call-update) | async-done | bytes 458768
  381.8 2.0 copy.30
  383.8 5.5 all-to-all-start.4
  389.3 9.6 %pad_maximum_fusion.1 = bf16[8,448,1536]{2,1,0:T(8,128)(2,1)} fusion(bf16[8,448,512]{2,1,0:T(8,128)(2,1)} %bitcast.47, bf16[8,448,1024]{2,1,0:T(8,128)(2,1)} %bitcast.46), kind=kLoop, calls=%fused_computation.10 | loop fusion | flops 22020096 | bytes 22020096 | tf_op jit(solution)/shard_map/concatenate | solution.py:101
  398.9 1.5 all-to-all-done.4
  400.3 6.2 all-to-all-start.5
  406.6 0.1 bitcast_convert_fusion.1
  406.7 0.8 gather_fusion.5
  407.5 0.9 gather_fusion.7
  408.4 0.8 select_convert_fusion
  409.2 0.8 fusion.15
  410.0 231.0 %all-to-all-done.5 = bf16[8,448,1536]{2,1,0:T(8,128)(2,1)} async-done(((bf16[8,448,1536]{2,1,0:T(8,128)(2,1)}), bf16[8,448,1536]{2,1,0:T(8,128)(2,1)}, u32[]{:S(2)}, u32[]{:S(2)}) %all-to-all-start.5) | async-done | bytes 11010080 | tf_op jit(solution)/shard_map/all_to_all | solution.py:102
  641.1 13.8 %fusion.2 = bf16[4,448,1536]{2,0,1:T(4,128)(2,1)} fusion(bf16[8,448,1536]{2,1,0:T(8,128)(2,1)} %all-to-all-done.5, s32[8]{0:T(128)S(1)} %get-tuple-element.28), kind=kOutput, calls=%fused_computation.13 | convolution fusion | flops 46792736 | bytes 16515104 | tf_op jit(solution)/shard_map/es,sdh->edh/dot_general | solution.py:112
  654.8 3.7 slice_bitcast_fusion
  658.5 1.6 copy.24
  660.1 1.6 copy.25
  661.7 1.6 copy.26
  (37 shorter events, 0.1 us)
Async XLA Ops:
  7.2 14.5 %copy-start = (bf16[4,448,512]{2,1,0:T(8,128)(2,1)S(1)}, bf16[4,448,512]{2,1,0:T(8,128)(2,1)}, u32[]{:S(2)}) copy-start(bf16[4,448,512]{2,1,0:T(8,128)(2,1)} %param.18) | copy-start | bytes 5505028
  7.2 5.8 copy-start.10
  10.8 10.7 %copy-start.11 = (s32[4]{0:T(128)S(1)}, s32[4]{0:T(128)}, u32[]{:S(2)}) copy-start(s32[4]{0:T(128)} %param.17) | copy-start | bytes 52
  15.8 27.2 %all-to-all-start = ((bf16[8,32,896]{2,1,0:T(8,128)(2,1)}), bf16[8,32,896]{2,1,0:T(8,128)(2,1)S(1)}, u32[]{:S(2)}, u32[]{:S(2)}) async-start(bf16[8,32,896]{2,1,0:T(8,128)(2,1)} %bitcast.3), calls=%async_computation | async-start | bytes 917504 | tf_op jit(solution)/shard_map/all_to_all | solution.py:52
  24.2 4.2 copy-start.8
  33.7 5.5 copy-start.2
  33.7 5.6 copy-start.3
  43.0 15.0 %copy-start.6 = (bf16[8,32,896]{2,1,0:T(8,128)(2,1)}, bf16[8,32,896]{2,1,0:T(8,128)(2,1)S(1)}, u32[]{:S(2)}) copy-start(bf16[8,32,896]{2,1,0:T(8,128)(2,1)S(1)} %all-to-all-done) | copy-start | bytes 1376260
  43.0 15.7 %all-to-all-start.3 = ((bf16[8,32,896]{2,1,0:T(8,128)(2,1)}), bf16[8,32,896]{2,1,0:T(8,128)(2,1)S(1)}, u32[]{:S(2)}, u32[]{:S(2)}) async-start(bf16[8,32,896]{2,1,0:T(8,128)(2,1)} %bitcast.12), calls=%async_computation.3 | async-start | bytes 917504 | tf_op jit(solution)/shard_map/all_to_all | solution.py:52
  58.7 0.8 copy-start.7
  59.5 239.1 %all-to-all-start.1 = ((bf16[8,448,1536]{2,1,0:T(8,128)(2,1)}), bf16[8,448,1536]{2,1,0:T(8,128)(2,1)}, u32[]{:S(2)}, u32[]{:S(2)}) async-start(bf16[8,448,1536]{2,1,0:T(8,128)(2,1)} %pad_maximum_fusion), calls=%async_computation.1 | async-start | bytes 22020096 | tf_op jit(solution)/shard_map/all_to_all | solution.py:36
  65.4 28.1 %all-gather.3.cloned.1.call-start = ((), (), s32[]{:S(2)}) async-start(), calls=%async_computation.8 | async-start | bytes 2293760 | tf_op jit(solution)/shard_map/all_gather | solution.py:55
  66.1 238.2 %all-gather.5.cloned.1.call-start = ((), (), s32[]{:S(2)}) async-start(), calls=%async_computation.9 | async-start | bytes 2293760 | tf_op jit(solution)/shard_map/all_gather | solution.py:55
  66.8 282.0 %reduce-scatter.7.cloned.1.call-start = ((), (), s32[]{:S(2)}) async-start(), calls=%async_computation.10 | async-start | bytes 2293760
  313.7 68.2 %reduce-scatter.9.cloned.1.call-start = ((), (), s32[]{:S(2)}) async-start(), calls=%async_computation.11 | async-start | bytes 2293760
  320.3 36.0 %copy-start.4 = (bf16[256,3584]{1,0:T(8,128)(2,1)S(1)}, bf16[256,3584]{1,0:T(8,128)(2,1)}, u32[]{:S(2)}) copy-start(bf16[256,3584]{1,0:T(8,128)(2,1)} %all-gather.5.cloned.1.call-done) | copy-start | bytes 5505028
  350.8 33.0 %all-to-all-start.2 = ((bf16[8,32,896]{2,1,0:T(8,128)(2,1)}), bf16[8,32,896]{2,1,0:T(8,128)(2,1)S(1)}, u32[]{:S(2)}, u32[]{:S(2)}) async-start(bf16[8,32,896]{2,1,0:T(8,128)(2,1)} %bitcast.9), calls=%async_computation.2 | async-start | bytes 917504 | tf_op jit(solution)/shard_map/all_to_all | solution.py:64
  356.3 3.0 copy-start.5
  383.8 16.5 %all-to-all-start.4 = ((bf16[8,32,896]{2,1,0:T(8,128)(2,1)}), bf16[8,32,896]{2,1,0:T(8,128)(2,1)S(1)}, u32[]{:S(2)}, u32[]{:S(2)}) async-start(bf16[8,32,896]{2,1,0:T(8,128)(2,1)} %bitcast.14), calls=%async_computation.4 | async-start | bytes 917504 | tf_op jit(solution)/shard_map/all_to_all | solution.py:64
  398.9 7.7 %copy-start.9 = (s32[128,1]{0,1:T(1,128)S(1)}, s32[128,1]{0,1:T(1,128)}, u32[]{:S(2)}) copy-start(s32[128,1]{0,1:T(1,128)} %param.15) | copy-start | bytes 1540
  400.3 240.7 %all-to-all-start.5 = ((bf16[8,448,1536]{2,1,0:T(8,128)(2,1)}), bf16[8,448,1536]{2,1,0:T(8,128)(2,1)}, u32[]{:S(2)}, u32[]{:S(2)}) async-start(bf16[8,448,1536]{2,1,0:T(8,128)(2,1)} %pad_maximum_fusion.1), calls=%async_computation.5 | async-start | bytes 22020096 | tf_op jit(solution)/shard_map/all_to_all | solution.py:102
  660.1 3.2 copy-start.1
Sparse Core Ops, SparseCore 0:
  68.3 25.1 all-gather.2
  95.6 21.1 all-gather.4
  313.8 35.0 reduce-scatter.6
  352.0 29.8 reduce-scatter.8
where the time goes:
time: 678 us; the launch traced here: 670 us
  waiting for transfers between devices  508 us (75%)
  matrix products  41.1 us (6%)
  local copies, waits for them, and re-layouts  38.4 us (6%)
  starting transfers between devices  34.4 us (5%)
  other arithmetic  33.7 us (5%)
  between operations  14 us (2%)
    all_to_all x1, waiting for transfers between devices, shards(): lax.all_to_all(slot_grad.reshape(ep_size, stored, 3 * hidden), 'ep', spli...  231 us
    all_to_all x1, waiting for transfers between devices, shards(): lax.all_to_all(packed, 'ep', split_axis=0, concat_axis=0, tiled=True)  205 us
    unnamed x6, waiting for transfers between devices  43.4 us
    all_gather x2, waiting for transfers between devices, deliver(): lax.all_gather(moved.reshape(pad_rows, -1), 'grp', axis=1, tiled=True)  26.6 us
    unnamed x31, local copies, waits for them, and re-layouts  15.8 us
    dot_general x1, matrix products, shards(): jnp.einsum('es,sdh->edh', host_onehot, owner_pieces, preferred_element_ty...  13.8 us
  transfers between devices with their start and end apart: 10, of which 7 were waited for; matrix products, arithmetic and copies ran while one was open for 11% of the time, Pallas kernels for 0%

commit v1 on v0

v1 whole, which is shorter than its diff:
```python
import jax
import jax.numpy as jnp
from jax import lax
from jax.sharding import PartitionSpec as P

AXES = ("grp", "ep")


def swap(block, grp_bits, ep_bits):
    grp_size, ep_size = lax.axis_size("grp"), lax.axis_size("ep")
    pairs = [
        (g * ep_size + p, (g ^ grp_bits) * ep_size + (p ^ ep_bits))
        for g in range(grp_size)
        for p in range(ep_size)
    ]
    return lax.ppermute(block, AXES, pairs)


def to_plane(block, offset):
    grp_size, ep_size = lax.axis_size("grp"), lax.axis_size("ep")
    return [
        (g * ep_size + p, ((p // 2) ^ offset) * ep_size + 2 * g + p % 2)
        for g in range(grp_size)
        for p in range(ep_size)
    ]


def f32(a):
    return a.astype(jnp.float32)


def spread(rows):
    grp_size = lax.axis_size("grp")
    y = lax.axis_index("ep") % 2
    tok = rows.shape[0]
    half = rows.shape[1] // 2
    mine = lax.dynamic_slice_in_dim(rows, y * half, half, 1)
    other = lax.dynamic_slice_in_dim(rows, (1 - y) * half, half, 1)
    got = swap(other, 0, 1)
    per = grp_size // 2
    size = tok // per
    pieces = []
    for k in range(grp_size):
        source = mine if k < per else got
        piece = lax.slice_in_dim(source, (k % per) * size, (k % per + 1) * size, axis=0)
        pieces.append(lax.ppermute(piece, AXES, to_plane(piece, k)))
    held = jnp.stack(pieces)[None]
    order = [0]
    bit = grp_size // 2
    while bit:
        held = jnp.concatenate([held, swap(held, bit, 0)])
        order = order + [m ^ bit for m in order]
        bit //= 2
    return held, order


def unspread(parts, order):
    grp_size = lax.axis_size("grp")
    y = lax.axis_index("ep") % 2
    bit = 1
    held = parts
    while bit < grp_size:
        n = held.shape[0] // 2
        got = swap(held[n:], bit, 0)
        held = (f32(held[:n]) + f32(got)).astype(jnp.bfloat16)
        bit *= 2
    held = held[0]
    pieces = []
    for k in range(grp_size):
        back = [(b, a) for a, b in to_plane(None, k)]
        pieces.append(lax.ppermute(held[k], AXES, back))
    per = grp_size // 2
    mine = jnp.concatenate(pieces[:per])
    got = swap(jnp.concatenate(pieces[per:]), 0, 1)
    first = jnp.where(y == 0, mine, got)
    second = jnp.where(y == 0, got, mine)
    return jnp.concatenate([first, second], axis=1)


def scatter_sum(parts):
    got = swap(parts[1], 0, 1)
    zs = parts.shape[1]
    held = [(f32(parts[0, d]) + f32(got[d])) for d in range(zs)]
    total = held[0]
    for d in range(1, zs):
        total = total + f32(swap(held[d].astype(jnp.bfloat16), 0, 2 * d))
    return total


def gather(own):
    zs = lax.axis_size("ep") // 2
    line = jnp.stack([own] + [swap(own, 0, 2 * d) for d in range(1, zs)])
    return jnp.stack([line, swap(line, 0, 1)])


def shards(tokens, routes, route_weights, hot_experts, w_gate, w_up, w_down, cotangent):
    grp_size, ep_size = lax.axis_size("grp"), lax.axis_size("ep")
    zs = ep_size // 2
    g, p = lax.axis_index("grp"), lax.axis_index("ep")
    tok = tokens.shape[0]
    count, stored, hidden = w_gate.shape
    total = tok * ep_size
    slot_host = jnp.concatenate([jnp.arange(count, dtype=jnp.int32), hot_experts])
    slots = jnp.arange(slot_host.shape[0], dtype=jnp.int32)
    expert = jnp.sum(jnp.where(routes == slots[None, :], slot_host[None, :], 0), axis=1)
    experts = lax.all_gather(expert, "ep", axis=0)
    rel = jnp.arange(ep_size, dtype=jnp.int32).reshape(zs, 2).T.reshape(-1)
    expert_rel = jnp.take(experts, rel ^ p, axis=0).reshape(total)
    mask = expert_rel[:, None] == jnp.arange(count, dtype=jnp.int32)[None, :]

    def masked(rows):
        return jnp.where(mask[:, :, None], rows[:, None, :], jnp.zeros((), rows.dtype))

    per = grp_size // 2
    shift = g ^ (p // 2)

    def place_of(order):
        at = {m: i for i, m in enumerate(order)}
        return jnp.array([at[m] for m in range(grp_size)], jnp.int32)

    def to_relative(held, order):
        place = place_of(order)
        cols = []
        for k in range(grp_size):
            idx = place[shift ^ jnp.arange(zs, dtype=jnp.int32) ^ k]
            cols.append(jnp.take(held[:, k], idx, axis=0))
        both = [jnp.stack(cols[a * per : (a + 1) * per], axis=1) for a in range(2)]
        return jnp.stack(both).reshape(total, -1)

    def from_relative(rows, order):
        blocks = rows.reshape(2, zs, per, -1, rows.shape[-1])
        cols = []
        for k in range(grp_size):
            idx = shift ^ jnp.array(order, jnp.int32) ^ k
            cols.append(jnp.take(blocks[k // per, :, k % per], idx, axis=0))
        return jnp.stack(cols, axis=1)

    def dot(a, b, ca, cb):
        return lax.dot_general(a, b, ((ca, cb), ((), ())), preferred_element_type=jnp.float32)

    def half(a):
        return a.astype(jnp.bfloat16)

    x_held, order = spread(tokens)
    x_rows = to_relative(x_held, order)
    x_mask = masked(x_rows)

    def blocks(rows):
        return half(rows).reshape(2, zs, tok, -1)

    gate_pre = scatter_sum(blocks(dot(x_mask, w_gate, (1, 2), (0, 1))))
    up_pre = scatter_sum(blocks(dot(x_mask, w_up, (1, 2), (0, 1))))
    dz = half(f32(cotangent) * route_weights)
    dz_held, _ = spread(dz)
    dz_rows = to_relative(dz_held, order)
    dz_mask = masked(dz_rows)
    act_grad = scatter_sum(blocks(dot(dz_mask, w_down, (1, 2), (0, 2))))
    sg = jax.nn.sigmoid(gate_pre)
    act = half(gate_pre * sg * up_pre)
    gate_grad = half(act_grad * up_pre * sg * (1.0 + gate_pre * (1.0 - sg)))
    up_grad = half(act_grad * gate_pre * sg)
    act_rows = gather(act).reshape(total, hidden)
    act_mask = masked(act_rows)
    out_parts = half(dot(act_mask, w_down, (1, 2), (0, 1)))
    layer_output = half(f32(unspread(from_relative(out_parts, order), order)) * route_weights)
    gg_rows = gather(gate_grad).reshape(total, hidden)
    ug_rows = gather(up_grad).reshape(total, hidden)
    tok_parts = dot(masked(gg_rows), w_gate, (1, 2), (0, 2))
    tok_parts = half(tok_parts + dot(masked(ug_rows), w_up, (1, 2), (0, 2)))
    grad_tokens = unspread(from_relative(tok_parts, order), order)
    grad_down = half(dot(act_mask, dz_rows, (0,), (0,)))
    grad_gate = half(dot(x_mask, gg_rows, (0,), (0,)))
    grad_up = half(dot(x_mask, ug_rows, (0,), (0,)))
    return (layer_output, grad_tokens, grad_gate, grad_up, grad_down)


def solution(mesh):
    placed = (
        P("ep", "grp"),
        P("ep", None),
        P("ep", None),
        P(),
        P(None, "ep", "grp"),
        P(None, "ep", "grp"),
        P(None, "grp", "ep"),
        P("ep", "grp"),
    )
    return jax.shard_map(
        shards,
        mesh=mesh,
        in_specs=placed,
        out_specs=(
            P("ep", "grp"),
            P("ep", "grp"),
            P(None, "ep", "grp"),
            P(None, "ep", "grp"),
            P(None, "grp", "ep"),
        ),
        check_vma=False,
    )
```

time: 678 us -> 265 us (0.39); the launches traced: 670 us -> 264 us
  waiting for transfers between devices: 508 us -> 76.2 us
  starting transfers between devices: 34.4 us -> 88.6 us
  other arithmetic: 33.7 us -> 20.4 us
  between operations: 14 us -> 1.67 us
  matrix products: 41.1 us -> 29.9 us
  blocking collectives: 0 us -> 10.4 us
    all_to_all x6 -> x0, waiting for transfers between devices: 438 us -> none  [the longest x1 231 us: shards(): lax.all_to_all(slot_grad.reshape(ep_size, stored, 3 * hidden), 'ep', spli...]
    ppermute x0 -> x52, starting transfers between devices: none -> 88.6 us  [the longest x36 43.2 us: swap(): return lax.ppermute(block, AXES, pairs)]
    ppermute x0 -> x52, waiting for transfers between devices: none -> 76.2 us  [the longest x36 67 us: swap(): return lax.ppermute(block, AXES, pairs)]
    unnamed x6 -> x0, waiting for transfers between devices: 43.4 us -> none
    all_to_all x6 -> x0, starting transfers between devices: 34.1 us -> none  [the longest x2 11 us: deliver(): lax.all_to_all(send_rows.reshape(ep_size, capacity, -1), 'ep', split_axis...]
    all_gather x2 -> x0, waiting for transfers between devices: 26.6 us -> none  [deliver(): lax.all_gather(moved.reshape(pad_rows, -1), 'grp', axis=1, tiled=True)]
    concatenate x3 -> x8, other arithmetic: 19.1 us -> 1.95 us  [the longest x1 0.79 us: unspread(): return jnp.concatenate([first, second], axis=1)]
    another operation x1 -> x22, other arithmetic: 0.17 us -> 13 us  [the longest x6 6.58 us: gather(): return jnp.stack([line, swap(line, 0, 1)])]
  transfers between devices with their start and end apart: 10 -> 52, of which waited for: 7 -> 25; matrix products, arithmetic and copies ran while one was open for 11% -> 17% of each run, Pallas kernels for 0% -> 0%
where the time goes in v1:
time: 265 us; the launch traced here: 264 us
  starting transfers between devices  88.6 us (33%)
  waiting for transfers between devices  76.2 us (29%)
  local copies, waits for them, and re-layouts  36.8 us (14%)
  matrix products  29.9 us (11%)
  other arithmetic  20.4 us (8%)
  blocking collectives  10.4 us (4%)
    ppermute x36, waiting for transfers between devices, swap(): return lax.ppermute(block, AXES, pairs)  67 us
    ppermute x36, starting transfers between devices, swap(): return lax.ppermute(block, AXES, pairs)  43.2 us
    dot_general x9, matrix products, dot(): lax.dot_general(a, b, ((ca, cb), ((), ())), preferred_element_type=jnp.fl...  29.9 us
    ppermute x8, starting transfers between devices, spread(): pieces.append(lax.ppermute(piece, AXES, to_plane(piece, k)))  24.2 us
    ppermute x8, starting transfers between devices, unspread(): pieces.append(lax.ppermute(held[k], AXES, back))  21.2 us
    all_gather x1, blocking collectives, shards(): experts = lax.all_gather(expert, 'ep', axis=0)  10.4 us
    gather x8, local copies, waits for them, and re-layouts, to_relative(): cols.append(jnp.take(held[:, k], idx, axis=0))  8.77 us
    gather x8, local copies, waits for them, and re-layouts, from_relative(): cols.append(jnp.take(blocks[k // per, :, k % per], idx, axis=0))  7.36 us
  transfers between devices with their start and end apart: 52, of which 25 were waited for; matrix products, arithmetic and copies ran while one was open for 17% of the time, Pallas kernels for 0%

profile of v1, /device:TPU:17, one launch (start us, length us, event | category | flops | bytes accessed | tf_op | source)
XLA Modules:
  0.0 263.9 jit_solution(11399132146192408780)
XLA Ops:
  5.3 4.3 %collective-permute-start = (bf16[64,448]{1,0:T(8,128)(2,1)S(1)}, bf16[64,448]{1,0:T(8,128)(2,1)S(1)}, u32[]{:S(2)}, u32[]{:S(2)}) collective-permute-start(bf16[64,448]{1,0:T(8,128)(2,1)S(1)} %get-tuple-element.60), channel_id=1, source_target_pairs={{0,0},{1,1},{2,8},{3,9},{4,16},{5,17},{6,24},{7,25},{8,2},{9,3},{1... | collective-permute-start | bytes 172040 | tf_op jit(solution)/shard_map/ppermute | solution.py:46
  11.1 1.8 collective-permute-start.27
  14.6 10.4 %all-gather.1 = s32[8,1,128]{2,1,0:T(1,128)S(1)} all-gather(s32[1,1,128]{2,1,0:T(1,128)S(1)} %bitcast.360), channel_id=2, replica_groups=mesh['grp'=4,'ep'=8] {'ep'}, dimensions={0}, use_global_device_ids=true | all-gather | bytes 4608 | tf_op jit(solution)/shard_map/all_gather | solution.py:106
  29.0 3.0 %collective-permute-start.4 = (bf16[64,448]{1,0:T(8,128)(2,1)S(1)}, bf16[64,448]{1,0:T(8,128)(2,1)S(1)}, u32[]{:S(2)}, u32[]{:S(2)}) collective-permute-start(bf16[64,448]{1,0:T(8,128)(2,1)S(1)} %get-tuple-element.65), channel_id=1, source_target_pairs={{0,24},{1,25},{2,16},{3,17},{4,8},{5,9},{6,0},{7,1},{8,26},{9,27},... | collective-permute-start | bytes 172040 | tf_op jit(solution)/shard_map/ppermute | solution.py:46
  31.9 6.8 %collective-permute-start.3 = (bf16[64,448]{1,0:T(8,128)(2,1)S(1)}, bf16[64,448]{1,0:T(8,128)(2,1)S(1)}, u32[]{:S(2)}, u32[]{:S(2)}) collective-permute-start(bf16[64,448]{1,0:T(8,128)(2,1)S(1)} %get-tuple-element.64), channel_id=1, source_target_pairs={{0,16},{1,17},{2,24},{3,25},{4,0},{5,1},{6,8},{7,9},{8,18},{9,19},... | collective-permute-start | bytes 172040 | tf_op jit(solution)/shard_map/ppermute | solution.py:46
  38.8 1.9 collective-permute-start.26
  40.8 5.2 %collective-permute-start.29 = (bf16[64,448]{1,0:T(8,128)(2,1)S(1)}, bf16[64,448]{1,0:T(8,128)(2,1)S(1)}, u32[]{:S(2)}, u32[]{:S(2)}) collective-permute-start(bf16[64,448]{1,0:T(8,128)(2,1)S(1)} %get-tuple-element.66), channel_id=1, source_target_pairs={{0,16},{1,17},{2,24},{3,25},{4,0},{5,1},{6,8},{7,9},{8,18},{9,19},... | collective-permute-start | bytes 172040 | tf_op jit(solution)/shard_map/ppermute | solution.py:46
  46.2 2.0 collective-permute-done.26
  49.6 1.4 collective-permute-done.29
  51.0 1.8 collective-permute-start.31
  54.1 2.2 collective-permute-start.6
  56.3 3.4 %collective-permute-done.31 = bf16[1,4,64,448]{3,2,1,0:T(8,128)(2,1)S(1)} collective-permute-done((bf16[1,4,64,448]{3,2,1,0:T(8,128)(2,1)S(1)}, bf16[1,4,64,448]{3,2,1,0:T(8,128)(2,1)S(1)}, u32[]{:S(2)}, u32[]{:S(2)}) %collective-permute-start.31) | collective-permute-done | bytes 229408 | tf_op jit(solution)/shard_map/ppermute | solution.py:16
  64.2 2.2 gather_fusion.16
  68.9 1.5 gather_fusion.14
  71.0 1.5 gather_fusion.13
  72.5 1.8 select_bitcast_fusion.12
  74.3 1.8 select_bitcast_fusion.13
  78.0 1.4 copy.53
  79.5 3.9 %bitcast_convert_fusion = bf16[1024,512]{1,0:T(8,128)(2,1)S(1)} fusion(bf16[4,512,448]{1,2,0:T(8,128)(2,1)} %param.26, pred[1024,4]{0,1:T(4,128)(4,1)S(1)} %iota_compare_fusion, bf16[1024,448]{0,1:T(8,128)(2,1)} %copy.53), kind=kOutput, calls=%fused_computation.48 | convolution fusion | flops 1881407488 | bytes 3805184 | tf_op jit(solution)/shard_map/dot_general | solution.py:139
  86.1 2.2 copy.47
  88.3 3.4 %bitcast_convert_fusion.2 = bf16[1024,512]{1,0:T(8,128)(2,1)S(1)} fusion(bf16[4,448,512]{2,1,0:T(8,128)(2,1)S(1)} %copy-done, pred[1024,4]{0,1:T(4,128)(4,1)S(1)} %iota_compare_fusion, bf16[1024,448]{0,1:T(8,128)(2,1)} %copy.47), kind=kOutput, calls=%fused_computation.50 | convolution fusion | flops 1881407488 | bytes 3805184 | tf_op jit(solution)/shard_map/dot_general | solution.py:139
  92.9 2.1 bitcast_convert_fusion.1
  95.5 2.1 collective-permute-done.33
  98.4 2.3 collective-permute-start.35
  100.9 8.0 %collective-permute-done.7 = bf16[4,128,512]{2,1,0:T(8,128)(2,1)S(1)} collective-permute-done((bf16[4,128,512]{2,1,0:T(8,128)(2,1)S(1)}, bf16[4,128,512]{2,1,0:T(8,128)(2,1)S(1)}, u32[]{:S(2)}, u32[]{:S(2)}) %collective-permute-start.7) | collective-permute-done | bytes 524320 | tf_op jit(solution)/shard_map/ppermute | solution.py:16
  109.6 10.5 %collective-permute-done.11 = bf16[4,128,512]{2,1,0:T(8,128)(2,1)S(1)} collective-permute-done((bf16[4,128,512]{2,1,0:T(8,128)(2,1)S(1)}, bf16[4,128,512]{2,1,0:T(8,128)(2,1)S(1)}, u32[]{:S(2)}, u32[]{:S(2)}) %collective-permute-start.11) | collective-permute-done | bytes 524320 | tf_op jit(solution)/shard_map/ppermute | solution.py:16
  120.1 1.9 collective-permute-start.9
  122.9 2.8 %collective-permute-start.13 = (bf16[128,512]{1,0:T(8,128)(2,1)S(1)}, bf16[128,512]{1,0:T(8,128)(2,1)S(1)}, u32[]{:S(2)}, u32[]{:S(2)}) collective-permute-start(bf16[128,512]{1,0:T(8,128)(2,1)S(1)} %get-tuple-element.20), channel_id=1, source_target_pairs={{0,4},{1,5},{2,6},{3,7},{4,0},{5,1},{6,2},{7,3},{8,12},{9,13},{10,... | collective-permute-start | bytes 393224 | tf_op jit(solution)/shard_map/ppermute | solution.py:16
  125.7 1.8 collective-permute-done.9
  128.4 8.4 %collective-permute-done.14 = bf16[128,512]{1,0:T(8,128)(2,1)S(1)} collective-permute-done((bf16[128,512]{1,0:T(8,128)(2,1)S(1)}, bf16[128,512]{1,0:T(8,128)(2,1)S(1)}, u32[]{:S(2)}, u32[]{:S(2)}) %collective-permute-start.14) | collective-permute-done | bytes 131104 | tf_op jit(solution)/shard_map/ppermute | solution.py:16
  136.8 1.7 collective-permute-done.13
  139.2 4.0 %collective-permute-start.38 = (bf16[128,512]{1,0:T(8,128)(2,1)S(1)}, bf16[128,512]{1,0:T(8,128)(2,1)S(1)}, u32[]{:S(2)}, u32[]{:S(2)}) collective-permute-start(bf16[128,512]{1,0:T(8,128)(2,1)S(1)} %get-tuple-element.16), channel_id=1, source_target_pairs={{0,4},{1,5},{2,6},{3,7},{4,0},{5,1},{6,2},{7,3},{8,12},{9,13},{10,... | collective-permute-start | bytes 393224 | tf_op jit(solution)/shard_map/ppermute | solution.py:16
  144.4 2.4 collective-permute-start.42
  146.8 5.7 %collective-permute-done.38 = bf16[128,512]{1,0:T(8,128)(2,1)S(1)} collective-permute-done((bf16[128,512]{1,0:T(8,128)(2,1)S(1)}, bf16[128,512]{1,0:T(8,128)(2,1)S(1)}, u32[]{:S(2)}, u32[]{:S(2)}) %collective-permute-start.38) | collective-permute-done | bytes 131104 | tf_op jit(solution)/shard_map/ppermute | solution.py:16
  153.5 7.5 %collective-permute-start.41 = (bf16[128,512]{1,0:T(8,128)(2,1)}, bf16[128,512]{1,0:T(8,128)(2,1)}, u32[]{:S(2)}, u32[]{:S(2)}) collective-permute-start(bf16[128,512]{1,0:T(8,128)(2,1)} %get-tuple-element.6), channel_id=1, source_target_pairs={{0,2},{1,3},{2,0},{3,1},{4,6},{5,7},{6,4},{7,5},{8,10},{9,11},{10,... | collective-permute-start | bytes 393224 | tf_op jit(solution)/shard_map/ppermute | solution.py:16
  161.3 1.9 collective-permute-start.16
  163.9 1.9 collective-permute-start.15
  165.9 2.8 %collective-permute-done.41 = bf16[128,512]{1,0:T(8,128)(2,1)} collective-permute-done((bf16[128,512]{1,0:T(8,128)(2,1)}, bf16[128,512]{1,0:T(8,128)(2,1)}, u32[]{:S(2)}, u32[]{:S(2)}) %collective-permute-start.41) | collective-permute-done | bytes 131104 | tf_op jit(solution)/shard_map/ppermute | solution.py:16
  170.0 1.7 collective-permute-done.17
  171.7 2.1 collective-permute-done.16
  173.9 2.1 fusion.99
  178.2 3.2 %fusion.14 = f32[1024,448,1]{0,1,2:T(8,128)S(1)} fusion(bf16[4,448,512]{2,1,0:T(8,128)(2,1)S(1)} %copy-done, pred[1024,4]{0,1:T(4,128)(4,1)S(1)} %copy-done.22, bf16[1024,512]{1,0:T(8,128)(2,1)S(1)} %bitcast.331), kind=kOutput, calls=%fused_computation.35 | convolution fusion | flops 1881145344 | bytes 4722688 | tf_op jit(solution)/shard_map/dot_general | solution.py:139
  183.9 3.8 %fusion.35 = bf16[1024,448]{0,1:T(8,128)(2,1)} fusion(f32[1024,448,1]{0,1,2:T(8,128)S(1)} %fusion.14, bf16[4,448,512]{2,1,0:T(8,128)(2,1)S(1)} %copy-done.31, pred[1024,4]{0,1:T(4,128)(4,1)S(1)} %copy-done.22, bf16[1024,512]{1,0:T(8,128)(2,1)S(1)} %bitcast.333), kind=kOutput, calls=%fused_computation.60 | convolution fusion | flops 1882062848 | bytes 5640192 | tf_op jit(solution)/shard_map/dot_general | solution.py:139
  187.8 1.5 copy.54
  190.1 4.1 %collective-permute-done.18 = bf16[4,128,512]{2,1,0:T(8,128)(2,1)} collective-permute-done((bf16[4,128,512]{2,1,0:T(8,128)(2,1)}, bf16[4,128,512]{2,1,0:T(8,128)(2,1)}, u32[]{:S(2)}, u32[]{:S(2)}) %collective-permute-start.18) | collective-permute-done | bytes 524320 | tf_op jit(solution)/shard_map/ppermute | solution.py:16
  196.3 3.3 %bitcast_convert_fusion.3 = bf16[1024,448]{0,1:T(8,128)(2,1)} fusion(bf16[4,512,448]{1,2,0:T(8,128)(2,1)S(1)} %copy-done.32, pred[1024,4]{0,1:T(4,128)(4,1)S(1)} %copy-done.23, bf16[1024,512]{1,0:T(8,128)(2,1)S(1)} %bitcast.335), kind=kOutput, calls=%fused_computation.61 | convolution fusion | flops 1881604096 | bytes 3805184 | tf_op jit(solution)/shard_map/dot_general | solution.py:139
  199.6 1.7 copy.48
  202.8 1.5 gather_fusion.12
  206.0 1.5 gather_fusion.10
  208.1 1.5 gather_fusion.9
  210.4 1.5 collective-permute-start.19
  212.3 3.3 %fusion.49 = bf16[4,448,512]{2,1,0:T(8,128)(2,1)} fusion(bf16[1024,512,1]{1,0,2:T(8,128)(2,1)S(1)} %bitcast.332, pred[1024,4]{0,1:T(4,128)(4,1)S(1)} %copy-done.23, bf16[1024,448]{0,1:T(8,128)(2,1)S(1)} %copy-done.18), kind=kOutput, calls=%fused_computation.73 | convolution fusion | flops 1881800704 | bytes 3805184 | tf_op jit(solution)/shard_map/dot_general | solution.py:139
  215.6 3.4 %fusion.46 = bf16[4,512,448]{1,2,0:T(8,128)(2,1)} fusion(bf16[1024,448,1]{1,0,2:T(8,128)(2,1)S(1)} %bitcast.321, pred[1024,4]{0,1:T(4,128)(4,1)S(1)} %copy-done.23, bf16[1024,512]{1,0:T(8,128)(2,1)S(1)} %bitcast.336), kind=kOutput, calls=%fused_computation.72 | convolution fusion | flops 1882062848 | bytes 3805184 | tf_op jit(solution)/shard_map/dot_general | solution.py:139
  219.0 3.3 %fusion.52 = bf16[4,448,512]{2,1,0:T(8,128)(2,1)} fusion(bf16[1024,512,1]{1,0,2:T(8,128)(2,1)S(1)} %bitcast.334, pred[1024,4]{0,1:T(4,128)(4,1)S(1)} %copy-done.23, bf16[1024,448]{0,1:T(8,128)(2,1)S(1)} %copy-done.18), kind=kOutput, calls=%fused_computation.74 | convolution fusion | flops 1881800704 | bytes 3805184 | tf_op jit(solution)/shard_map/dot_general | solution.py:139
  224.3 5.0 %collective-permute-done.20 = bf16[1,4,64,448]{3,2,0,1:T(8,128)(2,1)S(1)} collective-permute-done((bf16[1,4,64,448]{3,2,0,1:T(8,128)(2,1)S(1)}, bf16[1,4,64,448]{3,2,0,1:T(8,128)(2,1)S(1)}, u32[]{:S(2)}, u32[]{:S(2)}) %collective-permute-start.20) | collective-permute-done | bytes 229408 | tf_op jit(solution)/shard_map/ppermute | solution.py:16
  229.4 5.7 %collective-permute-start.21 = (bf16[64,448]{1,0:T(8,128)(2,1)S(1)}, bf16[64,448]{1,0:T(8,128)(2,1)S(1)}, u32[]{:S(2)}, u32[]{:S(2)}) collective-permute-start(bf16[64,448]{1,0:T(8,128)(2,1)S(1)} %get-tuple-element.59), channel_id=1, source_target_pairs={{0,0},{1,1},{8,2},{9,3},{16,4},{17,5},{24,6},{25,7},{2,8},{3,9},{1... | collective-permute-start | bytes 172040 | tf_op jit(solution)/shard_map/ppermute | solution.py:71
  235.2 3.3 %collective-permute-start.22 = (bf16[64,448]{1,0:T(8,128)(2,1)S(1)}, bf16[64,448]{1,0:T(8,128)(2,1)S(1)}, u32[]{:S(2)}, u32[]{:S(2)}) collective-permute-start(bf16[64,448]{1,0:T(8,128)(2,1)S(1)} %get-tuple-element.57), channel_id=1, source_target_pairs={{8,0},{9,1},{0,2},{1,3},{24,4},{25,5},{16,6},{17,7},{10,8},{11,9},... | collective-permute-start | bytes 172040 | tf_op jit(solution)/shard_map/ppermute | solution.py:71
  239.2 2.3 collective-permute-start.47
  241.5 2.1 collective-permute-done.24
  243.6 2.1 collective-permute-done.23
  245.7 1.7 collective-permute-start.49
  247.4 7.5 %collective-permute-start.48 = (bf16[64,448]{1,0:T(8,128)(2,1)S(1)}, bf16[64,448]{1,0:T(8,128)(2,1)S(1)}, u32[]{:S(2)}, u32[]{:S(2)}) collective-permute-start(bf16[64,448]{1,0:T(8,128)(2,1)S(1)} %get-tuple-element.51), channel_id=1, source_target_pairs={{8,0},{9,1},{0,2},{1,3},{24,4},{25,5},{16,6},{17,7},{10,8},{11,9},... | collective-permute-start | bytes 172040 | tf_op jit(solution)/shard_map/ppermute | solution.py:71
  256.7 3.8 %collective-permute-done.25 = bf16[128,448]{1,0:T(8,128)(2,1)S(1)} collective-permute-done((bf16[128,448]{1,0:T(8,128)(2,1)S(1)}, bf16[128,448]{1,0:T(8,128)(2,1)S(1)}, u32[]{:S(2)}, u32[]{:S(2)}) %collective-permute-start.25) | collective-permute-done | bytes 114720 | tf_op jit(solution)/shard_map/ppermute | solution.py:16
  261.3 1.7 collective-permute-done.51
  (243 shorter events, 55.4 us)
Async XLA Ops:
  0.6 87.7 %copy-start = (bf16[4,448,512]{2,1,0:T(8,128)(2,1)S(1)}, bf16[4,448,512]{2,1,0:T(8,128)(2,1)}, u32[]{:S(2)}) copy-start(bf16[4,448,512]{2,1,0:T(8,128)(2,1)} %param.24) | copy-start | bytes 5505028
  0.6 25.1 %copy-start.2 = (s32[4]{0:T(128)S(1)}, s32[4]{0:T(128)}, u32[]{:S(2)}) copy-start(s32[4]{0:T(128)} %constant.83.clone) | copy-start | bytes 52
  1.8 27.1 %collective-permute-start.2 = (bf16[128,448]{1,0:T(8,128)(2,1)S(1)}, bf16[128,448]{1,0:T(8,128)(2,1)S(1)}, u32[]{:S(2)}, u32[]{:S(2)}) collective-permute-start(bf16[128,448]{1,0:T(8,128)(2,1)S(1)} %constant_dynamic-slice_fusion.2), channel_id=1, source_target_pairs={{0,1},{1,0},{2,3},{3,2},{4,5},{5,4},{6,7},{7,6},{8,9},{9,8},{10,11... | collective-permute-start | bytes 344072 | tf_op jit(solution)/shard_map/ppermute | solution.py:16
  4.2 34.6 %collective-permute-start.1 = (bf16[64,448]{1,0:T(8,128)(2,1)S(1)}, bf16[64,448]{1,0:T(8,128)(2,1)S(1)}, u32[]{:S(2)}, u32[]{:S(2)}) collective-permute-start(bf16[64,448]{1,0:T(8,128)(2,1)S(1)} %get-tuple-element.61), channel_id=1, source_target_pairs={{0,8},{1,9},{2,0},{3,1},{4,24},{5,25},{6,16},{7,17},{8,10},{9,11},... | collective-permute-start | bytes 172040 | tf_op jit(solution)/shard_map/ppermute | solution.py:46
  5.3 35.4 %collective-permute-start = (bf16[64,448]{1,0:T(8,128)(2,1)S(1)}, bf16[64,448]{1,0:T(8,128)(2,1)S(1)}, u32[]{:S(2)}, u32[]{:S(2)}) collective-permute-start(bf16[64,448]{1,0:T(8,128)(2,1)S(1)} %get-tuple-element.60), channel_id=1, source_target_pairs={{0,0},{1,1},{2,8},{3,9},{4,16},{5,17},{6,24},{7,25},{8,2},{9,3},{1... | collective-permute-start | bytes 172040 | tf_op jit(solution)/shard_map/ppermute | solution.py:46
  10.8 21.1 %collective-permute-start.28 = (bf16[128,448]{1,0:T(8,128)(2,1)S(1)}, bf16[128,448]{1,0:T(8,128)(2,1)S(1)}, u32[]{:S(2)}, u32[]{:S(2)}) collective-permute-start(bf16[128,448]{1,0:T(8,128)(2,1)S(1)} %constant_dynamic-slice_fusion), channel_id=1, source_target_pairs={{0,1},{1,0},{2,3},{3,2},{4,5},{5,4},{6,7},{7,6},{8,9},{9,8},{10,11... | collective-permute-start | bytes 344072 | tf_op jit(solution)/shard_map/ppermute | solution.py:16
  11.1 35.0 %collective-permute-start.27 = (bf16[64,448]{1,0:T(8,128)(2,1)S(1)}, bf16[64,448]{1,0:T(8,128)(2,1)S(1)}, u32[]{:S(2)}, u32[]{:S(2)}) collective-permute-start(bf16[64,448]{1,0:T(8,128)(2,1)S(1)} %get-tuple-element.63), channel_id=1, source_target_pairs={{0,8},{1,9},{2,0},{3,1},{4,24},{5,25},{6,16},{7,17},{8,10},{9,11},... | collective-permute-start | bytes 172040 | tf_op jit(solution)/shard_map/ppermute | solution.py:46
  25.7 67.2 %copy-start.21 = (pred[1024,4]{0,1:T(4,128)(4,1)}, pred[1024,4]{0,1:T(4,128)(4,1)S(1)}, u32[]{:S(2)}) copy-start(pred[1024,4]{0,1:T(4,128)(4,1)S(1)} %iota_compare_fusion) | copy-start | bytes 12292
  29.0 11.8 %collective-permute-start.4 = (bf16[64,448]{1,0:T(8,128)(2,1)S(1)}, bf16[64,448]{1,0:T(8,128)(2,1)S(1)}, u32[]{:S(2)}, u32[]{:S(2)}) collective-permute-start(bf16[64,448]{1,0:T(8,128)(2,1)S(1)} %get-tuple-element.65), channel_id=1, source_target_pairs={{0,24},{1,25},{2,16},{3,17},{4,8},{5,9},{6,0},{7,1},{8,26},{9,27},... | collective-permute-start | bytes 172040 | tf_op jit(solution)/shard_map/ppermute | solution.py:46
  31.9 14.1 %collective-permute-start.3 = (bf16[64,448]{1,0:T(8,128)(2,1)S(1)}, bf16[64,448]{1,0:T(8,128)(2,1)S(1)}, u32[]{:S(2)}, u32[]{:S(2)}) collective-permute-start(bf16[64,448]{1,0:T(8,128)(2,1)S(1)} %get-tuple-element.64), channel_id=1, source_target_pairs={{0,16},{1,17},{2,24},{3,25},{4,0},{5,1},{6,8},{7,9},{8,18},{9,19},... | collective-permute-start | bytes 172040 | tf_op jit(solution)/shard_map/ppermute | solution.py:46
  38.8 9.4 %collective-permute-start.26 = (bf16[64,448]{1,0:T(8,128)(2,1)S(1)}, bf16[64,448]{1,0:T(8,128)(2,1)S(1)}, u32[]{:S(2)}, u32[]{:S(2)}) collective-permute-start(bf16[64,448]{1,0:T(8,128)(2,1)S(1)} %get-tuple-element.62), channel_id=1, source_target_pairs={{0,0},{1,1},{2,8},{3,9},{4,16},{5,17},{6,24},{7,25},{8,2},{9,3},{1... | collective-permute-start | bytes 172040 | tf_op jit(solution)/shard_map/ppermute | solution.py:46
  40.7 8.8 %collective-permute-start.30 = (bf16[64,448]{1,0:T(8,128)(2,1)S(1)}, bf16[64,448]{1,0:T(8,128)(2,1)S(1)}, u32[]{:S(2)}, u32[]{:S(2)}) collective-permute-start(bf16[64,448]{1,0:T(8,128)(2,1)S(1)} %get-tuple-element.67), channel_id=1, source_target_pairs={{0,24},{1,25},{2,16},{3,17},{4,8},{5,9},{6,0},{7,1},{8,26},{9,27},... | collective-permute-start | bytes 172040 | tf_op jit(solution)/shard_map/ppermute | solution.py:46
  40.8 10.2 %collective-permute-start.29 = (bf16[64,448]{1,0:T(8,128)(2,1)S(1)}, bf16[64,448]{1,0:T(8,128)(2,1)S(1)}, u32[]{:S(2)}, u32[]{:S(2)}) collective-permute-start(bf16[64,448]{1,0:T(8,128)(2,1)S(1)} %get-tuple-element.66), channel_id=1, source_target_pairs={{0,16},{1,17},{2,24},{3,25},{4,0},{5,1},{6,8},{7,9},{8,18},{9,19},... | collective-permute-start | bytes 172040 | tf_op jit(solution)/shard_map/ppermute | solution.py:46
  46.0 7.9 %collective-permute-start.5 = (bf16[1,4,64,448]{3,2,1,0:T(8,128)(2,1)S(1)}, bf16[1,4,64,448]{3,2,1,0:T(8,128)(2,1)S(1)}, u32[]{:S(2)}, u32[]{:S(2)}) collective-permute-start(bf16[1,4,64,448]{3,2,1,0:T(8,128)(2,1)S(1)} %maximum_bitcast_fusion.4), channel_id=1, source_target_pairs={{0,16},{1,17},{2,18},{3,19},{4,20},{5,21},{6,22},{7,23},{8,24},{9,... | collective-permute-start | bytes 688136 | tf_op jit(solution)/shard_map/ppermute | solution.py:16
  51.0 8.7 %collective-permute-start.31 = (bf16[1,4,64,448]{3,2,1,0:T(8,128)(2,1)S(1)}, bf16[1,4,64,448]{3,2,1,0:T(8,128)(2,1)S(1)}, u32[]{:S(2)}, u32[]{:S(2)}) collective-permute-start(bf16[1,4,64,448]{3,2,1,0:T(8,128)(2,1)S(1)} %maximum_bitcast_fusion.5), channel_id=1, source_target_pairs={{0,16},{1,17},{2,18},{3,19},{4,20},{5,21},{6,22},{7,23},{8,24},{9,... | collective-permute-start | bytes 688136 | tf_op jit(solution)/shard_map/ppermute | solution.py:16
  54.1 7.0 %collective-permute-start.6 = (bf16[2,4,64,448]{3,2,1,0:T(8,128)(2,1)S(1)}, bf16[2,4,64,448]{3,2,1,0:T(8,128)(2,1)S(1)}, u32[]{:S(2)}, u32[]{:S(2)}) collective-permute-start(bf16[2,4,64,448]{3,2,1,0:T(8,128)(2,1)S(1)} %pad_maximum_fusion.9), channel_id=1, source_target_pairs={{0,8},{1,9},{2,10},{3,11},{4,12},{5,13},{6,14},{7,15},{8,0},{9,1},... | collective-permute-start | bytes 1376264 | tf_op jit(solution)/shard_map/ppermute | solution.py:16
  59.8 2.8 %collective-permute-start.32 = (bf16[2,4,64,448]{3,2,1,0:T(8,128)(2,1)S(1)}, bf16[2,4,64,448]{3,2,1,0:T(8,128)(2,1)S(1)}, u32[]{:S(2)}, u32[]{:S(2)}) collective-permute-start(bf16[2,4,64,448]{3,2,1,0:T(8,128)(2,1)S(1)} %pad_maximum_fusion.11), channel_id=1, source_target_pairs={{0,8},{1,9},{2,10},{3,11},{4,12},{5,13},{6,14},{7,15},{8,0},{9,1},... | collective-permute-start | bytes 1376264 | tf_op jit(solution)/shard_map/ppermute | solution.py:16
  84.3 13.3 %collective-permute-start.33 = (bf16[4,128,512]{2,1,0:T(8,128)(2,1)}, bf16[4,128,512]{2,1,0:T(8,128)(2,1)S(1)}, u32[]{:S(2)}, u32[]{:S(2)}) collective-permute-start(bf16[4,128,512]{2,1,0:T(8,128)(2,1)} %bitcast.91), channel_id=1, source_target_pairs={{0,1},{1,0},{2,3},{3,2},{4,5},{5,4},{6,7},{7,6},{8,9},{9,8},{10,11... | collective-permute-start | bytes 1572872 | tf_op jit(solution)/shard_map/ppermute | solution.py:16
  91.8 5.8 %copy-start.5 = (bf16[1024,512]{1,0:T(8,128)(2,1)S(1)}, bf16[1024,512]{1,0:T(8,128)(2,1)}, u32[]{:S(2)}) copy-start(bf16[1024,512]{1,0:T(8,128)(2,1)} %copy-done.4) | copy-start | bytes 3145732
  91.8 17.1 %collective-permute-start.7 = (bf16[4,128,512]{2,1,0:T(8,128)(2,1)S(1)}, bf16[4,128,512]{2,1,0:T(8,128)(2,1)S(1)}, u32[]{:S(2)}, u32[]{:S(2)}) collective-permute-start(bf16[4,128,512]{2,1,0:T(8,128)(2,1)S(1)} %bitcast.342), channel_id=1, source_target_pairs={{0,1},{1,0},{2,3},{3,2},{4,5},{5,4},{6,7},{7,6},{8,9},{9,8},{10,11... | collective-permute-start | bytes 1572872 | tf_op jit(solution)/shard_map/ppermute | solution.py:16
  95.0 25.1 %collective-permute-start.11 = (bf16[4,128,512]{2,1,0:T(8,128)(2,1)S(1)}, bf16[4,128,512]{2,1,0:T(8,128)(2,1)S(1)}, u32[]{:S(2)}, u32[]{:S(2)}) collective-permute-start(bf16[4,128,512]{2,1,0:T(8,128)(2,1)S(1)} %bitcast.341), channel_id=1, source_target_pairs={{0,1},{1,0},{2,3},{3,2},{4,5},{5,4},{6,7},{7,6},{8,9},{9,8},{10,11... | collective-permute-start | bytes 1572872 | tf_op jit(solution)/shard_map/ppermute | solution.py:16
  97.7 24.2 %collective-permute-start.36 = (bf16[128,512]{1,0:T(8,128)(2,1)S(1)}, bf16[128,512]{1,0:T(8,128)(2,1)S(1)}, u32[]{:S(2)}, u32[]{:S(2)}) collective-permute-start(bf16[128,512]{1,0:T(8,128)(2,1)S(1)} %get-tuple-element.25), channel_id=1, source_target_pairs={{0,6},{1,7},{2,4},{3,5},{4,2},{5,3},{6,0},{7,1},{8,14},{9,15},{10,... | collective-permute-start | bytes 393224 | tf_op jit(solution)/shard_map/ppermute | solution.py:16
  98.4 23.7 %collective-permute-start.35 = (bf16[128,512]{1,0:T(8,128)(2,1)S(1)}, bf16[128,512]{1,0:T(8,128)(2,1)S(1)}, u32[]{:S(2)}, u32[]{:S(2)}) collective-permute-start(bf16[128,512]{1,0:T(8,128)(2,1)S(1)} %get-tuple-element.26), channel_id=1, source_target_pairs={{0,4},{1,5},{2,6},{3,7},{4,0},{5,1},{6,2},{7,3},{8,12},{9,13},{10,... | collective-permute-start | bytes 393224 | tf_op jit(solution)/shard_map/ppermute | solution.py:16
  100.7 22.3 %collective-permute-start.34 = (bf16[128,512]{1,0:T(8,128)(2,1)S(1)}, bf16[128,512]{1,0:T(8,128)(2,1)S(1)}, u32[]{:S(2)}, u32[]{:S(2)}) collective-permute-start(bf16[128,512]{1,0:T(8,128)(2,1)S(1)} %get-tuple-element.24), channel_id=1, source_target_pairs={{0,2},{1,3},{2,0},{3,1},{4,6},{5,7},{6,4},{7,5},{8,10},{9,11},{10,... | collective-permute-start | bytes 393224 | tf_op jit(solution)/shard_map/ppermute | solution.py:16
  109.0 16.7 %collective-permute-start.10 = (bf16[128,512]{1,0:T(8,128)(2,1)S(1)}, bf16[128,512]{1,0:T(8,128)(2,1)S(1)}, u32[]{:S(2)}, u32[]{:S(2)}) collective-permute-start(bf16[128,512]{1,0:T(8,128)(2,1)S(1)} %get-tuple-element.22), channel_id=1, source_target_pairs={{0,6},{1,7},{2,4},{3,5},{4,2},{5,3},{6,0},{7,1},{8,14},{9,15},{10,... | collective-permute-start | bytes 393224 | tf_op jit(solution)/shard_map/ppermute | solution.py:16
  120.1 7.5 %collective-permute-start.9 = (bf16[128,512]{1,0:T(8,128)(2,1)S(1)}, bf16[128,512]{1,0:T(8,128)(2,1)S(1)}, u32[]{:S(2)}, u32[]{:S(2)}) collective-permute-start(bf16[128,512]{1,0:T(8,128)(2,1)S(1)} %get-tuple-element.23), channel_id=1, source_target_pairs={{0,4},{1,5},{2,6},{3,7},{4,0},{5,1},{6,2},{7,3},{8,12},{9,13},{10,... | collective-permute-start | bytes 393224 | tf_op jit(solution)/shard_map/ppermute | solution.py:16
  122.0 5.6 %collective-permute-start.8 = (bf16[128,512]{1,0:T(8,128)(2,1)S(1)}, bf16[128,512]{1,0:T(8,128)(2,1)S(1)}, u32[]{:S(2)}, u32[]{:S(2)}) collective-permute-start(bf16[128,512]{1,0:T(8,128)(2,1)S(1)} %get-tuple-element.21), channel_id=1, source_target_pairs={{0,2},{1,3},{2,0},{3,1},{4,6},{5,7},{6,4},{7,5},{8,10},{9,11},{10,... | collective-permute-start | bytes 393224 | tf_op jit(solution)/shard_map/ppermute | solution.py:16
  122.1 14.7 %collective-permute-start.14 = (bf16[128,512]{1,0:T(8,128)(2,1)S(1)}, bf16[128,512]{1,0:T(8,128)(2,1)S(1)}, u32[]{:S(2)}, u32[]{:S(2)}) collective-permute-start(bf16[128,512]{1,0:T(8,128)(2,1)S(1)} %get-tuple-element.19), channel_id=1, source_target_pairs={{0,6},{1,7},{2,4},{3,5},{4,2},{5,3},{6,0},{7,1},{8,14},{9,15},{10,... | collective-permute-start | bytes 393224 | tf_op jit(solution)/shard_map/ppermute | solution.py:16
  122.9 15.6 %collective-permute-start.13 = (bf16[128,512]{1,0:T(8,128)(2,1)S(1)}, bf16[128,512]{1,0:T(8,128)(2,1)S(1)}, u32[]{:S(2)}, u32[]{:S(2)}) collective-permute-start(bf16[128,512]{1,0:T(8,128)(2,1)S(1)} %get-tuple-element.20), channel_id=1, source_target_pairs={{0,4},{1,5},{2,6},{3,7},{4,0},{5,1},{6,2},{7,3},{8,12},{9,13},{10,... | collective-permute-start | bytes 393224 | tf_op jit(solution)/shard_map/ppermute | solution.py:16
  125.7 12.8 %collective-permute-start.12 = (bf16[128,512]{1,0:T(8,128)(2,1)S(1)}, bf16[128,512]{1,0:T(8,128)(2,1)S(1)}, u32[]{:S(2)}, u32[]{:S(2)}) collective-permute-start(bf16[128,512]{1,0:T(8,128)(2,1)S(1)} %get-tuple-element.18), channel_id=1, source_target_pairs={{0,2},{1,3},{2,0},{3,1},{4,6},{5,7},{6,4},{7,5},{8,10},{9,11},{10,... | collective-permute-start | bytes 393224 | tf_op jit(solution)/shard_map/ppermute | solution.py:16
  128.4 37.4 %copy-start.28 = (s32[4]{0:T(128)S(1)}, s32[4]{0:T(128)}, u32[]{:S(2)}) copy-start(s32[4]{0:T(128)} %get-tuple-element.9) | copy-start | bytes 52
  138.8 8.0 %collective-permute-start.39 = (bf16[128,512]{1,0:T(8,128)(2,1)S(1)}, bf16[128,512]{1,0:T(8,128)(2,1)S(1)}, u32[]{:S(2)}, u32[]{:S(2)}) collective-permute-start(bf16[128,512]{1,0:T(8,128)(2,1)S(1)} %get-tuple-element.16), channel_id=1, source_target_pairs={{0,6},{1,7},{2,4},{3,5},{4,2},{5,3},{6,0},{7,1},{8,14},{9,15},{10,... | collective-permute-start | bytes 393224 | tf_op jit(solution)/shard_map/ppermute | solution.py:16
  139.2 13.2 %collective-permute-start.38 = (bf16[128,512]{1,0:T(8,128)(2,1)S(1)}, bf16[128,512]{1,0:T(8,128)(2,1)S(1)}, u32[]{:S(2)}, u32[]{:S(2)}) collective-permute-start(bf16[128,512]{1,0:T(8,128)(2,1)S(1)} %get-tuple-element.16), channel_id=1, source_target_pairs={{0,4},{1,5},{2,6},{3,7},{4,0},{5,1},{6,2},{7,3},{8,12},{9,13},{10,... | collective-permute-start | bytes 393224 | tf_op jit(solution)/shard_map/ppermute | solution.py:16
  143.2 9.2 %collective-permute-start.37 = (bf16[128,512]{1,0:T(8,128)(2,1)S(1)}, bf16[128,512]{1,0:T(8,128)(2,1)S(1)}, u32[]{:S(2)}, u32[]{:S(2)}) collective-permute-start(bf16[128,512]{1,0:T(8,128)(2,1)S(1)} %get-tuple-element.16), channel_id=1, source_target_pairs={{0,2},{1,3},{2,0},{3,1},{4,6},{5,7},{6,4},{7,5},{8,10},{9,11},{10,... | collective-permute-start | bytes 393224 | tf_op jit(solution)/shard_map/ppermute | solution.py:16
  143.2 18.1 %collective-permute-start.43 = (bf16[128,512]{1,0:T(8,128)(2,1)}, bf16[128,512]{1,0:T(8,128)(2,1)S(1)}, u32[]{:S(2)}, u32[]{:S(2)}) collective-permute-start(bf16[128,512]{1,0:T(8,128)(2,1)} %get-tuple-element.6), channel_id=1, source_target_pairs={{0,6},{1,7},{2,4},{3,5},{4,2},{5,3},{6,0},{7,1},{8,14},{9,15},{10,... | collective-permute-start | bytes 393224 | tf_op jit(solution)/shard_map/ppermute | solution.py:16
  144.4 18.9 %collective-permute-start.42 = (bf16[128,512]{1,0:T(8,128)(2,1)}, bf16[128,512]{1,0:T(8,128)(2,1)S(1)}, u32[]{:S(2)}, u32[]{:S(2)}) collective-permute-start(bf16[128,512]{1,0:T(8,128)(2,1)} %get-tuple-element.6), channel_id=1, source_target_pairs={{0,4},{1,5},{2,6},{3,7},{4,0},{5,1},{6,2},{7,3},{8,12},{9,13},{10,... | collective-permute-start | bytes 393224 | tf_op jit(solution)/shard_map/ppermute | solution.py:16
  153.3 23.7 %collective-permute-start.40 = (bf16[4,128,512]{2,1,0:T(8,128)(2,1)}, bf16[4,128,512]{2,1,0:T(8,128)(2,1)}, u32[]{:S(2)}, u32[]{:S(2)}) collective-permute-start(bf16[4,128,512]{2,1,0:T(8,128)(2,1)} %get-tuple-element.46), channel_id=1, source_target_pairs={{0,1},{1,0},{2,3},{3,2},{4,5},{5,4},{6,7},{7,6},{8,9},{9,8},{10,11... | collective-permute-start | bytes 1572872 | tf_op jit(solution)/shard_map/ppermute | solution.py:16
  153.5 15.2 %collective-permute-start.41 = (bf16[128,512]{1,0:T(8,128)(2,1)}, bf16[128,512]{1,0:T(8,128)(2,1)}, u32[]{:S(2)}, u32[]{:S(2)}) collective-permute-start(bf16[128,512]{1,0:T(8,128)(2,1)} %get-tuple-element.6), channel_id=1, source_target_pairs={{0,2},{1,3},{2,0},{3,1},{4,6},{5,7},{6,4},{7,5},{8,10},{9,11},{10,... | collective-permute-start | bytes 393224 | tf_op jit(solution)/shard_map/ppermute | solution.py:16
  161.1 10.6 %collective-permute-start.17 = (bf16[128,512]{1,0:T(8,128)(2,1)S(1)}, bf16[128,512]{1,0:T(8,128)(2,1)}, u32[]{:S(2)}, u32[]{:S(2)}) collective-permute-start(bf16[128,512]{1,0:T(8,128)(2,1)S(1)} %get-tuple-element.17), channel_id=1, source_target_pairs={{0,6},{1,7},{2,4},{3,5},{4,2},{5,3},{6,0},{7,1},{8,14},{9,15},{10,... | collective-permute-start | bytes 393224 | tf_op jit(solution)/shard_map/ppermute | solution.py:16
  161.3 12.5 %collective-permute-start.16 = (bf16[128,512]{1,0:T(8,128)(2,1)S(1)}, bf16[128,512]{1,0:T(8,128)(2,1)}, u32[]{:S(2)}, u32[]{:S(2)}) collective-permute-start(bf16[128,512]{1,0:T(8,128)(2,1)S(1)} %get-tuple-element.17), channel_id=1, source_target_pairs={{0,4},{1,5},{2,6},{3,7},{4,0},{5,1},{6,2},{7,3},{8,12},{9,13},{10,... | collective-permute-start | bytes 393224 | tf_op jit(solution)/shard_map/ppermute | solution.py:16
  163.9 9.9 %collective-permute-start.15 = (bf16[128,512]{1,0:T(8,128)(2,1)S(1)}, bf16[128,512]{1,0:T(8,128)(2,1)}, u32[]{:S(2)}, u32[]{:S(2)}) collective-permute-start(bf16[128,512]{1,0:T(8,128)(2,1)S(1)} %get-tuple-element.17), channel_id=1, source_target_pairs={{0,2},{1,3},{2,0},{3,1},{4,6},{5,7},{6,4},{7,5},{8,10},{9,11},{10,... | collective-permute-start | bytes 393224 | tf_op jit(solution)/shard_map/ppermute | solution.py:16
  169.9 12.9 %collective-permute-start.44 = (bf16[4,128,512]{2,1,0:T(8,128)(2,1)S(1)}, bf16[4,128,512]{2,1,0:T(8,128)(2,1)S(1)}, u32[]{:S(2)}, u32[]{:S(2)}) collective-permute-start(bf16[4,128,512]{2,1,0:T(8,128)(2,1)S(1)} %get-tuple-element.44), channel_id=1, source_target_pairs={{0,1},{1,0},{2,3},{3,2},{4,5},{5,4},{6,7},{7,6},{8,9},{9,8},{10,11... | collective-permute-start | bytes 1572872 | tf_op jit(solution)/shard_map/ppermute | solution.py:16
  176.0 18.2 %collective-permute-start.18 = (bf16[4,128,512]{2,1,0:T(8,128)(2,1)}, bf16[4,128,512]{2,1,0:T(8,128)(2,1)}, u32[]{:S(2)}, u32[]{:S(2)}) collective-permute-start(bf16[4,128,512]{2,1,0:T(8,128)(2,1)} %get-tuple-element.48), channel_id=1, source_target_pairs={{0,1},{1,0},{2,3},{3,2},{4,5},{5,4},{6,7},{7,6},{8,9},{9,8},{10,11... | collective-permute-start | bytes 1572872 | tf_op jit(solution)/shard_map/ppermute | solution.py:16
  187.8 6.4 %copy-start.3 = (bf16[1,4,128,512]{3,2,1,0:T(8,128)(2,1)S(1)}, bf16[1,4,128,512]{3,2,1,0:T(8,128)(2,1)}, u32[]{:S(2)}) copy-start(bf16[1,4,128,512]{3,2,1,0:T(8,128)(2,1)} %get-tuple-element.47) | copy-start | bytes 1572868
  189.3 7.0 %copy-start.23 = (pred[1024,4]{0,1:T(4,128)(4,1)S(1)}, pred[1024,4]{0,1:T(4,128)(4,1)}, u32[]{:S(2)}) copy-start(pred[1024,4]{0,1:T(4,128)(4,1)} %copy-done.21) | copy-start | bytes 12292
  189.3 7.0 %copy-start.32 = (bf16[4,512,448]{1,2,0:T(8,128)(2,1)S(1)}, bf16[4,512,448]{1,2,0:T(8,128)(2,1)}, u32[]{:S(2)}) copy-start(bf16[4,512,448]{1,2,0:T(8,128)(2,1)} %param.26) | copy-start | bytes 5505028
  202.7 6.9 %copy-start.27 = (pred[4]{0:T(512)(128)(4,1)S(1)}, pred[4]{0:T(512)(128)(4,1)}, u32[]{:S(2)}) copy-start(pred[4]{0:T(512)(128)(4,1)} %get-tuple-element.80) | copy-start | bytes 16
  204.9 4.9 %copy-start.26 = (pred[4]{0:T(512)(128)(4,1)S(1)}, pred[4]{0:T(512)(128)(4,1)}, u32[]{:S(2)}) copy-start(pred[4]{0:T(512)(128)(4,1)} %get-tuple-element.78) | copy-start | bytes 16
  210.4 12.0 %collective-permute-start.19 = (bf16[2,4,64,448]{3,2,0,1:T(8,128)(2,1)S(1)}, bf16[2,4,64,448]{3,2,0,1:T(8,128)(2,1)S(1)}, u32[]{:S(2)}, u32[]{:S(2)}) collective-permute-start(bf16[2,4,64,448]{3,2,0,1:T(8,128)(2,1)S(1)} %slice.350), channel_id=1, source_target_pairs={{0,8},{1,9},{2,10},{3,11},{4,12},{5,13},{6,14},{7,15},{8,0},{9,1},... | collective-permute-start | bytes 1376264 | tf_op jit(solution)/shard_map/ppermute | solution.py:16
  212.2 10.6 %collective-permute-start.45 = (bf16[2,4,64,448]{3,2,1,0:T(8,128)(2,1)S(1)}, bf16[2,4,64,448]{3,2,1,0:T(8,128)(2,1)S(1)}, u32[]{:S(2)}, u32[]{:S(2)}) collective-permute-start(bf16[2,4,64,448]{3,2,1,0:T(8,128)(2,1)S(1)} %slice.377), channel_id=1, source_target_pairs={{0,8},{1,9},{2,10},{3,11},{4,12},{5,13},{6,14},{7,15},{8,0},{9,1},... | collective-permute-start | bytes 1376264 | tf_op jit(solution)/shard_map/ppermute | solution.py:16
  222.5 6.8 %collective-permute-start.20 = (bf16[1,4,64,448]{3,2,0,1:T(8,128)(2,1)S(1)}, bf16[1,4,64,448]{3,2,0,1:T(8,128)(2,1)S(1)}, u32[]{:S(2)}, u32[]{:S(2)}) collective-permute-start(bf16[1,4,64,448]{3,2,0,1:T(8,128)(2,1)S(1)} %slice.352), channel_id=1, source_target_pairs={{0,16},{1,17},{2,18},{3,19},{4,20},{5,21},{6,22},{7,23},{8,24},{9,... | collective-permute-start | bytes 688136 | tf_op jit(solution)/shard_map/ppermute | solution.py:16
  222.9 16.1 %collective-permute-start.46 = (bf16[1,4,64,448]{3,2,1,0:T(8,128)(2,1)S(1)}, bf16[1,4,64,448]{3,2,1,0:T(8,128)(2,1)S(1)}, u32[]{:S(2)}, u32[]{:S(2)}) collective-permute-start(bf16[1,4,64,448]{3,2,1,0:T(8,128)(2,1)S(1)} %slice.379), channel_id=1, source_target_pairs={{0,16},{1,17},{2,18},{3,19},{4,20},{5,21},{6,22},{7,23},{8,24},{9,... | collective-permute-start | bytes 688136 | tf_op jit(solution)/shard_map/ppermute | solution.py:16
  229.4 31.1 %copy-start.29 = (f32[128,1]{0,1:T(1,128)S(1)}, f32[128,1]{0,1:T(1,128)}, u32[]{:S(2)}) copy-start(f32[128,1]{0,1:T(1,128)} %param.22) | copy-start | bytes 1540
  229.4 25.9 %collective-permute-start.21 = (bf16[64,448]{1,0:T(8,128)(2,1)S(1)}, bf16[64,448]{1,0:T(8,128)(2,1)S(1)}, u32[]{:S(2)}, u32[]{:S(2)}) collective-permute-start(bf16[64,448]{1,0:T(8,128)(2,1)S(1)} %get-tuple-element.59), channel_id=1, source_target_pairs={{0,0},{1,1},{8,2},{9,3},{16,4},{17,5},{24,6},{25,7},{2,8},{3,9},{1... | collective-permute-start | bytes 172040 | tf_op jit(solution)/shard_map/ppermute | solution.py:71
  235.2 21.4 %collective-permute-start.22 = (bf16[64,448]{1,0:T(8,128)(2,1)S(1)}, bf16[64,448]{1,0:T(8,128)(2,1)S(1)}, u32[]{:S(2)}, u32[]{:S(2)}) collective-permute-start(bf16[64,448]{1,0:T(8,128)(2,1)S(1)} %get-tuple-element.57), channel_id=1, source_target_pairs={{8,0},{9,1},{0,2},{1,3},{24,4},{25,5},{16,6},{17,7},{10,8},{11,9},... | collective-permute-start | bytes 172040 | tf_op jit(solution)/shard_map/ppermute | solution.py:71
  238.5 5.2 %collective-permute-start.24 = (bf16[64,448]{1,0:T(8,128)(2,1)S(1)}, bf16[64,448]{1,0:T(8,128)(2,1)S(1)}, u32[]{:S(2)}, u32[]{:S(2)}) collective-permute-start(bf16[64,448]{1,0:T(8,128)(2,1)S(1)} %slice_bitcast_fusion.44), channel_id=1, source_target_pairs={{24,0},{25,1},{16,2},{17,3},{8,4},{9,5},{0,6},{1,7},{26,8},{27,9},... | collective-permute-start | bytes 172040 | tf_op jit(solution)/shard_map/ppermute | solution.py:71
  238.5 7.3 %collective-permute-start.23 = (bf16[64,448]{1,0:T(8,128)(2,1)S(1)}, bf16[64,448]{1,0:T(8,128)(2,1)S(1)}, u32[]{:S(2)}, u32[]{:S(2)}) collective-permute-start(bf16[64,448]{1,0:T(8,128)(2,1)S(1)} %get-tuple-element.58), channel_id=1, source_target_pairs={{16,0},{17,1},{24,2},{25,3},{0,4},{1,5},{8,6},{9,7},{18,8},{19,9},... | collective-permute-start | bytes 172040 | tf_op jit(solution)/shard_map/ppermute | solution.py:71
  239.1 24.8 %copy-start.1 = (bf16[4,448,512]{2,1,0:T(8,128)(2,1)S(1)}, bf16[4,448,512]{2,1,0:T(8,128)(2,1)}, u32[]{:S(2)}) copy-start(bf16[4,448,512]{2,1,0:T(8,128)(2,1)} %param.24) | copy-start | bytes 5505028
  239.2 17.4 %collective-permute-start.47 = (bf16[64,448]{1,0:T(8,128)(2,1)S(1)}, bf16[64,448]{1,0:T(8,128)(2,1)S(1)}, u32[]{:S(2)}, u32[]{:S(2)}) collective-permute-start(bf16[64,448]{1,0:T(8,128)(2,1)S(1)} %get-tuple-element.54), channel_id=1, source_target_pairs={{0,0},{1,1},{8,2},{9,3},{16,4},{17,5},{24,6},{25,7},{2,8},{3,9},{1... | collective-permute-start | bytes 172040 | tf_op jit(solution)/shard_map/ppermute | solution.py:71
  243.6 3.8 %collective-permute-start.50 = (bf16[64,448]{1,0:T(8,128)(2,1)S(1)}, bf16[64,448]{1,0:T(8,128)(2,1)S(1)}, u32[]{:S(2)}, u32[]{:S(2)}) collective-permute-start(bf16[64,448]{1,0:T(8,128)(2,1)S(1)} %get-tuple-element.52), channel_id=1, source_target_pairs={{24,0},{25,1},{16,2},{17,3},{8,4},{9,5},{0,6},{1,7},{26,8},{27,9},... | collective-permute-start | bytes 172040 | tf_op jit(solution)/shard_map/ppermute | solution.py:71
  245.7 9.2 %collective-permute-start.49 = (bf16[64,448]{1,0:T(8,128)(2,1)S(1)}, bf16[64,448]{1,0:T(8,128)(2,1)S(1)}, u32[]{:S(2)}, u32[]{:S(2)}) collective-permute-start(bf16[64,448]{1,0:T(8,128)(2,1)S(1)} %get-tuple-element.53), channel_id=1, source_target_pairs={{16,0},{17,1},{24,2},{25,3},{0,4},{1,5},{8,6},{9,7},{18,8},{19,9},... | collective-permute-start | bytes 172040 | tf_op jit(solution)/shard_map/ppermute | solution.py:71
  247.4 9.3 %collective-permute-start.48 = (bf16[64,448]{1,0:T(8,128)(2,1)S(1)}, bf16[64,448]{1,0:T(8,128)(2,1)S(1)}, u32[]{:S(2)}, u32[]{:S(2)}) collective-permute-start(bf16[64,448]{1,0:T(8,128)(2,1)S(1)} %get-tuple-element.51), channel_id=1, source_target_pairs={{8,0},{9,1},{0,2},{1,3},{24,4},{25,5},{16,6},{17,7},{10,8},{11,9},... | collective-permute-start | bytes 172040 | tf_op jit(solution)/shard_map/ppermute | solution.py:71
  255.0 5.5 %collective-permute-start.25 = (bf16[128,448]{1,0:T(8,128)(2,1)S(1)}, bf16[128,448]{1,0:T(8,128)(2,1)S(1)}, u32[]{:S(2)}, u32[]{:S(2)}) collective-permute-start(bf16[128,448]{1,0:T(8,128)(2,1)S(1)} %pad_maximum_fusion.15), channel_id=1, source_target_pairs={{0,1},{1,0},{2,3},{3,2},{4,5},{5,4},{6,7},{7,6},{8,9},{9,8},{10,11... | collective-permute-start | bytes 344072 | tf_op jit(solution)/shard_map/ppermute | solution.py:16
  255.4 7.7 %collective-permute-start.51 = (bf16[128,448]{1,0:T(8,128)(2,1)S(1)}, bf16[128,448]{1,0:T(8,128)(2,1)S(1)}, u32[]{:S(2)}, u32[]{:S(2)}) collective-permute-start(bf16[128,448]{1,0:T(8,128)(2,1)S(1)} %pad_maximum_fusion.16), channel_id=1, source_target_pairs={{0,1},{1,0},{2,3},{3,2},{4,5},{5,4},{6,7},{7,6},{8,9},{9,8},{10,11... | collective-permute-start | bytes 344072 | tf_op jit(solution)/shard_map/ppermute | solution.py:16
  (21 other events, 56.9 us)

commit v2 on v1

v2 whole, which is shorter than its diff:
```python
import functools

import jax
import jax.numpy as jnp
from jax import lax
from jax.experimental import pallas as pl
from jax.experimental.pallas import tpu as pltpu
from jax.sharding import PartitionSpec as P

AXES = ("grp", "ep")
BF16 = jnp.bfloat16
VMEM = pl.BlockSpec(memory_space=pltpu.VMEM)
SMEM = pl.BlockSpec(memory_space=pltpu.SMEM)
PARAMS = pltpu.CompilerParams(vmem_limit_bytes=50 * 1024 * 1024)


def f32(a):
    return a.astype(jnp.float32)


def half(a):
    return a.astype(BF16)


def swap(block, grp_bits, ep_bits):
    grp_size, ep_size = lax.axis_size("grp"), lax.axis_size("ep")
    pairs = [
        (g * ep_size + p, (g ^ grp_bits) * ep_size + (p ^ ep_bits))
        for g in range(grp_size)
        for p in range(ep_size)
    ]
    return lax.ppermute(block, AXES, pairs)


def plane_pairs(k):
    grp_size, ep_size = lax.axis_size("grp"), lax.axis_size("ep")
    flip = k // (grp_size // 2)
    return [
        (g * ep_size + p, ((p // 2) ^ k) * ep_size + 2 * g + ((p % 2) ^ flip))
        for g in range(grp_size)
        for p in range(ep_size)
    ]


def spread(mine, other):
    grp_size = lax.axis_size("grp")
    per = grp_size // 2
    size = mine.shape[0] // per
    pieces = []
    for k in range(grp_size):
        rows = (mine, other)[k // per][(k % per) * size : (k % per + 1) * size]
        pieces.append(lax.ppermute(rows, AXES, plane_pairs(k)))
    held = jnp.concatenate(pieces)
    bit = grp_size // 2
    while bit > 1:
        held = jnp.concatenate([held, swap(held, bit, 0)])
        bit //= 2
    return held, swap(held, 1, 0)


def unspread(keep, send):
    grp_size = lax.axis_size("grp")
    per = grp_size // 2
    got = swap(send, 1, 0)
    bit = grp_size // 2
    while bit > 1:
        n = keep.shape[0] // 2
        got_next = swap(half(f32(keep[n:]) + f32(got[n:])), bit, 0)
        keep = half(f32(keep[:n]) + f32(got[:n]))
        got = got_next
        bit //= 2
    size = keep.shape[0] // grp_size
    pieces = []
    for k in range(grp_size):
        rows = slice(k * size, (k + 1) * size)
        back = [(b, a) for a, b in plane_pairs(k)]
        pieces.append(lax.ppermute(half(f32(keep[rows]) + f32(got[rows])), AXES, back))
    return jnp.concatenate(pieces[:per]), jnp.concatenate(pieces[per:])


def scatter_sum(keep, send, bits):
    got = swap(send, 0, 1 << bits[0])
    for bit in bits[1:]:
        n = keep.shape[0] // 2
        got_next = swap(half(f32(keep[n:]) + f32(got[n:])), 0, 1 << bit)
        keep = half(f32(keep[:n]) + f32(got[:n]))
        got = got_next
    return f32(keep) + f32(got)


def gather(own, bits):
    held = own
    for bit in bits[:-1]:
        held = jnp.concatenate([held, swap(held, 0, 1 << bit)])
    return held, swap(held, 0, 1 << bits[-1])


def block_order(bits):
    order = [0]
    for bit in reversed(bits):
        order = order + [j ^ (1 << bit) for j in order]
    return order


def masked_dot(lhs_of, w_ref, count, turned):
    dims = (((1,), (1 if turned else 0,)), ((), ()))
    total = None
    for e in range(count):
        part = lax.dot_general(lhs_of(e), w_ref[e], dims, preferred_element_type=jnp.float32)
        total = part if total is None else total + part
    return total


def first_body(geo, turned, ids, where_ref, held_ref, got_ref, *refs):
    grp_size, ep_size, tok, stored, count, order = geo
    id_ref = refs[0] if not ids else None
    w_ref, keep_ref, send_ref, rows_ref = refs[-4:]
    per = grp_size // 2
    sub = tok // per
    bits = grp_size.bit_length() - 1
    shift = where_ref[0] ^ (where_ref[1] // 2)
    for place, j in enumerate(order):
        for s in range(per):
            k = (j & 1) * per + s
            m = shift ^ ((j >> 1) ^ k)
            at = 0
            for b in range(bits - 1):
                at = at + (((m >> (bits - 1 - b)) & 1) << b)
            src = pl.ds(pl.multiple_of((at * grp_size + k) * sub, sub), sub)
            rows = jnp.where((m & 1) == 0, held_ref[src, :], got_ref[src, :])
            rows_ref[j * tok + s * sub : j * tok + (s + 1) * sub, :] = rows
    n = len(order) // 2
    for place, j in enumerate(order):
        out_ref = keep_ref if place < n else send_ref
        at = (place % n) * tok
        rows = rows_ref[j * tok : (j + 1) * tok, :]
        if ids:
            expert = rows[:, stored : stored + 1]
        else:
            expert = id_ref[j * tok : (j + 1) * tok, :][:, stored % 128 : stored % 128 + 1]
        rows = rows[:, :stored]
        total = masked_dot(
            lambda e: jnp.where(expert == e, rows, jnp.zeros((), BF16)), w_ref, count, turned
        )
        out_ref[at : at + tok, :] = half(total)


def matmul_body(geo, turned, id_ref, rows_ref, w_ref, keep_ref, send_ref):
    tok, stored, count, order = geo
    n = len(order) // 2
    for place, j in enumerate(order):
        out_ref = keep_ref if place < n else send_ref
        at = (place % n) * tok
        rows = rows_ref[j * tok : (j + 1) * tok, :stored]
        expert = id_ref[j * tok : (j + 1) * tok, :][:, stored % 128 : stored % 128 + 1]
        total = masked_dot(
            lambda e: jnp.where(expert == e, rows, jnp.zeros((), BF16)), w_ref, count, turned
        )
        out_ref[at : at + tok, :] = half(total)


def back_body(geo, turned, where_ref, id_ref, *refs):
    grp_size, tok, stored, count, orders = geo
    keep_ref, send_ref = refs[-2:]
    per = grp_size // 2
    sub = tok // per
    shift = where_ref[0] ^ (where_ref[1] // 2)
    zero = jnp.zeros((), BF16)
    for j in range(len(orders[0])):
        expert = id_ref[j * tok : (j + 1) * tok, :][:, stored % 128 : stored % 128 + 1]
        total = None
        for i, order in enumerate(orders):
            held_ref, got_ref, w_ref = refs[3 * i : 3 * i + 3]
            n = len(order) // 2
            place = order.index(j)
            src = held_ref if place < n else got_ref
            rows = src[(place % n) * tok : (place % n + 1) * tok, :]
            part = masked_dot(
                lambda e: jnp.where(expert == e, rows, zero), w_ref, count, turned
            )
            total = part if total is None else total + part
        total = half(total)
        for s in range(per):
            k = (j & 1) * per + s
            m = shift ^ ((j >> 1) ^ k)
            dst = pl.ds(pl.multiple_of(((m >> 1) * grp_size + k) * sub, sub), sub)

            @pl.when((m & 1) == 0)
            def _():
                keep_ref[dst, :] = total[s * sub : (s + 1) * sub]

            @pl.when((m & 1) == 1)
            def _():
                send_ref[dst, :] = total[s * sub : (s + 1) * sub]


def grad_body(geo, swapped, id_ref, rows_ref, held_ref, got_ref, out_ref):
    tok, stored, order = geo
    expert = half(pl.program_id(0).astype(jnp.float32))
    n = len(order) // 2
    total = None
    for part, src in enumerate((held_ref, got_ref)):
        seq = order[part * n : (part + 1) * n]
        rows = jnp.concatenate([rows_ref[j * tok : (j + 1) * tok, :stored] for j in seq])
        ident = jnp.concatenate(
            [id_ref[j * tok : (j + 1) * tok, :][:, stored % 128 : stored % 128 + 1] for j in seq]
        )
        rows = jnp.where(ident == expert, rows, jnp.zeros((), BF16))
        pair = (src[...], rows) if swapped else (rows, src[...])
        now = lax.dot_general(*pair, (((0,), (0,)), ((), ())), preferred_element_type=jnp.float32)
        total = now if total is None else total + now
    out_ref[0] = half(total)


def cost(flops, nbytes):
    return pl.CostEstimate(flops=flops, bytes_accessed=nbytes, transcendentals=0)


def shards(tokens, routes, route_weights, hot_experts, w_gate, w_up, w_down, cotangent):
    grp_size, ep_size = lax.axis_size("grp"), lax.axis_size("ep")
    g, p = lax.axis_index("grp"), lax.axis_index("ep")
    y = p % 2
    tok = tokens.shape[0]
    count, stored, hidden = w_gate.shape
    total = tok * ep_size
    width = (stored // 128 + 1) * 128
    bits = list(range(ep_size.bit_length() - 1))
    y_first, y_last = bits, bits[1:] + bits[:1]
    where = jnp.stack([g, p]).astype(jnp.int32)
    slot_host = jnp.concatenate([jnp.arange(count, dtype=jnp.int32), hot_experts])
    slots = jnp.arange(slot_host.shape[0], dtype=jnp.int32)
    expert = jnp.sum(jnp.where(routes == slots[None, :], slot_host[None, :], 0), axis=1)
    flops = 2 * total * count * stored * hidden
    one_cost = cost(flops, 2 * (total * (stored + hidden) + count * stored * hidden))

    def halves(rows):
        first, second = rows[:, :stored], rows[:, stored:]
        return jnp.where(y == 0, first, second), jnp.where(y == 0, second, first)

    ident = half(f32(expert))[:, None]
    pad = jnp.zeros((tok, width - stored - 1), BF16)
    x_held, x_got = spread(*[jnp.concatenate([h, ident, pad], axis=1) for h in halves(tokens)])
    dz_held, dz_got = spread(*halves(half(f32(cotangent) * route_weights)))

    split = [jax.ShapeDtypeStruct((total // 2, hidden), BF16)] * 2
    id_spec = pl.BlockSpec((total, 128), lambda *_: (0, stored // 128))
    full = lambda shape: pl.BlockSpec(shape, lambda *_: (0,) * len(shape))
    first_order = block_order(y_first)
    gate_keep, gate_send, x_rows = pl.pallas_call(
        functools.partial(
            first_body, (grp_size, ep_size, tok, stored, count, first_order), False, True
        ),
        out_shape=split + [jax.ShapeDtypeStruct((total, width), BF16)],
        in_specs=[SMEM, VMEM, VMEM, VMEM],
        out_specs=[VMEM] * 3,
        compiler_params=PARAMS,
        cost_estimate=one_cost,
        name="gate_rows",
    )(where, x_held, x_got, w_gate)
    up_keep, up_send = pl.pallas_call(
        functools.partial(matmul_body, (tok, stored, count, first_order), False),
        out_shape=split,
        grid=(1,),
        in_specs=[id_spec, full((total, width)), full(w_up.shape)],
        out_specs=[full((total // 2, hidden))] * 2,
        compiler_params=PARAMS,
        cost_estimate=one_cost,
        name="up_rows",
    )(x_rows, x_rows, w_up)
    ag_keep, ag_send, dz_rows = pl.pallas_call(
        functools.partial(
            first_body, (grp_size, ep_size, tok, stored, count, block_order(y_last)), True, False
        ),
        out_shape=split + [jax.ShapeDtypeStruct((total, stored), BF16)],
        grid=(1,),
        in_specs=[SMEM, full(dz_held.shape), full(dz_got.shape), id_spec, full(w_down.shape)],
        out_specs=[full((total // 2, hidden))] * 2 + [full((total, stored))],
        compiler_params=PARAMS,
        cost_estimate=one_cost,
        name="act_grad_rows",
    )(where, dz_held, dz_got, x_rows, w_down)

    gate_pre = scatter_sum(gate_keep, gate_send, y_first)
    up_pre = scatter_sum(up_keep, up_send, y_first)
    act_grad = scatter_sum(ag_keep, ag_send, y_last)
    sg = jax.nn.sigmoid(gate_pre)
    act = half(gate_pre * sg * up_pre)
    gate_grad = half(act_grad * up_pre * sg * (1.0 + gate_pre * (1.0 - sg)))
    up_grad = half(act_grad * gate_pre * sg)

    late, early = y_first[::-1], y_last[::-1]
    late_order, early_order = block_order(y_first), block_order(y_last)
    act_held, act_got = gather(act, late)
    gg_held, gg_got = gather(gate_grad, late)
    ug_held, ug_got = gather(up_grad, early)

    back_shape = [jax.ShapeDtypeStruct((total // 2, stored), BF16)] * 2
    half_spec = full((total // 2, hidden))

    def back(orders, turned, name, *args):
        return pl.pallas_call(
            functools.partial(back_body, (grp_size, tok, stored, count, orders), turned),
            out_shape=back_shape,
            grid=(1,),
            in_specs=[SMEM, id_spec]
            + [spec for i in range(len(orders)) for spec in (half_spec, half_spec, full(args[3 * i + 2].shape))],
            out_specs=[full((total // 2, stored))] * 2,
            compiler_params=PARAMS,
            cost_estimate=cost(flops * len(orders), one_cost.bytes_accessed * len(orders)),
            name=name,
        )(where, x_rows, *args)

    def grad(rows, held, got, order, swapped, name):
        shape = (hidden, stored) if swapped else (stored, hidden)
        return pl.pallas_call(
            functools.partial(grad_body, (tok, stored, order), swapped),
            out_shape=jax.ShapeDtypeStruct((count,) + shape, BF16),
            grid=(count,),
            in_specs=[id_spec, full(rows.shape), half_spec, half_spec],
            out_specs=pl.BlockSpec((1,) + shape, lambda e: (e, 0, 0)),
            compiler_params=PARAMS,
            cost_estimate=one_cost,
            name=name,
        )(x_rows, rows, held, got)

    out_keep, out_send = back([late_order], False, "out_rows", act_held, act_got, w_down)
    mine, other = unspread(out_keep, out_send)

    def joined(mine, other):
        return jnp.concatenate(
            [jnp.where(y == 0, mine, other), jnp.where(y == 0, other, mine)], axis=1
        )

    layer_output = half(f32(joined(mine, other)) * route_weights)
    tok_keep, tok_send = back(
        [late_order, early_order], True, "token_rows", gg_held, gg_got, w_gate, ug_held, ug_got, w_up
    )
    grad_tokens = joined(*unspread(tok_keep, tok_send))
    grad_down = grad(dz_rows, act_held, act_got, late_order, True, "grad_down")
    grad_gate = grad(x_rows, gg_held, gg_got, late_order, False, "grad_gate")
    grad_up = grad(x_rows, ug_held, ug_got, early_order, False, "grad_up")
    return (layer_output, grad_tokens, grad_gate, grad_up, grad_down)


def solution(mesh):
    placed = (
        P("ep", "grp"),
        P("ep", None),
        P("ep", None),
        P(),
        P(None, "ep", "grp"),
        P(None, "ep", "grp"),
        P(None, "grp", "ep"),
        P("ep", "grp"),
    )
    return jax.shard_map(
        shards,
        mesh=mesh,
        in_specs=placed,
        out_specs=(
            P("ep", "grp"),
            P("ep", "grp"),
            P(None, "ep", "grp"),
            P(None, "ep", "grp"),
            P(None, "grp", "ep"),
        ),
        check_vma=False,
    )
```

time: 265 us -> 227 us (0.86)
  Pallas kernels: 0 us -> 52.8 us
  matrix products: 29.9 us -> 0 us
  local copies, waits for them, and re-layouts: 36.8 us -> 8.06 us
  starting transfers between devices: 88.6 us -> 66.5 us
  blocking collectives: 10.4 us -> 0 us
  other arithmetic: 20.4 us -> 11 us
  waiting for transfers between devices: 76.2 us -> 84.1 us
    pallas_call x0 -> x8, Pallas kernels: none -> 52.8 us  [the longest x2 23.8 us: back(): pl.pallas_call(functools.partial(back_body, (grp_size, tok, stored, count...]
    dot_general x9 -> x0, matrix products: 29.9 us -> none  [dot(): lax.dot_general(a, b, ((ca, cb), ((), ())), preferred_element_type=jnp.fl...]
    gather x21 -> x0, local copies, waits for them, and re-layouts: 19.2 us -> none  [the longest x8 8.77 us: to_relative(): cols.append(jnp.take(held[:, k], idx, axis=0))]
    another operation x22 -> x1, other arithmetic: 13 us -> 0.08 us  [shards(): where = jnp.stack([g, p]).astype(jnp.int32)]
    ppermute x36 -> x26, starting transfers between devices: 43.2 us -> 31.7 us  [swap(): return lax.ppermute(block, AXES, pairs)]
    ppermute x16, starting transfers between devices: 45.4 us -> 34.8 us  [the longest x8 18 us: spread(): pieces.append(lax.ppermute(rows, AXES, plane_pairs(k)))]
    all_gather x1 -> x0, blocking collectives: 10.4 us -> none  [shards(): experts = lax.all_gather(expert, 'ep', axis=0)]
    ppermute x16, waiting for transfers between devices: 9.18 us -> 18.2 us  [the longest x8 11.7 us: unspread(): lax.ppermute(half(f32(keep[rows]) + f32(got[rows])), AXES, back)]
  transfers between devices with their start and end apart: 52 -> 42, of which waited for: 25 -> 19; matrix products, arithmetic and copies ran while one was open for 17% -> 7% of each run, Pallas kernels for 0% -> 24%
where the time goes in v2:
time: 227 us; the launch traced here: 224 us
  waiting for transfers between devices  84.1 us (37%)
  starting transfers between devices  66.5 us (29%)
  Pallas kernels  52.8 us (23%)
  other arithmetic  11 us (5%)
  local copies, waits for them, and re-layouts  8.06 us (4%)
    ppermute x26, waiting for transfers between devices, swap(): return lax.ppermute(block, AXES, pairs)  65.9 us
    ppermute x26, starting transfers between devices, swap(): return lax.ppermute(block, AXES, pairs)  31.7 us
    pallas_call x2, Pallas kernels, back(): pl.pallas_call(functools.partial(back_body, (grp_size, tok, stored, count...  23.8 us
    ppermute x8, starting transfers between devices, spread(): pieces.append(lax.ppermute(rows, AXES, plane_pairs(k)))  18 us
    ppermute x8, starting transfers between devices, unspread(): lax.ppermute(half(f32(keep[rows]) + f32(got[rows])), AXES, back)  16.8 us
    pallas_call x3, Pallas kernels, grad(): pl.pallas_call(functools.partial(grad_body, (tok, stored, order), swapped...  13 us
    pallas_call x2, Pallas kernels, shards(): pl.pallas_call(functools.partial(first_body, (grp_size, ep_size, tok, sto...  12.5 us
    ppermute x8, waiting for transfers between devices, unspread(): lax.ppermute(half(f32(keep[rows]) + f32(got[rows])), AXES, back)  11.7 us
  transfers between devices with their start and end apart: 42, of which 19 were waited for; matrix products, arithmetic and copies ran while one was open for 7% of the time, Pallas kernels for 24%

profile of v2, /device:TPU:17, one launch (start us, length us, event | category | flops | bytes accessed | tf_op | source)
XLA Modules:
  0.0 223.6 jit_solution(8215647879331987568)
XLA Ops:
  0.6 1.0 multiply_convert_fusion
  1.8 1.2 collective-permute-start.24
  3.0 1.9 collective-permute-start.23
  4.9 2.2 collective-permute-start.22
  7.1 2.1 collective-permute-start.21
  9.2 0.7 pad_add_fusion.1
  10.0 0.7 select_reduce_fusion
  10.9 1.1 broadcast_select_fusion.6
  12.5 5.9 %collective-permute-start.2 = (bf16[64,512]{1,0:T(8,128)(2,1)S(1)}, bf16[64,512]{1,0:T(8,128)(2,1)S(1)}, u32[]{:S(2)}, u32[]{:S(2)}) collective-permute-start(bf16[64,512]{1,0:T(8,128)(2,1)S(1)} %get-tuple-element.73), channel_id=1, source_target_pairs={{0,17},{1,16},{2,25},{3,24},{4,1},{5,0},{6,9},{7,8},{8,19},{9,18},... | collective-permute-start | bytes 196616 | tf_op jit(solution)/shard_map/ppermute | solution.py:52
  18.7 4.2 %collective-permute-start = (bf16[64,512]{1,0:T(8,128)(2,1)S(1)}, bf16[64,512]{1,0:T(8,128)(2,1)S(1)}, u32[]{:S(2)}, u32[]{:S(2)}) collective-permute-start(bf16[64,512]{1,0:T(8,128)(2,1)S(1)} %get-tuple-element.75), channel_id=1, source_target_pairs={{0,0},{1,1},{2,8},{3,9},{4,16},{5,17},{6,24},{7,25},{8,2},{9,3},{1... | collective-permute-start | bytes 196616 | tf_op jit(solution)/shard_map/ppermute | solution.py:52
  23.0 1.0 collective-permute-done.1
  24.0 5.4 %collective-permute-done = bf16[64,512]{1,0:T(8,128)(2,1)S(1)} collective-permute-done((bf16[64,512]{1,0:T(8,128)(2,1)S(1)}, bf16[64,512]{1,0:T(8,128)(2,1)S(1)}, u32[]{:S(2)}, u32[]{:S(2)}) %collective-permute-start) | collective-permute-done | bytes 65568 | tf_op jit(solution)/shard_map/ppermute | solution.py:52
  29.6 8.5 %collective-permute-done.4 = bf16[256,512]{1,0:T(8,128)(2,1)S(1)} collective-permute-done((bf16[256,512]{1,0:T(8,128)(2,1)S(1)}, bf16[256,512]{1,0:T(8,128)(2,1)S(1)}, u32[]{:S(2)}, u32[]{:S(2)}) %collective-permute-start.4) | collective-permute-done | bytes 262176 | tf_op jit(solution)/shard_map/ppermute | solution.py:32
  38.1 1.4 collective-permute-start.5
  39.7 1.3 collective-permute-done.5.got_ref
  41.0 4.9 %gate_rows.1 = (bf16[512,512]{1,0:T(8,128)(2,1)S(1)}, bf16[512,512]{1,0:T(8,128)(2,1)}, bf16[1024,512]{1,0:T(8,128)(2,1)S(1)}) custom-call(s32[2]{0:T(128)S(1)} %pad_add_fusion.where_ref, bf16[512,512]{1,0:T(8,128)(2,1)S(1)} %constant_dynamic-update-slice_fusion.held_ref, bf16[512,512]{1,0:T(8,128)(2,1)S(1)} %collective-permute-done.5.got_ref, ...), custom_call_target="tpu_custom_call" | custom-call | flops 1879048192 | bytes 3801088 | tf_op jit(solution)/shard_map/gate_rows/pallas_call | solution.py:249
  46.0 0.8 collective-permute-start.6
  46.8 3.5 %up_rows.1 = (bf16[512,512]{1,0:T(8,128)(2,1)S(1)}, bf16[512,512]{1,0:T(8,128)(2,1)}) custom-call(bf16[1024,512]{1,0:T(8,128)(2,1)S(1)} %get-tuple-element.17.id_ref.rows_ref.refs_0_, bf16[1024,512]{1,0:T(8,128)(2,1)S(1)} %get-tuple-element.17.id_ref.rows_ref.refs_0_, bf16[4,448,512]{2,1,0:T(8,128)(2,1)S(1)} %copy-done), custom_call_target="tpu_custom_call" | custom-call | flops 1879048192 | bytes 3801088 | tf_op jit(solution)/shard_map/up_rows/pallas_call | solution.py:260
  50.9 2.4 %copy.20.refs_2_.refs_1_ = bf16[4,512,448]{2,1,0:T(8,128)(2,1)} copy(bf16[4,512,448]{1,2,0:T(8,128)(2,1)S(1)} %copy-done.5) | data formatting | bytes 3670016 | tf_op args[6]
  53.3 7.6 %act_grad_rows.1 = (bf16[512,512]{1,0:T(8,128)(2,1)S(1)}, bf16[512,512]{1,0:T(8,128)(2,1)S(1)}, bf16[1024,448]{1,0:T(8,128)(2,1)S(1)}) custom-call(s32[2]{0:T(128)S(1)} %pad_add_fusion.where_ref, bf16[512,448]{1,0:T(8,128)(2,1)S(1)} %constant_dynamic-update-slice_fusion.9.held_ref, bf16[512,448]{1,0:T(8,128)(2,1)} %collective-permute-done.26.got_ref, ...), custom_call_target="tpu_custom_call" | custom-call | flops 1879048192 | bytes 3801088 | tf_op jit(solution)/shard_map/act_grad_rows/pallas_call | solution.py:270
  60.9 1.0 collective-permute-start.27
  61.9 1.2 add_convert_fusion.9
  63.7 7.0 %collective-permute-done.9 = bf16[512,512]{1,0:T(8,128)(2,1)} collective-permute-done((bf16[512,512]{1,0:T(8,128)(2,1)}, bf16[512,512]{1,0:T(8,128)(2,1)}, u32[]{:S(2)}, u32[]{:S(2)}) %collective-permute-start.9) | collective-permute-done | bytes 524320 | tf_op jit(solution)/shard_map/ppermute | solution.py:32
  70.7 1.2 add_convert_fusion.7
  71.8 1.0 collective-permute-start.10
  73.7 9.1 %collective-permute-done.7 = bf16[256,512]{1,0:T(8,128)(2,1)S(1)} collective-permute-done((bf16[256,512]{1,0:T(8,128)(2,1)S(1)}, bf16[256,512]{1,0:T(8,128)(2,1)S(1)}, u32[]{:S(2)}, u32[]{:S(2)}) %collective-permute-start.7) | collective-permute-done | bytes 262176 | tf_op jit(solution)/shard_map/ppermute | solution.py:32
  82.9 1.1 collective-permute-start.8
  84.0 5.1 %collective-permute-done.10 = bf16[256,512]{1,0:T(8,128)(2,1)S(1)} collective-permute-done((bf16[256,512]{1,0:T(8,128)(2,1)S(1)}, bf16[256,512]{1,0:T(8,128)(2,1)S(1)}, u32[]{:S(2)}, u32[]{:S(2)}) %collective-permute-start.10) | collective-permute-done | bytes 262176 | tf_op jit(solution)/shard_map/ppermute | solution.py:32
  89.1 1.6 collective-permute-start.11
  90.8 1.0 collective-permute-start.29
  91.7 5.0 %collective-permute-done.8 = bf16[128,512]{1,0:T(8,128)(2,1)S(1)} collective-permute-done((bf16[128,512]{1,0:T(8,128)(2,1)S(1)}, bf16[128,512]{1,0:T(8,128)(2,1)S(1)}, u32[]{:S(2)}, u32[]{:S(2)}) %collective-permute-start.8) | collective-permute-done | bytes 131104 | tf_op jit(solution)/shard_map/ppermute | solution.py:32
  96.7 3.0 %collective-permute-done.11 = bf16[128,512]{1,0:T(8,128)(2,1)S(1)} collective-permute-done((bf16[128,512]{1,0:T(8,128)(2,1)S(1)}, bf16[128,512]{1,0:T(8,128)(2,1)S(1)}, u32[]{:S(2)}, u32[]{:S(2)}) %collective-permute-start.11) | collective-permute-done | bytes 131104 | tf_op jit(solution)/shard_map/ppermute | solution.py:32
  100.0 3.2 %collective-permute-start.12 = (bf16[128,512]{1,0:T(8,128)(2,1)S(1)}, bf16[128,512]{1,0:T(8,128)(2,1)S(1)}, u32[]{:S(2)}, u32[]{:S(2)}) collective-permute-start(bf16[128,512]{1,0:T(8,128)(2,1)S(1)} %get-tuple-element.41), channel_id=1, source_target_pairs={{0,4},{1,5},{2,6},{3,7},{4,0},{5,1},{6,2},{7,3},{8,12},{9,13},{10,... | collective-permute-start | bytes 393224 | tf_op jit(solution)/shard_map/ppermute | solution.py:32
  103.3 7.7 %collective-permute-done.12 = bf16[128,512]{1,0:T(8,128)(2,1)S(1)} collective-permute-done((bf16[128,512]{1,0:T(8,128)(2,1)S(1)}, bf16[128,512]{1,0:T(8,128)(2,1)S(1)}, u32[]{:S(2)}, u32[]{:S(2)}) %collective-permute-start.12) | collective-permute-done | bytes 131104 | tf_op jit(solution)/shard_map/ppermute | solution.py:32
  111.0 3.0 %collective-permute-start.13 = (bf16[256,512]{1,0:T(8,128)(2,1)S(1)}, bf16[256,512]{1,0:T(8,128)(2,1)S(1)}, u32[]{:S(2)}, u32[]{:S(2)}) collective-permute-start(bf16[256,512]{1,0:T(8,128)(2,1)S(1)} %pad_maximum_fusion.4), channel_id=1, source_target_pairs={{0,2},{1,3},{2,0},{3,1},{4,6},{5,7},{6,4},{7,5},{8,10},{9,11},{10,... | collective-permute-start | bytes 786440 | tf_op jit(solution)/shard_map/ppermute | solution.py:32
  114.0 0.7 collective-permute-start.33
  114.8 2.1 collective-permute-start.31
  116.8 1.3 collective-permute-done.33
  118.8 1.4 collective-permute-done.13
  120.4 10.1 %collective-permute-done.31 = bf16[256,512]{1,0:T(8,128)(2,1)S(1)} collective-permute-done((bf16[256,512]{1,0:T(8,128)(2,1)S(1)}, bf16[256,512]{1,0:T(8,128)(2,1)S(1)}, u32[]{:S(2)}, u32[]{:S(2)}) %collective-permute-start.31) | collective-permute-done | bytes 262176 | tf_op jit(solution)/shard_map/ppermute | solution.py:32
  131.6 2.0 collective-permute-start.35
  133.6 5.8 %out_rows.1 = (bf16[512,448]{1,0:T(8,128)(2,1)S(1)}, bf16[512,448]{1,0:T(8,128)(2,1)S(1)}) custom-call(s32[2]{0:T(128)S(1)} %pad_add_fusion.where_ref, bf16[1024,512]{1,0:T(8,128)(2,1)S(1)} %copy-done.2, bf16[512,512]{1,0:T(8,128)(2,1)S(1)} %pad_maximum_fusion.refs_0_.held_ref, bf16[512,512]{1,0:T(8,128)(2,1)S(1)} %collective-permute-done.14.refs_1_.got_ref, ...), custom_call_target="tpu_custom_call" | custom-call | flops 1879048192 | bytes 3801088 | tf_op jit(solution)/shard_map/out_rows/pallas_call | solution.py:301
  139.5 5.2 %collective-permute-start.15 = (bf16[512,448]{1,0:T(8,128)(2,1)S(1)}, bf16[512,448]{1,0:T(8,128)(2,1)}, u32[]{:S(2)}, u32[]{:S(2)}) collective-permute-start(bf16[512,448]{1,0:T(8,128)(2,1)S(1)} %get-tuple-element.23), channel_id=1, source_target_pairs={{0,8},{1,9},{2,10},{3,11},{4,12},{5,13},{6,14},{7,15},{8,0},{9,1},... | collective-permute-start | bytes 1376264 | tf_op jit(solution)/shard_map/ppermute | solution.py:32
  144.7 18.0 %token_rows.1 = (bf16[512,448]{1,0:T(8,128)(2,1)S(1)}, bf16[512,448]{1,0:T(8,128)(2,1)S(1)}) custom-call(s32[2]{0:T(128)S(1)} %pad_add_fusion.where_ref, bf16[1024,512]{1,0:T(8,128)(2,1)} %copy-done.1, bf16[512,512]{1,0:T(8,128)(2,1)S(1)} %pad_maximum_fusion.1.refs_0_.held_ref, bf16[512,512]{1,0:T(8,128)(2,1)S(1)} %collective-permute-done.32.refs_1_.got_ref, ...), custom_call_target="tpu_custom_call" | custom-call | flops 3758096384 | bytes 7602176 | tf_op jit(solution)/shard_map/token_rows/pallas_call | solution.py:301
  162.7 2.8 %collective-permute-start.36 = (bf16[512,448]{1,0:T(8,128)(2,1)S(1)}, bf16[512,448]{1,0:T(8,128)(2,1)}, u32[]{:S(2)}, u32[]{:S(2)}) collective-permute-start(bf16[512,448]{1,0:T(8,128)(2,1)S(1)} %get-tuple-element.27), channel_id=1, source_target_pairs={{0,8},{1,9},{2,10},{3,11},{4,12},{5,13},{6,14},{7,15},{8,0},{9,1},... | collective-permute-start | bytes 1376264 | tf_op jit(solution)/shard_map/ppermute | solution.py:32
  165.5 4.4 %grad_up.1 = bf16[4,448,512]{2,1,0:T(8,128)(2,1)} custom-call(bf16[1024,512]{1,0:T(8,128)(2,1)S(1)} %copy-done.3, bf16[1024,512]{1,0:T(8,128)(2,1)S(1)} %copy-done.3, bf16[512,512]{1,0:T(8,128)(2,1)S(1)} %pad_maximum_fusion.2.refs_3_.held_ref, bf16[512,512]{1,0:T(8,128)(2,1)S(1)} %collective-permute-done.35.refs_4_.got_ref), custom_call_target="tpu_custom_call" | custom-call | flops 1879048192 | bytes 3801088 | tf_op jit(solution)/shard_map/grad_up/pallas_call | solution.py:315
  170.0 4.1 %grad_down.1 = bf16[4,512,448]{2,1,0:T(8,128)(2,1)} custom-call(bf16[1024,512]{1,0:T(8,128)(2,1)S(1)} %copy-done.3, bf16[1024,448]{1,0:T(8,128)(2,1)S(1)} %get-tuple-element.28.rows_ref, bf16[512,512]{1,0:T(8,128)(2,1)S(1)} %pad_maximum_fusion.refs_0_.held_ref, bf16[512,512]{1,0:T(8,128)(2,1)S(1)} %collective-permute-done.14.refs_1_.got_ref), custom_call_target="tpu_custom_call" | custom-call | flops 1879048192 | bytes 3801088 | tf_op jit(solution)/shard_map/grad_down/pallas_call | solution.py:315
  174.1 4.0 %copy.22 = bf16[4,512,448]{1,2,0:T(8,128)(2,1)} copy(bf16[4,512,448]{2,1,0:T(8,128)(2,1)} %grad_down.1) | data formatting | bytes 3670016
  178.1 1.2 copy-done.4
  179.3 4.5 %grad_gate.1 = bf16[4,448,512]{2,1,0:T(8,128)(2,1)} custom-call(bf16[1024,512]{1,0:T(8,128)(2,1)S(1)} %copy-done.4, bf16[1024,512]{1,0:T(8,128)(2,1)S(1)} %copy-done.4, bf16[512,512]{1,0:T(8,128)(2,1)S(1)} %pad_maximum_fusion.1.refs_0_.held_ref, bf16[512,512]{1,0:T(8,128)(2,1)S(1)} %collective-permute-done.32.refs_1_.got_ref), custom_call_target="tpu_custom_call" | custom-call | flops 1879048192 | bytes 3801088 | tf_op jit(solution)/shard_map/grad_gate/pallas_call | solution.py:315
  183.8 1.2 add_convert_fusion.5
  185.0 1.6 collective-permute-start.16
  186.6 1.2 add_convert_fusion.1
  187.8 5.2 %collective-permute-done.16 = bf16[256,448]{1,0:T(8,128)(2,1)S(1)} collective-permute-done((bf16[256,448]{1,0:T(8,128)(2,1)S(1)}, bf16[256,448]{1,0:T(8,128)(2,1)S(1)}, u32[]{:S(2)}, u32[]{:S(2)}) %collective-permute-start.16) | collective-permute-done | bytes 229408 | tf_op jit(solution)/shard_map/ppermute | solution.py:32
  193.2 5.2 %collective-permute-start.18 = (bf16[64,448]{1,0:T(8,128)(2,1)S(1)}, bf16[64,448]{1,0:T(8,128)(2,1)S(1)}, u32[]{:S(2)}, u32[]{:S(2)}) collective-permute-start(bf16[64,448]{1,0:T(8,128)(2,1)S(1)} %get-tuple-element.56), channel_id=1, source_target_pairs={{8,0},{9,1},{0,2},{1,3},{24,4},{25,5},{16,6},{17,7},{10,8},{11,9},... | collective-permute-start | bytes 172040 | tf_op jit(solution)/shard_map/ppermute | solution.py:77
  199.0 4.3 %collective-permute-start.17 = (bf16[64,448]{1,0:T(8,128)(2,1)S(1)}, bf16[64,448]{1,0:T(8,128)(2,1)S(1)}, u32[]{:S(2)}, u32[]{:S(2)}) collective-permute-start(bf16[64,448]{1,0:T(8,128)(2,1)S(1)} %get-tuple-element.59), channel_id=1, source_target_pairs={{0,0},{1,1},{8,2},{9,3},{16,4},{17,5},{24,6},{25,7},{2,8},{3,9},{1... | collective-permute-start | bytes 172040 | tf_op jit(solution)/shard_map/ppermute | solution.py:77
  203.3 1.9 collective-permute-start.39
  205.2 1.5 collective-permute-done.19
  206.7 1.4 collective-permute-start.40
  208.2 6.6 %collective-permute-done.40 = bf16[64,448]{1,0:T(8,128)(2,1)S(1)} collective-permute-done((bf16[64,448]{1,0:T(8,128)(2,1)S(1)}, bf16[64,448]{1,0:T(8,128)(2,1)S(1)}, u32[]{:S(2)}, u32[]{:S(2)}) %collective-permute-start.40) | collective-permute-done | bytes 57376 | tf_op jit(solution)/shard_map/ppermute | solution.py:77
  214.8 3.4 %collective-permute-start.38 = (bf16[64,448]{1,0:T(8,128)(2,1)S(1)}, bf16[64,448]{1,0:T(8,128)(2,1)S(1)}, u32[]{:S(2)}, u32[]{:S(2)}) collective-permute-start(bf16[64,448]{1,0:T(8,128)(2,1)S(1)} %get-tuple-element.55), channel_id=1, source_target_pairs={{0,0},{1,1},{8,2},{9,3},{16,4},{17,5},{24,6},{25,7},{2,8},{3,9},{1... | collective-permute-start | bytes 172040 | tf_op jit(solution)/shard_map/ppermute | solution.py:77
  218.2 3.7 %collective-permute-done.38 = bf16[64,448]{1,0:T(8,128)(2,1)S(1)} collective-permute-done((bf16[64,448]{1,0:T(8,128)(2,1)S(1)}, bf16[64,448]{1,0:T(8,128)(2,1)S(1)}, u32[]{:S(2)}, u32[]{:S(2)}) %collective-permute-start.38) | collective-permute-done | bytes 57376 | tf_op jit(solution)/shard_map/ppermute | solution.py:77
  222.0 0.8 pad_maximum_fusion.8
  222.8 0.8 multiply_convert_fusion.1
  (100 shorter events, 7.0 us)
Async XLA Ops:
  1.8 10.7 %collective-permute-start.24 = (bf16[64,448]{1,0:T(8,128)(2,1)S(1)}, bf16[64,448]{1,0:T(8,128)(2,1)S(1)}, u32[]{:S(2)}, u32[]{:S(2)}) collective-permute-start(bf16[64,448]{1,0:T(8,128)(2,1)S(1)} %get-tuple-element.68), channel_id=1, source_target_pairs={{0,25},{1,24},{2,17},{3,16},{4,9},{5,8},{6,1},{7,0},{8,27},{9,26},... | collective-permute-start | bytes 172040 | tf_op jit(solution)/shard_map/ppermute | solution.py:52
  3.0 15.4 %collective-permute-start.23 = (bf16[64,448]{1,0:T(8,128)(2,1)S(1)}, bf16[64,448]{1,0:T(8,128)(2,1)S(1)}, u32[]{:S(2)}, u32[]{:S(2)}) collective-permute-start(bf16[64,448]{1,0:T(8,128)(2,1)S(1)} %get-tuple-element.69), channel_id=1, source_target_pairs={{0,17},{1,16},{2,25},{3,24},{4,1},{5,0},{6,9},{7,8},{8,19},{9,18},... | collective-permute-start | bytes 172040 | tf_op jit(solution)/shard_map/ppermute | solution.py:52
  4.9 13.8 %collective-permute-start.22 = (bf16[64,448]{1,0:T(8,128)(2,1)S(1)}, bf16[64,448]{1,0:T(8,128)(2,1)S(1)}, u32[]{:S(2)}, u32[]{:S(2)}) collective-permute-start(bf16[64,448]{1,0:T(8,128)(2,1)S(1)} %get-tuple-element.70), channel_id=1, source_target_pairs={{0,8},{1,9},{2,0},{3,1},{4,24},{5,25},{6,16},{7,17},{8,10},{9,11},... | collective-permute-start | bytes 172040 | tf_op jit(solution)/shard_map/ppermute | solution.py:52
  7.1 15.8 %collective-permute-start.21 = (bf16[64,448]{1,0:T(8,128)(2,1)S(1)}, bf16[64,448]{1,0:T(8,128)(2,1)S(1)}, u32[]{:S(2)}, u32[]{:S(2)}) collective-permute-start(bf16[64,448]{1,0:T(8,128)(2,1)S(1)} %get-tuple-element.71), channel_id=1, source_target_pairs={{0,0},{1,1},{2,8},{3,9},{4,16},{5,17},{6,24},{7,25},{8,2},{9,3},{1... | collective-permute-start | bytes 172040 | tf_op jit(solution)/shard_map/ppermute | solution.py:52
  12.2 10.8 %collective-permute-start.3 = (bf16[64,512]{1,0:T(8,128)(2,1)S(1)}, bf16[64,512]{1,0:T(8,128)(2,1)S(1)}, u32[]{:S(2)}, u32[]{:S(2)}) collective-permute-start(bf16[64,512]{1,0:T(8,128)(2,1)S(1)} %get-tuple-element.72), channel_id=1, source_target_pairs={{0,25},{1,24},{2,17},{3,16},{4,9},{5,8},{6,1},{7,0},{8,27},{9,26},... | collective-permute-start | bytes 196616 | tf_op jit(solution)/shard_map/ppermute | solution.py:52
  12.5 10.4 %collective-permute-start.2 = (bf16[64,512]{1,0:T(8,128)(2,1)S(1)}, bf16[64,512]{1,0:T(8,128)(2,1)S(1)}, u32[]{:S(2)}, u32[]{:S(2)}) collective-permute-start(bf16[64,512]{1,0:T(8,128)(2,1)S(1)} %get-tuple-element.73), channel_id=1, source_target_pairs={{0,17},{1,16},{2,25},{3,24},{4,1},{5,0},{6,9},{7,8},{8,19},{9,18},... | collective-permute-start | bytes 196616 | tf_op jit(solution)/shard_map/ppermute | solution.py:52
  18.4 5.6 %collective-permute-start.1 = (bf16[64,512]{1,0:T(8,128)(2,1)S(1)}, bf16[64,512]{1,0:T(8,128)(2,1)S(1)}, u32[]{:S(2)}, u32[]{:S(2)}) collective-permute-start(bf16[64,512]{1,0:T(8,128)(2,1)S(1)} %get-tuple-element.74), channel_id=1, source_target_pairs={{0,8},{1,9},{2,0},{3,1},{4,24},{5,25},{6,16},{7,17},{8,10},{9,11},... | collective-permute-start | bytes 196616 | tf_op jit(solution)/shard_map/ppermute | solution.py:52
  18.7 10.8 %collective-permute-start = (bf16[64,512]{1,0:T(8,128)(2,1)S(1)}, bf16[64,512]{1,0:T(8,128)(2,1)S(1)}, u32[]{:S(2)}, u32[]{:S(2)}) collective-permute-start(bf16[64,512]{1,0:T(8,128)(2,1)S(1)} %get-tuple-element.75), channel_id=1, source_target_pairs={{0,0},{1,1},{2,8},{3,9},{4,16},{5,17},{6,24},{7,25},{8,2},{9,3},{1... | collective-permute-start | bytes 196616 | tf_op jit(solution)/shard_map/ppermute | solution.py:52
  22.9 16.6 %collective-permute-start.25 = (bf16[256,448]{1,0:T(8,128)(2,1)S(1)}, bf16[256,448]{1,0:T(8,128)(2,1)S(1)}, u32[]{:S(2)}, u32[]{:S(2)}) collective-permute-start(bf16[256,448]{1,0:T(8,128)(2,1)S(1)} %pad_maximum_fusion.5), channel_id=1, source_target_pairs={{0,16},{1,17},{2,18},{3,19},{4,20},{5,21},{6,22},{7,23},{8,24},{9,... | collective-permute-start | bytes 688136 | tf_op jit(solution)/shard_map/ppermute | solution.py:32
  29.5 8.6 %collective-permute-start.4 = (bf16[256,512]{1,0:T(8,128)(2,1)S(1)}, bf16[256,512]{1,0:T(8,128)(2,1)S(1)}, u32[]{:S(2)}, u32[]{:S(2)}) collective-permute-start(bf16[256,512]{1,0:T(8,128)(2,1)S(1)} %pad_maximum_fusion.3), channel_id=1, source_target_pairs={{0,16},{1,17},{2,18},{3,19},{4,20},{5,21},{6,22},{7,23},{8,24},{9,... | collective-permute-start | bytes 786440 | tf_op jit(solution)/shard_map/ppermute | solution.py:32
  38.1 2.9 %collective-permute-start.5 = (bf16[512,512]{1,0:T(8,128)(2,1)S(1)}, bf16[512,512]{1,0:T(8,128)(2,1)S(1)}, u32[]{:S(2)}, u32[]{:S(2)}) collective-permute-start(bf16[512,512]{1,0:T(8,128)(2,1)S(1)} %constant_dynamic-update-slice_fusion.held_ref), channel_id=1, source_target_pairs={{0,8},{1,9},{2,10},{3,11},{4,12},{5,13},{6,14},{7,15},{8,0},{9,1},... | collective-permute-start | bytes 1572872 | tf_op jit(solution)/shard_map/ppermute | solution.py:32
  39.6 7.2 %copy-start = (bf16[4,448,512]{2,1,0:T(8,128)(2,1)S(1)}, bf16[4,448,512]{2,1,0:T(8,128)(2,1)}, u32[]{:S(2)}) copy-start(bf16[4,448,512]{2,1,0:T(8,128)(2,1)} %refs_5_.1) | copy-start | bytes 5505028
  39.6 13.7 %collective-permute-start.26 = (bf16[512,448]{1,0:T(8,128)(2,1)S(1)}, bf16[512,448]{1,0:T(8,128)(2,1)}, u32[]{:S(2)}, u32[]{:S(2)}) collective-permute-start(bf16[512,448]{1,0:T(8,128)(2,1)S(1)} %constant_dynamic-update-slice_fusion.9.held_ref), channel_id=1, source_target_pairs={{0,8},{1,9},{2,10},{3,11},{4,12},{5,13},{6,14},{7,15},{8,0},{9,1},... | collective-permute-start | bytes 1376264 | tf_op jit(solution)/shard_map/ppermute | solution.py:32
  46.0 4.3 %copy-start.1 = (bf16[1024,512]{1,0:T(8,128)(2,1)}, bf16[1024,512]{1,0:T(8,128)(2,1)S(1)}, u32[]{:S(2)}) copy-start(bf16[1024,512]{1,0:T(8,128)(2,1)S(1)} %get-tuple-element.17.id_ref.rows_ref.refs_0_) | copy-start | bytes 3145732
  46.0 15.9 %collective-permute-start.6 = (bf16[512,512]{1,0:T(8,128)(2,1)}, bf16[512,512]{1,0:T(8,128)(2,1)}, u32[]{:S(2)}, u32[]{:S(2)}) collective-permute-start(bf16[512,512]{1,0:T(8,128)(2,1)} %get-tuple-element.19), channel_id=1, source_target_pairs={{0,1},{1,0},{2,3},{3,2},{4,5},{5,4},{6,7},{7,6},{8,9},{9,8},{10,11... | collective-permute-start | bytes 1572872 | tf_op jit(solution)/shard_map/ppermute | solution.py:32
  46.8 4.1 %copy-start.5 = (bf16[4,512,448]{1,2,0:T(8,128)(2,1)S(1)}, bf16[4,512,448]{1,2,0:T(8,128)(2,1)}, u32[]{:S(2)}) copy-start(bf16[4,512,448]{1,2,0:T(8,128)(2,1)} %param.14) | copy-start | bytes 5505028
  50.3 20.4 %collective-permute-start.9 = (bf16[512,512]{1,0:T(8,128)(2,1)}, bf16[512,512]{1,0:T(8,128)(2,1)}, u32[]{:S(2)}, u32[]{:S(2)}) collective-permute-start(bf16[512,512]{1,0:T(8,128)(2,1)} %get-tuple-element.21), channel_id=1, source_target_pairs={{0,1},{1,0},{2,3},{3,2},{4,5},{5,4},{6,7},{7,6},{8,9},{9,8},{10,11... | collective-permute-start | bytes 1572872 | tf_op jit(solution)/shard_map/ppermute | solution.py:32
  60.9 12.6 %collective-permute-start.27 = (bf16[512,512]{1,0:T(8,128)(2,1)S(1)}, bf16[512,512]{1,0:T(8,128)(2,1)S(1)}, u32[]{:S(2)}, u32[]{:S(2)}) collective-permute-start(bf16[512,512]{1,0:T(8,128)(2,1)S(1)} %get-tuple-element.25), channel_id=1, source_target_pairs={{0,2},{1,3},{2,0},{3,1},{4,6},{5,7},{6,4},{7,5},{8,10},{9,11},{10,... | collective-permute-start | bytes 1572872 | tf_op jit(solution)/shard_map/ppermute | solution.py:32
  63.0 19.8 %collective-permute-start.7 = (bf16[256,512]{1,0:T(8,128)(2,1)S(1)}, bf16[256,512]{1,0:T(8,128)(2,1)S(1)}, u32[]{:S(2)}, u32[]{:S(2)}) collective-permute-start(bf16[256,512]{1,0:T(8,128)(2,1)S(1)} %get-tuple-element.49), channel_id=1, source_target_pairs={{0,2},{1,3},{2,0},{3,1},{4,6},{5,7},{6,4},{7,5},{8,10},{9,11},{10,... | collective-permute-start | bytes 786440 | tf_op jit(solution)/shard_map/ppermute | solution.py:32
  71.8 17.3 %collective-permute-start.10 = (bf16[256,512]{1,0:T(8,128)(2,1)S(1)}, bf16[256,512]{1,0:T(8,128)(2,1)S(1)}, u32[]{:S(2)}, u32[]{:S(2)}) collective-permute-start(bf16[256,512]{1,0:T(8,128)(2,1)S(1)} %get-tuple-element.51), channel_id=1, source_target_pairs={{0,2},{1,3},{2,0},{3,1},{4,6},{5,7},{6,4},{7,5},{8,10},{9,11},{10,... | collective-permute-start | bytes 786440 | tf_op jit(solution)/shard_map/ppermute | solution.py:32
  73.6 17.1 %collective-permute-start.28 = (bf16[256,512]{1,0:T(8,128)(2,1)S(1)}, bf16[256,512]{1,0:T(8,128)(2,1)S(1)}, u32[]{:S(2)}, u32[]{:S(2)}) collective-permute-start(bf16[256,512]{1,0:T(8,128)(2,1)S(1)} %get-tuple-element.45), channel_id=1, source_target_pairs={{0,4},{1,5},{2,6},{3,7},{4,0},{5,1},{6,2},{7,3},{8,12},{9,13},{10,... | collective-permute-start | bytes 786440 | tf_op jit(solution)/shard_map/ppermute | solution.py:32
  82.9 13.9 %collective-permute-start.8 = (bf16[128,512]{1,0:T(8,128)(2,1)S(1)}, bf16[128,512]{1,0:T(8,128)(2,1)S(1)}, u32[]{:S(2)}, u32[]{:S(2)}) collective-permute-start(bf16[128,512]{1,0:T(8,128)(2,1)S(1)} %add_convert_fusion.14), channel_id=1, source_target_pairs={{0,4},{1,5},{2,6},{3,7},{4,0},{5,1},{6,2},{7,3},{8,12},{9,13},{10,... | collective-permute-start | bytes 393224 | tf_op jit(solution)/shard_map/ppermute | solution.py:32
  89.1 10.6 %collective-permute-start.11 = (bf16[128,512]{1,0:T(8,128)(2,1)S(1)}, bf16[128,512]{1,0:T(8,128)(2,1)S(1)}, u32[]{:S(2)}, u32[]{:S(2)}) collective-permute-start(bf16[128,512]{1,0:T(8,128)(2,1)S(1)} %add_convert_fusion.12), channel_id=1, source_target_pairs={{0,4},{1,5},{2,6},{3,7},{4,0},{5,1},{6,2},{7,3},{8,12},{9,13},{10,... | collective-permute-start | bytes 393224 | tf_op jit(solution)/shard_map/ppermute | solution.py:32
  90.8 9.0 %collective-permute-start.29 = (bf16[128,512]{1,0:T(8,128)(2,1)S(1)}, bf16[128,512]{1,0:T(8,128)(2,1)S(1)}, u32[]{:S(2)}, u32[]{:S(2)}) collective-permute-start(bf16[128,512]{1,0:T(8,128)(2,1)S(1)} %add_convert_fusion.10), channel_id=1, source_target_pairs={{0,1},{1,0},{2,3},{3,2},{4,5},{5,4},{6,7},{7,6},{8,9},{9,8},{10,11... | collective-permute-start | bytes 393224 | tf_op jit(solution)/shard_map/ppermute | solution.py:32
  100.0 11.0 %collective-permute-start.12 = (bf16[128,512]{1,0:T(8,128)(2,1)S(1)}, bf16[128,512]{1,0:T(8,128)(2,1)S(1)}, u32[]{:S(2)}, u32[]{:S(2)}) collective-permute-start(bf16[128,512]{1,0:T(8,128)(2,1)S(1)} %get-tuple-element.41), channel_id=1, source_target_pairs={{0,4},{1,5},{2,6},{3,7},{4,0},{5,1},{6,2},{7,3},{8,12},{9,13},{10,... | collective-permute-start | bytes 393224 | tf_op jit(solution)/shard_map/ppermute | solution.py:32
  103.2 11.6 %collective-permute-start.30 = (bf16[128,512]{1,0:T(8,128)(2,1)S(1)}, bf16[128,512]{1,0:T(8,128)(2,1)S(1)}, u32[]{:S(2)}, u32[]{:S(2)}) collective-permute-start(bf16[128,512]{1,0:T(8,128)(2,1)S(1)} %get-tuple-element.40), channel_id=1, source_target_pairs={{0,4},{1,5},{2,6},{3,7},{4,0},{5,1},{6,2},{7,3},{8,12},{9,13},{10,... | collective-permute-start | bytes 393224 | tf_op jit(solution)/shard_map/ppermute | solution.py:32
  111.0 9.2 %collective-permute-start.13 = (bf16[256,512]{1,0:T(8,128)(2,1)S(1)}, bf16[256,512]{1,0:T(8,128)(2,1)S(1)}, u32[]{:S(2)}, u32[]{:S(2)}) collective-permute-start(bf16[256,512]{1,0:T(8,128)(2,1)S(1)} %pad_maximum_fusion.4), channel_id=1, source_target_pairs={{0,2},{1,3},{2,0},{3,1},{4,6},{5,7},{6,4},{7,5},{8,10},{9,11},{10,... | collective-permute-start | bytes 786440 | tf_op jit(solution)/shard_map/ppermute | solution.py:32
  114.0 4.2 %collective-permute-start.33 = (bf16[128,512]{1,0:T(8,128)(2,1)S(1)}, bf16[128,512]{1,0:T(8,128)(2,1)S(1)}, u32[]{:S(2)}, u32[]{:S(2)}) collective-permute-start(bf16[128,512]{1,0:T(8,128)(2,1)S(1)} %get-tuple-element.39), channel_id=1, source_target_pairs={{0,1},{1,0},{2,3},{3,2},{4,5},{5,4},{6,7},{7,6},{8,9},{9,8},{10,11... | collective-permute-start | bytes 393224 | tf_op jit(solution)/shard_map/ppermute | solution.py:32
  114.7 18.9 %copy-start.2 = (bf16[1024,512]{1,0:T(8,128)(2,1)S(1)}, bf16[1024,512]{1,0:T(8,128)(2,1)}, u32[]{:S(2)}) copy-start(bf16[1024,512]{1,0:T(8,128)(2,1)} %copy-done.1) | copy-start | bytes 3145732
  114.8 15.8 %collective-permute-start.31 = (bf16[256,512]{1,0:T(8,128)(2,1)S(1)}, bf16[256,512]{1,0:T(8,128)(2,1)S(1)}, u32[]{:S(2)}, u32[]{:S(2)}) collective-permute-start(bf16[256,512]{1,0:T(8,128)(2,1)S(1)} %pad_maximum_fusion.6), channel_id=1, source_target_pairs={{0,2},{1,3},{2,0},{3,1},{4,6},{5,7},{6,4},{7,5},{8,10},{9,11},{10,... | collective-permute-start | bytes 786440 | tf_op jit(solution)/shard_map/ppermute | solution.py:32
  118.2 13.4 %collective-permute-start.34 = (bf16[256,512]{1,0:T(8,128)(2,1)S(1)}, bf16[256,512]{1,0:T(8,128)(2,1)S(1)}, u32[]{:S(2)}, u32[]{:S(2)}) collective-permute-start(bf16[256,512]{1,0:T(8,128)(2,1)S(1)} %pad_maximum_fusion.7), channel_id=1, source_target_pairs={{0,4},{1,5},{2,6},{3,7},{4,0},{5,1},{6,2},{7,3},{8,12},{9,13},{10,... | collective-permute-start | bytes 786440 | tf_op jit(solution)/shard_map/ppermute | solution.py:32
  120.2 13.4 %collective-permute-start.14 = (bf16[512,512]{1,0:T(8,128)(2,1)S(1)}, bf16[512,512]{1,0:T(8,128)(2,1)S(1)}, u32[]{:S(2)}, u32[]{:S(2)}) collective-permute-start(bf16[512,512]{1,0:T(8,128)(2,1)S(1)} %pad_maximum_fusion.refs_0_.held_ref), channel_id=1, source_target_pairs={{0,1},{1,0},{2,3},{3,2},{4,5},{5,4},{6,7},{7,6},{8,9},{9,8},{10,11... | collective-permute-start | bytes 1572872 | tf_op jit(solution)/shard_map/ppermute | solution.py:32
  130.6 14.1 %collective-permute-start.32 = (bf16[512,512]{1,0:T(8,128)(2,1)S(1)}, bf16[512,512]{1,0:T(8,128)(2,1)S(1)}, u32[]{:S(2)}, u32[]{:S(2)}) collective-permute-start(bf16[512,512]{1,0:T(8,128)(2,1)S(1)} %pad_maximum_fusion.1.refs_0_.held_ref), channel_id=1, source_target_pairs={{0,1},{1,0},{2,3},{3,2},{4,5},{5,4},{6,7},{7,6},{8,9},{9,8},{10,11... | collective-permute-start | bytes 1572872 | tf_op jit(solution)/shard_map/ppermute | solution.py:32
  131.6 13.1 %collective-permute-start.35 = (bf16[512,512]{1,0:T(8,128)(2,1)S(1)}, bf16[512,512]{1,0:T(8,128)(2,1)S(1)}, u32[]{:S(2)}, u32[]{:S(2)}) collective-permute-start(bf16[512,512]{1,0:T(8,128)(2,1)S(1)} %pad_maximum_fusion.2.refs_3_.held_ref), channel_id=1, source_target_pairs={{0,2},{1,3},{2,0},{3,1},{4,6},{5,7},{6,4},{7,5},{8,10},{9,11},{10,... | collective-permute-start | bytes 1572872 | tf_op jit(solution)/shard_map/ppermute | solution.py:32
  139.5 26.1 %copy-start.3 = (bf16[1024,512]{1,0:T(8,128)(2,1)S(1)}, bf16[1024,512]{1,0:T(8,128)(2,1)}, u32[]{:S(2)}) copy-start(bf16[1024,512]{1,0:T(8,128)(2,1)} %copy-done.1) | copy-start | bytes 3145732
  139.5 44.3 %collective-permute-start.15 = (bf16[512,448]{1,0:T(8,128)(2,1)S(1)}, bf16[512,448]{1,0:T(8,128)(2,1)}, u32[]{:S(2)}, u32[]{:S(2)}) collective-permute-start(bf16[512,448]{1,0:T(8,128)(2,1)S(1)} %get-tuple-element.23), channel_id=1, source_target_pairs={{0,8},{1,9},{2,10},{3,11},{4,12},{5,13},{6,14},{7,15},{8,0},{9,1},... | collective-permute-start | bytes 1376264 | tf_op jit(solution)/shard_map/ppermute | solution.py:32
  162.7 23.9 %collective-permute-start.36 = (bf16[512,448]{1,0:T(8,128)(2,1)S(1)}, bf16[512,448]{1,0:T(8,128)(2,1)}, u32[]{:S(2)}, u32[]{:S(2)}) collective-permute-start(bf16[512,448]{1,0:T(8,128)(2,1)S(1)} %get-tuple-element.27), channel_id=1, source_target_pairs={{0,8},{1,9},{2,10},{3,11},{4,12},{5,13},{6,14},{7,15},{8,0},{9,1},... | collective-permute-start | bytes 1376264 | tf_op jit(solution)/shard_map/ppermute | solution.py:32
  178.1 1.2 copy-start.4
  185.0 8.1 %collective-permute-start.16 = (bf16[256,448]{1,0:T(8,128)(2,1)S(1)}, bf16[256,448]{1,0:T(8,128)(2,1)S(1)}, u32[]{:S(2)}, u32[]{:S(2)}) collective-permute-start(bf16[256,448]{1,0:T(8,128)(2,1)S(1)} %get-tuple-element.47), channel_id=1, source_target_pairs={{0,16},{1,17},{2,18},{3,19},{4,20},{5,21},{6,22},{7,23},{8,24},{9,... | collective-permute-start | bytes 688136 | tf_op jit(solution)/shard_map/ppermute | solution.py:32
  187.8 15.5 %collective-permute-start.37 = (bf16[256,448]{1,0:T(8,128)(2,1)S(1)}, bf16[256,448]{1,0:T(8,128)(2,1)S(1)}, u32[]{:S(2)}, u32[]{:S(2)}) collective-permute-start(bf16[256,448]{1,0:T(8,128)(2,1)S(1)} %get-tuple-element.43), channel_id=1, source_target_pairs={{0,16},{1,17},{2,18},{3,19},{4,20},{5,21},{6,22},{7,23},{8,24},{9,... | collective-permute-start | bytes 688136 | tf_op jit(solution)/shard_map/ppermute | solution.py:32
  193.2 29.7 %copy-start.6 = (f32[128,1]{0,1:T(1,128)S(1)}, f32[128,1]{0,1:T(1,128)}, u32[]{:S(2)}) copy-start(f32[128,1]{0,1:T(1,128)} %param.10) | copy-start | bytes 1540
  193.2 28.7 %collective-permute-start.18 = (bf16[64,448]{1,0:T(8,128)(2,1)S(1)}, bf16[64,448]{1,0:T(8,128)(2,1)S(1)}, u32[]{:S(2)}, u32[]{:S(2)}) collective-permute-start(bf16[64,448]{1,0:T(8,128)(2,1)S(1)} %get-tuple-element.56), channel_id=1, source_target_pairs={{8,0},{9,1},{0,2},{1,3},{24,4},{25,5},{16,6},{17,7},{10,8},{11,9},... | collective-permute-start | bytes 172040 | tf_op jit(solution)/shard_map/ppermute | solution.py:77
  198.4 23.5 %collective-permute-start.20 = (bf16[64,448]{1,0:T(8,128)(2,1)S(1)}, bf16[64,448]{1,0:T(8,128)(2,1)S(1)}, u32[]{:S(2)}, u32[]{:S(2)}) collective-permute-start(bf16[64,448]{1,0:T(8,128)(2,1)S(1)} %get-tuple-element.57), channel_id=1, source_target_pairs={{25,0},{24,1},{17,2},{16,3},{9,4},{8,5},{1,6},{0,7},{27,8},{26,9},... | collective-permute-start | bytes 172040 | tf_op jit(solution)/shard_map/ppermute | solution.py:77
  199.0 7.8 %collective-permute-start.19 = (bf16[64,448]{1,0:T(8,128)(2,1)S(1)}, bf16[64,448]{1,0:T(8,128)(2,1)S(1)}, u32[]{:S(2)}, u32[]{:S(2)}) collective-permute-start(bf16[64,448]{1,0:T(8,128)(2,1)S(1)} %get-tuple-element.58), channel_id=1, source_target_pairs={{17,0},{16,1},{25,2},{24,3},{1,4},{0,5},{9,6},{8,7},{19,8},{18,9},... | collective-permute-start | bytes 172040 | tf_op jit(solution)/shard_map/ppermute | solution.py:77
  199.0 7.8 %collective-permute-start.17 = (bf16[64,448]{1,0:T(8,128)(2,1)S(1)}, bf16[64,448]{1,0:T(8,128)(2,1)S(1)}, u32[]{:S(2)}, u32[]{:S(2)}) collective-permute-start(bf16[64,448]{1,0:T(8,128)(2,1)S(1)} %get-tuple-element.59), channel_id=1, source_target_pairs={{0,0},{1,1},{8,2},{9,3},{16,4},{17,5},{24,6},{25,7},{2,8},{3,9},{1... | collective-permute-start | bytes 172040 | tf_op jit(solution)/shard_map/ppermute | solution.py:77
  203.3 18.6 %collective-permute-start.39 = (bf16[64,448]{1,0:T(8,128)(2,1)S(1)}, bf16[64,448]{1,0:T(8,128)(2,1)S(1)}, u32[]{:S(2)}, u32[]{:S(2)}) collective-permute-start(bf16[64,448]{1,0:T(8,128)(2,1)S(1)} %get-tuple-element.52), channel_id=1, source_target_pairs={{8,0},{9,1},{0,2},{1,3},{24,4},{25,5},{16,6},{17,7},{10,8},{11,9},... | collective-permute-start | bytes 172040 | tf_op jit(solution)/shard_map/ppermute | solution.py:77
  206.7 15.2 %collective-permute-start.41 = (bf16[64,448]{1,0:T(8,128)(2,1)S(1)}, bf16[64,448]{1,0:T(8,128)(2,1)S(1)}, u32[]{:S(2)}, u32[]{:S(2)}) collective-permute-start(bf16[64,448]{1,0:T(8,128)(2,1)S(1)} %get-tuple-element.53), channel_id=1, source_target_pairs={{25,0},{24,1},{17,2},{16,3},{9,4},{8,5},{1,6},{0,7},{27,8},{26,9},... | collective-permute-start | bytes 172040 | tf_op jit(solution)/shard_map/ppermute | solution.py:77
  206.7 8.0 %collective-permute-start.40 = (bf16[64,448]{1,0:T(8,128)(2,1)S(1)}, bf16[64,448]{1,0:T(8,128)(2,1)S(1)}, u32[]{:S(2)}, u32[]{:S(2)}) collective-permute-start(bf16[64,448]{1,0:T(8,128)(2,1)S(1)} %get-tuple-element.54), channel_id=1, source_target_pairs={{17,0},{16,1},{25,2},{24,3},{1,4},{0,5},{9,6},{8,7},{19,8},{18,9},... | collective-permute-start | bytes 172040 | tf_op jit(solution)/shard_map/ppermute | solution.py:77
  214.8 7.1 %collective-permute-start.38 = (bf16[64,448]{1,0:T(8,128)(2,1)S(1)}, bf16[64,448]{1,0:T(8,128)(2,1)S(1)}, u32[]{:S(2)}, u32[]{:S(2)}) collective-permute-start(bf16[64,448]{1,0:T(8,128)(2,1)S(1)} %get-tuple-element.55), channel_id=1, source_target_pairs={{0,0},{1,1},{8,2},{9,3},{16,4},{17,5},{24,6},{25,7},{2,8},{3,9},{1... | collective-permute-start | bytes 172040 | tf_op jit(solution)/shard_map/ppermute | solution.py:77

commit v3 on v1

v3 whole, which is shorter than its diff:
```python
import functools

import jax
import jax.numpy as jnp
from jax import lax
from jax.experimental import pallas as pl
from jax.experimental.pallas import tpu as pltpu
from jax.sharding import PartitionSpec as P

AXES = ("grp", "ep")
BF16 = jnp.bfloat16
VMEM = pl.BlockSpec(memory_space=pltpu.VMEM)
SMEM = pl.BlockSpec(memory_space=pltpu.SMEM)
PARAMS = pltpu.CompilerParams(vmem_limit_bytes=50 * 1024 * 1024)
PARTS = 2


def f32(a):
    return a.astype(jnp.float32)


def half(a):
    return a.astype(BF16)


def after(value, *others):
    return lax.optimization_barrier((value,) + others)[0]


def swap(block, grp_bits, ep_bits):
    grp_size, ep_size = lax.axis_size("grp"), lax.axis_size("ep")
    pairs = [
        (g * ep_size + p, (g ^ grp_bits) * ep_size + (p ^ ep_bits))
        for g in range(grp_size)
        for p in range(ep_size)
    ]
    return lax.ppermute(block, AXES, pairs)


def plane_pairs(k):
    grp_size, ep_size = lax.axis_size("grp"), lax.axis_size("ep")
    flip = k * (grp_size // 2)
    return [
        (g * ep_size + p, ((p // 2) ^ flip) * ep_size + 2 * g + ((p % 2) ^ k))
        for g in range(grp_size)
        for p in range(ep_size)
    ]


def spread(pieces):
    grp_size = lax.axis_size("grp")
    landed = [lax.ppermute(pieces[k], AXES, plane_pairs(k)) for k in range(2)]
    held = jnp.concatenate(landed)
    bit = grp_size // 2
    while bit > 1:
        held = jnp.concatenate([held, swap(held, bit, 0)])
        bit //= 2
    return held, swap(held, 1, 0), landed[0]


def unspread(keep, send):
    grp_size = lax.axis_size("grp")
    got = swap(send, 1, 0)
    marks = []
    bit = grp_size // 2
    while bit > 1:
        n = keep.shape[0] // 2
        out = half(f32(keep[n:]) + f32(got[n:]))
        marks.append(out)
        got_next = swap(out, bit, 0)
        keep = half(f32(keep[:n]) + f32(got[:n]))
        got = got_next
        bit //= 2
    size = keep.shape[0] // 2
    pieces = []
    for k in range(2):
        rows = slice(k * size, (k + 1) * size)
        back = [(b, a) for a, b in plane_pairs(k)]
        out = half(f32(keep[rows]) + f32(got[rows]))
        marks.append(out)
        pieces.append(lax.ppermute(out, AXES, back))
    return pieces, marks


def scatter_sum(keep, send, bits):
    got = swap(send, 0, 1 << bits[0])
    for bit in bits[1:]:
        n = keep.shape[0] // 2
        got_next = swap(half(f32(keep[n:]) + f32(got[n:])), 0, 1 << bit)
        keep = half(f32(keep[:n]) + f32(got[:n]))
        got = got_next
    return f32(keep) + f32(got)


def gather(own, bits):
    held = own
    for bit in bits[:-1]:
        held = jnp.concatenate([held, swap(held, 0, 1 << bit)])
    return held, swap(held, 0, 1 << bits[-1])


def block_order(bits):
    order = [0]
    for bit in reversed(bits):
        order = order + [j ^ (1 << bit) for j in order]
    return order


def upright(row):
    n = row.shape[1]
    at = lax.broadcasted_iota(jnp.int32, (n, n), 0) == lax.broadcasted_iota(jnp.int32, (n, n), 1)
    return jnp.sum(jnp.where(at, row, jnp.zeros((), row.dtype)), axis=1, keepdims=True)


def cut_body(stored, count, hot_ref, routes_ref, tokens_ref, own_ref, other_ref):
    y = lax.axis_index("ep") % 2
    slot = upright(routes_ref[...])
    expert = slot
    for r in range(hot_ref.shape[0]):
        expert = jnp.where(slot == count + r, hot_ref[r], expert)
    lane = lax.broadcasted_iota(jnp.int32, (slot.shape[0], own_ref.shape[1] - stored), 1)
    tail = half(jnp.where(lane == 0, f32(expert), 0.0))
    rows = tokens_ref[...]
    first, second = rows[:, :stored], rows[:, stored:]
    own_ref[:, :stored] = jnp.where(y == 0, first, second)
    own_ref[:, stored:] = tail
    other_ref[:, :stored] = jnp.where(y == 0, second, first)
    other_ref[:, stored:] = tail


def weigh_body(stored, weights_ref, rows_ref, own_ref, other_ref):
    y = lax.axis_index("ep") % 2
    rows = half(f32(rows_ref[...]) * upright(weights_ref[...]))
    tail = jnp.zeros((rows.shape[0], own_ref.shape[1] - stored), BF16)
    first, second = rows[:, :stored], rows[:, stored:]
    own_ref[:, :stored] = jnp.where(y == 0, first, second)
    own_ref[:, stored:] = tail
    other_ref[:, :stored] = jnp.where(y == 0, second, first)
    other_ref[:, stored:] = tail


def order_rows(geo, held_ref, got_ref, rows_ref):
    grp_size, tok, order = geo
    sub = tok // PARTS
    bits = grp_size.bit_length() - 1
    shift = lax.axis_index("grp") ^ (lax.axis_index("ep") // 2)
    for place, j in enumerate(order):
        k = j & 1
        m = shift ^ ((j >> 1) ^ (k * (grp_size // 2)))
        at = 0
        for b in range(bits - 1):
            at = at + (((m >> (bits - 1 - b)) & 1) << b)
        src = pl.ds(pl.multiple_of((at * 2 + k) * tok, tok), tok)
        rows = jnp.where((m & 1) == 0, held_ref[src, :], got_ref[src, :])
        for part in range(PARTS):
            to = (part * len(order) + place) * sub
            rows_ref[to : to + sub, :] = rows[part * sub : (part + 1) * sub]


def expert_dot(rows, expert, w_ref, count, turned):
    dims = (((1,), (1 if turned else 0,)), ((), ()))
    total = None
    for e in range(count):
        own = jnp.where(expert == e, rows, jnp.zeros((), BF16))
        part = lax.dot_general(own, w_ref[e], dims, preferred_element_type=jnp.float32)
        total = part if total is None else total + part
    return total


def id_of(id_ref, stored, rows):
    return id_ref[rows, :][:, stored % 128 : stored % 128 + 1]


def first_body(geo, stored, count, n_w, own_ids, held_ref, got_ref, *refs):
    rows_ref = refs[-1]
    order_rows(geo, held_ref, got_ref, rows_ref)
    n = rows_ref.shape[0] // PARTS
    rows = rows_ref[:n, :]
    if own_ids:
        expert = rows[:, stored : stored + 1]
        refs = refs[:-1]
    else:
        expert = id_of(refs[0], stored, slice(0, n))
        refs = refs[1:-1]
    products(rows[:, :stored], expert, count, n_w, refs)


def products(rows, expert, count, n_w, refs):
    keep_ref, send_ref = refs[-2:]
    n = rows.shape[0] // 2
    hidden = keep_ref.shape[1] // n_w
    for i in range(n_w):
        result = half(expert_dot(rows, expert, refs[i], count, False))
        cols = slice(i * hidden, (i + 1) * hidden)
        keep_ref[:, cols] = result[:n]
        send_ref[:, cols] = result[n:]


def later_body(stored, count, n_w, id_ref, rows_ref, *refs):
    expert = id_of(id_ref, stored, slice(None))
    products(rows_ref[:, :stored], expert, count, n_w, refs)


def back_body(geo, stored, count, n_w, id_ref, *refs):
    grp_size, tok, order = geo
    keep_ref, send_ref = refs[-2:]
    sub = tok // PARTS
    shift = lax.axis_index("grp") ^ (lax.axis_index("ep") // 2)
    n = len(order) // 2
    for part in range(PARTS):
        for side in range(2):
            src = refs[n_w + 2 * part + side]
            hidden = src.shape[1] // n_w
            at = (part * 2 + side) * n * sub
            expert = id_of(id_ref, stored, slice(at, at + n * sub))
            total = None
            for i in range(n_w):
                rows = src[:, i * hidden : (i + 1) * hidden]
                now = expert_dot(rows, expert, refs[i], count, True)
                total = now if total is None else total + now
            total = half(total)
            for place in range(n):
                j = order[side * n + place]
                k = j & 1
                m = shift ^ ((j >> 1) ^ (k * (grp_size // 2)))
                to = ((m >> 1) * 2 + k) * tok + part * sub
                to = pl.ds(pl.multiple_of(to, sub), sub)
                block = total[place * sub : (place + 1) * sub]

                @pl.when((m & 1) == 0)
                def _():
                    keep_ref[to, :] = block

                @pl.when((m & 1) == 1)
                def _():
                    send_ref[to, :] = block


def grad_body(stored, cols, id_ref, rows_ref, *refs):
    out_ref = refs[-1]
    expert = half(pl.program_id(0).astype(jnp.float32))
    right = jnp.concatenate([ref[:, cols] for ref in refs[:-1]])
    right = jnp.where(id_of(id_ref, stored, slice(None)) == expert, right, jnp.zeros((), BF16))
    out_ref[0] = half(
        lax.dot_general(
            rows_ref[:, :stored],
            right,
            (((0,), (0,)), ((), ())),
            preferred_element_type=jnp.float32,
        )
    )


def cost(flops, nbytes):
    return pl.CostEstimate(flops=flops, bytes_accessed=nbytes, transcendentals=0)


def full(shape):
    return pl.BlockSpec(shape, lambda *_: (0,) * len(shape))


def shards(tokens, routes, route_weights, hot_experts, w_gate, w_up, w_down, cotangent):
    grp_size, ep_size = lax.axis_size("grp"), lax.axis_size("ep")
    y = lax.axis_index("ep") % 2
    tok = tokens.shape[0]
    w_down = jnp.swapaxes(w_down, 1, 2)
    count, stored, hidden = w_gate.shape
    total = tok * ep_size
    n = total // PARTS
    width = (stored // 128 + 1) * 128
    bits = list(range(ep_size.bit_length() - 1))
    order = block_order(bits)
    geo = (grp_size, tok, order)
    flops = 2 * total * count * stored * hidden
    nbytes = 2 * (total * (stored + hidden) + count * stored * hidden)
    piece = [jax.ShapeDtypeStruct((tok, width), BF16)] * 2

    def call(body, out_shape, args, in_specs=None, part=1.0, name=None, **kw):
        return pl.pallas_call(
            body,
            out_shape=out_shape,
            grid=kw.get("grid", (1,)),
            in_specs=in_specs or [full(a.shape) for a in args],
            out_specs=kw.get("out_specs") or [full(o.shape) for o in out_shape],
            compiler_params=PARAMS,
            cost_estimate=cost(int(flops * part), int(nbytes * part)),
            name=name,
        )(*args)

    x_pieces = call(
        functools.partial(cut_body, stored, count),
        piece,
        (hot_experts, routes.reshape(1, tok), tokens),
        in_specs=[SMEM, full((1, tok)), full(tokens.shape)],
        part=0.01,
        name="token_pieces",
    )
    x_held, x_got, landed = spread(x_pieces)
    cot, _ = lax.optimization_barrier((cotangent, landed))
    dz_pieces = call(
        functools.partial(weigh_body, stored),
        piece,
        (route_weights.reshape(1, tok), cot),
        part=0.01,
        name="cotangent_pieces",
    )
    dz_held, dz_got, _ = spread(dz_pieces)

    rows_shape = jax.ShapeDtypeStruct((total, width), BF16)

    def id_spec(rows, at):
        return pl.BlockSpec((rows, 128), lambda *_: (at, stored // 128))

    def split(n_w):
        return [jax.ShapeDtypeStruct((n // 2, n_w * hidden), BF16)] * 2

    def later(part, rows, weights, name):
        return call(
            functools.partial(later_body, stored, count, len(weights)),
            split(len(weights)),
            (x_rows, rows) + weights,
            in_specs=[
                id_spec(n, part),
                pl.BlockSpec((n, width), lambda *_: (part, 0)),
            ]
            + [full(w.shape) for w in weights],
            part=len(weights) / PARTS,
            name=name,
        )

    gu_keep, gu_send, x_rows = call(
        functools.partial(first_body, geo, stored, count, 2, True),
        split(2) + [rows_shape],
        (x_held, x_got, w_gate, w_up),
        part=2 / PARTS,
        name="gate_up_first",
    )
    ag_keep, ag_send, dz_rows = call(
        functools.partial(first_body, geo, stored, count, 1, False),
        split(1) + [rows_shape],
        (dz_held, dz_got, x_rows, w_down),
        in_specs=[full(dz_held.shape), full(dz_got.shape), id_spec(total, 0), full(w_down.shape)],
        part=1 / PARTS,
        name="act_grad_first",
    )
    gate_up = [(gu_keep, gu_send)]
    act_grad = [(ag_keep, ag_send)]
    mark = ag_send
    for part in range(1, PARTS):
        gate_up.append(later(part, after(x_rows, mark), (w_gate, w_up), "gate_up_later"))
        act_grad.append(later(part, after(dz_rows, gate_up[-1][1]), (w_down,), "act_grad_later"))
        mark = act_grad[-1][1]

    acts, grads = [], []
    for part in range(PARTS):
        gu = scatter_sum(*gate_up[part], bits)
        ag = scatter_sum(*act_grad[part], bits)
        gate_pre, up_pre = gu[:, :hidden], gu[:, hidden:]
        sg = jax.nn.sigmoid(gate_pre)
        act = half(gate_pre * sg * up_pre)
        gate_grad = ag * up_pre * sg * (1.0 + gate_pre * (1.0 - sg))
        up_grad = ag * gate_pre * sg
        both = half(jnp.concatenate([gate_grad, up_grad], axis=1))
        acts.extend(gather(act, bits[::-1]))
        grads.extend(gather(both, bits[::-1]))

    def back(n_w, weights, gathered, name):
        return call(
            functools.partial(back_body, geo, stored, count, n_w),
            [jax.ShapeDtypeStruct((total // 2, stored), BF16)] * 2,
            (x_rows,) + weights + tuple(gathered),
            in_specs=[id_spec(total, 0)] + [full(a.shape) for a in weights + tuple(gathered)],
            part=n_w,
            name=name,
        )

    def grad(rows, gathered, at, name):
        return call(
            functools.partial(grad_body, stored, slice(at * hidden, (at + 1) * hidden)),
            jax.ShapeDtypeStruct((count, stored, hidden), BF16),
            (x_rows, rows) + tuple(gathered),
            in_specs=[id_spec(total, 0)] + [full(a.shape) for a in (rows,) + tuple(gathered)],
            grid=(count,),
            out_specs=pl.BlockSpec((1, stored, hidden), lambda e: (e, 0, 0)),
            name=name,
        )

    def joined(mine, other):
        return jnp.concatenate(
            [jnp.where(y == 0, mine, other), jnp.where(y == 0, other, mine)], axis=1
        )

    pieces, _ = unspread(*back(1, (w_down,), acts, "out_rows"))
    layer_output = half(f32(joined(*pieces)) * route_weights)
    tok_keep, tok_send = back(2, (w_gate, w_up), grads, "token_rows")
    pieces, marks = unspread(tok_keep, tok_send)
    grad_tokens = joined(*pieces)
    grad_down = grad(after(dz_rows, tok_send), acts, 0, "grad_down")
    grad_gate = grad(after(x_rows, marks[0]), grads, 0, "grad_gate")
    grad_up = grad(after(x_rows, *marks), grads, 1, "grad_up")
    return (layer_output, grad_tokens, grad_gate, grad_up, jnp.swapaxes(grad_down, 1, 2))


def solution(mesh):
    placed = (
        P("ep", "grp"),
        P("ep", None),
        P("ep", None),
        P(),
        P(None, "ep", "grp"),
        P(None, "ep", "grp"),
        P(None, "grp", "ep"),
        P("ep", "grp"),
    )
    return jax.shard_map(
        shards,
        mesh=mesh,
        in_specs=placed,
        out_specs=(
            P("ep", "grp"),
            P("ep", "grp"),
            P(None, "ep", "grp"),
            P(None, "ep", "grp"),
            P(None, "grp", "ep"),
        ),
        check_vma=False,
    )
```

time: 265 us -> 213 us (0.80)
  Pallas kernels: 0 us -> 42 us
  starting transfers between devices: 88.6 us -> 53.9 us
  local copies, waits for them, and re-layouts: 36.8 us -> 6.83 us
  matrix products: 29.9 us -> 0 us
  waiting for transfers between devices: 76.2 us -> 102 us
  other arithmetic: 20.4 us -> 5.39 us
  blocking collectives: 10.4 us -> 0 us
    pallas_call x0 -> x11, Pallas kernels: none -> 42 us  [call(): pl.pallas_call(body, out_shape=out_shape, grid=kw.get('grid', (1,)), in_s...]
    dot_general x9 -> x0, matrix products: 29.9 us -> none  [dot(): lax.dot_general(a, b, ((ca, cb), ((), ())), preferred_element_type=jnp.fl...]
    ppermute x16 -> x8, starting transfers between devices: 45.4 us -> 18 us  [the longest x4 10.8 us: unspread(): pieces.append(lax.ppermute(out, AXES, back))]
    gather x21 -> x0, local copies, waits for them, and re-layouts: 19.2 us -> none  [the longest x8 8.77 us: to_relative(): cols.append(jnp.take(held[:, k], idx, axis=0))]
    ppermute x16 -> x8, waiting for transfers between devices: 9.18 us -> 22.4 us  [the longest x4 19.3 us: spread(): landed = [lax.ppermute(pieces[k], AXES, plane_pairs(k)) for k in range(2)]]
    another operation x22 -> x2, other arithmetic: 13 us -> 0.2 us  [the longest x6 6.58 us: gather(): return jnp.stack([line, swap(line, 0, 1)])]
    ppermute x36 -> x32, waiting for transfers between devices: 67 us -> 79.7 us  [swap(): return lax.ppermute(block, AXES, pairs)]
    all_gather x1 -> x0, blocking collectives: 10.4 us -> none  [shards(): experts = lax.all_gather(expert, 'ep', axis=0)]
  transfers between devices with their start and end apart: 52 -> 40, of which waited for: 25 -> 19; matrix products, arithmetic and copies ran while one was open for 17% -> 2% of each run, Pallas kernels for 0% -> 18%
where the time goes in v3:
time: 213 us; the launch traced here: 211 us
  waiting for transfers between devices  102 us (48%)
  starting transfers between devices  53.9 us (25%)
  Pallas kernels  42 us (20%)
  local copies, waits for them, and re-layouts  6.83 us (3%)
  other arithmetic  5.39 us (3%)
    ppermute x32, waiting for transfers between devices, swap(): return lax.ppermute(block, AXES, pairs)  79.7 us
    pallas_call x11, Pallas kernels, call(): pl.pallas_call(body, out_shape=out_shape, grid=kw.get('grid', (1,)), in_s...  42 us
    ppermute x32, starting transfers between devices, swap(): return lax.ppermute(block, AXES, pairs)  35.9 us
    ppermute x4, waiting for transfers between devices, spread(): landed = [lax.ppermute(pieces[k], AXES, plane_pairs(k)) for k in range(2)]  19.3 us
    ppermute x4, starting transfers between devices, unspread(): pieces.append(lax.ppermute(out, AXES, back))  10.8 us
    ppermute x4, starting transfers between devices, spread(): landed = [lax.ppermute(pieces[k], AXES, plane_pairs(k)) for k in range(2)]  7.28 us
    unnamed x50, local copies, waits for them, and re-layouts  6.79 us
  transfers between devices with their start and end apart: 40, of which 19 were waited for; matrix products, arithmetic and copies ran while one was open for 2% of the time, Pallas kernels for 18%

profile of v3, /device:TPU:17, one launch (start us, length us, event | category | flops | bytes accessed | tf_op | source)
XLA Modules:
  0.0 211.4 jit_solution(13180800094144696529)
XLA Ops:
  0.6 0.9 copy-done.8
  1.6 0.7 copy-done.12
  2.2 0.7 copy-done.13
  2.9 0.7 token_pieces.1
  3.6 3.6 %collective-permute-start = (bf16[128,512]{1,0:T(8,128)(2,1)S(1)}, bf16[128,512]{1,0:T(8,128)(2,1)S(1)}, u32[]{:S(2)}, u32[]{:S(2)}) collective-permute-start(bf16[128,512]{1,0:T(8,128)(2,1)S(1)} %get-tuple-element.29), channel_id=1, source_target_pairs={{0,0},{1,1},{2,8},{3,9},{4,16},{5,17},{6,24},{7,25},{8,2},{9,3},{1... | collective-permute-start | bytes 393224 | tf_op jit(solution)/shard_map/ppermute | solution.py:52
  7.3 10.2 %collective-permute-done = bf16[128,512]{1,0:T(8,128)(2,1)S(1)} collective-permute-done((bf16[128,512]{1,0:T(8,128)(2,1)S(1)}, bf16[128,512]{1,0:T(8,128)(2,1)S(1)}, u32[]{:S(2)}, u32[]{:S(2)}) %collective-permute-start) | collective-permute-done | bytes 131104 | tf_op jit(solution)/shard_map/ppermute | solution.py:52
  17.5 0.9 copy-done.9
  18.4 0.7 copy-done.10
  19.3 3.6 %collective-permute-start.10 = (bf16[128,512]{1,0:T(8,128)(2,1)S(1)}, bf16[128,512]{1,0:T(8,128)(2,1)S(1)}, u32[]{:S(2)}, u32[]{:S(2)}) collective-permute-start(bf16[128,512]{1,0:T(8,128)(2,1)S(1)} %get-tuple-element.35), channel_id=1, source_target_pairs={{0,0},{1,1},{2,8},{3,9},{4,16},{5,17},{6,24},{7,25},{8,2},{9,3},{1... | collective-permute-start | bytes 393224 | tf_op jit(solution)/shard_map/ppermute | solution.py:52
  23.1 9.1 %collective-permute-done.10 = bf16[128,512]{1,0:T(8,128)(2,1)S(1)} collective-permute-done((bf16[128,512]{1,0:T(8,128)(2,1)S(1)}, bf16[128,512]{1,0:T(8,128)(2,1)S(1)}, u32[]{:S(2)}, u32[]{:S(2)}) %collective-permute-start.10) | collective-permute-done | bytes 131104 | tf_op jit(solution)/shard_map/ppermute | solution.py:52
  32.3 3.8 %collective-permute-start.12 = (bf16[256,512]{1,0:T(8,128)(2,1)S(1)}, bf16[256,512]{1,0:T(8,128)(2,1)S(1)}, u32[]{:S(2)}, u32[]{:S(2)}) collective-permute-start(bf16[256,512]{1,0:T(8,128)(2,1)S(1)} %pad_maximum_fusion.4), channel_id=1, source_target_pairs={{0,16},{1,17},{2,18},{3,19},{4,20},{5,21},{6,22},{7,23},{8,24},{9,... | collective-permute-start | bytes 786440 | tf_op jit(solution)/shard_map/ppermute | solution.py:37
  36.1 1.3 collective-permute-start.3
  37.5 4.5 %collective-permute-done.12 = bf16[256,512]{1,0:T(8,128)(2,1)S(1)} collective-permute-done((bf16[256,512]{1,0:T(8,128)(2,1)S(1)}, bf16[256,512]{1,0:T(8,128)(2,1)S(1)}, u32[]{:S(2)}, u32[]{:S(2)}) %collective-permute-start.12) | collective-permute-done | bytes 262176 | tf_op jit(solution)/shard_map/ppermute | solution.py:37
  42.0 1.4 collective-permute-start.13
  43.4 4.7 %gate_up_first.1 = (bf16[256,1024]{1,0:T(8,128)(2,1)S(1)}, bf16[256,1024]{1,0:T(8,128)(2,1)S(1)}, bf16[1024,512]{1,0:T(8,128)(2,1)S(1)}) custom-call(bf16[512,512]{1,0:T(8,128)(2,1)S(1)} %constant_dynamic-update-slice_fusion.held_ref, bf16[512,512]{1,0:T(8,128)(2,1)S(1)} %collective-permute-done.3.got_ref, bf16[4,448,512]{2,1,0:T(8,128)(2,1)} %refs_0_.5, ...), custom_call_target="tpu_custom_call" | custom-call | flops 1879048192 | bytes 3801088 | tf_op jit(solution)/shard_map/gate_up_first/pallas_call | solution.py:279
  48.1 3.3 %act_grad_first.1 = (bf16[256,512]{1,0:T(8,128)(2,1)S(1)}, bf16[256,512]{1,0:T(8,128)(2,1)S(1)}, bf16[1024,512]{1,0:T(8,128)(2,1)S(1)}) custom-call(bf16[512,512]{1,0:T(8,128)(2,1)S(1)} %constant_dynamic-update-slice_fusion.3.held_ref, bf16[512,512]{1,0:T(8,128)(2,1)S(1)} %collective-permute-done.13.got_ref, ...), custom_call_target="tpu_custom_call" | custom-call | flops 939524096 | bytes 1900544 | tf_op jit(solution)/shard_map/act_grad_first/pallas_call | solution.py:279
  51.5 1.0 collective-permute-start.24
  52.4 4.0 %gate_up_later.1 = (bf16[256,1024]{1,0:T(8,128)(2,1)S(1)}, bf16[256,1024]{1,0:T(8,128)(2,1)S(1)}) custom-call(bf16[1024,512]{1,0:T(8,128)(2,1)S(1)} %get-tuple-element.51.refs_0_.id_ref.rows_ref, bf16[1024,512]{1,0:T(8,128)(2,1)S(1)} %get-tuple-element.51.refs_0_.id_ref.rows_ref, bf16[4,448,512]{2,1,0:T(8,128)(2,1)S(1)} %copy-done.14, ...), custom_call_target="tpu_custom_call" | custom-call | flops 1879048192 | bytes 3801088 | tf_op jit(solution)/shard_map/gate_up_later/pallas_call | solution.py:279
  56.4 2.9 %act_grad_later.1 = (bf16[256,512]{1,0:T(8,128)(2,1)S(1)}, bf16[256,512]{1,0:T(8,128)(2,1)S(1)}) custom-call(bf16[1024,512]{1,0:T(8,128)(2,1)S(1)} %get-tuple-element.51.refs_0_.id_ref.rows_ref, bf16[1024,512]{1,0:T(8,128)(2,1)S(1)} %get-tuple-element.52.rows_ref, bf16[4,448,512]{2,1,0:T(8,128)(2,1)} %bitcast.9), custom_call_target="tpu_custom_call" | custom-call | flops 939524096 | bytes 1900544 | tf_op jit(solution)/shard_map/act_grad_later/pallas_call | solution.py:279
  59.3 0.6 collective-permute-start.30
  59.9 0.9 collective-permute-start.4
  60.8 0.6 collective-permute-start.14
  61.5 5.4 %collective-permute-done.30 = bf16[256,512]{1,0:T(8,128)(2,1)S(1)} collective-permute-done((bf16[256,512]{1,0:T(8,128)(2,1)S(1)}, bf16[256,512]{1,0:T(8,128)(2,1)S(1)}, u32[]{:S(2)}, u32[]{:S(2)}) %collective-permute-start.30) | collective-permute-done | bytes 262176 | tf_op jit(solution)/shard_map/ppermute | solution.py:37
  67.5 10.7 %collective-permute-done.4 = bf16[256,1024]{1,0:T(8,128)(2,1)S(1)} collective-permute-done((bf16[256,1024]{1,0:T(8,128)(2,1)S(1)}, bf16[256,1024]{1,0:T(8,128)(2,1)S(1)}, u32[]{:S(2)}, u32[]{:S(2)}) %collective-permute-start.4) | collective-permute-done | bytes 524320 | tf_op jit(solution)/shard_map/ppermute | solution.py:37
  78.5 11.0 %collective-permute-done.14 = bf16[256,1024]{1,0:T(8,128)(2,1)S(1)} collective-permute-done((bf16[256,1024]{1,0:T(8,128)(2,1)S(1)}, bf16[256,1024]{1,0:T(8,128)(2,1)S(1)}, u32[]{:S(2)}, u32[]{:S(2)}) %collective-permute-start.14) | collective-permute-done | bytes 524320 | tf_op jit(solution)/shard_map/ppermute | solution.py:37
  90.1 2.1 %collective-permute-start.6 = (bf16[64,1024]{1,0:T(8,128)(2,1)S(1)}, bf16[64,1024]{1,0:T(8,128)(2,1)S(1)}, u32[]{:S(2)}, u32[]{:S(2)}) collective-permute-start(bf16[64,1024]{1,0:T(8,128)(2,1)S(1)} %add_convert_fusion.18), channel_id=1, source_target_pairs={{0,4},{1,5},{2,6},{3,7},{4,0},{5,1},{6,2},{7,3},{8,12},{9,13},{10,... | collective-permute-start | bytes 393224 | tf_op jit(solution)/shard_map/ppermute | solution.py:37
  92.3 4.9 %collective-permute-done.15 = bf16[128,1024]{1,0:T(8,128)(2,1)S(1)} collective-permute-done((bf16[128,1024]{1,0:T(8,128)(2,1)S(1)}, bf16[128,1024]{1,0:T(8,128)(2,1)S(1)}, u32[]{:S(2)}, u32[]{:S(2)}) %collective-permute-start.15) | collective-permute-done | bytes 262176 | tf_op jit(solution)/shard_map/ppermute | solution.py:37
  97.2 1.9 collective-permute-start.16
  99.9 2.1 %collective-permute-start.27 = (bf16[64,1024]{1,0:T(8,128)(2,1)S(1)}, bf16[64,1024]{1,0:T(8,128)(2,1)S(1)}, u32[]{:S(2)}, u32[]{:S(2)}) collective-permute-start(bf16[64,1024]{1,0:T(8,128)(2,1)S(1)} %pad_maximum_fusion.11), channel_id=1, source_target_pairs={{0,4},{1,5},{2,6},{3,7},{4,0},{5,1},{6,2},{7,3},{8,12},{9,13},{10,... | collective-permute-start | bytes 393224 | tf_op jit(solution)/shard_map/ppermute | solution.py:37
  102.1 6.8 %collective-permute-done.16 = bf16[64,1024]{1,0:T(8,128)(2,1)S(1)} collective-permute-done((bf16[64,1024]{1,0:T(8,128)(2,1)S(1)}, bf16[64,1024]{1,0:T(8,128)(2,1)S(1)}, u32[]{:S(2)}, u32[]{:S(2)}) %collective-permute-start.16) | collective-permute-done | bytes 131104 | tf_op jit(solution)/shard_map/ppermute | solution.py:37
  109.0 3.2 %collective-permute-start.33 = (bf16[64,1024]{1,0:T(8,128)(2,1)S(1)}, bf16[64,1024]{1,0:T(8,128)(2,1)S(1)}, u32[]{:S(2)}, u32[]{:S(2)}) collective-permute-start(bf16[64,1024]{1,0:T(8,128)(2,1)S(1)} %pad_maximum_fusion.12), channel_id=1, source_target_pairs={{0,4},{1,5},{2,6},{3,7},{4,0},{5,1},{6,2},{7,3},{8,12},{9,13},{10,... | collective-permute-start | bytes 393224 | tf_op jit(solution)/shard_map/ppermute | solution.py:37
  112.2 1.5 collective-permute-start.8
  113.7 1.2 collective-permute-start.17
  115.0 3.6 %collective-permute-start.28 = (bf16[128,1024]{1,0:T(8,128)(2,1)S(1)}, bf16[128,1024]{1,0:T(8,128)(2,1)S(1)}, u32[]{:S(2)}, u32[]{:S(2)}) collective-permute-start(bf16[128,1024]{1,0:T(8,128)(2,1)S(1)} %pad_maximum_fusion.6), channel_id=1, source_target_pairs={{0,2},{1,3},{2,0},{3,1},{4,6},{5,7},{6,4},{7,5},{8,10},{9,11},{10,... | collective-permute-start | bytes 786440 | tf_op jit(solution)/shard_map/ppermute | solution.py:37
  118.7 2.8 %collective-permute-done.33 = bf16[64,1024]{1,0:T(8,128)(2,1)S(1)} collective-permute-done((bf16[64,1024]{1,0:T(8,128)(2,1)S(1)}, bf16[64,1024]{1,0:T(8,128)(2,1)S(1)}, u32[]{:S(2)}, u32[]{:S(2)}) %collective-permute-start.33) | collective-permute-done | bytes 131104 | tf_op jit(solution)/shard_map/ppermute | solution.py:37
  121.5 0.6 collective-permute-start.34
  122.2 0.7 collective-permute-done.17
  122.9 0.7 collective-permute-start.18
  123.6 2.1 %collective-permute-start.9 = (bf16[256,512]{1,0:T(8,128)(2,1)S(1)}, bf16[256,512]{1,0:T(8,128)(2,1)S(1)}, u32[]{:S(2)}, u32[]{:S(2)}) collective-permute-start(bf16[256,512]{1,0:T(8,128)(2,1)S(1)} %pad_maximum_fusion.3.refs_1_.refs_0_), channel_id=1, source_target_pairs={{0,1},{1,0},{2,3},{3,2},{4,5},{5,4},{6,7},{7,6},{8,9},{9,8},{10,11... | collective-permute-start | bytes 786440 | tf_op jit(solution)/shard_map/ppermute | solution.py:37
  125.8 2.7 %collective-permute-done.28 = bf16[128,1024]{1,0:T(8,128)(2,1)S(1)} collective-permute-done((bf16[128,1024]{1,0:T(8,128)(2,1)S(1)}, bf16[128,1024]{1,0:T(8,128)(2,1)S(1)}, u32[]{:S(2)}, u32[]{:S(2)}) %collective-permute-start.28) | collective-permute-done | bytes 262176 | tf_op jit(solution)/shard_map/ppermute | solution.py:37
  128.6 5.5 %collective-permute-done.34 = bf16[128,1024]{1,0:T(8,128)(2,1)S(1)} collective-permute-done((bf16[128,1024]{1,0:T(8,128)(2,1)S(1)}, bf16[128,1024]{1,0:T(8,128)(2,1)S(1)}, u32[]{:S(2)}, u32[]{:S(2)}) %collective-permute-start.34) | collective-permute-done | bytes 262176 | tf_op jit(solution)/shard_map/ppermute | solution.py:37
  134.2 2.7 %collective-permute-done.18 = bf16[128,512]{1,0:T(8,128)(2,1)S(1)} collective-permute-done((bf16[128,512]{1,0:T(8,128)(2,1)S(1)}, bf16[128,512]{1,0:T(8,128)(2,1)S(1)}, u32[]{:S(2)}, u32[]{:S(2)}) %collective-permute-start.18) | collective-permute-done | bytes 131104 | tf_op jit(solution)/shard_map/ppermute | solution.py:37
  137.0 21.1 %collective-permute-done.19.refs_4_.refs_3_ = bf16[256,512]{1,0:T(8,128)(2,1)S(1)} collective-permute-done((bf16[256,512]{1,0:T(8,128)(2,1)S(1)}, bf16[256,512]{1,0:T(8,128)(2,1)S(1)}, u32[]{:S(2)}, u32[]{:S(2)}) %collective-permute-start.19) | collective-permute-done | bytes 262176 | tf_op jit(solution)/shard_map/ppermute | solution.py:37
  158.1 5.8 %out_rows.1 = (bf16[512,448]{1,0:T(8,128)(2,1)S(1)}, bf16[512,448]{1,0:T(8,128)(2,1)}) custom-call(bf16[1024,512]{1,0:T(8,128)(2,1)S(1)} %get-tuple-element.51.refs_0_.id_ref.rows_ref, bf16[4,448,512]{2,1,0:T(8,128)(2,1)} %bitcast.10, bf16[256,512]{1,0:T(8,128)(2,1)S(1)} %pad_maximum_fusion.3.refs_1_.refs_0_, ...), custom_call_target="tpu_custom_call" | custom-call | flops 1879048192 | bytes 3801088 | tf_op jit(solution)/shard_map/out_rows/pallas_call | solution.py:279
  164.0 3.1 %collective-permute-start.20 = (bf16[512,448]{1,0:T(8,128)(2,1)}, bf16[512,448]{1,0:T(8,128)(2,1)}, u32[]{:S(2)}, u32[]{:S(2)}) collective-permute-start(bf16[512,448]{1,0:T(8,128)(2,1)} %get-tuple-element.42), channel_id=1, source_target_pairs={{0,8},{1,9},{2,10},{3,11},{4,12},{5,13},{6,14},{7,15},{8,0},{9,1},... | collective-permute-start | bytes 1376264 | tf_op jit(solution)/shard_map/ppermute | solution.py:37
  167.1 9.0 %token_rows.1 = (bf16[512,448]{1,0:T(8,128)(2,1)S(1)}, bf16[512,448]{1,0:T(8,128)(2,1)}) custom-call(bf16[1024,512]{1,0:T(8,128)(2,1)} %copy-done, bf16[4,448,512]{2,1,0:T(8,128)(2,1)} %refs_0_.5, bf16[4,448,512]{2,1,0:T(8,128)(2,1)} %refs_1_.5, bf16[256,1024]{1,0:T(8,128)(2,1)S(1)} %pad_maximum_fusion.refs_2_.refs_0_, ...), custom_call_target="tpu_custom_call" | custom-call | flops 3758096384 | bytes 7602176 | tf_op jit(solution)/shard_map/token_rows/pallas_call | solution.py:279
  176.2 1.2 add_convert_fusion.3
  177.4 2.1 %collective-permute-start.21 = (bf16[256,448]{1,0:T(8,128)(2,1)S(1)}, bf16[256,448]{1,0:T(8,128)(2,1)S(1)}, u32[]{:S(2)}, u32[]{:S(2)}) collective-permute-start(bf16[256,448]{1,0:T(8,128)(2,1)S(1)} %get-tuple-element.56), channel_id=1, source_target_pairs={{0,16},{1,17},{2,18},{3,19},{4,20},{5,21},{6,22},{7,23},{8,24},{9,... | collective-permute-start | bytes 688136 | tf_op jit(solution)/shard_map/ppermute | solution.py:37
  179.5 0.9 copy-done.7
  180.5 0.9 copy-done.20
  181.4 0.9 copy-done.22
  182.4 3.8 %grad_down.1 = bf16[4,448,512]{2,1,0:T(8,128)(2,1)} custom-call(bf16[1024,512]{1,0:T(8,128)(2,1)S(1)} %copy-done.1, bf16[1024,512]{1,0:T(8,128)(2,1)S(1)} %get-tuple-element.52.rows_ref, bf16[256,512]{1,0:T(8,128)(2,1)S(1)} %pad_maximum_fusion.3.refs_1_.refs_0_, bf16[256,512]{1,0:T(8,128)(2,1)S(1)} %copy-done.20, bf16[256,512]{1,0:T(8,128)(2,1)S(1)} %copy-done.7, ...), custom_call_target="tpu_custom_call" | custom-call | flops 1879048192 | bytes 3801088 | tf_op jit(solution)/shard_map/grad_down/pallas_call | solution.py:279
  186.2 1.3 add_convert_fusion.1
  187.7 3.7 %collective-permute-start.22 = (bf16[128,448]{1,0:T(8,128)(2,1)S(1)}, bf16[128,448]{1,0:T(8,128)(2,1)S(1)}, u32[]{:S(2)}, u32[]{:S(2)}) collective-permute-start(bf16[128,448]{1,0:T(8,128)(2,1)S(1)} %get-tuple-element.71), channel_id=1, source_target_pairs={{0,0},{1,1},{8,2},{9,3},{16,4},{17,5},{24,6},{25,7},{2,8},{3,9},{1... | collective-permute-start | bytes 344072 | tf_op jit(solution)/shard_map/ppermute | solution.py:81
  191.4 0.9 collective-permute-start.23
  192.3 3.8 %grad_gate.1 = bf16[4,448,512]{2,1,0:T(8,128)(2,1)} custom-call(bf16[1024,512]{1,0:T(8,128)(2,1)S(1)} %copy-done.1, bf16[1024,512]{1,0:T(8,128)(2,1)S(1)} %copy-done.1, bf16[256,1024]{1,0:T(8,128)(2,1)S(1)} %copy-done.3, bf16[256,1024]{1,0:T(8,128)(2,1)S(1)} %copy-done.16, bf16[256,1024]{1,0:T(8,128)(2,1)S(1)} %copy-done.5, bf16[256,1024]{1,0:T(8,128)(2,1)S(1)} %copy-done.18), custom_call_target="tpu_custom_call" | custom-call | flops 1879048192 | bytes 3801088 | tf_op jit(solution)/shard_map/grad_gate/pallas_call | solution.py:279
  196.1 0.5 collective-permute-done.37
  196.7 5.3 %collective-permute-start.38 = (bf16[128,448]{1,0:T(8,128)(2,1)S(1)}, bf16[128,448]{1,0:T(8,128)(2,1)S(1)}, u32[]{:S(2)}, u32[]{:S(2)}) collective-permute-start(bf16[128,448]{1,0:T(8,128)(2,1)S(1)} %get-tuple-element.65), channel_id=1, source_target_pairs={{0,0},{1,1},{8,2},{9,3},{16,4},{17,5},{24,6},{25,7},{2,8},{3,9},{1... | collective-permute-start | bytes 344072 | tf_op jit(solution)/shard_map/ppermute | solution.py:81
  202.1 0.8 collective-permute-start.39
  202.9 3.8 %grad_up.1 = bf16[4,448,512]{2,1,0:T(8,128)(2,1)} custom-call(bf16[1024,512]{1,0:T(8,128)(2,1)S(1)} %copy-done.1, bf16[1024,512]{1,0:T(8,128)(2,1)S(1)} %copy-done.1, bf16[256,1024]{1,0:T(8,128)(2,1)S(1)} %copy-done.3, bf16[256,1024]{1,0:T(8,128)(2,1)S(1)} %copy-done.16, bf16[256,1024]{1,0:T(8,128)(2,1)S(1)} %copy-done.5, bf16[256,1024]{1,0:T(8,128)(2,1)S(1)} %copy-done.18), custom_call_target="tpu_custom_call" | custom-call | flops 1879048192 | bytes 3801088 | tf_op jit(solution)/shard_map/grad_up/pallas_call | solution.py:279
  206.7 0.5 collective-permute-done.38
  207.2 2.6 %collective-permute-done.39 = bf16[128,448]{1,0:T(8,128)(2,1)S(1)} collective-permute-done((bf16[128,448]{1,0:T(8,128)(2,1)S(1)}, bf16[128,448]{1,0:T(8,128)(2,1)S(1)}, u32[]{:S(2)}, u32[]{:S(2)}) %collective-permute-start.39) | collective-permute-done | bytes 114720 | tf_op jit(solution)/shard_map/ppermute | solution.py:81
  209.8 0.8 pad_maximum_fusion.8
  210.6 0.8 multiply_convert_fusion
  (110 shorter events, 4.1 us)
Async XLA Ops:
  0.6 0.9 copy-start.8
  1.6 0.7 copy-start.12
  2.2 0.7 copy-start.13
  3.6 13.8 %collective-permute-start = (bf16[128,512]{1,0:T(8,128)(2,1)S(1)}, bf16[128,512]{1,0:T(8,128)(2,1)S(1)}, u32[]{:S(2)}, u32[]{:S(2)}) collective-permute-start(bf16[128,512]{1,0:T(8,128)(2,1)S(1)} %get-tuple-element.29), channel_id=1, source_target_pairs={{0,0},{1,1},{2,8},{3,9},{4,16},{5,17},{6,24},{7,25},{8,2},{9,3},{1... | collective-permute-start | bytes 393224 | tf_op jit(solution)/shard_map/ppermute | solution.py:52
  7.2 15.8 %collective-permute-start.1 = (bf16[128,512]{1,0:T(8,128)(2,1)S(1)}, bf16[128,512]{1,0:T(8,128)(2,1)S(1)}, u32[]{:S(2)}, u32[]{:S(2)}) collective-permute-start(bf16[128,512]{1,0:T(8,128)(2,1)S(1)} %get-tuple-element.30), channel_id=1, source_target_pairs={{0,17},{1,16},{2,25},{3,24},{4,1},{5,0},{6,9},{7,8},{8,19},{9,18},... | collective-permute-start | bytes 393224 | tf_op jit(solution)/shard_map/ppermute | solution.py:52
  17.5 0.9 copy-start.9
  18.4 0.7 copy-start.10
  19.3 12.9 %collective-permute-start.10 = (bf16[128,512]{1,0:T(8,128)(2,1)S(1)}, bf16[128,512]{1,0:T(8,128)(2,1)S(1)}, u32[]{:S(2)}, u32[]{:S(2)}) collective-permute-start(bf16[128,512]{1,0:T(8,128)(2,1)S(1)} %get-tuple-element.35), channel_id=1, source_target_pairs={{0,0},{1,1},{2,8},{3,9},{4,16},{5,17},{6,24},{7,25},{8,2},{9,3},{1... | collective-permute-start | bytes 393224 | tf_op jit(solution)/shard_map/ppermute | solution.py:52
  22.9 9.3 %collective-permute-start.11 = (bf16[128,512]{1,0:T(8,128)(2,1)S(1)}, bf16[128,512]{1,0:T(8,128)(2,1)S(1)}, u32[]{:S(2)}, u32[]{:S(2)}) collective-permute-start(bf16[128,512]{1,0:T(8,128)(2,1)S(1)} %get-tuple-element.36), channel_id=1, source_target_pairs={{0,17},{1,16},{2,25},{3,24},{4,1},{5,0},{6,9},{7,8},{8,19},{9,18},... | collective-permute-start | bytes 393224 | tf_op jit(solution)/shard_map/ppermute | solution.py:52
  23.0 13.1 %collective-permute-start.2 = (bf16[256,512]{1,0:T(8,128)(2,1)S(1)}, bf16[256,512]{1,0:T(8,128)(2,1)S(1)}, u32[]{:S(2)}, u32[]{:S(2)}) collective-permute-start(bf16[256,512]{1,0:T(8,128)(2,1)S(1)} %pad_maximum_fusion.2), channel_id=1, source_target_pairs={{0,16},{1,17},{2,18},{3,19},{4,20},{5,21},{6,22},{7,23},{8,24},{9,... | collective-permute-start | bytes 786440 | tf_op jit(solution)/shard_map/ppermute | solution.py:37
  32.3 9.7 %collective-permute-start.12 = (bf16[256,512]{1,0:T(8,128)(2,1)S(1)}, bf16[256,512]{1,0:T(8,128)(2,1)S(1)}, u32[]{:S(2)}, u32[]{:S(2)}) collective-permute-start(bf16[256,512]{1,0:T(8,128)(2,1)S(1)} %pad_maximum_fusion.4), channel_id=1, source_target_pairs={{0,16},{1,17},{2,18},{3,19},{4,20},{5,21},{6,22},{7,23},{8,24},{9,... | collective-permute-start | bytes 786440 | tf_op jit(solution)/shard_map/ppermute | solution.py:37
  36.1 7.3 %collective-permute-start.3 = (bf16[512,512]{1,0:T(8,128)(2,1)S(1)}, bf16[512,512]{1,0:T(8,128)(2,1)S(1)}, u32[]{:S(2)}, u32[]{:S(2)}) collective-permute-start(bf16[512,512]{1,0:T(8,128)(2,1)S(1)} %constant_dynamic-update-slice_fusion.held_ref), channel_id=1, source_target_pairs={{0,8},{1,9},{2,10},{3,11},{4,12},{5,13},{6,14},{7,15},{8,0},{9,1},... | collective-permute-start | bytes 1572872 | tf_op jit(solution)/shard_map/ppermute | solution.py:37
  42.0 6.1 %collective-permute-start.13 = (bf16[512,512]{1,0:T(8,128)(2,1)S(1)}, bf16[512,512]{1,0:T(8,128)(2,1)S(1)}, u32[]{:S(2)}, u32[]{:S(2)}) collective-permute-start(bf16[512,512]{1,0:T(8,128)(2,1)S(1)} %constant_dynamic-update-slice_fusion.3.held_ref), channel_id=1, source_target_pairs={{0,8},{1,9},{2,10},{3,11},{4,12},{5,13},{6,14},{7,15},{8,0},{9,1},... | collective-permute-start | bytes 1572872 | tf_op jit(solution)/shard_map/ppermute | solution.py:37
  48.1 110.0 %copy-start = (bf16[1024,512]{1,0:T(8,128)(2,1)}, bf16[1024,512]{1,0:T(8,128)(2,1)S(1)}, u32[]{:S(2)}) copy-start(bf16[1024,512]{1,0:T(8,128)(2,1)S(1)} %get-tuple-element.51.refs_0_.id_ref.rows_ref) | copy-start | bytes 3145732
  48.1 4.3 %copy-start.14 = (bf16[4,448,512]{2,1,0:T(8,128)(2,1)S(1)}, bf16[4,448,512]{2,1,0:T(8,128)(2,1)}, u32[]{:S(2)}) copy-start(bf16[4,448,512]{2,1,0:T(8,128)(2,1)} %refs_0_.5) | copy-start | bytes 5505028
  51.5 9.9 %collective-permute-start.24 = (bf16[256,512]{1,0:T(8,128)(2,1)S(1)}, bf16[256,512]{1,0:T(8,128)(2,1)S(1)}, u32[]{:S(2)}, u32[]{:S(2)}) collective-permute-start(bf16[256,512]{1,0:T(8,128)(2,1)S(1)} %get-tuple-element.37), channel_id=1, source_target_pairs={{0,1},{1,0},{2,3},{3,2},{4,5},{5,4},{6,7},{7,6},{8,9},{9,8},{10,11... | collective-permute-start | bytes 786440 | tf_op jit(solution)/shard_map/ppermute | solution.py:37
  59.3 7.7 %collective-permute-start.30 = (bf16[256,512]{1,0:T(8,128)(2,1)S(1)}, bf16[256,512]{1,0:T(8,128)(2,1)S(1)}, u32[]{:S(2)}, u32[]{:S(2)}) collective-permute-start(bf16[256,512]{1,0:T(8,128)(2,1)S(1)} %get-tuple-element.47), channel_id=1, source_target_pairs={{0,1},{1,0},{2,3},{3,2},{4,5},{5,4},{6,7},{7,6},{8,9},{9,8},{10,11... | collective-permute-start | bytes 786440 | tf_op jit(solution)/shard_map/ppermute | solution.py:37
  59.9 18.3 %collective-permute-start.4 = (bf16[256,1024]{1,0:T(8,128)(2,1)S(1)}, bf16[256,1024]{1,0:T(8,128)(2,1)S(1)}, u32[]{:S(2)}, u32[]{:S(2)}) collective-permute-start(bf16[256,1024]{1,0:T(8,128)(2,1)S(1)} %get-tuple-element.33), channel_id=1, source_target_pairs={{0,1},{1,0},{2,3},{3,2},{4,5},{5,4},{6,7},{7,6},{8,9},{9,8},{10,11... | collective-permute-start | bytes 1572872 | tf_op jit(solution)/shard_map/ppermute | solution.py:37
  60.8 28.6 %collective-permute-start.14 = (bf16[256,1024]{1,0:T(8,128)(2,1)S(1)}, bf16[256,1024]{1,0:T(8,128)(2,1)S(1)}, u32[]{:S(2)}, u32[]{:S(2)}) collective-permute-start(bf16[256,1024]{1,0:T(8,128)(2,1)S(1)} %get-tuple-element.40), channel_id=1, source_target_pairs={{0,1},{1,0},{2,3},{3,2},{4,5},{5,4},{6,7},{7,6},{8,9},{9,8},{10,11... | collective-permute-start | bytes 1572872 | tf_op jit(solution)/shard_map/ppermute | solution.py:37
  61.5 5.6 %collective-permute-start.25 = (bf16[128,512]{1,0:T(8,128)(2,1)S(1)}, bf16[128,512]{1,0:T(8,128)(2,1)S(1)}, u32[]{:S(2)}, u32[]{:S(2)}) collective-permute-start(bf16[128,512]{1,0:T(8,128)(2,1)S(1)} %get-tuple-element.70), channel_id=1, source_target_pairs={{0,2},{1,3},{2,0},{3,1},{4,6},{5,7},{6,4},{7,5},{8,10},{9,11},{10,... | collective-permute-start | bytes 393224 | tf_op jit(solution)/shard_map/ppermute | solution.py:37
  67.0 22.7 %collective-permute-start.31 = (bf16[128,512]{1,0:T(8,128)(2,1)S(1)}, bf16[128,512]{1,0:T(8,128)(2,1)S(1)}, u32[]{:S(2)}, u32[]{:S(2)}) collective-permute-start(bf16[128,512]{1,0:T(8,128)(2,1)S(1)} %get-tuple-element.68), channel_id=1, source_target_pairs={{0,2},{1,3},{2,0},{3,1},{4,6},{5,7},{6,4},{7,5},{8,10},{9,11},{10,... | collective-permute-start | bytes 393224 | tf_op jit(solution)/shard_map/ppermute | solution.py:37
  67.1 32.3 %collective-permute-start.26 = (bf16[64,512]{1,0:T(8,128)(2,1)S(1)}, bf16[64,512]{1,0:T(8,128)(2,1)S(1)}, u32[]{:S(2)}, u32[]{:S(2)}) collective-permute-start(bf16[64,512]{1,0:T(8,128)(2,1)S(1)} %add_convert_fusion.22), channel_id=1, source_target_pairs={{0,4},{1,5},{2,6},{3,7},{4,0},{5,1},{6,2},{7,3},{8,12},{9,13},{10,... | collective-permute-start | bytes 196616 | tf_op jit(solution)/shard_map/ppermute | solution.py:37
  78.4 11.7 %collective-permute-start.5 = (bf16[128,1024]{1,0:T(8,128)(2,1)S(1)}, bf16[128,1024]{1,0:T(8,128)(2,1)S(1)}, u32[]{:S(2)}, u32[]{:S(2)}) collective-permute-start(bf16[128,1024]{1,0:T(8,128)(2,1)S(1)} %get-tuple-element.60), channel_id=1, source_target_pairs={{0,2},{1,3},{2,0},{3,1},{4,6},{5,7},{6,4},{7,5},{8,10},{9,11},{10,... | collective-permute-start | bytes 786440 | tf_op jit(solution)/shard_map/ppermute | solution.py:37
  89.6 7.6 %collective-permute-start.15 = (bf16[128,1024]{1,0:T(8,128)(2,1)S(1)}, bf16[128,1024]{1,0:T(8,128)(2,1)S(1)}, u32[]{:S(2)}, u32[]{:S(2)}) collective-permute-start(bf16[128,1024]{1,0:T(8,128)(2,1)S(1)} %get-tuple-element.58), channel_id=1, source_target_pairs={{0,2},{1,3},{2,0},{3,1},{4,6},{5,7},{6,4},{7,5},{8,10},{9,11},{10,... | collective-permute-start | bytes 786440 | tf_op jit(solution)/shard_map/ppermute | solution.py:37
  89.7 19.1 %collective-permute-start.32 = (bf16[64,512]{1,0:T(8,128)(2,1)S(1)}, bf16[64,512]{1,0:T(8,128)(2,1)S(1)}, u32[]{:S(2)}, u32[]{:S(2)}) collective-permute-start(bf16[64,512]{1,0:T(8,128)(2,1)S(1)} %add_convert_fusion.20), channel_id=1, source_target_pairs={{0,4},{1,5},{2,6},{3,7},{4,0},{5,1},{6,2},{7,3},{8,12},{9,13},{10,... | collective-permute-start | bytes 196616 | tf_op jit(solution)/shard_map/ppermute | solution.py:37
  90.1 9.3 %collective-permute-start.6 = (bf16[64,1024]{1,0:T(8,128)(2,1)S(1)}, bf16[64,1024]{1,0:T(8,128)(2,1)S(1)}, u32[]{:S(2)}, u32[]{:S(2)}) collective-permute-start(bf16[64,1024]{1,0:T(8,128)(2,1)S(1)} %add_convert_fusion.18), channel_id=1, source_target_pairs={{0,4},{1,5},{2,6},{3,7},{4,0},{5,1},{6,2},{7,3},{8,12},{9,13},{10,... | collective-permute-start | bytes 393224 | tf_op jit(solution)/shard_map/ppermute | solution.py:37
  97.2 11.6 %collective-permute-start.16 = (bf16[64,1024]{1,0:T(8,128)(2,1)S(1)}, bf16[64,1024]{1,0:T(8,128)(2,1)S(1)}, u32[]{:S(2)}, u32[]{:S(2)}) collective-permute-start(bf16[64,1024]{1,0:T(8,128)(2,1)S(1)} %add_convert_fusion.16), channel_id=1, source_target_pairs={{0,4},{1,5},{2,6},{3,7},{4,0},{5,1},{6,2},{7,3},{8,12},{9,13},{10,... | collective-permute-start | bytes 393224 | tf_op jit(solution)/shard_map/ppermute | solution.py:37
  99.6 12.6 %collective-permute-start.7 = (bf16[64,512]{1,0:T(8,128)(2,1)S(1)}, bf16[64,512]{1,0:T(8,128)(2,1)S(1)}, u32[]{:S(2)}, u32[]{:S(2)}) collective-permute-start(bf16[64,512]{1,0:T(8,128)(2,1)S(1)} %get-tuple-element.76), channel_id=1, source_target_pairs={{0,4},{1,5},{2,6},{3,7},{4,0},{5,1},{6,2},{7,3},{8,12},{9,13},{10,... | collective-permute-start | bytes 196616 | tf_op jit(solution)/shard_map/ppermute | solution.py:37
  99.9 15.1 %collective-permute-start.27 = (bf16[64,1024]{1,0:T(8,128)(2,1)S(1)}, bf16[64,1024]{1,0:T(8,128)(2,1)S(1)}, u32[]{:S(2)}, u32[]{:S(2)}) collective-permute-start(bf16[64,1024]{1,0:T(8,128)(2,1)S(1)} %pad_maximum_fusion.11), channel_id=1, source_target_pairs={{0,4},{1,5},{2,6},{3,7},{4,0},{5,1},{6,2},{7,3},{8,12},{9,13},{10,... | collective-permute-start | bytes 393224 | tf_op jit(solution)/shard_map/ppermute | solution.py:37
  109.0 12.5 %collective-permute-start.33 = (bf16[64,1024]{1,0:T(8,128)(2,1)S(1)}, bf16[64,1024]{1,0:T(8,128)(2,1)S(1)}, u32[]{:S(2)}, u32[]{:S(2)}) collective-permute-start(bf16[64,1024]{1,0:T(8,128)(2,1)S(1)} %pad_maximum_fusion.12), channel_id=1, source_target_pairs={{0,4},{1,5},{2,6},{3,7},{4,0},{5,1},{6,2},{7,3},{8,12},{9,13},{10,... | collective-permute-start | bytes 393224 | tf_op jit(solution)/shard_map/ppermute | solution.py:37
  112.2 11.4 %collective-permute-start.8 = (bf16[128,512]{1,0:T(8,128)(2,1)S(1)}, bf16[128,512]{1,0:T(8,128)(2,1)S(1)}, u32[]{:S(2)}, u32[]{:S(2)}) collective-permute-start(bf16[128,512]{1,0:T(8,128)(2,1)S(1)} %pad_maximum_fusion.9), channel_id=1, source_target_pairs={{0,2},{1,3},{2,0},{3,1},{4,6},{5,7},{6,4},{7,5},{8,10},{9,11},{10,... | collective-permute-start | bytes 393224 | tf_op jit(solution)/shard_map/ppermute | solution.py:37
  113.7 9.2 %collective-permute-start.17 = (bf16[64,512]{1,0:T(8,128)(2,1)S(1)}, bf16[64,512]{1,0:T(8,128)(2,1)S(1)}, u32[]{:S(2)}, u32[]{:S(2)}) collective-permute-start(bf16[64,512]{1,0:T(8,128)(2,1)S(1)} %get-tuple-element.75), channel_id=1, source_target_pairs={{0,4},{1,5},{2,6},{3,7},{4,0},{5,1},{6,2},{7,3},{8,12},{9,13},{10,... | collective-permute-start | bytes 196616 | tf_op jit(solution)/shard_map/ppermute | solution.py:37
  115.0 13.4 %collective-permute-start.28 = (bf16[128,1024]{1,0:T(8,128)(2,1)S(1)}, bf16[128,1024]{1,0:T(8,128)(2,1)S(1)}, u32[]{:S(2)}, u32[]{:S(2)}) collective-permute-start(bf16[128,1024]{1,0:T(8,128)(2,1)S(1)} %pad_maximum_fusion.6), channel_id=1, source_target_pairs={{0,2},{1,3},{2,0},{3,1},{4,6},{5,7},{6,4},{7,5},{8,10},{9,11},{10,... | collective-permute-start | bytes 786440 | tf_op jit(solution)/shard_map/ppermute | solution.py:37
  121.5 12.5 %collective-permute-start.34 = (bf16[128,1024]{1,0:T(8,128)(2,1)S(1)}, bf16[128,1024]{1,0:T(8,128)(2,1)S(1)}, u32[]{:S(2)}, u32[]{:S(2)}) collective-permute-start(bf16[128,1024]{1,0:T(8,128)(2,1)S(1)} %pad_maximum_fusion.7), channel_id=1, source_target_pairs={{0,2},{1,3},{2,0},{3,1},{4,6},{5,7},{6,4},{7,5},{8,10},{9,11},{10,... | collective-permute-start | bytes 786440 | tf_op jit(solution)/shard_map/ppermute | solution.py:37
  122.9 13.9 %collective-permute-start.18 = (bf16[128,512]{1,0:T(8,128)(2,1)S(1)}, bf16[128,512]{1,0:T(8,128)(2,1)S(1)}, u32[]{:S(2)}, u32[]{:S(2)}) collective-permute-start(bf16[128,512]{1,0:T(8,128)(2,1)S(1)} %pad_maximum_fusion.10), channel_id=1, source_target_pairs={{0,2},{1,3},{2,0},{3,1},{4,6},{5,7},{6,4},{7,5},{8,10},{9,11},{10,... | collective-permute-start | bytes 393224 | tf_op jit(solution)/shard_map/ppermute | solution.py:37
  123.6 13.3 %collective-permute-start.9 = (bf16[256,512]{1,0:T(8,128)(2,1)S(1)}, bf16[256,512]{1,0:T(8,128)(2,1)S(1)}, u32[]{:S(2)}, u32[]{:S(2)}) collective-permute-start(bf16[256,512]{1,0:T(8,128)(2,1)S(1)} %pad_maximum_fusion.3.refs_1_.refs_0_), channel_id=1, source_target_pairs={{0,1},{1,0},{2,3},{3,2},{4,5},{5,4},{6,7},{7,6},{8,9},{9,8},{10,11... | collective-permute-start | bytes 786440 | tf_op jit(solution)/shard_map/ppermute | solution.py:37
  128.5 38.6 %copy-start.2 = (bf16[256,1024]{1,0:T(8,128)(2,1)}, bf16[256,1024]{1,0:T(8,128)(2,1)S(1)}, u32[]{:S(2)}) copy-start(bf16[256,1024]{1,0:T(8,128)(2,1)S(1)} %pad_maximum_fusion.refs_2_.refs_0_) | copy-start | bytes 1572868
  128.5 38.5 %collective-permute-start.29 = (bf16[256,1024]{1,0:T(8,128)(2,1)S(1)}, bf16[256,1024]{1,0:T(8,128)(2,1)S(1)}, u32[]{:S(2)}, u32[]{:S(2)}) collective-permute-start(bf16[256,1024]{1,0:T(8,128)(2,1)S(1)} %pad_maximum_fusion.refs_2_.refs_0_), channel_id=1, source_target_pairs={{0,1},{1,0},{2,3},{3,2},{4,5},{5,4},{6,7},{7,6},{8,9},{9,8},{10,11... | collective-permute-start | bytes 1572872 | tf_op jit(solution)/shard_map/ppermute | solution.py:37
  134.1 33.0 %copy-start.4 = (bf16[256,1024]{1,0:T(8,128)(2,1)}, bf16[256,1024]{1,0:T(8,128)(2,1)S(1)}, u32[]{:S(2)}) copy-start(bf16[256,1024]{1,0:T(8,128)(2,1)S(1)} %pad_maximum_fusion.1.refs_4_.refs_2_) | copy-start | bytes 1572868
  134.1 32.9 %collective-permute-start.35 = (bf16[256,1024]{1,0:T(8,128)(2,1)S(1)}, bf16[256,1024]{1,0:T(8,128)(2,1)S(1)}, u32[]{:S(2)}, u32[]{:S(2)}) collective-permute-start(bf16[256,1024]{1,0:T(8,128)(2,1)S(1)} %pad_maximum_fusion.1.refs_4_.refs_2_), channel_id=1, source_target_pairs={{0,1},{1,0},{2,3},{3,2},{4,5},{5,4},{6,7},{7,6},{8,9},{9,8},{10,11... | collective-permute-start | bytes 1572872 | tf_op jit(solution)/shard_map/ppermute | solution.py:37
  136.9 27.0 %copy-start.6 = (bf16[256,512]{1,0:T(8,128)(2,1)}, bf16[256,512]{1,0:T(8,128)(2,1)S(1)}, u32[]{:S(2)}) copy-start(bf16[256,512]{1,0:T(8,128)(2,1)S(1)} %pad_maximum_fusion.5.refs_3_.refs_2_) | copy-start | bytes 786436
  136.9 21.2 %collective-permute-start.19 = (bf16[256,512]{1,0:T(8,128)(2,1)S(1)}, bf16[256,512]{1,0:T(8,128)(2,1)S(1)}, u32[]{:S(2)}, u32[]{:S(2)}) collective-permute-start(bf16[256,512]{1,0:T(8,128)(2,1)S(1)} %pad_maximum_fusion.5.refs_3_.refs_2_), channel_id=1, source_target_pairs={{0,1},{1,0},{2,3},{3,2},{4,5},{5,4},{6,7},{7,6},{8,9},{9,8},{10,11... | collective-permute-start | bytes 786440 | tf_op jit(solution)/shard_map/ppermute | solution.py:37
  137.0 26.9 %copy-start.19 = (bf16[256,512]{1,0:T(8,128)(2,1)}, bf16[256,512]{1,0:T(8,128)(2,1)S(1)}, u32[]{:S(2)}) copy-start(bf16[256,512]{1,0:T(8,128)(2,1)S(1)} %collective-permute-done.9.refs_2_.refs_1_) | copy-start | bytes 786436
  158.1 5.8 %copy-start.21 = (bf16[256,512]{1,0:T(8,128)(2,1)}, bf16[256,512]{1,0:T(8,128)(2,1)S(1)}, u32[]{:S(2)}) copy-start(bf16[256,512]{1,0:T(8,128)(2,1)S(1)} %collective-permute-done.19.refs_4_.refs_3_) | copy-start | bytes 786436
  163.9 15.6 %copy-start.1 = (bf16[1024,512]{1,0:T(8,128)(2,1)S(1)}, bf16[1024,512]{1,0:T(8,128)(2,1)}, u32[]{:S(2)}) copy-start(bf16[1024,512]{1,0:T(8,128)(2,1)} %copy-done) | copy-start | bytes 3145732
  164.0 12.3 %collective-permute-start.20 = (bf16[512,448]{1,0:T(8,128)(2,1)}, bf16[512,448]{1,0:T(8,128)(2,1)}, u32[]{:S(2)}, u32[]{:S(2)}) collective-permute-start(bf16[512,448]{1,0:T(8,128)(2,1)} %get-tuple-element.42), channel_id=1, source_target_pairs={{0,8},{1,9},{2,10},{3,11},{4,12},{5,13},{6,14},{7,15},{8,0},{9,1},... | collective-permute-start | bytes 1376264 | tf_op jit(solution)/shard_map/ppermute | solution.py:37
  167.0 9.0 %copy-start.15 = (bf16[256,1024]{1,0:T(8,128)(2,1)}, bf16[256,1024]{1,0:T(8,128)(2,1)S(1)}, u32[]{:S(2)}) copy-start(bf16[256,1024]{1,0:T(8,128)(2,1)S(1)} %collective-permute-done.29.refs_3_.refs_1_) | copy-start | bytes 1572868
  167.1 9.0 %copy-start.17 = (bf16[256,1024]{1,0:T(8,128)(2,1)}, bf16[256,1024]{1,0:T(8,128)(2,1)S(1)}, u32[]{:S(2)}) copy-start(bf16[256,1024]{1,0:T(8,128)(2,1)S(1)} %collective-permute-done.35.refs_5_.refs_3_) | copy-start | bytes 1572868
  176.1 10.1 %collective-permute-start.36 = (bf16[512,448]{1,0:T(8,128)(2,1)}, bf16[512,448]{1,0:T(8,128)(2,1)}, u32[]{:S(2)}, u32[]{:S(2)}) collective-permute-start(bf16[512,448]{1,0:T(8,128)(2,1)} %get-tuple-element.49), channel_id=1, source_target_pairs={{0,8},{1,9},{2,10},{3,11},{4,12},{5,13},{6,14},{7,15},{8,0},{9,1},... | collective-permute-start | bytes 1376264 | tf_op jit(solution)/shard_map/ppermute | solution.py:37
  177.4 10.2 %collective-permute-start.21 = (bf16[256,448]{1,0:T(8,128)(2,1)S(1)}, bf16[256,448]{1,0:T(8,128)(2,1)S(1)}, u32[]{:S(2)}, u32[]{:S(2)}) collective-permute-start(bf16[256,448]{1,0:T(8,128)(2,1)S(1)} %get-tuple-element.56), channel_id=1, source_target_pairs={{0,16},{1,17},{2,18},{3,19},{4,20},{5,21},{6,22},{7,23},{8,24},{9,... | collective-permute-start | bytes 688136 | tf_op jit(solution)/shard_map/ppermute | solution.py:37
  179.5 1.0 copy-start.7
  180.5 0.9 copy-start.20
  181.4 0.9 copy-start.22
  186.2 6.1 %copy-start.3 = (bf16[256,1024]{1,0:T(8,128)(2,1)S(1)}, bf16[256,1024]{1,0:T(8,128)(2,1)}, u32[]{:S(2)}) copy-start(bf16[256,1024]{1,0:T(8,128)(2,1)} %copy-done.2) | copy-start | bytes 1572868
  186.2 6.1 %copy-start.5 = (bf16[256,1024]{1,0:T(8,128)(2,1)S(1)}, bf16[256,1024]{1,0:T(8,128)(2,1)}, u32[]{:S(2)}) copy-start(bf16[256,1024]{1,0:T(8,128)(2,1)} %copy-done.4) | copy-start | bytes 1572868
  186.2 6.1 %copy-start.16 = (bf16[256,1024]{1,0:T(8,128)(2,1)S(1)}, bf16[256,1024]{1,0:T(8,128)(2,1)}, u32[]{:S(2)}) copy-start(bf16[256,1024]{1,0:T(8,128)(2,1)} %copy-done.15) | copy-start | bytes 1572868
  186.2 6.1 %copy-start.18 = (bf16[256,1024]{1,0:T(8,128)(2,1)S(1)}, bf16[256,1024]{1,0:T(8,128)(2,1)}, u32[]{:S(2)}) copy-start(bf16[256,1024]{1,0:T(8,128)(2,1)} %copy-done.17) | copy-start | bytes 1572868
  187.5 9.2 %collective-permute-start.37 = (bf16[256,448]{1,0:T(8,128)(2,1)S(1)}, bf16[256,448]{1,0:T(8,128)(2,1)S(1)}, u32[]{:S(2)}, u32[]{:S(2)}) collective-permute-start(bf16[256,448]{1,0:T(8,128)(2,1)S(1)} %get-tuple-element.54), channel_id=1, source_target_pairs={{0,16},{1,17},{2,18},{3,19},{4,20},{5,21},{6,22},{7,23},{8,24},{9,... | collective-permute-start | bytes 688136 | tf_op jit(solution)/shard_map/ppermute | solution.py:37
  187.7 19.0 %collective-permute-start.22 = (bf16[128,448]{1,0:T(8,128)(2,1)S(1)}, bf16[128,448]{1,0:T(8,128)(2,1)S(1)}, u32[]{:S(2)}, u32[]{:S(2)}) collective-permute-start(bf16[128,448]{1,0:T(8,128)(2,1)S(1)} %get-tuple-element.71), channel_id=1, source_target_pairs={{0,0},{1,1},{8,2},{9,3},{16,4},{17,5},{24,6},{25,7},{2,8},{3,9},{1... | collective-permute-start | bytes 344072 | tf_op jit(solution)/shard_map/ppermute | solution.py:81
  191.4 15.3 %collective-permute-start.23 = (bf16[128,448]{1,0:T(8,128)(2,1)S(1)}, bf16[128,448]{1,0:T(8,128)(2,1)S(1)}, u32[]{:S(2)}, u32[]{:S(2)}) collective-permute-start(bf16[128,448]{1,0:T(8,128)(2,1)S(1)} %get-tuple-element.72), channel_id=1, source_target_pairs={{17,0},{16,1},{25,2},{24,3},{1,4},{0,5},{9,6},{8,7},{19,8},{18,9},... | collective-permute-start | bytes 344072 | tf_op jit(solution)/shard_map/ppermute | solution.py:81
  196.7 10.5 %collective-permute-start.38 = (bf16[128,448]{1,0:T(8,128)(2,1)S(1)}, bf16[128,448]{1,0:T(8,128)(2,1)S(1)}, u32[]{:S(2)}, u32[]{:S(2)}) collective-permute-start(bf16[128,448]{1,0:T(8,128)(2,1)S(1)} %get-tuple-element.65), channel_id=1, source_target_pairs={{0,0},{1,1},{8,2},{9,3},{16,4},{17,5},{24,6},{25,7},{2,8},{3,9},{1... | collective-permute-start | bytes 344072 | tf_op jit(solution)/shard_map/ppermute | solution.py:81
  202.1 8.5 %copy-start.11 = (f32[128,1]{0,1:T(1,128)S(1)}, f32[128,1]{0,1:T(1,128)}, u32[]{:S(2)}) copy-start(f32[128,1]{0,1:T(1,128)} %param.10) | copy-start | bytes 1540
  202.1 7.7 %collective-permute-start.39 = (bf16[128,448]{1,0:T(8,128)(2,1)S(1)}, bf16[128,448]{1,0:T(8,128)(2,1)S(1)}, u32[]{:S(2)}, u32[]{:S(2)}) collective-permute-start(bf16[128,448]{1,0:T(8,128)(2,1)S(1)} %get-tuple-element.66), channel_id=1, source_target_pairs={{17,0},{16,1},{25,2},{24,3},{1,4},{0,5},{9,6},{8,7},{19,8},{18,9},... | collective-permute-start | bytes 344072 | tf_op jit(solution)/shard_map/ppermute | solution.py:81

commit v4 on v3

v4 whole, which is shorter than its diff:
```python
import functools

import jax
import jax.numpy as jnp
from jax import lax
from jax.experimental import pallas as pl
from jax.experimental.pallas import tpu as pltpu
from jax.sharding import PartitionSpec as P

AXES = ("grp", "ep")
BF16 = jnp.bfloat16
VMEM = pl.BlockSpec(memory_space=pltpu.VMEM)
SMEM = pl.BlockSpec(memory_space=pltpu.SMEM)
PARAMS = pltpu.CompilerParams(vmem_limit_bytes=50 * 1024 * 1024)
PARTS = 2


def f32(a):
    return a.astype(jnp.float32)


def half(a):
    return a.astype(BF16)


def after(value, *others):
    return lax.optimization_barrier((value,) + others)[0]


def swap(block, grp_bits, ep_bits):
    grp_size, ep_size = lax.axis_size("grp"), lax.axis_size("ep")
    pairs = [
        (g * ep_size + p, (g ^ grp_bits) * ep_size + (p ^ ep_bits))
        for g in range(grp_size)
        for p in range(ep_size)
    ]
    return lax.ppermute(block, AXES, pairs)


def plane_pairs(k):
    grp_size, ep_size = lax.axis_size("grp"), lax.axis_size("ep")
    flip = k * (grp_size // 2)
    return [
        (g * ep_size + p, ((p // 2) ^ flip) * ep_size + 2 * g + ((p % 2) ^ k))
        for g in range(grp_size)
        for p in range(ep_size)
    ]


def column_pairs(across):
    grp_size, ep_size = lax.axis_size("grp"), lax.axis_size("ep")
    top = grp_size // 2
    pairs = []
    for g in range(grp_size):
        for p in range(ep_size):
            z = p // 2
            k = 1 if (g ^ z) & top else 0
            source = g ^ (top if k ^ across else 0)
            target = z ^ (k * top)
            pairs.append((g * ep_size + p, target * ep_size + 2 * source + ((p % 2) ^ k)))
    return pairs


def crossing():
    top = lax.axis_size("grp") // 2
    apart = (lax.axis_index("grp") ^ (lax.axis_index("ep") // 2)) & top
    return (apart != 0).astype(jnp.int32)


class Line:
    def __init__(self):
        self.last = None

    def begin(self, *values):
        if self.last is None:
            return values
        return lax.optimization_barrier(values + (self.last,))[:-1]

    def end(self, value):
        self.last = value
        return value


def summed(terms, rows):
    return functools.reduce(lambda a, b: a + b, [f32(term[rows]) for term in terms])


class Sum:
    def __init__(self, line, keep, send, swaps):
        self.line, self.swaps = line, list(swaps)
        self.terms = [keep]
        self.got = self.swaps.pop(0)(send)

    def fold(self):
        n = self.got.shape[0] // 2
        self.terms[0], self.got = self.line.begin(self.terms[0], self.got)
        terms = self.terms + [self.got]
        send = self.line.end(half(summed(terms, slice(n, None))))
        self.terms = [term[:n] for term in terms]
        self.got = self.swaps.pop(0)(send)

    def finish(self):
        self.terms[0], self.got = self.line.begin(self.terms[0], self.got)
        self.total = self.line.end(summed(self.terms + [self.got], slice(None)))


class Gather:
    def __init__(self, line, own, swaps):
        self.line, self.swaps = line, list(swaps)
        self.held = own
        self.got = self.swaps.pop(0)(own)

    def grow(self):
        held, got = self.line.begin(self.held, self.got)
        self.held = self.line.end(jnp.concatenate([held, got]))
        self.got = self.swaps.pop(0)(self.held)

    def result(self):
        return [self.held, self.got]


class Return:
    def __init__(self, line, keep, send):
        bits = lax.axis_size("grp").bit_length() - 1
        swaps = [functools.partial(swap, grp_bits=1, ep_bits=0)]
        for bit in range(bits - 1, 0, -1):
            swaps.append(functools.partial(swap, grp_bits=1 << bit, ep_bits=0))
        self.rounds = bits - 1
        self.line = line
        self.sum = Sum(line, keep, send, swaps)

    def fold(self):
        self.sum.fold()

    def leave(self):
        total = self.sum
        total.terms[0], total.got = self.line.begin(total.terms[0], total.got)
        n = total.got.shape[0] // 2
        self.pieces = []
        for k in range(2):
            back = [(b, a) for a, b in plane_pairs(k)]
            piece = half(summed(total.terms + [total.got], slice(k * n, (k + 1) * n)))
            self.line.end(piece)
            self.pieces.append(lax.ppermute(piece, AXES, back))


def block_order(bits):
    order = [0]
    for bit in reversed(bits):
        order = order + [j ^ (1 << bit) for j in order]
    return order


def upright(row):
    n = row.shape[1]
    at = lax.broadcasted_iota(jnp.int32, (n, n), 0) == lax.broadcasted_iota(jnp.int32, (n, n), 1)
    return jnp.sum(jnp.where(at, row, jnp.zeros((), row.dtype)), axis=1, keepdims=True)


def cut_body(stored, count, hot_ref, routes_ref, tokens_ref, own_ref, other_ref):
    y = (lax.axis_index("ep") % 2) ^ crossing()
    slot = upright(routes_ref[...])
    expert = slot
    for r in range(hot_ref.shape[0]):
        expert = jnp.where(slot == count + r, hot_ref[r], expert)
    lane = lax.broadcasted_iota(jnp.int32, (slot.shape[0], own_ref.shape[1] - stored), 1)
    tail = half(jnp.where(lane == 0, f32(expert), 0.0))
    rows = tokens_ref[...]
    first, second = rows[:, :stored], rows[:, stored:]
    own_ref[:, :stored] = jnp.where(y == 0, first, second)
    own_ref[:, stored:] = tail
    other_ref[:, :stored] = jnp.where(y == 0, second, first)
    other_ref[:, stored:] = tail


def weigh_body(stored, weights_ref, rows_ref, own_ref, other_ref):
    y = (lax.axis_index("ep") % 2) ^ crossing()
    rows = half(f32(rows_ref[...]) * upright(weights_ref[...]))
    tail = jnp.zeros((rows.shape[0], own_ref.shape[1] - stored), BF16)
    first, second = rows[:, :stored], rows[:, stored:]
    own_ref[:, :stored] = jnp.where(y == 0, first, second)
    own_ref[:, stored:] = tail
    other_ref[:, :stored] = jnp.where(y == 0, second, first)
    other_ref[:, stored:] = tail


def order_rows(geo, held_ref, got_ref, rows_ref):
    grp_size, tok, order = geo
    sub = tok // PARTS
    bits = grp_size.bit_length() - 1
    shift = lax.axis_index("grp") ^ (lax.axis_index("ep") // 2)
    for place, j in enumerate(order):
        k = j & 1
        m = shift ^ ((j >> 1) ^ (k * (grp_size // 2)))
        at = 0
        for b in range(bits - 1):
            at = at + (((m >> (bits - 1 - b)) & 1) << b)
        landed = 1 if (j >> 1) & (grp_size // 2) else 0
        src = pl.ds(pl.multiple_of((at * 2 + landed) * tok, tok), tok)
        rows = jnp.where((m & 1) == 0, held_ref[src, :], got_ref[src, :])
        for part in range(PARTS):
            to = (part * len(order) + place) * sub
            rows_ref[to : to + sub, :] = rows[part * sub : (part + 1) * sub]


def expert_dot(rows, expert, w_ref, count, turned):
    zero = jnp.zeros((), BF16)
    own = jnp.concatenate([jnp.where(expert == e, rows, zero) for e in range(count)], axis=1)
    if turned:
        weights = jnp.concatenate([w_ref[e] for e in range(count)], axis=1)
    else:
        weights = w_ref[...].reshape(own.shape[1], w_ref.shape[2])
    dims = (((1,), (1 if turned else 0,)), ((), ()))
    return lax.dot_general(own, weights, dims, preferred_element_type=jnp.float32)


def id_of(id_ref, stored, rows):
    return id_ref[rows, :][:, stored % 128 : stored % 128 + 1]


def first_body(geo, stored, count, n_w, own_ids, held_ref, got_ref, *refs):
    rows_ref = refs[-1]
    order_rows(geo, held_ref, got_ref, rows_ref)
    n = rows_ref.shape[0] // PARTS
    rows = rows_ref[:n, :]
    if own_ids:
        expert = rows[:, stored : stored + 1]
        refs = refs[:-1]
    else:
        expert = id_of(refs[0], stored, slice(0, n))
        refs = refs[1:-1]
    products(rows[:, :stored], expert, count, n_w, refs)


def products(rows, expert, count, n_w, refs, places=None):
    keep_ref, send_ref = refs[-2:]
    n = rows.shape[0] // 2
    hidden = keep_ref.shape[1] // n_w
    places = places or (0, 1)
    size = rows.shape[0] // len(places)
    for i in range(n_w):
        result = half(expert_dot(rows, expert, refs[i], count, False))
        cols = slice(i * hidden, (i + 1) * hidden)
        for block, place in enumerate(places):
            out_ref, at = (keep_ref, place * size) if place * size < n else (send_ref, place * size - n)
            out_ref[at : at + size, cols] = result[block * size : (block + 1) * size]


def later_body(stored, count, n_w, places, id_ref, rows_ref, *refs):
    expert = id_of(id_ref, stored, slice(None))
    products(rows_ref[:, :stored], expert, count, n_w, refs, places)


def in_order(held, got, source, order):
    n = len(source) // 2
    sub = held.shape[0] // n
    if source == order:
        return [held, got]
    blocks = []
    for j in order:
        place = source.index(j)
        half_of = held if place < n else got
        blocks.append(half_of[(place % n) * sub : (place % n + 1) * sub])
    return [jnp.concatenate(blocks[:n]), jnp.concatenate(blocks[n:])]


def back_body(geo, stored, count, jobs, id_ref, *refs):
    grp_size, tok, order = geo
    keep_ref, send_ref = refs[-2:]
    sub = tok // PARTS
    shift = lax.axis_index("grp") ^ (lax.axis_index("ep") // 2)
    n = len(order) // 2
    for number, (part, terms) in enumerate(jobs):
        for side in range(2):
            at = (part * 2 + side) * n * sub
            expert = id_of(id_ref, stored, slice(at, at + n * sub))
            total = None
            for weight, pair, col, source in terms:
                hidden = refs[weight].shape[2]
                cols = slice(col * hidden, (col + 1) * hidden)
                rows = in_order(refs[pair][:, cols], refs[pair + 1][:, cols], source, order)[side]
                now = expert_dot(rows, expert, refs[weight], count, True)
                total = now if total is None else total + now
            total = half(total)
            for place in range(n):
                j = order[side * n + place]
                k = j & 1
                m = shift ^ ((j >> 1) ^ (k * (grp_size // 2)))
                to = (((m >> 1) * 2 + k) * len(jobs) + number) * sub
                to = pl.ds(pl.multiple_of(to, sub), sub)
                block = total[place * sub : (place + 1) * sub]

                @pl.when((m & 1) == 0)
                def _():
                    keep_ref[to, :] = block

                @pl.when((m & 1) == 1)
                def _():
                    send_ref[to, :] = block


def grad_body(stored, cols, sources, order, id_ref, rows_ref, *refs):
    out_ref = refs[-1]
    expert = half(pl.program_id(0).astype(jnp.float32))
    right = []
    for part, source in enumerate(sources):
        right += in_order(refs[2 * part][:, cols], refs[2 * part + 1][:, cols], source, order)
    right = jnp.concatenate(right)
    right = jnp.where(id_of(id_ref, stored, slice(None)) == expert, right, jnp.zeros((), BF16))
    out_ref[0] = half(
        lax.dot_general(
            rows_ref[:, :stored],
            right,
            (((0,), (0,)), ((), ())),
            preferred_element_type=jnp.float32,
        )
    )


def full(shape):
    return pl.BlockSpec(shape, lambda *_: (0,) * len(shape))


def shards(tokens, routes, route_weights, hot_experts, w_gate, w_up, w_down, cotangent):
    grp_size, ep_size = lax.axis_size("grp"), lax.axis_size("ep")
    y = lax.axis_index("ep") % 2
    tok = tokens.shape[0]
    w_down = jnp.swapaxes(w_down, 1, 2)
    count, stored, hidden = w_gate.shape
    total = tok * ep_size
    n = total // PARTS
    width = (stored // 128 + 1) * 128
    bits = list(range(ep_size.bit_length() - 1))
    order = block_order(bits)
    geo = (grp_size, tok, order)
    piece = [jax.ShapeDtypeStruct((tok, width), BF16)] * 2

    def call(body, out_shape, args, in_specs=None, name=None, **kw):
        return pl.pallas_call(
            body,
            out_shape=out_shape,
            grid=kw.get("grid", (1,)),
            in_specs=in_specs or [full(a.shape) for a in args],
            out_specs=kw.get("out_specs") or [full(o.shape) for o in out_shape],
            compiler_params=PARAMS,
            cost_estimate=pl.CostEstimate(flops=1, bytes_accessed=1, transcendentals=0),
            name=name,
        )(*args)

    x_pieces = call(
        functools.partial(cut_body, stored, count),
        piece,
        (hot_experts, routes.reshape(1, tok), tokens),
        in_specs=[SMEM, full((1, tok)), full(tokens.shape)],
        name="token_pieces",
    )
    line = Line()
    bit_swaps = [functools.partial(swap, grp_bits=0, ep_bits=1 << bit) for bit in bits]
    grp_bits = range(grp_size.bit_length() - 2, 0, -1)

    apart = crossing()

    def hop(pieces):
        return pieces[0], swap(pieces[1], grp_size // 2, 0)

    def land(pieces):
        stay, got = line.begin(*pieces)
        near = jnp.where(apart == 0, stay, got)
        far = line.end(jnp.where(apart == 0, got, stay))
        return [
            lax.ppermute(near, AXES, column_pairs(0)),
            lax.ppermute(far, AXES, column_pairs(1)),
        ]

    def joined_up(pieces):
        return line.end(jnp.concatenate(line.begin(*pieces)))

    dz_pieces = call(
        functools.partial(weigh_body, stored),
        piece,
        (route_weights.reshape(1, tok), cotangent),
        name="cotangent_pieces",
    )
    x_pieces, dz_pieces = hop(x_pieces), hop(dz_pieces)
    x_landed = land(x_pieces)
    dz_landed = land(dz_pieces)
    x_held, dz_held = joined_up(x_landed), None

    def widened(held):
        return [swap(held, 1 << bit, 0) for bit in grp_bits[:1]]

    def doubled(held, got):
        for i, bit in enumerate(grp_bits):
            held = joined_up((held, got[0] if i == 0 else swap(held, 1 << bit, 0)))
        return held

    x_next = widened(x_held)
    dz_held = joined_up(dz_landed)
    dz_next = widened(dz_held)
    x_held = doubled(x_held, x_next)
    x_got = swap(x_held, 1, 0)

    rows_shape = jax.ShapeDtypeStruct((total, width), BF16)

    def id_spec(rows, at):
        return pl.BlockSpec((rows, 128), lambda *_: (at, stored // 128))

    def split(n_w):
        return [jax.ShapeDtypeStruct((n // 2, n_w * hidden), BF16)] * 2

    def later(part, rows, weights, name, places=None):
        return call(
            functools.partial(later_body, stored, count, len(weights), places),
            split(len(weights)),
            (x_rows, rows) + weights,
            in_specs=[
                id_spec(n, part),
                pl.BlockSpec((n, width), lambda *_: (part, 0)),
            ]
            + [full(w.shape) for w in weights],
            name=name,
        )

    x_held, x_got = line.begin(x_held, x_got)
    gu_keep, gu_send, x_rows = call(
        functools.partial(first_body, geo, stored, count, 2, True),
        split(2) + [rows_shape],
        (x_held, x_got, w_gate, w_up),
        name="gate_up_first",
    )
    line.end(gu_send)
    gu = [Sum(line, gu_keep, gu_send, bit_swaps)]
    turned_bits = [bits[1], bits[0]] + bits[2:]
    turned_order = block_order(turned_bits)
    turned_swaps = [bit_swaps[1], bit_swaps[0]] + bit_swaps[2:]
    places = [turned_order.index(j) for j in order]
    dz_held = doubled(dz_held, dz_next)
    dz_got = swap(dz_held, 1, 0)
    (rows,) = line.begin(x_rows)
    keep, send = later(1, rows, (w_gate, w_up), "gate_up_later", places)
    line.end(send)
    gu.append(Sum(line, keep, send, turned_swaps))
    dz_held, dz_got = line.begin(dz_held, dz_got)
    ag_keep, ag_send, dz_rows = call(
        functools.partial(first_body, geo, stored, count, 1, False),
        split(1) + [rows_shape],
        (dz_held, dz_got, x_rows, w_down),
        in_specs=[full(dz_held.shape), full(dz_got.shape), id_spec(total, 0), full(w_down.shape)],
        name="act_grad_first",
    )
    line.end(ag_send)
    ag = [Sum(line, ag_keep, ag_send, bit_swaps)]
    (rows,) = line.begin(dz_rows)
    keep, send = later(1, rows, (w_down,), "act_grad_later", places)
    line.end(send)
    ag.append(Sum(line, keep, send, turned_swaps))
    acts, grads = [None] * PARTS, [None] * PARTS
    sources = [order, turned_order]
    back_swaps = [bit_swaps[::-1], turned_swaps[::-1]]

    def middle(part):
        ag[part].finish()
        gate_up, act_grad = gu[part].total, ag[part].total
        gate_pre, up_pre = gate_up[:, :hidden], gate_up[:, hidden:]
        sg = jax.nn.sigmoid(gate_pre)
        act = half(gate_pre * sg * up_pre)
        gate_grad = act_grad * up_pre * sg * (1.0 + gate_pre * (1.0 - sg))
        up_grad = act_grad * gate_pre * sg
        both = half(jnp.concatenate([gate_grad, up_grad], axis=1))
        line.end(both)
        acts[part] = Gather(line, act, back_swaps[part])
        grads[part] = Gather(line, both, back_swaps[part])

    rounds = len(bits) - 1

    def both(step, pair):
        for one in pair:
            step(one)

    both(Sum.fold, gu)
    ag[0].fold()
    for _ in range(1, rounds):
        gu[0].fold()
        ag[1].fold()
        gu[1].fold()
        ag[0].fold()
    ag[1].fold()
    both(Sum.finish, gu)
    middle(0)
    middle(1)
    both(Gather.grow, grads)
    for _ in range(1, rounds):
        both(Gather.grow, grads)
        both(Gather.grow, acts)
    both(Gather.grow, acts)

    def back(ids, weights, pairs, jobs, name):
        args = tuple(weights) + tuple(pairs)
        return call(
            functools.partial(back_body, geo, stored, count, jobs),
            [jax.ShapeDtypeStruct((n // 2 * len(jobs), stored), BF16)] * 2,
            (ids,) + args,
            in_specs=[id_spec(total, 0)] + [full(a.shape) for a in args],
            name=name,
        )

    def grad(rows, gathered, at, sources, name):
        cols = slice(at * hidden, (at + 1) * hidden)
        return call(
            functools.partial(grad_body, stored, cols, sources, order),
            jax.ShapeDtypeStruct((count, stored, hidden), BF16),
            (x_rows, rows) + tuple(gathered),
            in_specs=[id_spec(total, 0)] + [full(a.shape) for a in (rows,) + tuple(gathered)],
            grid=(count,),
            out_specs=pl.BlockSpec((1, stored, hidden), lambda e: (e, 0, 0)),
            name=name,
        )

    def joined(mine, other):
        return jnp.concatenate(
            [jnp.where(y == 0, mine, other), jnp.where(y == 0, other, mine)], axis=1
        )

    act_pairs = acts[0].result() + acts[1].result()
    grad_pairs = grads[0].result() + grads[1].result()

    jobs = [(i, ((0, 2 + 2 * i, 0, s), (1, 2 + 2 * i, 1, s))) for i, s in enumerate(sources)]
    keep, send = back(x_rows, (w_gate, w_up), line.begin(*grad_pairs), jobs, "token_rows")
    line.end(send)
    token = Return(line, keep, send)
    (rows,) = line.begin(x_rows)
    grad_gate = line.end(grad(rows, grad_pairs, 0, sources, "grad_gate"))
    jobs = [(i, ((0, 1 + 2 * i, 0, s),)) for i, s in enumerate(sources)]
    keep, send = back(x_rows, (w_down,), line.begin(*act_pairs), jobs, "out_rows")
    line.end(send)
    out = Return(line, keep, send)
    token.fold()
    out.fold()
    for _ in range(1, out.rounds):
        both(Return.fold, (token, out))
    (rows,) = line.begin(x_rows)
    grad_up = line.end(grad(rows, grad_pairs, 1, sources, "grad_up"))
    both(Return.leave, (token, out))
    (rows,) = line.begin(dz_rows)
    grad_down = line.end(grad(rows, act_pairs, 0, sources, "grad_down"))
    token.pieces = line.begin(*token.pieces)
    grad_tokens = joined(*token.pieces)
    out.pieces = line.begin(*out.pieces)
    layer_output = half(f32(joined(*out.pieces)) * route_weights)
    return (layer_output, grad_tokens, grad_gate, grad_up, jnp.swapaxes(grad_down, 1, 2))


def solution(mesh):
    placed = (
        P("ep", "grp"),
        P("ep", None),
        P("ep", None),
        P(),
        P(None, "ep", "grp"),
        P(None, "ep", "grp"),
        P(None, "grp", "ep"),
        P("ep", "grp"),
    )
    return jax.shard_map(
        shards,
        mesh=mesh,
        in_specs=placed,
        out_specs=(
            P("ep", "grp"),
            P("ep", "grp"),
            P(None, "ep", "grp"),
            P(None, "ep", "grp"),
            P(None, "grp", "ep"),
        ),
        check_vma=False,
    )
```

time: 213 us -> 176 us (0.83)
  waiting for transfers between devices: 102 us -> 57.2 us
  starting transfers between devices: 53.9 us -> 67.7 us
  Pallas kernels: 42 us -> 38.9 us
  local copies, waits for them, and re-layouts: 6.83 us -> 4.28 us
    ppermute x32 -> x34, waiting for transfers between devices: 79.7 us -> 45.8 us  [swap(): return lax.ppermute(block, AXES, pairs)]
    ppermute x8, waiting for transfers between devices: 22.4 us -> 11.4 us  [the longest x2 6.91 us: land(): lax.ppermute(far, AXES, column_pairs(1))]
    ppermute x32 -> x34, starting transfers between devices: 35.9 us -> 45.8 us  [swap(): return lax.ppermute(block, AXES, pairs)]
    ppermute x8, starting transfers between devices: 18 us -> 21.9 us  [the longest x4 11.7 us: leave(): self.pieces.append(lax.ppermute(piece, AXES, back))]
    pallas_call x11, Pallas kernels: 42 us -> 38.9 us  [call(): pl.pallas_call(body, out_shape=out_shape, grid=kw.get('grid', (1,)), in_s...]
    unnamed x50 -> x30, local copies, waits for them, and re-layouts: 6.79 us -> 4 us
  transfers between devices with their start and end apart: 40 -> 42, of which waited for: 19 -> 22; matrix products, arithmetic and copies ran while one was open for 2% -> 2% of each run, Pallas kernels for 18% -> 22%
where the time goes in v4:
time: 176 us; the launch traced here: 174 us
  starting transfers between devices  67.7 us (38%)
  waiting for transfers between devices  57.2 us (32%)
  Pallas kernels  38.9 us (22%)
  other arithmetic  5.08 us (3%)
  local copies, waits for them, and re-layouts  4.28 us (2%)
    ppermute x34, starting transfers between devices, swap(): return lax.ppermute(block, AXES, pairs)  45.8 us
    ppermute x34, waiting for transfers between devices, swap(): return lax.ppermute(block, AXES, pairs)  45.8 us
    pallas_call x11, Pallas kernels, call(): pl.pallas_call(body, out_shape=out_shape, grid=kw.get('grid', (1,)), in_s...  38.9 us
    ppermute x4, starting transfers between devices, leave(): self.pieces.append(lax.ppermute(piece, AXES, back))  11.7 us
    ppermute x2, starting transfers between devices, land(): lax.ppermute(near, AXES, column_pairs(0))  8.94 us
    ppermute x2, waiting for transfers between devices, land(): lax.ppermute(far, AXES, column_pairs(1))  6.91 us
    ppermute x4, waiting for transfers between devices, leave(): self.pieces.append(lax.ppermute(piece, AXES, back))  4.49 us
    unnamed x30, local copies, waits for them, and re-layouts  4 us
  transfers between devices with their start and end apart: 42, of which 22 were waited for; matrix products, arithmetic and copies ran while one was open for 2% of the time, Pallas kernels for 22%

profile of v4, /device:TPU:17, one launch (start us, length us, event | category | flops | bytes accessed | tf_op | source)
XLA Modules:
  0.0 174.3 jit_solution(18440305793278091374)
XLA Ops:
  0.6 0.9 copy-done.3
  1.6 0.7 copy-done.7
  2.2 0.7 copy-done.8
  2.9 0.7 token_pieces.1
  3.6 1.3 collective-permute-start
  4.9 0.9 copy-done.4
  7.1 1.0 collective-permute-done
  8.1 5.6 %collective-permute-start.1 = (bf16[128,512]{1,0:T(8,128)(2,1)S(1)}, bf16[128,512]{1,0:T(8,128)(2,1)S(1)}, u32[]{:S(2)}, u32[]{:S(2)}) collective-permute-start(bf16[128,512]{1,0:T(8,128)(2,1)S(1)} %get-tuple-element.216), channel_id=1, source_target_pairs={{0,0},{1,1},{2,8},{3,9},{4,5},{5,4},{6,13},{7,12},{8,2},{9,3},{10,... | collective-permute-start | bytes 393224 | tf_op jit(solution)/shard_map/ppermute | solution.py:371
  13.8 3.3 %collective-permute-start.5 = (bf16[128,512]{1,0:T(8,128)(2,1)S(1)}, bf16[128,512]{1,0:T(8,128)(2,1)S(1)}, u32[]{:S(2)}, u32[]{:S(2)}) collective-permute-start(bf16[128,512]{1,0:T(8,128)(2,1)S(1)} %get-tuple-element.213), channel_id=1, source_target_pairs={{0,0},{1,1},{2,8},{3,9},{4,5},{5,4},{6,13},{7,12},{8,2},{9,3},{10,... | collective-permute-start | bytes 393224 | tf_op jit(solution)/shard_map/ppermute | solution.py:371
  17.1 1.2 collective-permute-start.6
  18.4 6.4 %collective-permute-done.2 = bf16[128,512]{1,0:T(8,128)(2,1)S(1)} collective-permute-done((bf16[128,512]{1,0:T(8,128)(2,1)S(1)}, bf16[128,512]{1,0:T(8,128)(2,1)S(1)}, u32[]{:S(2)}, u32[]{:S(2)}) %collective-permute-start.2) | collective-permute-done | bytes 131104 | tf_op jit(solution)/shard_map/ppermute | solution.py:372
  24.8 0.9 collective-permute-start.4
  26.3 3.7 %collective-permute-done.4 = bf16[256,512]{1,0:T(8,128)(2,1)S(1)} collective-permute-done((bf16[256,512]{1,0:T(8,128)(2,1)S(1)}, bf16[256,512]{1,0:T(8,128)(2,1)S(1)}, u32[]{:S(2)}, u32[]{:S(2)}) %collective-permute-start.4) | collective-permute-done | bytes 262176 | tf_op jit(solution)/shard_map/ppermute | solution.py:37
  30.2 0.9 collective-permute-start.9
  31.1 0.9 collective-permute-done.7.got_ref
  32.1 4.5 %gate_up_first.1 = (bf16[256,1024]{1,0:T(8,128)(2,1)S(1)}, bf16[256,1024]{1,0:T(8,128)(2,1)S(1)}, bf16[1024,512]{1,0:T(8,128)(2,1)S(1)}) custom-call(bf16[512,512]{1,0:T(8,128)(2,1)S(1)} %constant_dynamic-update-slice_fusion.4.held_ref, bf16[512,512]{1,0:T(8,128)(2,1)S(1)} %collective-permute-done.7.got_ref, bf16[4,448,512]{2,1,0:T(8,128)(2,1)} %refs_0_.5, ...), custom_call_target="tpu_custom_call" | custom-call | flops 1 | bytes 1 | tf_op jit(solution)/shard_map/gate_up_first/pallas_call | solution.py:339
  36.6 1.1 collective-permute-done.9
  37.8 1.3 collective-permute-start.10
  39.1 0.7 collective-permute-start.8
  39.8 3.8 %gate_up_later.1 = (bf16[256,1024]{1,0:T(8,128)(2,1)S(1)}, bf16[256,1024]{1,0:T(8,128)(2,1)S(1)}) custom-call(bf16[1024,512]{1,0:T(8,128)(2,1)S(1)} %get-tuple-element.189.id_ref.rows_ref.refs_0_, bf16[1024,512]{1,0:T(8,128)(2,1)S(1)} %get-tuple-element.189.id_ref.rows_ref.refs_0_, bf16[4,448,512]{2,1,0:T(8,128)(2,1)S(1)} %copy-done.2, ...), custom_call_target="tpu_custom_call" | custom-call | flops 1 | bytes 1 | tf_op jit(solution)/shard_map/gate_up_later/pallas_call | solution.py:339
  43.7 2.9 %act_grad_first.1 = (bf16[256,512]{1,0:T(8,128)(2,1)S(1)}, bf16[256,512]{1,0:T(8,128)(2,1)S(1)}, bf16[1024,512]{1,0:T(8,128)(2,1)S(1)}) custom-call(bf16[512,512]{1,0:T(8,128)(2,1)S(1)} %constant_dynamic-update-slice_fusion.6.held_ref, bf16[512,512]{1,0:T(8,128)(2,1)S(1)} %collective-permute-done.10.got_ref, ...), custom_call_target="tpu_custom_call" | custom-call | flops 1 | bytes 1 | tf_op jit(solution)/shard_map/act_grad_first/pallas_call | solution.py:339
  46.6 0.8 collective-permute-start.12
  47.4 2.8 %act_grad_later.1 = (bf16[256,512]{1,0:T(8,128)(2,1)S(1)}, bf16[256,512]{1,0:T(8,128)(2,1)S(1)}) custom-call(bf16[1024,512]{1,0:T(8,128)(2,1)S(1)} %get-tuple-element.189.id_ref.rows_ref.refs_0_, bf16[1024,512]{1,0:T(8,128)(2,1)S(1)} %get-tuple-element.194.rows_ref, bf16[4,448,512]{2,1,0:T(8,128)(2,1)} %bitcast.9), custom_call_target="tpu_custom_call" | custom-call | flops 1 | bytes 1 | tf_op jit(solution)/shard_map/act_grad_later/pallas_call | solution.py:339
  50.3 1.5 collective-permute-start.15
  51.8 0.8 collective-permute-done.8
  52.7 4.1 %collective-permute-done.13 = bf16[256,1024]{1,0:T(8,128)(2,1)S(1)} collective-permute-done((bf16[256,1024]{1,0:T(8,128)(2,1)S(1)}, bf16[256,1024]{1,0:T(8,128)(2,1)S(1)}, u32[]{:S(2)}, u32[]{:S(2)}) %collective-permute-start.13) | collective-permute-done | bytes 524320 | tf_op jit(solution)/shard_map/ppermute | solution.py:37
  56.9 0.8 collective-permute-start.18
  58.3 9.7 %collective-permute-done.11 = bf16[128,1024]{1,0:T(8,128)(2,1)S(1)} collective-permute-done((bf16[128,1024]{1,0:T(8,128)(2,1)S(1)}, bf16[128,1024]{1,0:T(8,128)(2,1)S(1)}, u32[]{:S(2)}, u32[]{:S(2)}) %collective-permute-start.11) | collective-permute-done | bytes 262176 | tf_op jit(solution)/shard_map/ppermute | solution.py:37
  68.8 0.7 collective-permute-start.16
  69.6 2.0 %collective-permute-start.22 = (bf16[64,1024]{1,0:T(8,128)(2,1)S(1)}, bf16[64,1024]{1,0:T(8,128)(2,1)S(1)}, u32[]{:S(2)}, u32[]{:S(2)}) collective-permute-start(bf16[64,1024]{1,0:T(8,128)(2,1)S(1)} %add_convert_fusion.8), channel_id=1, source_target_pairs={{0,4},{1,5},{2,6},{3,7},{4,0},{5,1},{6,2},{7,3},{8,12},{9,13},{10,... | collective-permute-start | bytes 393224 | tf_op jit(solution)/shard_map/ppermute | solution.py:37
  72.7 2.2 %collective-permute-start.20 = (bf16[64,512]{1,0:T(8,128)(2,1)S(1)}, bf16[64,512]{1,0:T(8,128)(2,1)S(1)}, u32[]{:S(2)}, u32[]{:S(2)}) collective-permute-start(bf16[64,512]{1,0:T(8,128)(2,1)S(1)} %add_convert_fusion.12), channel_id=1, source_target_pairs={{0,4},{1,5},{2,6},{3,7},{4,0},{5,1},{6,2},{7,3},{8,12},{9,13},{10,... | collective-permute-start | bytes 196616 | tf_op jit(solution)/shard_map/ppermute | solution.py:37
  75.0 6.9 %collective-permute-done.22 = bf16[64,1024]{1,0:T(8,128)(2,1)S(1)} collective-permute-done((bf16[64,1024]{1,0:T(8,128)(2,1)S(1)}, bf16[64,1024]{1,0:T(8,128)(2,1)S(1)}, u32[]{:S(2)}, u32[]{:S(2)}) %collective-permute-start.22) | collective-permute-done | bytes 131104 | tf_op jit(solution)/shard_map/ppermute | solution.py:37
  82.0 1.3 collective-permute-done.21
  83.5 3.2 %collective-permute-start.24 = (bf16[64,1024]{1,0:T(8,128)(2,1)S(1)}, bf16[64,1024]{1,0:T(8,128)(2,1)S(1)}, u32[]{:S(2)}, u32[]{:S(2)}) collective-permute-start(bf16[64,1024]{1,0:T(8,128)(2,1)S(1)} %pad_maximum_fusion.1), channel_id=1, source_target_pairs={{0,4},{1,5},{2,6},{3,7},{4,0},{5,1},{6,2},{7,3},{8,12},{9,13},{10,... | collective-permute-start | bytes 393224 | tf_op jit(solution)/shard_map/ppermute | solution.py:37
  86.8 1.3 collective-permute-start.23
  88.0 1.5 collective-permute-done.24
  89.5 5.3 %collective-permute-start.26 = (bf16[128,1024]{1,0:T(8,128)(2,1)S(1)}, bf16[128,1024]{1,0:T(8,128)(2,1)S(1)}, u32[]{:S(2)}, u32[]{:S(2)}) collective-permute-start(bf16[128,1024]{1,0:T(8,128)(2,1)S(1)} %constant_dynamic-update-slice_fusion.8), channel_id=1, source_target_pairs={{0,2},{1,3},{2,0},{3,1},{4,6},{5,7},{6,4},{7,5},{8,10},{9,11},{10,... | collective-permute-start | bytes 786440 | tf_op jit(solution)/shard_map/ppermute | solution.py:37
  94.8 1.8 %collective-permute-done.23 = bf16[64,1024]{1,0:T(8,128)(2,1)S(1)} collective-permute-done((bf16[64,1024]{1,0:T(8,128)(2,1)S(1)}, bf16[64,1024]{1,0:T(8,128)(2,1)S(1)}, u32[]{:S(2)}, u32[]{:S(2)}) %collective-permute-start.23) | collective-permute-done | bytes 131104 | tf_op jit(solution)/shard_map/ppermute | solution.py:37
  96.6 1.1 collective-permute-start.25
  97.7 3.1 %collective-permute-start.28 = (bf16[64,512]{1,0:T(8,128)(2,1)S(1)}, bf16[64,512]{1,0:T(8,128)(2,1)S(1)}, u32[]{:S(2)}, u32[]{:S(2)}) collective-permute-start(bf16[64,512]{1,0:T(8,128)(2,1)S(1)} %get-tuple-element.166), channel_id=1, source_target_pairs={{0,4},{1,5},{2,6},{3,7},{4,0},{5,1},{6,2},{7,3},{8,12},{9,13},{10,... | collective-permute-start | bytes 196616 | tf_op jit(solution)/shard_map/ppermute | solution.py:37
  101.4 0.8 collective-permute-start.32
  102.3 2.9 %collective-permute-start.33 = (bf16[256,1024]{1,0:T(8,128)(2,1)S(1)}, bf16[256,1024]{1,0:T(8,128)(2,1)S(1)}, u32[]{:S(2)}, u32[]{:S(2)}) collective-permute-start(bf16[256,1024]{1,0:T(8,128)(2,1)S(1)} %constant_dynamic-update-slice_fusion.14.refs_4_.refs_2_), channel_id=1, source_target_pairs={{0,2},{1,3},{2,0},{3,1},{4,6},{5,7},{6,4},{7,5},{8,10},{9,11},{10,... | collective-permute-start | bytes 1572872 | tf_op jit(solution)/shard_map/ppermute | solution.py:37
  105.1 0.7 collective-permute-done.19
  106.2 10.0 %collective-permute-done.27 = bf16[128,512]{1,0:T(8,128)(2,1)S(1)} collective-permute-done((bf16[128,512]{1,0:T(8,128)(2,1)S(1)}, bf16[128,512]{1,0:T(8,128)(2,1)S(1)}, u32[]{:S(2)}, u32[]{:S(2)}) %collective-permute-start.27) | collective-permute-done | bytes 131104 | tf_op jit(solution)/shard_map/ppermute | solution.py:37
  116.3 1.8 %collective-permute-start.31 = (bf16[256,512]{1,0:T(8,128)(2,1)S(1)}, bf16[256,512]{1,0:T(8,128)(2,1)S(1)}, u32[]{:S(2)}, u32[]{:S(2)}) collective-permute-start(bf16[256,512]{1,0:T(8,128)(2,1)S(1)} %constant_dynamic-update-slice_fusion.22.refs_3_.refs_2_), channel_id=1, source_target_pairs={{0,2},{1,3},{2,0},{3,1},{4,6},{5,7},{6,4},{7,5},{8,10},{9,11},{10,... | collective-permute-start | bytes 786440 | tf_op jit(solution)/shard_map/ppermute | solution.py:37
  118.1 1.5 collective-permute-start.29
  119.7 7.8 %token_rows.1 = (bf16[512,448]{1,0:T(8,128)(2,1)S(1)}, bf16[512,448]{1,0:T(8,128)(2,1)S(1)}) custom-call(bf16[1024,512]{1,0:T(8,128)(2,1)} %copy-done, bf16[4,448,512]{2,1,0:T(8,128)(2,1)} %refs_0_.5, bf16[4,448,512]{2,1,0:T(8,128)(2,1)} %refs_1_.5, bf16[256,1024]{1,0:T(8,128)(2,1)S(1)} %constant_dynamic-update-slice_fusion.12.refs_2_.refs_0_, ...), custom_call_target="tpu_custom_call" | custom-call | flops 1 | bytes 1 | tf_op jit(solution)/shard_map/token_rows/pallas_call | solution.py:339
  127.5 6.1 %collective-permute-start.35 = (bf16[512,448]{1,0:T(8,128)(2,1)S(1)}, bf16[512,448]{1,0:T(8,128)(2,1)S(1)}, u32[]{:S(2)}, u32[]{:S(2)}) collective-permute-start(bf16[512,448]{1,0:T(8,128)(2,1)S(1)} %get-tuple-element.176), channel_id=1, source_target_pairs={{0,8},{1,9},{2,10},{3,11},{4,12},{5,13},{6,14},{7,15},{8,0},{9,1},... | collective-permute-start | bytes 1376264 | tf_op jit(solution)/shard_map/ppermute | solution.py:37
  133.6 3.8 %grad_gate.1 = bf16[4,448,512]{2,1,0:T(8,128)(2,1)} custom-call(bf16[1024,512]{1,0:T(8,128)(2,1)S(1)} %copy-done.1, bf16[1024,512]{1,0:T(8,128)(2,1)S(1)} %copy-done.1, bf16[256,1024]{1,0:T(8,128)(2,1)S(1)} %constant_dynamic-update-slice_fusion.12.refs_2_.refs_0_, bf16[256,1024]{1,0:T(8,128)(2,1)S(1)} %collective-permute-done.32.refs_3_.refs_1_, ...), custom_call_target="tpu_custom_call" | custom-call | flops 1 | bytes 1 | tf_op jit(solution)/shard_map/grad_gate/pallas_call | solution.py:339
  137.4 4.8 %out_rows.1 = (bf16[512,448]{1,0:T(8,128)(2,1)S(1)}, bf16[512,448]{1,0:T(8,128)(2,1)S(1)}) custom-call(bf16[1024,512]{1,0:T(8,128)(2,1)S(1)} %copy-done.1, bf16[4,448,512]{2,1,0:T(8,128)(2,1)} %bitcast.10, bf16[256,512]{1,0:T(8,128)(2,1)S(1)} %constant_dynamic-update-slice_fusion.20.refs_1_.refs_0_, ...), custom_call_target="tpu_custom_call" | custom-call | flops 1 | bytes 1 | tf_op jit(solution)/shard_map/out_rows/pallas_call | solution.py:339
  142.4 1.7 collective-permute-start.37
  144.2 1.7 collective-permute-start.36
  145.9 3.8 %grad_up.1 = bf16[4,448,512]{2,1,0:T(8,128)(2,1)} custom-call(bf16[1024,512]{1,0:T(8,128)(2,1)S(1)} %copy-done.1, bf16[1024,512]{1,0:T(8,128)(2,1)S(1)} %copy-done.1, bf16[256,1024]{1,0:T(8,128)(2,1)S(1)} %constant_dynamic-update-slice_fusion.12.refs_2_.refs_0_, bf16[256,1024]{1,0:T(8,128)(2,1)S(1)} %collective-permute-done.32.refs_3_.refs_1_, ...), custom_call_target="tpu_custom_call" | custom-call | flops 1 | bytes 1 | tf_op jit(solution)/shard_map/grad_up/pallas_call | solution.py:339
  150.2 0.8 add_convert_fusion.4
  150.9 7.0 %collective-permute-start.40 = (bf16[128,448]{1,0:T(8,128)(2,1)}, bf16[128,448]{1,0:T(8,128)(2,1)S(1)}, u32[]{:S(2)}, u32[]{:S(2)}) collective-permute-start(bf16[128,448]{1,0:T(8,128)(2,1)} %get-tuple-element.199), channel_id=1, source_target_pairs={{0,0},{1,1},{8,2},{9,3},{16,4},{17,5},{24,6},{25,7},{2,8},{3,9},{1... | collective-permute-start | bytes 344072 | tf_op jit(solution)/shard_map/ppermute | solution.py:144
  158.0 0.8 add_convert_fusion.5
  158.8 3.9 %collective-permute-start.38 = (bf16[128,448]{1,0:T(8,128)(2,1)}, bf16[128,448]{1,0:T(8,128)(2,1)}, u32[]{:S(2)}, u32[]{:S(2)}) collective-permute-start(bf16[128,448]{1,0:T(8,128)(2,1)} %get-tuple-element.202), channel_id=1, source_target_pairs={{0,0},{1,1},{8,2},{9,3},{16,4},{17,5},{24,6},{25,7},{2,8},{3,9},{1... | collective-permute-start | bytes 344072 | tf_op jit(solution)/shard_map/ppermute | solution.py:144
  162.7 0.7 collective-permute-start.39
  163.4 3.8 %grad_down.1 = bf16[4,448,512]{2,1,0:T(8,128)(2,1)} custom-call(bf16[1024,512]{1,0:T(8,128)(2,1)S(1)} %copy-done.1, bf16[1024,512]{1,0:T(8,128)(2,1)S(1)} %get-tuple-element.194.rows_ref, bf16[256,512]{1,0:T(8,128)(2,1)S(1)} %constant_dynamic-update-slice_fusion.20.refs_1_.refs_0_, bf16[256,512]{1,0:T(8,128)(2,1)S(1)} %collective-permute-done.29.refs_2_.refs_1_, ...), custom_call_target="tpu_custom_call" | custom-call | flops 1 | bytes 1 | tf_op jit(solution)/shard_map/grad_down/pallas_call | solution.py:339
  167.2 2.2 %collective-permute-done.38 = bf16[128,448]{1,0:T(8,128)(2,1)} collective-permute-done((bf16[128,448]{1,0:T(8,128)(2,1)}, bf16[128,448]{1,0:T(8,128)(2,1)}, u32[]{:S(2)}, u32[]{:S(2)}) %collective-permute-start.38) | collective-permute-done | bytes 114720 | tf_op jit(solution)/shard_map/ppermute | solution.py:144
  169.4 2.3 %collective-permute-done.39 = bf16[128,448]{1,0:T(8,128)(2,1)} collective-permute-done((bf16[128,448]{1,0:T(8,128)(2,1)}, bf16[128,448]{1,0:T(8,128)(2,1)}, u32[]{:S(2)}, u32[]{:S(2)}) %collective-permute-start.39) | collective-permute-done | bytes 114720 | tf_op jit(solution)/shard_map/ppermute | solution.py:144
  171.7 1.0 broadcast_select_fusion.5
  172.7 0.8 pad_maximum_fusion
  173.5 0.8 multiply_convert_fusion
  (106 shorter events, 7.3 us)
Async XLA Ops:
  0.6 0.9 copy-start.3
  1.6 0.7 copy-start.7
  2.2 0.7 copy-start.8
  3.6 4.4 %collective-permute-start = (bf16[128,512]{1,0:T(8,128)(2,1)S(1)}, bf16[128,512]{1,0:T(8,128)(2,1)S(1)}, u32[]{:S(2)}, u32[]{:S(2)}) collective-permute-start(bf16[128,512]{1,0:T(8,128)(2,1)S(1)} %get-tuple-element.103), channel_id=1, source_target_pairs={{0,16},{1,17},{2,18},{3,19},{4,20},{5,21},{6,22},{7,23},{8,24},{9,... | collective-permute-start | bytes 393224 | tf_op jit(solution)/shard_map/ppermute | solution.py:37
  4.9 0.9 copy-start.4
  5.8 0.7 copy-start.5
  6.8 7.0 %collective-permute-start.3 = (bf16[128,512]{1,0:T(8,128)(2,1)S(1)}, bf16[128,512]{1,0:T(8,128)(2,1)S(1)}, u32[]{:S(2)}, u32[]{:S(2)}) collective-permute-start(bf16[128,512]{1,0:T(8,128)(2,1)S(1)} %get-tuple-element.105), channel_id=1, source_target_pairs={{0,16},{1,17},{2,18},{3,19},{4,20},{5,21},{6,22},{7,23},{8,24},{9,... | collective-permute-start | bytes 393224 | tf_op jit(solution)/shard_map/ppermute | solution.py:37
  8.1 10.3 %collective-permute-start.1 = (bf16[128,512]{1,0:T(8,128)(2,1)S(1)}, bf16[128,512]{1,0:T(8,128)(2,1)S(1)}, u32[]{:S(2)}, u32[]{:S(2)}) collective-permute-start(bf16[128,512]{1,0:T(8,128)(2,1)S(1)} %get-tuple-element.216), channel_id=1, source_target_pairs={{0,0},{1,1},{2,8},{3,9},{4,5},{5,4},{6,13},{7,12},{8,2},{9,3},{10,... | collective-permute-start | bytes 393224 | tf_op jit(solution)/shard_map/ppermute | solution.py:371
  13.7 11.1 %collective-permute-start.2 = (bf16[128,512]{1,0:T(8,128)(2,1)S(1)}, bf16[128,512]{1,0:T(8,128)(2,1)S(1)}, u32[]{:S(2)}, u32[]{:S(2)}) collective-permute-start(bf16[128,512]{1,0:T(8,128)(2,1)S(1)} %get-tuple-element.215), channel_id=1, source_target_pairs={{0,4},{1,5},{2,12},{3,13},{4,1},{5,0},{6,9},{7,8},{8,6},{9,7},{10,... | collective-permute-start | bytes 393224 | tf_op jit(solution)/shard_map/ppermute | solution.py:372
  13.8 11.9 %collective-permute-start.5 = (bf16[128,512]{1,0:T(8,128)(2,1)S(1)}, bf16[128,512]{1,0:T(8,128)(2,1)S(1)}, u32[]{:S(2)}, u32[]{:S(2)}) collective-permute-start(bf16[128,512]{1,0:T(8,128)(2,1)S(1)} %get-tuple-element.213), channel_id=1, source_target_pairs={{0,0},{1,1},{2,8},{3,9},{4,5},{5,4},{6,13},{7,12},{8,2},{9,3},{10,... | collective-permute-start | bytes 393224 | tf_op jit(solution)/shard_map/ppermute | solution.py:371
  17.1 9.1 %collective-permute-start.6 = (bf16[128,512]{1,0:T(8,128)(2,1)S(1)}, bf16[128,512]{1,0:T(8,128)(2,1)S(1)}, u32[]{:S(2)}, u32[]{:S(2)}) collective-permute-start(bf16[128,512]{1,0:T(8,128)(2,1)S(1)} %get-tuple-element.214), channel_id=1, source_target_pairs={{0,4},{1,5},{2,12},{3,13},{4,1},{5,0},{6,9},{7,8},{8,6},{9,7},{10,... | collective-permute-start | bytes 393224 | tf_op jit(solution)/shard_map/ppermute | solution.py:372
  24.8 5.3 %collective-permute-start.4 = (bf16[256,512]{1,0:T(8,128)(2,1)S(1)}, bf16[256,512]{1,0:T(8,128)(2,1)S(1)}, u32[]{:S(2)}, u32[]{:S(2)}) collective-permute-start(bf16[256,512]{1,0:T(8,128)(2,1)S(1)} %constant_dynamic-update-slice_fusion), channel_id=1, source_target_pairs={{0,16},{1,17},{2,18},{3,19},{4,20},{5,21},{6,22},{7,23},{8,24},{9,... | collective-permute-start | bytes 786440 | tf_op jit(solution)/shard_map/ppermute | solution.py:37
  30.1 9.7 %copy-start.2 = (bf16[4,448,512]{2,1,0:T(8,128)(2,1)S(1)}, bf16[4,448,512]{2,1,0:T(8,128)(2,1)}, u32[]{:S(2)}) copy-start(bf16[4,448,512]{2,1,0:T(8,128)(2,1)} %refs_0_.5) | copy-start | bytes 5505028
  30.1 2.0 %collective-permute-start.7 = (bf16[512,512]{1,0:T(8,128)(2,1)S(1)}, bf16[512,512]{1,0:T(8,128)(2,1)S(1)}, u32[]{:S(2)}, u32[]{:S(2)}) collective-permute-start(bf16[512,512]{1,0:T(8,128)(2,1)S(1)} %constant_dynamic-update-slice_fusion.4.held_ref), channel_id=1, source_target_pairs={{0,8},{1,9},{2,10},{3,11},{4,12},{5,13},{6,14},{7,15},{8,0},{9,1},... | collective-permute-start | bytes 1572872 | tf_op jit(solution)/shard_map/ppermute | solution.py:37
  30.2 7.5 %collective-permute-start.9 = (bf16[256,512]{1,0:T(8,128)(2,1)S(1)}, bf16[256,512]{1,0:T(8,128)(2,1)S(1)}, u32[]{:S(2)}, u32[]{:S(2)}) collective-permute-start(bf16[256,512]{1,0:T(8,128)(2,1)S(1)} %constant_dynamic-update-slice_fusion.2), channel_id=1, source_target_pairs={{0,16},{1,17},{2,18},{3,19},{4,20},{5,21},{6,22},{7,23},{8,24},{9,... | collective-permute-start | bytes 786440 | tf_op jit(solution)/shard_map/ppermute | solution.py:37
  36.6 10.8 %copy-start = (bf16[1024,512]{1,0:T(8,128)(2,1)}, bf16[1024,512]{1,0:T(8,128)(2,1)S(1)}, u32[]{:S(2)}) copy-start(bf16[1024,512]{1,0:T(8,128)(2,1)S(1)} %get-tuple-element.189.id_ref.rows_ref.refs_0_) | copy-start | bytes 3145732
  37.8 5.9 %collective-permute-start.10 = (bf16[512,512]{1,0:T(8,128)(2,1)S(1)}, bf16[512,512]{1,0:T(8,128)(2,1)S(1)}, u32[]{:S(2)}, u32[]{:S(2)}) collective-permute-start(bf16[512,512]{1,0:T(8,128)(2,1)S(1)} %constant_dynamic-update-slice_fusion.6.held_ref), channel_id=1, source_target_pairs={{0,8},{1,9},{2,10},{3,11},{4,12},{5,13},{6,14},{7,15},{8,0},{9,1},... | collective-permute-start | bytes 1572872 | tf_op jit(solution)/shard_map/ppermute | solution.py:37
  39.1 13.5 %collective-permute-start.8 = (bf16[256,1024]{1,0:T(8,128)(2,1)S(1)}, bf16[256,1024]{1,0:T(8,128)(2,1)S(1)}, u32[]{:S(2)}, u32[]{:S(2)}) collective-permute-start(bf16[256,1024]{1,0:T(8,128)(2,1)S(1)} %get-tuple-element.118), channel_id=1, source_target_pairs={{0,1},{1,0},{2,3},{3,2},{4,5},{5,4},{6,7},{7,6},{8,9},{9,8},{10,11... | collective-permute-start | bytes 1572872 | tf_op jit(solution)/shard_map/ppermute | solution.py:37
  43.6 13.2 %collective-permute-start.13 = (bf16[256,1024]{1,0:T(8,128)(2,1)S(1)}, bf16[256,1024]{1,0:T(8,128)(2,1)S(1)}, u32[]{:S(2)}, u32[]{:S(2)}) collective-permute-start(bf16[256,1024]{1,0:T(8,128)(2,1)S(1)} %get-tuple-element.122), channel_id=1, source_target_pairs={{0,2},{1,3},{2,0},{3,1},{4,6},{5,7},{6,4},{7,5},{8,10},{9,11},{10,... | collective-permute-start | bytes 1572872 | tf_op jit(solution)/shard_map/ppermute | solution.py:37
  46.6 11.6 %collective-permute-start.12 = (bf16[256,512]{1,0:T(8,128)(2,1)S(1)}, bf16[256,512]{1,0:T(8,128)(2,1)S(1)}, u32[]{:S(2)}, u32[]{:S(2)}) collective-permute-start(bf16[256,512]{1,0:T(8,128)(2,1)S(1)} %get-tuple-element.126), channel_id=1, source_target_pairs={{0,1},{1,0},{2,3},{3,2},{4,5},{5,4},{6,7},{7,6},{8,9},{9,8},{10,11... | collective-permute-start | bytes 786440 | tf_op jit(solution)/shard_map/ppermute | solution.py:37
  50.3 18.5 %collective-permute-start.15 = (bf16[256,512]{1,0:T(8,128)(2,1)S(1)}, bf16[256,512]{1,0:T(8,128)(2,1)S(1)}, u32[]{:S(2)}, u32[]{:S(2)}) collective-permute-start(bf16[256,512]{1,0:T(8,128)(2,1)S(1)} %get-tuple-element.128), channel_id=1, source_target_pairs={{0,2},{1,3},{2,0},{3,1},{4,6},{5,7},{6,4},{7,5},{8,10},{9,11},{10,... | collective-permute-start | bytes 786440 | tf_op jit(solution)/shard_map/ppermute | solution.py:37
  52.7 15.4 %collective-permute-start.11 = (bf16[128,1024]{1,0:T(8,128)(2,1)S(1)}, bf16[128,1024]{1,0:T(8,128)(2,1)S(1)}, u32[]{:S(2)}, u32[]{:S(2)}) collective-permute-start(bf16[128,1024]{1,0:T(8,128)(2,1)S(1)} %add_convert_fusion.3), channel_id=1, source_target_pairs={{0,2},{1,3},{2,0},{3,1},{4,6},{5,7},{6,4},{7,5},{8,10},{9,11},{10,... | collective-permute-start | bytes 786440 | tf_op jit(solution)/shard_map/ppermute | solution.py:37
  56.9 12.6 %collective-permute-start.18 = (bf16[128,1024]{1,0:T(8,128)(2,1)S(1)}, bf16[128,1024]{1,0:T(8,128)(2,1)S(1)}, u32[]{:S(2)}, u32[]{:S(2)}) collective-permute-start(bf16[128,1024]{1,0:T(8,128)(2,1)S(1)} %add_convert_fusion.2), channel_id=1, source_target_pairs={{0,1},{1,0},{2,3},{3,2},{4,5},{5,4},{6,7},{7,6},{8,9},{9,8},{10,11... | collective-permute-start | bytes 786440 | tf_op jit(solution)/shard_map/ppermute | solution.py:37
  58.3 13.3 %collective-permute-start.17 = (bf16[128,512]{1,0:T(8,128)(2,1)S(1)}, bf16[128,512]{1,0:T(8,128)(2,1)S(1)}, u32[]{:S(2)}, u32[]{:S(2)}) collective-permute-start(bf16[128,512]{1,0:T(8,128)(2,1)S(1)} %add_convert_fusion.11), channel_id=1, source_target_pairs={{0,2},{1,3},{2,0},{3,1},{4,6},{5,7},{6,4},{7,5},{8,10},{9,11},{10,... | collective-permute-start | bytes 393224 | tf_op jit(solution)/shard_map/ppermute | solution.py:37
  68.1 6.8 %collective-permute-start.14 = (bf16[64,1024]{1,0:T(8,128)(2,1)S(1)}, bf16[64,1024]{1,0:T(8,128)(2,1)S(1)}, u32[]{:S(2)}, u32[]{:S(2)}) collective-permute-start(bf16[64,1024]{1,0:T(8,128)(2,1)S(1)} %add_convert_fusion.10), channel_id=1, source_target_pairs={{0,4},{1,5},{2,6},{3,7},{4,0},{5,1},{6,2},{7,3},{8,12},{9,13},{10,... | collective-permute-start | bytes 393224 | tf_op jit(solution)/shard_map/ppermute | solution.py:37
  68.8 3.9 %collective-permute-start.16 = (bf16[128,512]{1,0:T(8,128)(2,1)S(1)}, bf16[128,512]{1,0:T(8,128)(2,1)S(1)}, u32[]{:S(2)}, u32[]{:S(2)}) collective-permute-start(bf16[128,512]{1,0:T(8,128)(2,1)S(1)} %add_convert_fusion.9), channel_id=1, source_target_pairs={{0,1},{1,0},{2,3},{3,2},{4,5},{5,4},{6,7},{7,6},{8,9},{9,8},{10,11... | collective-permute-start | bytes 393224 | tf_op jit(solution)/shard_map/ppermute | solution.py:37
  69.6 12.3 %collective-permute-start.22 = (bf16[64,1024]{1,0:T(8,128)(2,1)S(1)}, bf16[64,1024]{1,0:T(8,128)(2,1)S(1)}, u32[]{:S(2)}, u32[]{:S(2)}) collective-permute-start(bf16[64,1024]{1,0:T(8,128)(2,1)S(1)} %add_convert_fusion.8), channel_id=1, source_target_pairs={{0,4},{1,5},{2,6},{3,7},{4,0},{5,1},{6,2},{7,3},{8,12},{9,13},{10,... | collective-permute-start | bytes 393224 | tf_op jit(solution)/shard_map/ppermute | solution.py:37
  71.6 11.7 %collective-permute-start.21 = (bf16[64,512]{1,0:T(8,128)(2,1)S(1)}, bf16[64,512]{1,0:T(8,128)(2,1)S(1)}, u32[]{:S(2)}, u32[]{:S(2)}) collective-permute-start(bf16[64,512]{1,0:T(8,128)(2,1)S(1)} %add_convert_fusion.13), channel_id=1, source_target_pairs={{0,4},{1,5},{2,6},{3,7},{4,0},{5,1},{6,2},{7,3},{8,12},{9,13},{10,... | collective-permute-start | bytes 196616 | tf_op jit(solution)/shard_map/ppermute | solution.py:37
  72.7 13.9 %collective-permute-start.20 = (bf16[64,512]{1,0:T(8,128)(2,1)S(1)}, bf16[64,512]{1,0:T(8,128)(2,1)S(1)}, u32[]{:S(2)}, u32[]{:S(2)}) collective-permute-start(bf16[64,512]{1,0:T(8,128)(2,1)S(1)} %add_convert_fusion.12), channel_id=1, source_target_pairs={{0,4},{1,5},{2,6},{3,7},{4,0},{5,1},{6,2},{7,3},{8,12},{9,13},{10,... | collective-permute-start | bytes 196616 | tf_op jit(solution)/shard_map/ppermute | solution.py:37
  83.5 6.1 %collective-permute-start.24 = (bf16[64,1024]{1,0:T(8,128)(2,1)S(1)}, bf16[64,1024]{1,0:T(8,128)(2,1)S(1)}, u32[]{:S(2)}, u32[]{:S(2)}) collective-permute-start(bf16[64,1024]{1,0:T(8,128)(2,1)S(1)} %pad_maximum_fusion.1), channel_id=1, source_target_pairs={{0,4},{1,5},{2,6},{3,7},{4,0},{5,1},{6,2},{7,3},{8,12},{9,13},{10,... | collective-permute-start | bytes 393224 | tf_op jit(solution)/shard_map/ppermute | solution.py:37
  86.8 9.8 %collective-permute-start.23 = (bf16[64,1024]{1,0:T(8,128)(2,1)S(1)}, bf16[64,1024]{1,0:T(8,128)(2,1)S(1)}, u32[]{:S(2)}, u32[]{:S(2)}) collective-permute-start(bf16[64,1024]{1,0:T(8,128)(2,1)S(1)} %pad_maximum_fusion.2), channel_id=1, source_target_pairs={{0,4},{1,5},{2,6},{3,7},{4,0},{5,1},{6,2},{7,3},{8,12},{9,13},{10,... | collective-permute-start | bytes 393224 | tf_op jit(solution)/shard_map/ppermute | solution.py:37
  89.5 11.8 %collective-permute-start.26 = (bf16[128,1024]{1,0:T(8,128)(2,1)S(1)}, bf16[128,1024]{1,0:T(8,128)(2,1)S(1)}, u32[]{:S(2)}, u32[]{:S(2)}) collective-permute-start(bf16[128,1024]{1,0:T(8,128)(2,1)S(1)} %constant_dynamic-update-slice_fusion.8), channel_id=1, source_target_pairs={{0,2},{1,3},{2,0},{3,1},{4,6},{5,7},{6,4},{7,5},{8,10},{9,11},{10,... | collective-permute-start | bytes 786440 | tf_op jit(solution)/shard_map/ppermute | solution.py:37
  96.6 5.6 %collective-permute-start.25 = (bf16[128,1024]{1,0:T(8,128)(2,1)S(1)}, bf16[128,1024]{1,0:T(8,128)(2,1)S(1)}, u32[]{:S(2)}, u32[]{:S(2)}) collective-permute-start(bf16[128,1024]{1,0:T(8,128)(2,1)S(1)} %constant_dynamic-update-slice_fusion.10), channel_id=1, source_target_pairs={{0,1},{1,0},{2,3},{3,2},{4,5},{5,4},{6,7},{7,6},{8,9},{9,8},{10,11... | collective-permute-start | bytes 786440 | tf_op jit(solution)/shard_map/ppermute | solution.py:37
  97.7 8.3 %collective-permute-start.28 = (bf16[64,512]{1,0:T(8,128)(2,1)S(1)}, bf16[64,512]{1,0:T(8,128)(2,1)S(1)}, u32[]{:S(2)}, u32[]{:S(2)}) collective-permute-start(bf16[64,512]{1,0:T(8,128)(2,1)S(1)} %get-tuple-element.166), channel_id=1, source_target_pairs={{0,4},{1,5},{2,6},{3,7},{4,0},{5,1},{6,2},{7,3},{8,12},{9,13},{10,... | collective-permute-start | bytes 196616 | tf_op jit(solution)/shard_map/ppermute | solution.py:37
  100.8 5.1 %collective-permute-start.19 = (bf16[64,512]{1,0:T(8,128)(2,1)S(1)}, bf16[64,512]{1,0:T(8,128)(2,1)S(1)}, u32[]{:S(2)}, u32[]{:S(2)}) collective-permute-start(bf16[64,512]{1,0:T(8,128)(2,1)S(1)} %get-tuple-element.164), channel_id=1, source_target_pairs={{0,4},{1,5},{2,6},{3,7},{4,0},{5,1},{6,2},{7,3},{8,12},{9,13},{10,... | collective-permute-start | bytes 196616 | tf_op jit(solution)/shard_map/ppermute | solution.py:37
  101.4 18.3 %collective-permute-start.32 = (bf16[256,1024]{1,0:T(8,128)(2,1)S(1)}, bf16[256,1024]{1,0:T(8,128)(2,1)S(1)}, u32[]{:S(2)}, u32[]{:S(2)}) collective-permute-start(bf16[256,1024]{1,0:T(8,128)(2,1)S(1)} %constant_dynamic-update-slice_fusion.12.refs_2_.refs_0_), channel_id=1, source_target_pairs={{0,1},{1,0},{2,3},{3,2},{4,5},{5,4},{6,7},{7,6},{8,9},{9,8},{10,11... | collective-permute-start | bytes 1572872 | tf_op jit(solution)/shard_map/ppermute | solution.py:37
  102.3 17.4 %collective-permute-start.33 = (bf16[256,1024]{1,0:T(8,128)(2,1)S(1)}, bf16[256,1024]{1,0:T(8,128)(2,1)S(1)}, u32[]{:S(2)}, u32[]{:S(2)}) collective-permute-start(bf16[256,1024]{1,0:T(8,128)(2,1)S(1)} %constant_dynamic-update-slice_fusion.14.refs_4_.refs_2_), channel_id=1, source_target_pairs={{0,2},{1,3},{2,0},{3,1},{4,6},{5,7},{6,4},{7,5},{8,10},{9,11},{10,... | collective-permute-start | bytes 1572872 | tf_op jit(solution)/shard_map/ppermute | solution.py:37
  105.9 10.4 %collective-permute-start.27 = (bf16[128,512]{1,0:T(8,128)(2,1)S(1)}, bf16[128,512]{1,0:T(8,128)(2,1)S(1)}, u32[]{:S(2)}, u32[]{:S(2)}) collective-permute-start(bf16[128,512]{1,0:T(8,128)(2,1)S(1)} %constant_dynamic-update-slice_fusion.16), channel_id=1, source_target_pairs={{0,2},{1,3},{2,0},{3,1},{4,6},{5,7},{6,4},{7,5},{8,10},{9,11},{10,... | collective-permute-start | bytes 393224 | tf_op jit(solution)/shard_map/ppermute | solution.py:37
  106.0 10.3 %collective-permute-start.30 = (bf16[128,512]{1,0:T(8,128)(2,1)S(1)}, bf16[128,512]{1,0:T(8,128)(2,1)S(1)}, u32[]{:S(2)}, u32[]{:S(2)}) collective-permute-start(bf16[128,512]{1,0:T(8,128)(2,1)S(1)} %constant_dynamic-update-slice_fusion.18), channel_id=1, source_target_pairs={{0,1},{1,0},{2,3},{3,2},{4,5},{5,4},{6,7},{7,6},{8,9},{9,8},{10,11... | collective-permute-start | bytes 393224 | tf_op jit(solution)/shard_map/ppermute | solution.py:37
  116.3 17.3 %copy-start.1 = (bf16[1024,512]{1,0:T(8,128)(2,1)S(1)}, bf16[1024,512]{1,0:T(8,128)(2,1)}, u32[]{:S(2)}) copy-start(bf16[1024,512]{1,0:T(8,128)(2,1)} %copy-done) | copy-start | bytes 3145732
  116.3 21.1 %collective-permute-start.31 = (bf16[256,512]{1,0:T(8,128)(2,1)S(1)}, bf16[256,512]{1,0:T(8,128)(2,1)S(1)}, u32[]{:S(2)}, u32[]{:S(2)}) collective-permute-start(bf16[256,512]{1,0:T(8,128)(2,1)S(1)} %constant_dynamic-update-slice_fusion.22.refs_3_.refs_2_), channel_id=1, source_target_pairs={{0,2},{1,3},{2,0},{3,1},{4,6},{5,7},{6,4},{7,5},{8,10},{9,11},{10,... | collective-permute-start | bytes 786440 | tf_op jit(solution)/shard_map/ppermute | solution.py:37
  118.1 19.3 %collective-permute-start.29 = (bf16[256,512]{1,0:T(8,128)(2,1)S(1)}, bf16[256,512]{1,0:T(8,128)(2,1)S(1)}, u32[]{:S(2)}, u32[]{:S(2)}) collective-permute-start(bf16[256,512]{1,0:T(8,128)(2,1)S(1)} %constant_dynamic-update-slice_fusion.20.refs_1_.refs_0_), channel_id=1, source_target_pairs={{0,1},{1,0},{2,3},{3,2},{4,5},{5,4},{6,7},{7,6},{8,9},{9,8},{10,11... | collective-permute-start | bytes 786440 | tf_op jit(solution)/shard_map/ppermute | solution.py:37
  127.5 14.8 %collective-permute-start.35 = (bf16[512,448]{1,0:T(8,128)(2,1)S(1)}, bf16[512,448]{1,0:T(8,128)(2,1)S(1)}, u32[]{:S(2)}, u32[]{:S(2)}) collective-permute-start(bf16[512,448]{1,0:T(8,128)(2,1)S(1)} %get-tuple-element.176), channel_id=1, source_target_pairs={{0,8},{1,9},{2,10},{3,11},{4,12},{5,13},{6,14},{7,15},{8,0},{9,1},... | collective-permute-start | bytes 1376264 | tf_op jit(solution)/shard_map/ppermute | solution.py:37
  142.2 2.0 %collective-permute-start.34 = (bf16[512,448]{1,0:T(8,128)(2,1)S(1)}, bf16[512,448]{1,0:T(8,128)(2,1)S(1)}, u32[]{:S(2)}, u32[]{:S(2)}) collective-permute-start(bf16[512,448]{1,0:T(8,128)(2,1)S(1)} %get-tuple-element.183), channel_id=1, source_target_pairs={{0,8},{1,9},{2,10},{3,11},{4,12},{5,13},{6,14},{7,15},{8,0},{9,1},... | collective-permute-start | bytes 1376264 | tf_op jit(solution)/shard_map/ppermute | solution.py:37
  142.4 7.8 %collective-permute-start.37 = (bf16[256,448]{1,0:T(8,128)(2,1)S(1)}, bf16[256,448]{1,0:T(8,128)(2,1)S(1)}, u32[]{:S(2)}, u32[]{:S(2)}) collective-permute-start(bf16[256,448]{1,0:T(8,128)(2,1)S(1)} %add_convert_fusion.1), channel_id=1, source_target_pairs={{0,16},{1,17},{2,18},{3,19},{4,20},{5,21},{6,22},{7,23},{8,24},{9,... | collective-permute-start | bytes 688136 | tf_op jit(solution)/shard_map/ppermute | solution.py:37
  144.2 13.8 %collective-permute-start.36 = (bf16[256,448]{1,0:T(8,128)(2,1)S(1)}, bf16[256,448]{1,0:T(8,128)(2,1)S(1)}, u32[]{:S(2)}, u32[]{:S(2)}) collective-permute-start(bf16[256,448]{1,0:T(8,128)(2,1)S(1)} %add_convert_fusion), channel_id=1, source_target_pairs={{0,16},{1,17},{2,18},{3,19},{4,20},{5,21},{6,22},{7,23},{8,24},{9,... | collective-permute-start | bytes 688136 | tf_op jit(solution)/shard_map/ppermute | solution.py:37
  150.9 16.3 %collective-permute-start.40 = (bf16[128,448]{1,0:T(8,128)(2,1)}, bf16[128,448]{1,0:T(8,128)(2,1)S(1)}, u32[]{:S(2)}, u32[]{:S(2)}) collective-permute-start(bf16[128,448]{1,0:T(8,128)(2,1)} %get-tuple-element.199), channel_id=1, source_target_pairs={{0,0},{1,1},{8,2},{9,3},{16,4},{17,5},{24,6},{25,7},{2,8},{3,9},{1... | collective-permute-start | bytes 344072 | tf_op jit(solution)/shard_map/ppermute | solution.py:144
  157.9 9.3 %collective-permute-start.41 = (bf16[128,448]{1,0:T(8,128)(2,1)S(1)}, bf16[128,448]{1,0:T(8,128)(2,1)S(1)}, u32[]{:S(2)}, u32[]{:S(2)}) collective-permute-start(bf16[128,448]{1,0:T(8,128)(2,1)S(1)} %get-tuple-element.200), channel_id=1, source_target_pairs={{17,0},{16,1},{25,2},{24,3},{1,4},{0,5},{9,6},{8,7},{19,8},{18,9},... | collective-permute-start | bytes 344072 | tf_op jit(solution)/shard_map/ppermute | solution.py:144
  158.8 10.6 %collective-permute-start.38 = (bf16[128,448]{1,0:T(8,128)(2,1)}, bf16[128,448]{1,0:T(8,128)(2,1)}, u32[]{:S(2)}, u32[]{:S(2)}) collective-permute-start(bf16[128,448]{1,0:T(8,128)(2,1)} %get-tuple-element.202), channel_id=1, source_target_pairs={{0,0},{1,1},{8,2},{9,3},{16,4},{17,5},{24,6},{25,7},{2,8},{3,9},{1... | collective-permute-start | bytes 344072 | tf_op jit(solution)/shard_map/ppermute | solution.py:144
  162.7 9.0 %collective-permute-start.39 = (bf16[128,448]{1,0:T(8,128)(2,1)}, bf16[128,448]{1,0:T(8,128)(2,1)}, u32[]{:S(2)}, u32[]{:S(2)}) collective-permute-start(bf16[128,448]{1,0:T(8,128)(2,1)} %get-tuple-element.201), channel_id=1, source_target_pairs={{17,0},{16,1},{25,2},{24,3},{1,4},{0,5},{9,6},{8,7},{19,8},{18,9},... | collective-permute-start | bytes 344072 | tf_op jit(solution)/shard_map/ppermute | solution.py:144
  163.4 10.1 %copy-start.6 = (f32[128,1]{0,1:T(1,128)S(1)}, f32[128,1]{0,1:T(1,128)}, u32[]{:S(2)}) copy-start(f32[128,1]{0,1:T(1,128)} %param.10) | copy-start | bytes 1540

commit v5 on v4

--- a/solution.py
+++ b/solution.py
@@ -11,7 +11,7 @@
 BF16 = jnp.bfloat16
 VMEM = pl.BlockSpec(memory_space=pltpu.VMEM)
 SMEM = pl.BlockSpec(memory_space=pltpu.SMEM)
-PARAMS = pltpu.CompilerParams(vmem_limit_bytes=50 * 1024 * 1024)
+ROOM = 24
 PARTS = 2
 
 
@@ -182,6 +182,19 @@
     own_ref[:, stored:] = tail
     other_ref[:, :stored] = jnp.where(y == 0, second, first)
     other_ref[:, stored:] = tail
+
+
+def join_body(mine_ref, other_ref, *refs):
+    out_ref = refs[-1]
+    y = lax.axis_index("ep") % 2
+    mine, other = mine_ref[...], other_ref[...]
+    n = mine.shape[1]
+    halves = jnp.where(y == 0, mine, other), jnp.where(y == 0, other, mine)
+    if len(refs) > 1:
+        weight = upright(refs[0][...])
+        halves = [half(f32(a) * weight) for a in halves]
+    out_ref[:, :n] = halves[0]
+    out_ref[:, n:] = halves[1]
 
 
 def order_rows(geo, held_ref, got_ref, rows_ref):
@@ -218,32 +231,31 @@
     return id_ref[rows, :][:, stored % 128 : stored % 128 + 1]
 
 
-def first_body(geo, stored, count, n_w, own_ids, held_ref, got_ref, *refs):
+def first_body(geo, stored, count, n_w, own_ids, part, places, held_ref, got_ref, *refs):
     rows_ref = refs[-1]
     order_rows(geo, held_ref, got_ref, rows_ref)
     n = rows_ref.shape[0] // PARTS
-    rows = rows_ref[:n, :]
+    at = slice(part * n, (part + 1) * n)
+    rows = rows_ref[at, :]
     if own_ids:
         expert = rows[:, stored : stored + 1]
         refs = refs[:-1]
     else:
-        expert = id_of(refs[0], stored, slice(0, n))
+        expert = id_of(refs[0], stored, at)
         refs = refs[1:-1]
-    products(rows[:, :stored], expert, count, n_w, refs)
+    products(rows[:, :stored], expert, count, n_w, refs, places)
 
 
 def products(rows, expert, count, n_w, refs, places=None):
-    keep_ref, send_ref = refs[-2:]
     n = rows.shape[0] // 2
-    hidden = keep_ref.shape[1] // n_w
     places = places or (0, 1)
     size = rows.shape[0] // len(places)
     for i in range(n_w):
+        keep_ref, send_ref = refs[n_w + 2 * i : n_w + 2 * i + 2]
         result = half(expert_dot(rows, expert, refs[i], count, False))
-        cols = slice(i * hidden, (i + 1) * hidden)
         for block, place in enumerate(places):
             out_ref, at = (keep_ref, place * size) if place * size < n else (send_ref, place * size - n)
-            out_ref[at : at + size, cols] = result[block * size : (block + 1) * size]
+            out_ref[at : at + size, :] = result[block * size : (block + 1) * size]
 
 
 def later_body(stored, count, n_w, places, id_ref, rows_ref, *refs):
@@ -275,10 +287,8 @@
             at = (part * 2 + side) * n * sub
             expert = id_of(id_ref, stored, slice(at, at + n * sub))
             total = None
-            for weight, pair, col, source in terms:
-                hidden = refs[weight].shape[2]
-                cols = slice(col * hidden, (col + 1) * hidden)
-                rows = in_order(refs[pair][:, cols], refs[pair + 1][:, cols], source, order)[side]
+            for weight, pair, source in terms:
+                rows = in_order(refs[pair][...], refs[pair + 1][...], source, order)[side]
                 now = expert_dot(rows, expert, refs[weight], count, True)
                 total = now if total is None else total + now
             total = half(total)
@@ -299,12 +309,12 @@
                     send_ref[to, :] = block
 
 
-def grad_body(stored, cols, sources, order, id_ref, rows_ref, *refs):
+def grad_body(stored, sources, order, id_ref, rows_ref, *refs):
     out_ref = refs[-1]
     expert = half(pl.program_id(0).astype(jnp.float32))
     right = []
     for part, source in enumerate(sources):
-        right += in_order(refs[2 * part][:, cols], refs[2 * part + 1][:, cols], source, order)
+        right += in_order(refs[2 * part][...], refs[2 * part + 1][...], source, order)
     right = jnp.concatenate(right)
     right = jnp.where(id_of(id_ref, stored, slice(None)) == expert, right, jnp.zeros((), BF16))
     out_ref[0] = half(
@@ -341,8 +351,8 @@
             out_shape=out_shape,
             grid=kw.get("grid", (1,)),
             in_specs=in_specs or [full(a.shape) for a in args],
-            out_specs=kw.get("out_specs") or [full(o.shape) for o in out_shape],
-            compiler_params=PARAMS,
+            out_specs=kw.get("out_specs") or jax.tree.map(lambda o: full(o.shape), out_shape),
+            compiler_params=pltpu.CompilerParams(vmem_limit_bytes=kw.get("room", ROOM) << 20),
             cost_estimate=pl.CostEstimate(flops=1, bytes_accessed=1, transcendentals=0),
             name=name,
         )(*args)
@@ -353,6 +363,7 @@
         (hot_experts, routes.reshape(1, tok), tokens),
         in_specs=[SMEM, full((1, tok)), full(tokens.shape)],
         name="token_pieces",
+        room=60,
     )
     line = Line()
     bit_swaps = [functools.partial(swap, grp_bits=0, ep_bits=1 << bit) for bit in bits]
@@ -365,12 +376,10 @@
 
     def land(pieces):
         stay, got = line.begin(*pieces)
-        near = jnp.where(apart == 0, stay, got)
-        far = line.end(jnp.where(apart == 0, got, stay))
-        return [
-            lax.ppermute(near, AXES, column_pairs(0)),
-            lax.ppermute(far, AXES, column_pairs(1)),
-        ]
+        far = jnp.where(apart == 0, got, stay)
+        near = line.end(jnp.where(apart == 0, stay, got))
+        far = lax.ppermute(far, AXES, column_pairs(1))
+        return [lax.ppermute(near, AXES, column_pairs(0)), far]
 
     def joined_up(pieces):
         return line.end(jnp.concatenate(line.begin(*pieces)))
@@ -380,6 +389,7 @@
         piece,
         (route_weights.reshape(1, tok), cotangent),
         name="cotangent_pieces",
+        room=60,
     )
     x_pieces, dz_pieces = hop(x_pieces), hop(dz_pieces)
     x_landed = land(x_pieces)
@@ -406,7 +416,7 @@
         return pl.BlockSpec((rows, 128), lambda *_: (at, stored // 128))
 
     def split(n_w):
-        return [jax.ShapeDtypeStruct((n // 2, n_w * hidden), BF16)] * 2
+        return [jax.ShapeDtypeStruct((n // 2, hidden), BF16)] * (2 * n_w)
 
     def later(part, rows, weights, name, places=None):
         return call(
@@ -421,78 +431,101 @@
             name=name,
         )
 
+    turned_bits = [bits[1], bits[0]] + bits[2:]
+    turned_order = block_order(turned_bits)
+    turned_swaps = [bit_swaps[1], bit_swaps[0]] + bit_swaps[2:]
+    places = [turned_order.index(j) for j in order]
     x_held, x_got = line.begin(x_held, x_got)
-    gu_keep, gu_send, x_rows = call(
-        functools.partial(first_body, geo, stored, count, 2, True),
+    keep_g, send_g, keep_u, send_u, x_rows = call(
+        functools.partial(first_body, geo, stored, count, 2, True, 1, places),
         split(2) + [rows_shape],
         (x_held, x_got, w_gate, w_up),
         name="gate_up_first",
     )
-    line.end(gu_send)
-    gu = [Sum(line, gu_keep, gu_send, bit_swaps)]
-    turned_bits = [bits[1], bits[0]] + bits[2:]
-    turned_order = block_order(turned_bits)
-    turned_swaps = [bit_swaps[1], bit_swaps[0]] + bit_swaps[2:]
-    places = [turned_order.index(j) for j in order]
+    line.end(send_g)
+    gate_1 = Sum(line, keep_g, send_g, turned_swaps)
+    up_1 = Sum(line, keep_u, send_u, turned_swaps)
+    (rows,) = line.begin(x_rows)
+    keep_g, send_g, keep_u, send_u = later(0, rows, (w_gate, w_up), "gate_up_later")
+    line.end(send_g)
+    gate_0 = Sum(line, keep_g, send_g, bit_swaps)
+    up_0 = Sum(line, keep_u, send_u, bit_swaps)
     dz_held = doubled(dz_held, dz_next)
     dz_got = swap(dz_held, 1, 0)
-    (rows,) = line.begin(x_rows)
-    keep, send = later(1, rows, (w_gate, w_up), "gate_up_later", places)
-    line.end(send)
-    gu.append(Sum(line, keep, send, turned_swaps))
+    gate_1.fold()
     dz_held, dz_got = line.begin(dz_held, dz_got)
-    ag_keep, ag_send, dz_rows = call(
-        functools.partial(first_body, geo, stored, count, 1, False),
+    keep, send, dz_rows = call(
+        functools.partial(first_body, geo, stored, count, 1, False, 1, places),
         split(1) + [rows_shape],
         (dz_held, dz_got, x_rows, w_down),
         in_specs=[full(dz_held.shape), full(dz_got.shape), id_spec(total, 0), full(w_down.shape)],
         name="act_grad_first",
     )
+    line.end(send)
+    ag_1 = Sum(line, keep, send, turned_swaps)
+    (rows,) = line.begin(dz_rows)
+    ag_keep, ag_send = later(0, rows, (w_down,), "act_grad_later")
     line.end(ag_send)
-    ag = [Sum(line, ag_keep, ag_send, bit_swaps)]
-    (rows,) = line.begin(dz_rows)
-    keep, send = later(1, rows, (w_down,), "act_grad_later", places)
-    line.end(send)
-    ag.append(Sum(line, keep, send, turned_swaps))
-    acts, grads = [None] * PARTS, [None] * PARTS
+
+    rounds = len(bits) - 1
+
+    def rest(one):
+        for _ in range(1, rounds):
+            one.fold()
+
+    gate_0.fold()
+    up_1.fold()
+    ag_0 = Sum(line, ag_keep, *line.begin(ag_send), bit_swaps)
+    up_0.fold()
+    rest(gate_1)
+    ag_1.fold()
+    rest(gate_0)
+    rest(up_1)
+    gate_1.finish()
+    ag_0.fold()
+    rest(up_0)
+    gate_0.finish()
+    rest(ag_1)
+    up_1.finish()
+    rest(ag_0)
+    up_0.finish()
+    gate, up, ag = (gate_0, gate_1), (up_0, up_1), (ag_0, ag_1)
+    acts, gate_grads, up_grads = [None] * PARTS, [None] * PARTS, [None] * PARTS
     sources = [order, turned_order]
     back_swaps = [bit_swaps[::-1], turned_swaps[::-1]]
 
-    def middle(part):
-        ag[part].finish()
-        gate_up, act_grad = gu[part].total, ag[part].total
-        gate_pre, up_pre = gate_up[:, :hidden], gate_up[:, hidden:]
+    def start_act(part):
+        gate_pre, up_pre = gate[part].total, up[part].total
+        act = line.end(half(gate_pre * jax.nn.sigmoid(gate_pre) * up_pre))
+        acts[part] = Gather(line, act, back_swaps[part])
+
+    def start_grads(part):
+        gate_pre, up_pre, act_grad = gate[part].total, up[part].total, ag[part].total
         sg = jax.nn.sigmoid(gate_pre)
-        act = half(gate_pre * sg * up_pre)
-        gate_grad = act_grad * up_pre * sg * (1.0 + gate_pre * (1.0 - sg))
-        up_grad = act_grad * gate_pre * sg
-        both = half(jnp.concatenate([gate_grad, up_grad], axis=1))
-        line.end(both)
-        acts[part] = Gather(line, act, back_swaps[part])
-        grads[part] = Gather(line, both, back_swaps[part])
-
-    rounds = len(bits) - 1
-
-    def both(step, pair):
-        for one in pair:
-            step(one)
-
-    both(Sum.fold, gu)
-    ag[0].fold()
+        gate_grad = half(act_grad * up_pre * sg * (1.0 + gate_pre * (1.0 - sg)))
+        up_grad = half(act_grad * gate_pre * sg)
+        line.end(gate_grad)
+        gate_grads[part] = Gather(line, gate_grad, back_swaps[part])
+        up_grads[part] = Gather(line, up_grad, back_swaps[part])
+
+    start_act(1)
+    start_act(0)
+    ag_1.finish()
+    start_grads(1)
+    ag_0.finish()
+    start_grads(0)
+
+    def grow(pair):
+        pair[1].grow()
+        pair[0].grow()
+
+    grow(acts)
+    grow(gate_grads)
     for _ in range(1, rounds):
-        gu[0].fold()
-        ag[1].fold()
-        gu[1].fold()
-        ag[0].fold()
-    ag[1].fold()
-    both(Sum.finish, gu)
-    middle(0)
-    middle(1)
-    both(Gather.grow, grads)
+        grow(acts)
+    grow(up_grads)
     for _ in range(1, rounds):
-        both(Gather.grow, grads)
-        both(Gather.grow, acts)
-    both(Gather.grow, acts)
+        grow(gate_grads)
 
     def back(ids, weights, pairs, jobs, name):
         args = tuple(weights) + tuple(pairs)
@@ -504,10 +537,9 @@
             name=name,
         )
 
-    def grad(rows, gathered, at, sources, name):
-        cols = slice(at * hidden, (at + 1) * hidden)
+    def grad(rows, gathered, name):
         return call(
-            functools.partial(grad_body, stored, cols, sources, order),
+            functools.partial(grad_body, stored, sources, order),
             jax.ShapeDtypeStruct((count, stored, hidden), BF16),
             (x_rows, rows) + tuple(gathered),
             in_specs=[id_spec(total, 0)] + [full(a.shape) for a in (rows,) + tuple(gathered)],
@@ -516,37 +548,39 @@
             name=name,
         )
 
-    def joined(mine, other):
-        return jnp.concatenate(
-            [jnp.where(y == 0, mine, other), jnp.where(y == 0, other, mine)], axis=1
-        )
+    def joined(pieces, weights, name):
+        args = tuple(pieces) + weights
+        return call(join_body, jax.ShapeDtypeStruct(tokens.shape, BF16), args, name=name)
 
     act_pairs = acts[0].result() + acts[1].result()
-    grad_pairs = grads[0].result() + grads[1].result()
-
-    jobs = [(i, ((0, 2 + 2 * i, 0, s), (1, 2 + 2 * i, 1, s))) for i, s in enumerate(sources)]
-    keep, send = back(x_rows, (w_gate, w_up), line.begin(*grad_pairs), jobs, "token_rows")
-    line.end(send)
-    token = Return(line, keep, send)
-    (rows,) = line.begin(x_rows)
-    grad_gate = line.end(grad(rows, grad_pairs, 0, sources, "grad_gate"))
-    jobs = [(i, ((0, 1 + 2 * i, 0, s),)) for i, s in enumerate(sources)]
+    jobs = [(i, ((0, 1 + 2 * i, s),)) for i, s in enumerate(sources)]
     keep, send = back(x_rows, (w_down,), line.begin(*act_pairs), jobs, "out_rows")
     line.end(send)
     out = Return(line, keep, send)
-    token.fold()
-    out.fold()
-    for _ in range(1, out.rounds):
-        both(Return.fold, (token, out))
+    for _ in range(1, rounds):
+        grow(up_grads)
+    gate_pairs = gate_grads[0].result() + gate_grads[1].result()
+    gate_pairs = line.begin(*gate_pairs)
+    grad_gate = line.end(grad(x_rows, gate_pairs, "grad_gate"))
+    for _ in range(out.rounds):
+        out.fold()
+    up_pairs = up_grads[0].result() + up_grads[1].result()
+    pairs = line.begin(*up_pairs)
+    jobs = [(i, ((0, 2 + 2 * i, s), (1, 6 + 2 * i, s))) for i, s in enumerate(sources)]
+    keep, send = back(x_rows, (w_gate, w_up), gate_pairs + pairs, jobs, "token_rows")
+    line.end(send)
+    token = Return(line, keep, send)
+    for _ in range(token.rounds):
+        token.fold()
+    out.leave()
+    (rows,) = line.begin(dz_rows)
+    grad_down = line.end(grad(rows, act_pairs, "grad_down"))
+    token.leave()
     (rows,) = line.begin(x_rows)
-    grad_up = line.end(grad(rows, grad_pairs, 1, sources, "grad_up"))
-    both(Return.leave, (token, out))
-    (rows,) = line.begin(dz_rows)
-    grad_down = line.end(grad(rows, act_pairs, 0, sources, "grad_down"))
-    token.pieces = line.begin(*token.pieces)
-    grad_tokens = joined(*token.pieces)
-    out.pieces = line.begin(*out.pieces)
-    layer_output = half(f32(joined(*out.pieces)) * route_weights)
+    grad_up = line.end(grad(rows, pairs, "grad_up"))
+    weights = (route_weights.reshape(1, tok),)
+    layer_output = line.end(joined(line.begin(*out.pieces), weights, "join_output"))
+    grad_tokens = line.end(joined(line.begin(*token.pieces), (), "join_tokens"))
     return (layer_output, grad_tokens, grad_gate, grad_up, jnp.swapaxes(grad_down, 1, 2))
 
 

time: 176 us -> 161 us (0.915)
  waiting for transfers between devices: 57.2 us -> 43.9 us
  starting transfers between devices: 67.7 us -> 76 us
  Pallas kernels: 38.9 us -> 33.4 us
  local copies, waits for them, and re-layouts: 4.28 us -> 0.46 us
  other arithmetic: 5.08 us -> 3 us
    ppermute x34 -> x46, starting transfers between devices: 45.8 us -> 55.4 us  [swap(): return lax.ppermute(block, AXES, pairs)]
    ppermute x34 -> x46, waiting for transfers between devices: 45.8 us -> 39 us  [swap(): return lax.ppermute(block, AXES, pairs)]
    pallas_call x11 -> x13, Pallas kernels: 38.9 us -> 33.4 us  [call(): pl.pallas_call(body, out_shape=out_shape, grid=kw.get('grid', (1,)), in_s...]
    ppermute x4, waiting for transfers between devices: 6.92 us -> 2.36 us  [the longest x2 1.85 us: land(): return [lax.ppermute(near, AXES, column_pairs(0)), far]]
    unnamed x30 -> x24, local copies, waits for them, and re-layouts: 4 us -> 0.17 us
    ppermute x4, starting transfers between devices: 11.7 us -> 9.48 us  [leave(): self.pieces.append(lax.ppermute(piece, AXES, back))]
    ppermute x4, waiting for transfers between devices: 4.49 us -> 2.62 us  [leave(): self.pieces.append(lax.ppermute(piece, AXES, back))]
    convert_element_type x13 -> x20, other arithmetic: 2.85 us -> 1.08 us  [half(): return a.astype(BF16)]
  transfers between devices with their start and end apart: 42 -> 54, of which waited for: 22 -> 23; matrix products, arithmetic and copies ran while one was open for 2% -> 2% of each run, Pallas kernels for 22% -> 16%
where the time goes in v5:
time: 161 us; the launch traced here: 158 us
  starting transfers between devices  76 us (47%)
  waiting for transfers between devices  43.9 us (27%)
  Pallas kernels  33.4 us (21%)
  other arithmetic  3 us (2%)
    ppermute x46, starting transfers between devices, swap(): return lax.ppermute(block, AXES, pairs)  55.4 us
    ppermute x46, waiting for transfers between devices, swap(): return lax.ppermute(block, AXES, pairs)  39 us
    pallas_call x13, Pallas kernels, call(): pl.pallas_call(body, out_shape=out_shape, grid=kw.get('grid', (1,)), in_s...  33.4 us
    ppermute x4, starting transfers between devices, leave(): self.pieces.append(lax.ppermute(piece, AXES, back))  9.48 us
    ppermute x2, starting transfers between devices, land(): return [lax.ppermute(near, AXES, column_pairs(0)), far]  5.8 us
    ppermute x2, starting transfers between devices, land(): far = lax.ppermute(far, AXES, column_pairs(1))  5.28 us
  transfers between devices with their start and end apart: 54, of which 23 were waited for; matrix products, arithmetic and copies ran while one was open for 2% of the time, Pallas kernels for 16%

profile of v5, /device:TPU:17, one launch (start us, length us, event | category | flops | bytes accessed | tf_op | source)
XLA Modules:
  0.0 158.0 jit_solution(19214034962307648)
XLA Ops:
  0.6 2.0 %token_pieces.1 = (bf16[128,512]{1,0:T(8,128)(2,1)}, bf16[128,512]{1,0:T(8,128)(2,1)}) custom-call(s32[4]{0:T(128)} %hot_ref.1, s32[1,128]{1,0:T(1,128)} %bitcast.10, bf16[128,896]{1,0:T(8,128)(2,1)} %tokens_ref.1), custom_call_target="tpu_custom_call" | custom-call | flops 1 | bytes 1 | tf_op jit(solution)/shard_map/token_pieces/pallas_call | solution.py:349
  2.6 1.2 collective-permute-start
  3.8 1.9 %cotangent_pieces.1 = (bf16[128,512]{1,0:T(8,128)(2,1)}, bf16[128,512]{1,0:T(8,128)(2,1)}) custom-call(f32[1,128]{1,0:T(1,128)} %bitcast.7, bf16[128,896]{1,0:T(8,128)(2,1)} %rows_ref.1), custom_call_target="tpu_custom_call" | custom-call | flops 1 | bytes 1 | tf_op jit(solution)/shard_map/cotangent_pieces/pallas_call | solution.py:349
  6.0 1.2 collective-permute-done
  7.2 0.9 broadcast_select_fusion.2
  8.1 2.6 %collective-permute-start.2 = (bf16[128,512]{1,0:T(8,128)(2,1)S(1)}, bf16[128,512]{1,0:T(8,128)(2,1)S(1)}, u32[]{:S(2)}, u32[]{:S(2)}) collective-permute-start(bf16[128,512]{1,0:T(8,128)(2,1)S(1)} %get-tuple-element.267), channel_id=1, source_target_pairs={{0,4},{1,5},{2,12},{3,13},{4,1},{5,0},{6,9},{7,8},{8,6},{9,7},{10,... | collective-permute-start | bytes 393224 | tf_op jit(solution)/shard_map/ppermute | solution.py:381
  10.7 3.0 %collective-permute-start.1 = (bf16[128,512]{1,0:T(8,128)(2,1)S(1)}, bf16[128,512]{1,0:T(8,128)(2,1)S(1)}, u32[]{:S(2)}, u32[]{:S(2)}) collective-permute-start(bf16[128,512]{1,0:T(8,128)(2,1)S(1)} %get-tuple-element.268), channel_id=1, source_target_pairs={{0,0},{1,1},{2,8},{3,9},{4,5},{5,4},{6,13},{7,12},{8,2},{9,3},{10,... | collective-permute-start | bytes 393224 | tf_op jit(solution)/shard_map/ppermute | solution.py:382
  13.8 0.9 broadcast_select_fusion
  14.7 2.7 %collective-permute-start.6 = (bf16[128,512]{1,0:T(8,128)(2,1)S(1)}, bf16[128,512]{1,0:T(8,128)(2,1)S(1)}, u32[]{:S(2)}, u32[]{:S(2)}) collective-permute-start(bf16[128,512]{1,0:T(8,128)(2,1)S(1)} %get-tuple-element.265), channel_id=1, source_target_pairs={{0,4},{1,5},{2,12},{3,13},{4,1},{5,0},{6,9},{7,8},{8,6},{9,7},{10,... | collective-permute-start | bytes 393224 | tf_op jit(solution)/shard_map/ppermute | solution.py:381
  17.4 2.8 %collective-permute-start.5 = (bf16[128,512]{1,0:T(8,128)(2,1)S(1)}, bf16[128,512]{1,0:T(8,128)(2,1)S(1)}, u32[]{:S(2)}, u32[]{:S(2)}) collective-permute-start(bf16[128,512]{1,0:T(8,128)(2,1)S(1)} %get-tuple-element.266), channel_id=1, source_target_pairs={{0,0},{1,1},{2,8},{3,9},{4,5},{5,4},{6,13},{7,12},{8,2},{9,3},{10,... | collective-permute-start | bytes 393224 | tf_op jit(solution)/shard_map/ppermute | solution.py:382
  20.2 2.0 %collective-permute-start.4 = (bf16[256,512]{1,0:T(8,128)(2,1)S(1)}, bf16[256,512]{1,0:T(8,128)(2,1)S(1)}, u32[]{:S(2)}, u32[]{:S(2)}) collective-permute-start(bf16[256,512]{1,0:T(8,128)(2,1)S(1)} %constant_dynamic-update-slice_fusion), channel_id=1, source_target_pairs={{0,16},{1,17},{2,18},{3,19},{4,20},{5,21},{6,22},{7,23},{8,24},{9,... | collective-permute-start | bytes 786440 | tf_op jit(solution)/shard_map/ppermute | solution.py:37
  22.7 1.9 %collective-permute-done.5 = bf16[128,512]{1,0:T(8,128)(2,1)S(1)} collective-permute-done((bf16[128,512]{1,0:T(8,128)(2,1)S(1)}, bf16[128,512]{1,0:T(8,128)(2,1)S(1)}, u32[]{:S(2)}, u32[]{:S(2)}) %collective-permute-start.5) | collective-permute-done | bytes 131104 | tf_op jit(solution)/shard_map/ppermute | solution.py:382
  24.6 3.2 %collective-permute-done.4 = bf16[256,512]{1,0:T(8,128)(2,1)S(1)} collective-permute-done((bf16[256,512]{1,0:T(8,128)(2,1)S(1)}, bf16[256,512]{1,0:T(8,128)(2,1)S(1)}, u32[]{:S(2)}, u32[]{:S(2)}) %collective-permute-start.4) | collective-permute-done | bytes 262176 | tf_op jit(solution)/shard_map/ppermute | solution.py:37
  28.4 1.5 collective-permute-done.7.got_ref
  29.9 2.5 %gate_up_first.1 = (bf16[256,512]{1,0:T(8,128)(2,1)S(1)}, bf16[256,512]{1,0:T(8,128)(2,1)S(1)}, bf16[256,512]{1,0:T(8,128)(2,1)S(1)}, bf16[256,512]{1,0:T(8,128)(2,1)S(1)}, bf16[1024,512]{1,0:T(8,128)(2,1)S(1)}) custom-call(bf16[512,512]{1,0:T(8,128)(2,1)S(1)} %constant_dynamic-update-slice_fusion.4.held_ref, ...), custom_call_target="tpu_custom_call" | custom-call | flops 1 | bytes 1 | tf_op jit(solution)/shard_map/gate_up_first/pallas_call | solution.py:349
  32.4 2.3 %gate_up_later.1 = (bf16[256,512]{1,0:T(8,128)(2,1)S(1)}, bf16[256,512]{1,0:T(8,128)(2,1)S(1)}, bf16[256,512]{1,0:T(8,128)(2,1)S(1)}, bf16[256,512]{1,0:T(8,128)(2,1)S(1)}) custom-call(bf16[1024,512]{1,0:T(8,128)(2,1)S(1)} %get-tuple-element.250.id_ref.rows_ref.refs_0_, bf16[1024,512]{1,0:T(8,128)(2,1)S(1)} %get-tuple-element.250.id_ref.rows_ref.refs_0_, ...), custom_call_target="tpu_custom_call" | custom-call | flops 1 | bytes 1 | tf_op jit(solution)/shard_map/gate_up_later/pallas_call | solution.py:349
  35.6 1.3 collective-permute-start.10
  37.0 1.2 collective-permute-start.8
  38.5 1.4 collective-permute-start.15
  39.8 4.9 %collective-permute-done.11 = bf16[256,512]{1,0:T(8,128)(2,1)S(1)} collective-permute-done((bf16[256,512]{1,0:T(8,128)(2,1)S(1)}, bf16[256,512]{1,0:T(8,128)(2,1)S(1)}, u32[]{:S(2)}, u32[]{:S(2)}) %collective-permute-start.11) | collective-permute-done | bytes 262176 | tf_op jit(solution)/shard_map/ppermute | solution.py:37
  45.0 1.4 act_grad_first.1
  46.4 1.3 collective-permute-start.13
  47.7 1.3 act_grad_later.1
  49.4 1.0 collective-permute-done.16
  51.0 1.0 collective-permute-start.18
  52.0 1.0 collective-permute-done.14
  53.0 2.7 %collective-permute-start.20 = (bf16[64,512]{1,0:T(8,128)(2,1)S(1)}, bf16[64,512]{1,0:T(8,128)(2,1)S(1)}, u32[]{:S(2)}, u32[]{:S(2)}) collective-permute-start(bf16[64,512]{1,0:T(8,128)(2,1)S(1)} %add_convert_fusion.17), channel_id=1, source_target_pairs={{0,4},{1,5},{2,6},{3,7},{4,0},{5,1},{6,2},{7,3},{8,12},{9,13},{10,... | collective-permute-start | bytes 196616 | tf_op jit(solution)/shard_map/ppermute | solution.py:37
  56.3 2.5 %collective-permute-done.12 = bf16[128,512]{1,0:T(8,128)(2,1)S(1)} collective-permute-done((bf16[128,512]{1,0:T(8,128)(2,1)S(1)}, bf16[128,512]{1,0:T(8,128)(2,1)S(1)}, u32[]{:S(2)}, u32[]{:S(2)}) %collective-permute-start.12) | collective-permute-done | bytes 131104 | tf_op jit(solution)/shard_map/ppermute | solution.py:37
  58.9 3.5 %collective-permute-start.17 = (bf16[64,512]{1,0:T(8,128)(2,1)S(1)}, bf16[64,512]{1,0:T(8,128)(2,1)S(1)}, u32[]{:S(2)}, u32[]{:S(2)}) collective-permute-start(bf16[64,512]{1,0:T(8,128)(2,1)S(1)} %add_convert_fusion.16), channel_id=1, source_target_pairs={{0,4},{1,5},{2,6},{3,7},{4,0},{5,1},{6,2},{7,3},{8,12},{9,13},{10,... | collective-permute-start | bytes 196616 | tf_op jit(solution)/shard_map/ppermute | solution.py:37
  62.7 1.1 collective-permute-done.20
  63.9 1.6 %collective-permute-start.23 = (bf16[128,512]{1,0:T(8,128)(2,1)S(1)}, bf16[128,512]{1,0:T(8,128)(2,1)S(1)}, u32[]{:S(2)}, u32[]{:S(2)}) collective-permute-start(bf16[128,512]{1,0:T(8,128)(2,1)S(1)} %add_convert_fusion.6), channel_id=1, source_target_pairs={{0,2},{1,3},{2,0},{3,1},{4,6},{5,7},{6,4},{7,5},{8,10},{9,11},{10,... | collective-permute-start | bytes 393224 | tf_op jit(solution)/shard_map/ppermute | solution.py:37
  66.7 1.6 collective-permute-start.29
  68.3 1.5 collective-permute-start.27
  69.9 2.1 %collective-permute-start.28 = (bf16[64,512]{1,0:T(8,128)(2,1)S(1)}, bf16[64,512]{1,0:T(8,128)(2,1)S(1)}, u32[]{:S(2)}, u32[]{:S(2)}) collective-permute-start(bf16[64,512]{1,0:T(8,128)(2,1)S(1)} %add_convert_fusion.12), channel_id=1, source_target_pairs={{0,4},{1,5},{2,6},{3,7},{4,0},{5,1},{6,2},{7,3},{8,12},{9,13},{10,... | collective-permute-start | bytes 196616 | tf_op jit(solution)/shard_map/ppermute | solution.py:37
  72.1 1.4 collective-permute-start.26
  73.5 1.1 collective-permute-done.29
  74.8 3.3 %collective-permute-start.39 = (bf16[64,512]{1,0:T(8,128)(2,1)S(1)}, bf16[64,512]{1,0:T(8,128)(2,1)S(1)}, u32[]{:S(2)}, u32[]{:S(2)}) collective-permute-start(bf16[64,512]{1,0:T(8,128)(2,1)S(1)} %get-tuple-element.213), channel_id=1, source_target_pairs={{0,4},{1,5},{2,6},{3,7},{4,0},{5,1},{6,2},{7,3},{8,12},{9,13},{10,... | collective-permute-start | bytes 196616 | tf_op jit(solution)/shard_map/ppermute | solution.py:37
  78.2 2.8 %collective-permute-done.28 = bf16[64,512]{1,0:T(8,128)(2,1)S(1)} collective-permute-done((bf16[64,512]{1,0:T(8,128)(2,1)S(1)}, bf16[64,512]{1,0:T(8,128)(2,1)S(1)}, u32[]{:S(2)}, u32[]{:S(2)}) %collective-permute-start.28) | collective-permute-done | bytes 65568 | tf_op jit(solution)/shard_map/ppermute | solution.py:37
  81.1 3.3 %collective-permute-start.32 = (bf16[64,512]{1,0:T(8,128)(2,1)S(1)}, bf16[64,512]{1,0:T(8,128)(2,1)S(1)}, u32[]{:S(2)}, u32[]{:S(2)}) collective-permute-start(bf16[64,512]{1,0:T(8,128)(2,1)S(1)} %get-tuple-element.207), channel_id=1, source_target_pairs={{0,4},{1,5},{2,6},{3,7},{4,0},{5,1},{6,2},{7,3},{8,12},{9,13},{10,... | collective-permute-start | bytes 196616 | tf_op jit(solution)/shard_map/ppermute | solution.py:37
  84.6 2.5 %collective-permute-start.38 = (bf16[64,512]{1,0:T(8,128)(2,1)S(1)}, bf16[64,512]{1,0:T(8,128)(2,1)S(1)}, u32[]{:S(2)}, u32[]{:S(2)}) collective-permute-start(bf16[64,512]{1,0:T(8,128)(2,1)S(1)} %get-tuple-element.215), channel_id=1, source_target_pairs={{0,4},{1,5},{2,6},{3,7},{4,0},{5,1},{6,2},{7,3},{8,12},{9,13},{10,... | collective-permute-start | bytes 196616 | tf_op jit(solution)/shard_map/ppermute | solution.py:37
  87.1 2.5 %collective-permute-done.33 = bf16[64,512]{1,0:T(8,128)(2,1)S(1)} collective-permute-done((bf16[64,512]{1,0:T(8,128)(2,1)S(1)}, bf16[64,512]{1,0:T(8,128)(2,1)S(1)}, u32[]{:S(2)}, u32[]{:S(2)}) %collective-permute-start.33) | collective-permute-done | bytes 65568 | tf_op jit(solution)/shard_map/ppermute | solution.py:37
  89.6 2.4 %collective-permute-start.30 = (bf16[128,512]{1,0:T(8,128)(2,1)S(1)}, bf16[128,512]{1,0:T(8,128)(2,1)S(1)}, u32[]{:S(2)}, u32[]{:S(2)}) collective-permute-start(bf16[128,512]{1,0:T(8,128)(2,1)S(1)} %constant_dynamic-update-slice_fusion.10), channel_id=1, source_target_pairs={{0,2},{1,3},{2,0},{3,1},{4,6},{5,7},{6,4},{7,5},{8,10},{9,11},{10,... | collective-permute-start | bytes 393224 | tf_op jit(solution)/shard_map/ppermute | solution.py:37
  92.1 1.6 %collective-permute-start.36 = (bf16[128,512]{1,0:T(8,128)(2,1)S(1)}, bf16[128,512]{1,0:T(8,128)(2,1)S(1)}, u32[]{:S(2)}, u32[]{:S(2)}) collective-permute-start(bf16[128,512]{1,0:T(8,128)(2,1)S(1)} %constant_dynamic-update-slice_fusion.14), channel_id=1, source_target_pairs={{0,2},{1,3},{2,0},{3,1},{4,6},{5,7},{6,4},{7,5},{8,10},{9,11},{10,... | collective-permute-start | bytes 393224 | tf_op jit(solution)/shard_map/ppermute | solution.py:37
  93.7 0.9 collective-permute-done.30
  94.7 1.9 %collective-permute-start.35 = (bf16[256,512]{1,0:T(8,128)(2,1)S(1)}, bf16[256,512]{1,0:T(8,128)(2,1)S(1)}, u32[]{:S(2)}, u32[]{:S(2)}) collective-permute-start(bf16[256,512]{1,0:T(8,128)(2,1)S(1)} %constant_dynamic-update-slice_fusion.16.refs_3_.refs_2_), channel_id=1, source_target_pairs={{0,2},{1,3},{2,0},{3,1},{4,6},{5,7},{6,4},{7,5},{8,10},{9,11},{10,... | collective-permute-start | bytes 786440 | tf_op jit(solution)/shard_map/ppermute | solution.py:37
  97.0 1.3 collective-permute-start.44
  98.4 1.5 collective-permute-start.42
  100.0 2.3 %collective-permute-done.34.refs_2_.refs_1_ = bf16[256,512]{1,0:T(8,128)(2,1)S(1)} collective-permute-done((bf16[256,512]{1,0:T(8,128)(2,1)S(1)}, bf16[256,512]{1,0:T(8,128)(2,1)S(1)}, u32[]{:S(2)}, u32[]{:S(2)}) %collective-permute-start.34) | collective-permute-done | bytes 262176 | tf_op jit(solution)/shard_map/ppermute | solution.py:37
  102.5 3.4 %out_rows.1 = (bf16[512,448]{1,0:T(8,128)(2,1)S(1)}, bf16[512,448]{1,0:T(8,128)(2,1)S(1)}) custom-call(bf16[1024,512]{1,0:T(8,128)(2,1)S(1)} %get-tuple-element.250.id_ref.rows_ref.refs_0_, bf16[4,448,512]{2,1,0:T(8,128)(2,1)S(1)} %bitcast.6, bf16[256,512]{1,0:T(8,128)(2,1)S(1)} %constant_dynamic-update-slice_fusion.18.refs_1_.refs_0_, ...), custom_call_target="tpu_custom_call" | custom-call | flops 1 | bytes 1 | tf_op jit(solution)/shard_map/out_rows/pallas_call | solution.py:349
  105.9 6.4 %collective-permute-start.40 = (bf16[512,448]{1,0:T(8,128)(2,1)S(1)}, bf16[512,448]{1,0:T(8,128)(2,1)S(1)}, u32[]{:S(2)}, u32[]{:S(2)}) collective-permute-start(bf16[512,448]{1,0:T(8,128)(2,1)S(1)} %get-tuple-element.226), channel_id=1, source_target_pairs={{0,8},{1,9},{2,10},{3,11},{4,12},{5,13},{6,14},{7,15},{8,0},{9,1},... | collective-permute-start | bytes 1376264 | tf_op jit(solution)/shard_map/ppermute | solution.py:37
  112.4 1.7 %collective-permute-start.46 = (bf16[256,512]{1,0:T(8,128)(2,1)S(1)}, bf16[256,512]{1,0:T(8,128)(2,1)S(1)}, u32[]{:S(2)}, u32[]{:S(2)}) collective-permute-start(bf16[256,512]{1,0:T(8,128)(2,1)S(1)} %constant_dynamic-update-slice_fusion.30.refs_6_.refs_0_), channel_id=1, source_target_pairs={{0,1},{1,0},{2,3},{3,2},{4,5},{5,4},{6,7},{7,6},{8,9},{9,8},{10,11... | collective-permute-start | bytes 786440 | tf_op jit(solution)/shard_map/ppermute | solution.py:37
  114.1 3.8 %grad_gate.1 = bf16[4,448,512]{2,1,0:T(8,128)(2,1)} custom-call(bf16[1024,512]{1,0:T(8,128)(2,1)S(1)} %get-tuple-element.250.id_ref.rows_ref.refs_0_, bf16[1024,512]{1,0:T(8,128)(2,1)S(1)} %get-tuple-element.250.id_ref.rows_ref.refs_0_, bf16[256,512]{1,0:T(8,128)(2,1)S(1)} %constant_dynamic-update-slice_fusion.26.refs_0_.refs_2_, ...), custom_call_target="tpu_custom_call" | custom-call | flops 1 | bytes 1 | tf_op jit(solution)/shard_map/grad_gate/pallas_call | solution.py:349
  118.0 2.7 %collective-permute-done.46.refs_7_.refs_1_ = bf16[256,512]{1,0:T(8,128)(2,1)S(1)} collective-permute-done((bf16[256,512]{1,0:T(8,128)(2,1)S(1)}, bf16[256,512]{1,0:T(8,128)(2,1)S(1)}, u32[]{:S(2)}, u32[]{:S(2)}) %collective-permute-start.46) | collective-permute-done | bytes 262176 | tf_op jit(solution)/shard_map/ppermute | solution.py:37
  120.7 1.0 collective-permute-done.47.refs_9_.refs_3_
  121.6 5.6 %token_rows.1 = (bf16[512,448]{1,0:T(8,128)(2,1)S(1)}, bf16[512,448]{1,0:T(8,128)(2,1)S(1)}) custom-call(bf16[1024,512]{1,0:T(8,128)(2,1)S(1)} %get-tuple-element.250.id_ref.rows_ref.refs_0_, bf16[4,448,512]{2,1,0:T(8,128)(2,1)S(1)} %copy-done.1, bf16[4,448,512]{2,1,0:T(8,128)(2,1)S(1)} %copy-done.2, ...), custom_call_target="tpu_custom_call" | custom-call | flops 1 | bytes 1 | tf_op jit(solution)/shard_map/token_rows/pallas_call | solution.py:349
  127.2 1.2 collective-permute-start.48
  128.6 1.4 collective-permute-done.48
  130.2 6.2 %collective-permute-done.45 = bf16[256,448]{1,0:T(8,128)(2,1)S(1)} collective-permute-done((bf16[256,448]{1,0:T(8,128)(2,1)S(1)}, bf16[256,448]{1,0:T(8,128)(2,1)S(1)}, u32[]{:S(2)}, u32[]{:S(2)}) %collective-permute-start.45) | collective-permute-done | bytes 229408 | tf_op jit(solution)/shard_map/ppermute | solution.py:37
  136.5 2.6 %collective-permute-start.50 = (bf16[128,448]{1,0:T(8,128)(2,1)S(1)}, bf16[128,448]{1,0:T(8,128)(2,1)S(1)}, u32[]{:S(2)}, u32[]{:S(2)}) collective-permute-start(bf16[128,448]{1,0:T(8,128)(2,1)S(1)} %get-tuple-element.259), channel_id=1, source_target_pairs={{17,0},{16,1},{25,2},{24,3},{1,4},{0,5},{9,6},{8,7},{19,8},{18,9},... | collective-permute-start | bytes 344072 | tf_op jit(solution)/shard_map/ppermute | solution.py:144
  139.2 2.6 %collective-permute-start.49 = (bf16[128,448]{1,0:T(8,128)(2,1)S(1)}, bf16[128,448]{1,0:T(8,128)(2,1)S(1)}, u32[]{:S(2)}, u32[]{:S(2)}) collective-permute-start(bf16[128,448]{1,0:T(8,128)(2,1)S(1)} %get-tuple-element.260), channel_id=1, source_target_pairs={{0,0},{1,1},{8,2},{9,3},{16,4},{17,5},{24,6},{25,7},{2,8},{3,9},{1... | collective-permute-start | bytes 344072 | tf_op jit(solution)/shard_map/ppermute | solution.py:144
  141.7 3.8 %grad_down.1 = bf16[4,448,512]{2,1,0:T(8,128)(2,1)} custom-call(bf16[1024,512]{1,0:T(8,128)(2,1)S(1)} %get-tuple-element.250.id_ref.rows_ref.refs_0_, bf16[1024,512]{1,0:T(8,128)(2,1)S(1)} %get-tuple-element.247.rows_ref, bf16[256,512]{1,0:T(8,128)(2,1)S(1)} %constant_dynamic-update-slice_fusion.18.refs_1_.refs_0_, ...), custom_call_target="tpu_custom_call" | custom-call | flops 1 | bytes 1 | tf_op jit(solution)/shard_map/grad_down/pallas_call | solution.py:349
  145.6 3.9 %collective-permute-start.52 = (bf16[128,448]{1,0:T(8,128)(2,1)S(1)}, bf16[128,448]{1,0:T(8,128)(2,1)S(1)}, u32[]{:S(2)}, u32[]{:S(2)}) collective-permute-start(bf16[128,448]{1,0:T(8,128)(2,1)S(1)} %get-tuple-element.257), channel_id=1, source_target_pairs={{0,0},{1,1},{8,2},{9,3},{16,4},{17,5},{24,6},{25,7},{2,8},{3,9},{1... | collective-permute-start | bytes 344072 | tf_op jit(solution)/shard_map/ppermute | solution.py:144
  149.9 3.8 %grad_up.1 = bf16[4,448,512]{2,1,0:T(8,128)(2,1)} custom-call(bf16[1024,512]{1,0:T(8,128)(2,1)S(1)} %get-tuple-element.250.id_ref.rows_ref.refs_0_, bf16[1024,512]{1,0:T(8,128)(2,1)S(1)} %get-tuple-element.250.id_ref.rows_ref.refs_0_, bf16[256,512]{1,0:T(8,128)(2,1)S(1)} %constant_dynamic-update-slice_fusion.30.refs_6_.refs_0_, ...), custom_call_target="tpu_custom_call" | custom-call | flops 1 | bytes 1 | tf_op jit(solution)/shard_map/grad_up/pallas_call | solution.py:349
  154.6 2.6 %collective-permute-done.52.mine_ref = bf16[128,448]{1,0:T(8,128)(2,1)S(1)} collective-permute-done((bf16[128,448]{1,0:T(8,128)(2,1)S(1)}, bf16[128,448]{1,0:T(8,128)(2,1)S(1)}, u32[]{:S(2)}, u32[]{:S(2)}) %collective-permute-start.52) | collective-permute-done | bytes 114720 | tf_op jit(solution)/shard_map/ppermute | solution.py:144
  (135 shorter events, 9.9 us)
Async XLA Ops:
  0.6 29.3 %copy-start.1 = (bf16[4,448,512]{2,1,0:T(8,128)(2,1)S(1)}, bf16[4,448,512]{2,1,0:T(8,128)(2,1)}, u32[]{:S(2)}) copy-start(bf16[4,448,512]{2,1,0:T(8,128)(2,1)} %refs_0_.5) | copy-start | bytes 5505028
  2.6 4.6 %collective-permute-start = (bf16[128,512]{1,0:T(8,128)(2,1)}, bf16[128,512]{1,0:T(8,128)(2,1)S(1)}, u32[]{:S(2)}, u32[]{:S(2)}) collective-permute-start(bf16[128,512]{1,0:T(8,128)(2,1)} %get-tuple-element.131), channel_id=1, source_target_pairs={{0,16},{1,17},{2,18},{3,19},{4,20},{5,21},{6,22},{7,23},{8,24},{9,... | collective-permute-start | bytes 393224 | tf_op jit(solution)/shard_map/ppermute | solution.py:37
  5.7 8.1 %collective-permute-start.3 = (bf16[128,512]{1,0:T(8,128)(2,1)}, bf16[128,512]{1,0:T(8,128)(2,1)S(1)}, u32[]{:S(2)}, u32[]{:S(2)}) collective-permute-start(bf16[128,512]{1,0:T(8,128)(2,1)} %get-tuple-element.133), channel_id=1, source_target_pairs={{0,16},{1,17},{2,18},{3,19},{4,20},{5,21},{6,22},{7,23},{8,24},{9,... | collective-permute-start | bytes 393224 | tf_op jit(solution)/shard_map/ppermute | solution.py:37
  6.0 23.9 %copy-start.2 = (bf16[4,448,512]{2,1,0:T(8,128)(2,1)S(1)}, bf16[4,448,512]{2,1,0:T(8,128)(2,1)}, u32[]{:S(2)}) copy-start(bf16[4,448,512]{2,1,0:T(8,128)(2,1)} %refs_1_.5) | copy-start | bytes 5505028
  8.1 12.0 %collective-permute-start.2 = (bf16[128,512]{1,0:T(8,128)(2,1)S(1)}, bf16[128,512]{1,0:T(8,128)(2,1)S(1)}, u32[]{:S(2)}, u32[]{:S(2)}) collective-permute-start(bf16[128,512]{1,0:T(8,128)(2,1)S(1)} %get-tuple-element.267), channel_id=1, source_target_pairs={{0,4},{1,5},{2,12},{3,13},{4,1},{5,0},{6,9},{7,8},{8,6},{9,7},{10,... | collective-permute-start | bytes 393224 | tf_op jit(solution)/shard_map/ppermute | solution.py:381
  10.7 9.4 %collective-permute-start.1 = (bf16[128,512]{1,0:T(8,128)(2,1)S(1)}, bf16[128,512]{1,0:T(8,128)(2,1)S(1)}, u32[]{:S(2)}, u32[]{:S(2)}) collective-permute-start(bf16[128,512]{1,0:T(8,128)(2,1)S(1)} %get-tuple-element.268), channel_id=1, source_target_pairs={{0,0},{1,1},{2,8},{3,9},{4,5},{5,4},{6,13},{7,12},{8,2},{9,3},{10,... | collective-permute-start | bytes 393224 | tf_op jit(solution)/shard_map/ppermute | solution.py:382
  14.7 8.0 %collective-permute-start.6 = (bf16[128,512]{1,0:T(8,128)(2,1)S(1)}, bf16[128,512]{1,0:T(8,128)(2,1)S(1)}, u32[]{:S(2)}, u32[]{:S(2)}) collective-permute-start(bf16[128,512]{1,0:T(8,128)(2,1)S(1)} %get-tuple-element.265), channel_id=1, source_target_pairs={{0,4},{1,5},{2,12},{3,13},{4,1},{5,0},{6,9},{7,8},{8,6},{9,7},{10,... | collective-permute-start | bytes 393224 | tf_op jit(solution)/shard_map/ppermute | solution.py:381
  17.4 7.2 %collective-permute-start.5 = (bf16[128,512]{1,0:T(8,128)(2,1)S(1)}, bf16[128,512]{1,0:T(8,128)(2,1)S(1)}, u32[]{:S(2)}, u32[]{:S(2)}) collective-permute-start(bf16[128,512]{1,0:T(8,128)(2,1)S(1)} %get-tuple-element.266), channel_id=1, source_target_pairs={{0,0},{1,1},{2,8},{3,9},{4,5},{5,4},{6,13},{7,12},{8,2},{9,3},{10,... | collective-permute-start | bytes 393224 | tf_op jit(solution)/shard_map/ppermute | solution.py:382
  20.2 7.6 %collective-permute-start.4 = (bf16[256,512]{1,0:T(8,128)(2,1)S(1)}, bf16[256,512]{1,0:T(8,128)(2,1)S(1)}, u32[]{:S(2)}, u32[]{:S(2)}) collective-permute-start(bf16[256,512]{1,0:T(8,128)(2,1)S(1)} %constant_dynamic-update-slice_fusion), channel_id=1, source_target_pairs={{0,16},{1,17},{2,18},{3,19},{4,20},{5,21},{6,22},{7,23},{8,24},{9,... | collective-permute-start | bytes 786440 | tf_op jit(solution)/shard_map/ppermute | solution.py:37
  27.9 2.0 %collective-permute-start.7 = (bf16[512,512]{1,0:T(8,128)(2,1)S(1)}, bf16[512,512]{1,0:T(8,128)(2,1)S(1)}, u32[]{:S(2)}, u32[]{:S(2)}) collective-permute-start(bf16[512,512]{1,0:T(8,128)(2,1)S(1)} %constant_dynamic-update-slice_fusion.4.held_ref), channel_id=1, source_target_pairs={{0,8},{1,9},{2,10},{3,11},{4,12},{5,13},{6,14},{7,15},{8,0},{9,1},... | collective-permute-start | bytes 1572872 | tf_op jit(solution)/shard_map/ppermute | solution.py:37
  28.0 7.5 %collective-permute-start.9 = (bf16[256,512]{1,0:T(8,128)(2,1)S(1)}, bf16[256,512]{1,0:T(8,128)(2,1)S(1)}, u32[]{:S(2)}, u32[]{:S(2)}) collective-permute-start(bf16[256,512]{1,0:T(8,128)(2,1)S(1)} %constant_dynamic-update-slice_fusion.2), channel_id=1, source_target_pairs={{0,16},{1,17},{2,18},{3,19},{4,20},{5,21},{6,22},{7,23},{8,24},{9,... | collective-permute-start | bytes 786440 | tf_op jit(solution)/shard_map/ppermute | solution.py:37
  32.4 12.6 %copy-start = (bf16[4,512,448]{1,2,0:T(8,128)(2,1)S(1)}, bf16[4,512,448]{1,2,0:T(8,128)(2,1)}, u32[]{:S(2)}) copy-start(bf16[4,512,448]{1,2,0:T(8,128)(2,1)} %param.14) | copy-start | bytes 5505028
  35.6 9.4 %collective-permute-start.10 = (bf16[512,512]{1,0:T(8,128)(2,1)S(1)}, bf16[512,512]{1,0:T(8,128)(2,1)S(1)}, u32[]{:S(2)}, u32[]{:S(2)}) collective-permute-start(bf16[512,512]{1,0:T(8,128)(2,1)S(1)} %constant_dynamic-update-slice_fusion.6.held_ref), channel_id=1, source_target_pairs={{0,8},{1,9},{2,10},{3,11},{4,12},{5,13},{6,14},{7,15},{8,0},{9,1},... | collective-permute-start | bytes 1572872 | tf_op jit(solution)/shard_map/ppermute | solution.py:37
  36.9 7.9 %collective-permute-start.11 = (bf16[256,512]{1,0:T(8,128)(2,1)S(1)}, bf16[256,512]{1,0:T(8,128)(2,1)S(1)}, u32[]{:S(2)}, u32[]{:S(2)}) collective-permute-start(bf16[256,512]{1,0:T(8,128)(2,1)S(1)} %get-tuple-element.145), channel_id=1, source_target_pairs={{0,2},{1,3},{2,0},{3,1},{4,6},{5,7},{6,4},{7,5},{8,10},{9,11},{10,... | collective-permute-start | bytes 786440 | tf_op jit(solution)/shard_map/ppermute | solution.py:37
  37.0 12.0 %collective-permute-start.8 = (bf16[256,512]{1,0:T(8,128)(2,1)S(1)}, bf16[256,512]{1,0:T(8,128)(2,1)S(1)}, u32[]{:S(2)}, u32[]{:S(2)}) collective-permute-start(bf16[256,512]{1,0:T(8,128)(2,1)S(1)} %get-tuple-element.148), channel_id=1, source_target_pairs={{0,1},{1,0},{2,3},{3,2},{4,5},{5,4},{6,7},{7,6},{8,9},{9,8},{10,11... | collective-permute-start | bytes 786440 | tf_op jit(solution)/shard_map/ppermute | solution.py:37
  38.2 12.2 %collective-permute-start.16 = (bf16[256,512]{1,0:T(8,128)(2,1)S(1)}, bf16[256,512]{1,0:T(8,128)(2,1)S(1)}, u32[]{:S(2)}, u32[]{:S(2)}) collective-permute-start(bf16[256,512]{1,0:T(8,128)(2,1)S(1)} %get-tuple-element.166), channel_id=1, source_target_pairs={{0,2},{1,3},{2,0},{3,1},{4,6},{5,7},{6,4},{7,5},{8,10},{9,11},{10,... | collective-permute-start | bytes 786440 | tf_op jit(solution)/shard_map/ppermute | solution.py:37
  38.5 12.4 %collective-permute-start.15 = (bf16[256,512]{1,0:T(8,128)(2,1)S(1)}, bf16[256,512]{1,0:T(8,128)(2,1)S(1)}, u32[]{:S(2)}, u32[]{:S(2)}) collective-permute-start(bf16[256,512]{1,0:T(8,128)(2,1)S(1)} %get-tuple-element.164), channel_id=1, source_target_pairs={{0,1},{1,0},{2,3},{3,2},{4,5},{5,4},{6,7},{7,6},{8,9},{9,8},{10,11... | collective-permute-start | bytes 786440 | tf_op jit(solution)/shard_map/ppermute | solution.py:37
  44.8 8.1 %collective-permute-start.14 = (bf16[128,512]{1,0:T(8,128)(2,1)S(1)}, bf16[128,512]{1,0:T(8,128)(2,1)S(1)}, u32[]{:S(2)}, u32[]{:S(2)}) collective-permute-start(bf16[128,512]{1,0:T(8,128)(2,1)S(1)} %add_convert_fusion.11), channel_id=1, source_target_pairs={{0,1},{1,0},{2,3},{3,2},{4,5},{5,4},{6,7},{7,6},{8,9},{9,8},{10,11... | collective-permute-start | bytes 393224 | tf_op jit(solution)/shard_map/ppermute | solution.py:37
  46.4 9.6 %collective-permute-start.13 = (bf16[256,512]{1,0:T(8,128)(2,1)S(1)}, bf16[256,512]{1,0:T(8,128)(2,1)S(1)}, u32[]{:S(2)}, u32[]{:S(2)}) collective-permute-start(bf16[256,512]{1,0:T(8,128)(2,1)S(1)} %get-tuple-element.157), channel_id=1, source_target_pairs={{0,2},{1,3},{2,0},{3,1},{4,6},{5,7},{6,4},{7,5},{8,10},{9,11},{10,... | collective-permute-start | bytes 786440 | tf_op jit(solution)/shard_map/ppermute | solution.py:37
  49.1 9.8 %collective-permute-start.12 = (bf16[128,512]{1,0:T(8,128)(2,1)S(1)}, bf16[128,512]{1,0:T(8,128)(2,1)S(1)}, u32[]{:S(2)}, u32[]{:S(2)}) collective-permute-start(bf16[128,512]{1,0:T(8,128)(2,1)S(1)} %add_convert_fusion.10), channel_id=1, source_target_pairs={{0,2},{1,3},{2,0},{3,1},{4,6},{5,7},{6,4},{7,5},{8,10},{9,11},{10,... | collective-permute-start | bytes 393224 | tf_op jit(solution)/shard_map/ppermute | solution.py:37
  50.4 12.0 %collective-permute-start.21 = (bf16[128,512]{1,0:T(8,128)(2,1)S(1)}, bf16[128,512]{1,0:T(8,128)(2,1)S(1)}, u32[]{:S(2)}, u32[]{:S(2)}) collective-permute-start(bf16[128,512]{1,0:T(8,128)(2,1)S(1)} %add_convert_fusion.9), channel_id=1, source_target_pairs={{0,1},{1,0},{2,3},{3,2},{4,5},{5,4},{6,7},{7,6},{8,9},{9,8},{10,11... | collective-permute-start | bytes 393224 | tf_op jit(solution)/shard_map/ppermute | solution.py:37
  51.0 14.6 %collective-permute-start.18 = (bf16[128,512]{1,0:T(8,128)(2,1)S(1)}, bf16[128,512]{1,0:T(8,128)(2,1)S(1)}, u32[]{:S(2)}, u32[]{:S(2)}) collective-permute-start(bf16[128,512]{1,0:T(8,128)(2,1)S(1)} %add_convert_fusion.8), channel_id=1, source_target_pairs={{0,2},{1,3},{2,0},{3,1},{4,6},{5,7},{6,4},{7,5},{8,10},{9,11},{10,... | collective-permute-start | bytes 393224 | tf_op jit(solution)/shard_map/ppermute | solution.py:37
  53.0 10.8 %collective-permute-start.20 = (bf16[64,512]{1,0:T(8,128)(2,1)S(1)}, bf16[64,512]{1,0:T(8,128)(2,1)S(1)}, u32[]{:S(2)}, u32[]{:S(2)}) collective-permute-start(bf16[64,512]{1,0:T(8,128)(2,1)S(1)} %add_convert_fusion.17), channel_id=1, source_target_pairs={{0,4},{1,5},{2,6},{3,7},{4,0},{5,1},{6,2},{7,3},{8,12},{9,13},{10,... | collective-permute-start | bytes 196616 | tf_op jit(solution)/shard_map/ppermute | solution.py:37
  56.0 7.8 %collective-permute-start.19 = (bf16[256,512]{1,0:T(8,128)(2,1)S(1)}, bf16[256,512]{1,0:T(8,128)(2,1)S(1)}, u32[]{:S(2)}, u32[]{:S(2)}) collective-permute-start(bf16[256,512]{1,0:T(8,128)(2,1)S(1)} %get-tuple-element.178), channel_id=1, source_target_pairs={{0,1},{1,0},{2,3},{3,2},{4,5},{5,4},{6,7},{7,6},{8,9},{9,8},{10,11... | collective-permute-start | bytes 786440 | tf_op jit(solution)/shard_map/ppermute | solution.py:37
  58.9 7.6 %collective-permute-start.17 = (bf16[64,512]{1,0:T(8,128)(2,1)S(1)}, bf16[64,512]{1,0:T(8,128)(2,1)S(1)}, u32[]{:S(2)}, u32[]{:S(2)}) collective-permute-start(bf16[64,512]{1,0:T(8,128)(2,1)S(1)} %add_convert_fusion.16), channel_id=1, source_target_pairs={{0,4},{1,5},{2,6},{3,7},{4,0},{5,1},{6,2},{7,3},{8,12},{9,13},{10,... | collective-permute-start | bytes 196616 | tf_op jit(solution)/shard_map/ppermute | solution.py:37
  62.4 4.2 %collective-permute-start.25 = (bf16[128,512]{1,0:T(8,128)(2,1)S(1)}, bf16[128,512]{1,0:T(8,128)(2,1)S(1)}, u32[]{:S(2)}, u32[]{:S(2)}) collective-permute-start(bf16[128,512]{1,0:T(8,128)(2,1)S(1)} %add_convert_fusion.7), channel_id=1, source_target_pairs={{0,1},{1,0},{2,3},{3,2},{4,5},{5,4},{6,7},{7,6},{8,9},{9,8},{10,11... | collective-permute-start | bytes 393224 | tf_op jit(solution)/shard_map/ppermute | solution.py:37
  63.8 4.4 %collective-permute-start.24 = (bf16[64,512]{1,0:T(8,128)(2,1)S(1)}, bf16[64,512]{1,0:T(8,128)(2,1)S(1)}, u32[]{:S(2)}, u32[]{:S(2)}) collective-permute-start(bf16[64,512]{1,0:T(8,128)(2,1)S(1)} %add_convert_fusion.15), channel_id=1, source_target_pairs={{0,4},{1,5},{2,6},{3,7},{4,0},{5,1},{6,2},{7,3},{8,12},{9,13},{10,... | collective-permute-start | bytes 196616 | tf_op jit(solution)/shard_map/ppermute | solution.py:37
  63.9 5.9 %collective-permute-start.23 = (bf16[128,512]{1,0:T(8,128)(2,1)S(1)}, bf16[128,512]{1,0:T(8,128)(2,1)S(1)}, u32[]{:S(2)}, u32[]{:S(2)}) collective-permute-start(bf16[128,512]{1,0:T(8,128)(2,1)S(1)} %add_convert_fusion.6), channel_id=1, source_target_pairs={{0,2},{1,3},{2,0},{3,1},{4,6},{5,7},{6,4},{7,5},{8,10},{9,11},{10,... | collective-permute-start | bytes 393224 | tf_op jit(solution)/shard_map/ppermute | solution.py:37
  65.6 6.4 %collective-permute-start.22 = (bf16[64,512]{1,0:T(8,128)(2,1)S(1)}, bf16[64,512]{1,0:T(8,128)(2,1)S(1)}, u32[]{:S(2)}, u32[]{:S(2)}) collective-permute-start(bf16[64,512]{1,0:T(8,128)(2,1)S(1)} %add_convert_fusion.14), channel_id=1, source_target_pairs={{0,4},{1,5},{2,6},{3,7},{4,0},{5,1},{6,2},{7,3},{8,12},{9,13},{10,... | collective-permute-start | bytes 196616 | tf_op jit(solution)/shard_map/ppermute | solution.py:37
  66.7 8.0 %collective-permute-start.29 = (bf16[64,512]{1,0:T(8,128)(2,1)S(1)}, bf16[64,512]{1,0:T(8,128)(2,1)S(1)}, u32[]{:S(2)}, u32[]{:S(2)}) collective-permute-start(bf16[64,512]{1,0:T(8,128)(2,1)S(1)} %add_convert_fusion.13), channel_id=1, source_target_pairs={{0,4},{1,5},{2,6},{3,7},{4,0},{5,1},{6,2},{7,3},{8,12},{9,13},{10,... | collective-permute-start | bytes 196616 | tf_op jit(solution)/shard_map/ppermute | solution.py:37
  68.3 16.2 %collective-permute-start.27 = (bf16[64,512]{1,0:T(8,128)(2,1)S(1)}, bf16[64,512]{1,0:T(8,128)(2,1)S(1)}, u32[]{:S(2)}, u32[]{:S(2)}) collective-permute-start(bf16[64,512]{1,0:T(8,128)(2,1)S(1)} %get-tuple-element.201), channel_id=1, source_target_pairs={{0,4},{1,5},{2,6},{3,7},{4,0},{5,1},{6,2},{7,3},{8,12},{9,13},{10,... | collective-permute-start | bytes 196616 | tf_op jit(solution)/shard_map/ppermute | solution.py:37
  69.9 11.1 %collective-permute-start.28 = (bf16[64,512]{1,0:T(8,128)(2,1)S(1)}, bf16[64,512]{1,0:T(8,128)(2,1)S(1)}, u32[]{:S(2)}, u32[]{:S(2)}) collective-permute-start(bf16[64,512]{1,0:T(8,128)(2,1)S(1)} %add_convert_fusion.12), channel_id=1, source_target_pairs={{0,4},{1,5},{2,6},{3,7},{4,0},{5,1},{6,2},{7,3},{8,12},{9,13},{10,... | collective-permute-start | bytes 196616 | tf_op jit(solution)/shard_map/ppermute | solution.py:37
  72.1 12.4 %collective-permute-start.26 = (bf16[64,512]{1,0:T(8,128)(2,1)S(1)}, bf16[64,512]{1,0:T(8,128)(2,1)S(1)}, u32[]{:S(2)}, u32[]{:S(2)}) collective-permute-start(bf16[64,512]{1,0:T(8,128)(2,1)S(1)} %multiply_convert_fusion.5), channel_id=1, source_target_pairs={{0,4},{1,5},{2,6},{3,7},{4,0},{5,1},{6,2},{7,3},{8,12},{9,13},{10,... | collective-permute-start | bytes 196616 | tf_op jit(solution)/shard_map/ppermute | solution.py:37
  74.8 21.8 %collective-permute-start.39 = (bf16[64,512]{1,0:T(8,128)(2,1)S(1)}, bf16[64,512]{1,0:T(8,128)(2,1)S(1)}, u32[]{:S(2)}, u32[]{:S(2)}) collective-permute-start(bf16[64,512]{1,0:T(8,128)(2,1)S(1)} %get-tuple-element.213), channel_id=1, source_target_pairs={{0,4},{1,5},{2,6},{3,7},{4,0},{5,1},{6,2},{7,3},{8,12},{9,13},{10,... | collective-permute-start | bytes 196616 | tf_op jit(solution)/shard_map/ppermute | solution.py:37
  78.1 11.5 %collective-permute-start.33 = (bf16[64,512]{1,0:T(8,128)(2,1)S(1)}, bf16[64,512]{1,0:T(8,128)(2,1)S(1)}, u32[]{:S(2)}, u32[]{:S(2)}) collective-permute-start(bf16[64,512]{1,0:T(8,128)(2,1)S(1)} %get-tuple-element.205), channel_id=1, source_target_pairs={{0,4},{1,5},{2,6},{3,7},{4,0},{5,1},{6,2},{7,3},{8,12},{9,13},{10,... | collective-permute-start | bytes 196616 | tf_op jit(solution)/shard_map/ppermute | solution.py:37
  81.1 10.8 %collective-permute-start.32 = (bf16[64,512]{1,0:T(8,128)(2,1)S(1)}, bf16[64,512]{1,0:T(8,128)(2,1)S(1)}, u32[]{:S(2)}, u32[]{:S(2)}) collective-permute-start(bf16[64,512]{1,0:T(8,128)(2,1)S(1)} %get-tuple-element.207), channel_id=1, source_target_pairs={{0,4},{1,5},{2,6},{3,7},{4,0},{5,1},{6,2},{7,3},{8,12},{9,13},{10,... | collective-permute-start | bytes 196616 | tf_op jit(solution)/shard_map/ppermute | solution.py:37
  84.5 7.6 %collective-permute-start.31 = (bf16[128,512]{1,0:T(8,128)(2,1)S(1)}, bf16[128,512]{1,0:T(8,128)(2,1)S(1)}, u32[]{:S(2)}, u32[]{:S(2)}) collective-permute-start(bf16[128,512]{1,0:T(8,128)(2,1)S(1)} %constant_dynamic-update-slice_fusion.8), channel_id=1, source_target_pairs={{0,1},{1,0},{2,3},{3,2},{4,5},{5,4},{6,7},{7,6},{8,9},{9,8},{10,11... | collective-permute-start | bytes 393224 | tf_op jit(solution)/shard_map/ppermute | solution.py:37
  84.6 12.4 %collective-permute-start.38 = (bf16[64,512]{1,0:T(8,128)(2,1)S(1)}, bf16[64,512]{1,0:T(8,128)(2,1)S(1)}, u32[]{:S(2)}, u32[]{:S(2)}) collective-permute-start(bf16[64,512]{1,0:T(8,128)(2,1)S(1)} %get-tuple-element.215), channel_id=1, source_target_pairs={{0,4},{1,5},{2,6},{3,7},{4,0},{5,1},{6,2},{7,3},{8,12},{9,13},{10,... | collective-permute-start | bytes 196616 | tf_op jit(solution)/shard_map/ppermute | solution.py:37
  89.6 5.1 %collective-permute-start.30 = (bf16[128,512]{1,0:T(8,128)(2,1)S(1)}, bf16[128,512]{1,0:T(8,128)(2,1)S(1)}, u32[]{:S(2)}, u32[]{:S(2)}) collective-permute-start(bf16[128,512]{1,0:T(8,128)(2,1)S(1)} %constant_dynamic-update-slice_fusion.10), channel_id=1, source_target_pairs={{0,2},{1,3},{2,0},{3,1},{4,6},{5,7},{6,4},{7,5},{8,10},{9,11},{10,... | collective-permute-start | bytes 393224 | tf_op jit(solution)/shard_map/ppermute | solution.py:37
  92.0 6.3 %collective-permute-start.37 = (bf16[128,512]{1,0:T(8,128)(2,1)S(1)}, bf16[128,512]{1,0:T(8,128)(2,1)S(1)}, u32[]{:S(2)}, u32[]{:S(2)}) collective-permute-start(bf16[128,512]{1,0:T(8,128)(2,1)S(1)} %constant_dynamic-update-slice_fusion.12), channel_id=1, source_target_pairs={{0,1},{1,0},{2,3},{3,2},{4,5},{5,4},{6,7},{7,6},{8,9},{9,8},{10,11... | collective-permute-start | bytes 393224 | tf_op jit(solution)/shard_map/ppermute | solution.py:37
  92.1 6.3 %collective-permute-start.36 = (bf16[128,512]{1,0:T(8,128)(2,1)S(1)}, bf16[128,512]{1,0:T(8,128)(2,1)S(1)}, u32[]{:S(2)}, u32[]{:S(2)}) collective-permute-start(bf16[128,512]{1,0:T(8,128)(2,1)S(1)} %constant_dynamic-update-slice_fusion.14), channel_id=1, source_target_pairs={{0,2},{1,3},{2,0},{3,1},{4,6},{5,7},{6,4},{7,5},{8,10},{9,11},{10,... | collective-permute-start | bytes 393224 | tf_op jit(solution)/shard_map/ppermute | solution.py:37
  94.7 7.8 %collective-permute-start.35 = (bf16[256,512]{1,0:T(8,128)(2,1)S(1)}, bf16[256,512]{1,0:T(8,128)(2,1)S(1)}, u32[]{:S(2)}, u32[]{:S(2)}) collective-permute-start(bf16[256,512]{1,0:T(8,128)(2,1)S(1)} %constant_dynamic-update-slice_fusion.16.refs_3_.refs_2_), channel_id=1, source_target_pairs={{0,2},{1,3},{2,0},{3,1},{4,6},{5,7},{6,4},{7,5},{8,10},{9,11},{10,... | collective-permute-start | bytes 786440 | tf_op jit(solution)/shard_map/ppermute | solution.py:37
  96.6 5.6 %collective-permute-start.34 = (bf16[256,512]{1,0:T(8,128)(2,1)S(1)}, bf16[256,512]{1,0:T(8,128)(2,1)S(1)}, u32[]{:S(2)}, u32[]{:S(2)}) collective-permute-start(bf16[256,512]{1,0:T(8,128)(2,1)S(1)} %constant_dynamic-update-slice_fusion.18.refs_1_.refs_0_), channel_id=1, source_target_pairs={{0,1},{1,0},{2,3},{3,2},{4,5},{5,4},{6,7},{7,6},{8,9},{9,8},{10,11... | collective-permute-start | bytes 786440 | tf_op jit(solution)/shard_map/ppermute | solution.py:37
  97.0 15.3 %collective-permute-start.44 = (bf16[128,512]{1,0:T(8,128)(2,1)S(1)}, bf16[128,512]{1,0:T(8,128)(2,1)S(1)}, u32[]{:S(2)}, u32[]{:S(2)}) collective-permute-start(bf16[128,512]{1,0:T(8,128)(2,1)S(1)} %constant_dynamic-update-slice_fusion.20), channel_id=1, source_target_pairs={{0,1},{1,0},{2,3},{3,2},{4,5},{5,4},{6,7},{7,6},{8,9},{9,8},{10,11... | collective-permute-start | bytes 393224 | tf_op jit(solution)/shard_map/ppermute | solution.py:37
  98.3 14.1 %collective-permute-start.43 = (bf16[128,512]{1,0:T(8,128)(2,1)S(1)}, bf16[128,512]{1,0:T(8,128)(2,1)S(1)}, u32[]{:S(2)}, u32[]{:S(2)}) collective-permute-start(bf16[128,512]{1,0:T(8,128)(2,1)S(1)} %constant_dynamic-update-slice_fusion.22), channel_id=1, source_target_pairs={{0,2},{1,3},{2,0},{3,1},{4,6},{5,7},{6,4},{7,5},{8,10},{9,11},{10,... | collective-permute-start | bytes 393224 | tf_op jit(solution)/shard_map/ppermute | solution.py:37
  98.4 15.7 %collective-permute-start.42 = (bf16[256,512]{1,0:T(8,128)(2,1)S(1)}, bf16[256,512]{1,0:T(8,128)(2,1)S(1)}, u32[]{:S(2)}, u32[]{:S(2)}) collective-permute-start(bf16[256,512]{1,0:T(8,128)(2,1)S(1)} %constant_dynamic-update-slice_fusion.24.refs_2_.refs_4_), channel_id=1, source_target_pairs={{0,2},{1,3},{2,0},{3,1},{4,6},{5,7},{6,4},{7,5},{8,10},{9,11},{10,... | collective-permute-start | bytes 786440 | tf_op jit(solution)/shard_map/ppermute | solution.py:37
  102.2 11.8 %collective-permute-start.41 = (bf16[256,512]{1,0:T(8,128)(2,1)S(1)}, bf16[256,512]{1,0:T(8,128)(2,1)S(1)}, u32[]{:S(2)}, u32[]{:S(2)}) collective-permute-start(bf16[256,512]{1,0:T(8,128)(2,1)S(1)} %constant_dynamic-update-slice_fusion.26.refs_0_.refs_2_), channel_id=1, source_target_pairs={{0,1},{1,0},{2,3},{3,2},{4,5},{5,4},{6,7},{7,6},{8,9},{9,8},{10,11... | collective-permute-start | bytes 786440 | tf_op jit(solution)/shard_map/ppermute | solution.py:37
  105.9 12.0 %collective-permute-start.40 = (bf16[512,448]{1,0:T(8,128)(2,1)S(1)}, bf16[512,448]{1,0:T(8,128)(2,1)S(1)}, u32[]{:S(2)}, u32[]{:S(2)}) collective-permute-start(bf16[512,448]{1,0:T(8,128)(2,1)S(1)} %get-tuple-element.226), channel_id=1, source_target_pairs={{0,8},{1,9},{2,10},{3,11},{4,12},{5,13},{6,14},{7,15},{8,0},{9,1},... | collective-permute-start | bytes 1376264 | tf_op jit(solution)/shard_map/ppermute | solution.py:37
  112.4 8.3 %collective-permute-start.46 = (bf16[256,512]{1,0:T(8,128)(2,1)S(1)}, bf16[256,512]{1,0:T(8,128)(2,1)S(1)}, u32[]{:S(2)}, u32[]{:S(2)}) collective-permute-start(bf16[256,512]{1,0:T(8,128)(2,1)S(1)} %constant_dynamic-update-slice_fusion.30.refs_6_.refs_0_), channel_id=1, source_target_pairs={{0,1},{1,0},{2,3},{3,2},{4,5},{5,4},{6,7},{7,6},{8,9},{9,8},{10,11... | collective-permute-start | bytes 786440 | tf_op jit(solution)/shard_map/ppermute | solution.py:37
  114.1 7.6 %collective-permute-start.47 = (bf16[256,512]{1,0:T(8,128)(2,1)S(1)}, bf16[256,512]{1,0:T(8,128)(2,1)S(1)}, u32[]{:S(2)}, u32[]{:S(2)}) collective-permute-start(bf16[256,512]{1,0:T(8,128)(2,1)S(1)} %constant_dynamic-update-slice_fusion.28.refs_8_.refs_2_), channel_id=1, source_target_pairs={{0,2},{1,3},{2,0},{3,1},{4,6},{5,7},{6,4},{7,5},{8,10},{9,11},{10,... | collective-permute-start | bytes 786440 | tf_op jit(solution)/shard_map/ppermute | solution.py:37
  127.2 2.7 %collective-permute-start.48 = (bf16[512,448]{1,0:T(8,128)(2,1)S(1)}, bf16[512,448]{1,0:T(8,128)(2,1)S(1)}, u32[]{:S(2)}, u32[]{:S(2)}) collective-permute-start(bf16[512,448]{1,0:T(8,128)(2,1)S(1)} %get-tuple-element.242), channel_id=1, source_target_pairs={{0,8},{1,9},{2,10},{3,11},{4,12},{5,13},{6,14},{7,15},{8,0},{9,1},... | collective-permute-start | bytes 1376264 | tf_op jit(solution)/shard_map/ppermute | solution.py:37
  128.4 8.0 %collective-permute-start.45 = (bf16[256,448]{1,0:T(8,128)(2,1)S(1)}, bf16[256,448]{1,0:T(8,128)(2,1)S(1)}, u32[]{:S(2)}, u32[]{:S(2)}) collective-permute-start(bf16[256,448]{1,0:T(8,128)(2,1)S(1)} %add_convert_fusion.1), channel_id=1, source_target_pairs={{0,16},{1,17},{2,18},{3,19},{4,20},{5,21},{6,22},{7,23},{8,24},{9,... | collective-permute-start | bytes 688136 | tf_op jit(solution)/shard_map/ppermute | solution.py:37
  130.0 15.5 %collective-permute-start.51 = (bf16[256,448]{1,0:T(8,128)(2,1)S(1)}, bf16[256,448]{1,0:T(8,128)(2,1)S(1)}, u32[]{:S(2)}, u32[]{:S(2)}) collective-permute-start(bf16[256,448]{1,0:T(8,128)(2,1)S(1)} %add_convert_fusion), channel_id=1, source_target_pairs={{0,16},{1,17},{2,18},{3,19},{4,20},{5,21},{6,22},{7,23},{8,24},{9,... | collective-permute-start | bytes 688136 | tf_op jit(solution)/shard_map/ppermute | solution.py:37
  136.5 17.2 %collective-permute-start.50 = (bf16[128,448]{1,0:T(8,128)(2,1)S(1)}, bf16[128,448]{1,0:T(8,128)(2,1)S(1)}, u32[]{:S(2)}, u32[]{:S(2)}) collective-permute-start(bf16[128,448]{1,0:T(8,128)(2,1)S(1)} %get-tuple-element.259), channel_id=1, source_target_pairs={{17,0},{16,1},{25,2},{24,3},{1,4},{0,5},{9,6},{8,7},{19,8},{18,9},... | collective-permute-start | bytes 344072 | tf_op jit(solution)/shard_map/ppermute | solution.py:144
  139.2 14.6 %collective-permute-start.49 = (bf16[128,448]{1,0:T(8,128)(2,1)S(1)}, bf16[128,448]{1,0:T(8,128)(2,1)S(1)}, u32[]{:S(2)}, u32[]{:S(2)}) collective-permute-start(bf16[128,448]{1,0:T(8,128)(2,1)S(1)} %get-tuple-element.260), channel_id=1, source_target_pairs={{0,0},{1,1},{8,2},{9,3},{16,4},{17,5},{24,6},{25,7},{2,8},{3,9},{1... | collective-permute-start | bytes 344072 | tf_op jit(solution)/shard_map/ppermute | solution.py:144
  145.6 11.6 %collective-permute-start.52 = (bf16[128,448]{1,0:T(8,128)(2,1)S(1)}, bf16[128,448]{1,0:T(8,128)(2,1)S(1)}, u32[]{:S(2)}, u32[]{:S(2)}) collective-permute-start(bf16[128,448]{1,0:T(8,128)(2,1)S(1)} %get-tuple-element.257), channel_id=1, source_target_pairs={{0,0},{1,1},{8,2},{9,3},{16,4},{17,5},{24,6},{25,7},{2,8},{3,9},{1... | collective-permute-start | bytes 344072 | tf_op jit(solution)/shard_map/ppermute | solution.py:144
  149.6 4.2 %copy-start.3 = (f32[128,1]{0,1:T(1,128)S(1)}, f32[128,1]{0,1:T(1,128)}, u32[]{:S(2)}) copy-start(f32[128,1]{0,1:T(1,128)} %param.10) | copy-start | bytes 1540
  149.6 7.7 %collective-permute-start.53 = (bf16[128,448]{1,0:T(8,128)(2,1)S(1)}, bf16[128,448]{1,0:T(8,128)(2,1)S(1)}, u32[]{:S(2)}, u32[]{:S(2)}) collective-permute-start(bf16[128,448]{1,0:T(8,128)(2,1)S(1)} %get-tuple-element.258), channel_id=1, source_target_pairs={{17,0},{16,1},{25,2},{24,3},{1,4},{0,5},{9,6},{8,7},{19,8},{18,9},... | collective-permute-start | bytes 344072 | tf_op jit(solution)/shard_map/ppermute | solution.py:144

commit v6 on v5

--- a/solution.py
+++ b/solution.py
@@ -136,12 +136,12 @@
         total = self.sum
         total.terms[0], total.got = self.line.begin(total.terms[0], total.got)
         n = total.got.shape[0] // 2
-        self.pieces = []
-        for k in range(2):
+        self.pieces = [None, None]
+        for k in (1, 0):
             back = [(b, a) for a, b in plane_pairs(k)]
             piece = half(summed(total.terms + [total.got], slice(k * n, (k + 1) * n)))
             self.line.end(piece)
-            self.pieces.append(lax.ppermute(piece, AXES, back))
+            self.pieces[k] = lax.ppermute(piece, AXES, back)
 
 
 def block_order(bits):
@@ -276,27 +276,36 @@
     return [jnp.concatenate(blocks[:n]), jnp.concatenate(blocks[n:])]
 
 
-def back_body(geo, stored, count, jobs, id_ref, *refs):
+def turned_body(geo, stored, count, sources, id_ref, w_ref, *refs):
+    tok, order = geo
+    out_ref = refs[-1]
+    n = len(order) // 2 * (tok // PARTS)
+    for part, source in enumerate(sources):
+        pair = in_order(refs[2 * part][...], refs[2 * part + 1][...], source, order)
+        for side in range(2):
+            at = slice((part * 2 + side) * n, (part * 2 + side + 1) * n)
+            out_ref[at, :] = expert_dot(pair[side], id_of(id_ref, stored, at), w_ref, count, True)
+
+
+def back_body(geo, stored, count, sources, based, id_ref, w_ref, *refs):
     grp_size, tok, order = geo
     keep_ref, send_ref = refs[-2:]
     sub = tok // PARTS
     shift = lax.axis_index("grp") ^ (lax.axis_index("ep") // 2)
     n = len(order) // 2
-    for number, (part, terms) in enumerate(jobs):
+    for part, source in enumerate(sources):
+        pair = in_order(refs[2 * part][...], refs[2 * part + 1][...], source, order)
         for side in range(2):
-            at = (part * 2 + side) * n * sub
-            expert = id_of(id_ref, stored, slice(at, at + n * sub))
-            total = None
-            for weight, pair, source in terms:
-                rows = in_order(refs[pair][...], refs[pair + 1][...], source, order)[side]
-                now = expert_dot(rows, expert, refs[weight], count, True)
-                total = now if total is None else total + now
+            at = slice((part * 2 + side) * n * sub, (part * 2 + side + 1) * n * sub)
+            total = expert_dot(pair[side], id_of(id_ref, stored, at), w_ref, count, True)
+            if based:
+                total = total + refs[-3][at, :]
             total = half(total)
             for place in range(n):
                 j = order[side * n + place]
                 k = j & 1
                 m = shift ^ ((j >> 1) ^ (k * (grp_size // 2)))
-                to = (((m >> 1) * 2 + k) * len(jobs) + number) * sub
+                to = (((m >> 1) * 2 + k) * len(sources) + part) * sub
                 to = pl.ds(pl.multiple_of(to, sub), sub)
                 block = total[place * sub : (place + 1) * sub]
 
@@ -452,7 +461,6 @@
     up_0 = Sum(line, keep_u, send_u, bit_swaps)
     dz_held = doubled(dz_held, dz_next)
     dz_got = swap(dz_held, 1, 0)
-    gate_1.fold()
     dz_held, dz_got = line.begin(dz_held, dz_got)
     keep, send, dz_rows = call(
         functools.partial(first_body, geo, stored, count, 1, False, 1, places),
@@ -473,24 +481,26 @@
         for _ in range(1, rounds):
             one.fold()
 
+    gate_1.fold()
+    ag_0 = Sum(line, ag_keep, *line.begin(ag_send), bit_swaps)
     gate_0.fold()
     up_1.fold()
-    ag_0 = Sum(line, ag_keep, *line.begin(ag_send), bit_swaps)
     up_0.fold()
     rest(gate_1)
     ag_1.fold()
     rest(gate_0)
+    ag_0.fold()
     rest(up_1)
     gate_1.finish()
-    ag_0.fold()
     rest(up_0)
     gate_0.finish()
     rest(ag_1)
+    rest(ag_0)
     up_1.finish()
-    rest(ag_0)
     up_0.finish()
     gate, up, ag = (gate_0, gate_1), (up_0, up_1), (ag_0, ag_1)
     acts, gate_grads, up_grads = [None] * PARTS, [None] * PARTS, [None] * PARTS
+    pre_grads = [None] * PARTS
     sources = [order, turned_order]
     back_swaps = [bit_swaps[::-1], turned_swaps[::-1]]
 
@@ -506,7 +516,7 @@
         up_grad = half(act_grad * gate_pre * sg)
         line.end(gate_grad)
         gate_grads[part] = Gather(line, gate_grad, back_swaps[part])
-        up_grads[part] = Gather(line, up_grad, back_swaps[part])
+        pre_grads[part] = gate_grad, up_grad
 
     start_act(1)
     start_act(0)
@@ -520,6 +530,9 @@
         pair[0].grow()
 
     grow(acts)
+    for part in (1, 0):
+        (up_grad,) = line.begin(pre_grads[part][1])
+        up_grads[part] = Gather(line, up_grad, back_swaps[part])
     grow(gate_grads)
     for _ in range(1, rounds):
         grow(acts)
@@ -527,12 +540,12 @@
     for _ in range(1, rounds):
         grow(gate_grads)
 
-    def back(ids, weights, pairs, jobs, name):
-        args = tuple(weights) + tuple(pairs)
+    def back(weight, pairs, name, base=()):
+        args = (weight,) + tuple(pairs) + base
         return call(
-            functools.partial(back_body, geo, stored, count, jobs),
-            [jax.ShapeDtypeStruct((n // 2 * len(jobs), stored), BF16)] * 2,
-            (ids,) + args,
+            functools.partial(back_body, geo, stored, count, sources, bool(base)),
+            [jax.ShapeDtypeStruct((total // 2, stored), BF16)] * 2,
+            (x_rows,) + args,
             in_specs=[id_spec(total, 0)] + [full(a.shape) for a in args],
             name=name,
         )
@@ -553,26 +566,35 @@
         return call(join_body, jax.ShapeDtypeStruct(tokens.shape, BF16), args, name=name)
 
     act_pairs = acts[0].result() + acts[1].result()
-    jobs = [(i, ((0, 1 + 2 * i, s),)) for i, s in enumerate(sources)]
-    keep, send = back(x_rows, (w_down,), line.begin(*act_pairs), jobs, "out_rows")
+    keep, send = back(w_down, line.begin(*act_pairs), "out_rows")
     line.end(send)
     out = Return(line, keep, send)
     for _ in range(1, rounds):
         grow(up_grads)
+    for _ in range(out.rounds):
+        out.fold()
     gate_pairs = gate_grads[0].result() + gate_grads[1].result()
     gate_pairs = line.begin(*gate_pairs)
-    grad_gate = line.end(grad(x_rows, gate_pairs, "grad_gate"))
-    for _ in range(out.rounds):
-        out.fold()
+    args = (w_gate,) + tuple(gate_pairs)
+    base = line.end(
+        call(
+            functools.partial(turned_body, geo[1:], stored, count, sources),
+            jax.ShapeDtypeStruct((total, stored), jnp.float32),
+            (x_rows,) + args,
+            in_specs=[id_spec(total, 0)] + [full(a.shape) for a in args],
+            name="token_gate_rows",
+        )
+    )
+    (rows,) = line.begin(x_rows)
+    grad_gate = line.end(grad(rows, gate_pairs, "grad_gate"))
     up_pairs = up_grads[0].result() + up_grads[1].result()
     pairs = line.begin(*up_pairs)
-    jobs = [(i, ((0, 2 + 2 * i, s), (1, 6 + 2 * i, s))) for i, s in enumerate(sources)]
-    keep, send = back(x_rows, (w_gate, w_up), gate_pairs + pairs, jobs, "token_rows")
+    keep, send = back(w_up, pairs, "token_rows", (base,))
     line.end(send)
     token = Return(line, keep, send)
+    out.leave()
     for _ in range(token.rounds):
         token.fold()
-    out.leave()
     (rows,) = line.begin(dz_rows)
     grad_down = line.end(grad(rows, act_pairs, "grad_down"))
     token.leave()

time: 161 us -> 155 us (0.963)
  waiting for transfers between devices: 43.9 us -> 33.9 us
  starting transfers between devices: 76 us -> 79.9 us
    ppermute x46, waiting for transfers between devices: 39 us -> 30.3 us  [swap(): return lax.ppermute(block, AXES, pairs)]
    ppermute x4, starting transfers between devices: 9.48 us -> 11.5 us  [leave(): self.pieces[k] = lax.ppermute(piece, AXES, back)]
    ppermute x46, starting transfers between devices: 55.4 us -> 57.3 us  [swap(): return lax.ppermute(block, AXES, pairs)]
    pallas_call x13 -> x14, Pallas kernels: 33.4 us -> 33.6 us  [call(): pl.pallas_call(body, out_shape=out_shape, grid=kw.get('grid', (1,)), in_s...]
  transfers between devices with their start and end apart: 54 -> 54, of which waited for: 23 -> 22; matrix products, arithmetic and copies ran while one was open for 2% -> 2% of each run, Pallas kernels for 16% -> 20%
where the time goes in v6:
time: 155 us; the launch traced here: 152 us
  starting transfers between devices  79.9 us (52%)
  waiting for transfers between devices  33.9 us (22%)
  Pallas kernels  33.6 us (22%)
  other arithmetic  3 us (2%)
    ppermute x46, starting transfers between devices, swap(): return lax.ppermute(block, AXES, pairs)  57.3 us
    pallas_call x14, Pallas kernels, call(): pl.pallas_call(body, out_shape=out_shape, grid=kw.get('grid', (1,)), in_s...  33.6 us
    ppermute x46, waiting for transfers between devices, swap(): return lax.ppermute(block, AXES, pairs)  30.3 us
    ppermute x4, starting transfers between devices, leave(): self.pieces[k] = lax.ppermute(piece, AXES, back)  11.5 us
    ppermute x2, starting transfers between devices, land(): return [lax.ppermute(near, AXES, column_pairs(0)), far]  5.8 us
    ppermute x2, starting transfers between devices, land(): far = lax.ppermute(far, AXES, column_pairs(1))  5.28 us
  transfers between devices with their start and end apart: 54, of which 22 were waited for; matrix products, arithmetic and copies ran while one was open for 2% of the time, Pallas kernels for 20%

profile of v6, /device:TPU:17, one launch (start us, length us, event | category | flops | bytes accessed | tf_op | source)
XLA Modules:
  0.0 152.1 jit_solution(14784022281398124064)
XLA Ops:
  0.6 2.0 %token_pieces.1 = (bf16[128,512]{1,0:T(8,128)(2,1)}, bf16[128,512]{1,0:T(8,128)(2,1)}) custom-call(s32[4]{0:T(128)} %hot_ref.1, s32[1,128]{1,0:T(1,128)} %bitcast.10, bf16[128,896]{1,0:T(8,128)(2,1)} %tokens_ref.1), custom_call_target="tpu_custom_call" | custom-call | flops 1 | bytes 1 | tf_op jit(solution)/shard_map/token_pieces/pallas_call | solution.py:358
  2.6 1.2 collective-permute-start
  3.8 1.9 %cotangent_pieces.1 = (bf16[128,512]{1,0:T(8,128)(2,1)}, bf16[128,512]{1,0:T(8,128)(2,1)}) custom-call(f32[1,128]{1,0:T(1,128)} %bitcast.7, bf16[128,896]{1,0:T(8,128)(2,1)} %rows_ref.1), custom_call_target="tpu_custom_call" | custom-call | flops 1 | bytes 1 | tf_op jit(solution)/shard_map/cotangent_pieces/pallas_call | solution.py:358
  6.0 1.2 collective-permute-done
  7.2 0.9 broadcast_select_fusion.2
  8.1 2.6 %collective-permute-start.2 = (bf16[128,512]{1,0:T(8,128)(2,1)S(1)}, bf16[128,512]{1,0:T(8,128)(2,1)S(1)}, u32[]{:S(2)}, u32[]{:S(2)}) collective-permute-start(bf16[128,512]{1,0:T(8,128)(2,1)S(1)} %get-tuple-element.273), channel_id=1, source_target_pairs={{0,4},{1,5},{2,12},{3,13},{4,1},{5,0},{6,9},{7,8},{8,6},{9,7},{10,... | collective-permute-start | bytes 393224 | tf_op jit(solution)/shard_map/ppermute | solution.py:390
  10.7 3.0 %collective-permute-start.1 = (bf16[128,512]{1,0:T(8,128)(2,1)S(1)}, bf16[128,512]{1,0:T(8,128)(2,1)S(1)}, u32[]{:S(2)}, u32[]{:S(2)}) collective-permute-start(bf16[128,512]{1,0:T(8,128)(2,1)S(1)} %get-tuple-element.274), channel_id=1, source_target_pairs={{0,0},{1,1},{2,8},{3,9},{4,5},{5,4},{6,13},{7,12},{8,2},{9,3},{10,... | collective-permute-start | bytes 393224 | tf_op jit(solution)/shard_map/ppermute | solution.py:391
  13.8 0.9 broadcast_select_fusion
  14.7 2.7 %collective-permute-start.6 = (bf16[128,512]{1,0:T(8,128)(2,1)S(1)}, bf16[128,512]{1,0:T(8,128)(2,1)S(1)}, u32[]{:S(2)}, u32[]{:S(2)}) collective-permute-start(bf16[128,512]{1,0:T(8,128)(2,1)S(1)} %get-tuple-element.271), channel_id=1, source_target_pairs={{0,4},{1,5},{2,12},{3,13},{4,1},{5,0},{6,9},{7,8},{8,6},{9,7},{10,... | collective-permute-start | bytes 393224 | tf_op jit(solution)/shard_map/ppermute | solution.py:390
  17.4 2.8 %collective-permute-start.5 = (bf16[128,512]{1,0:T(8,128)(2,1)S(1)}, bf16[128,512]{1,0:T(8,128)(2,1)S(1)}, u32[]{:S(2)}, u32[]{:S(2)}) collective-permute-start(bf16[128,512]{1,0:T(8,128)(2,1)S(1)} %get-tuple-element.272), channel_id=1, source_target_pairs={{0,0},{1,1},{2,8},{3,9},{4,5},{5,4},{6,13},{7,12},{8,2},{9,3},{10,... | collective-permute-start | bytes 393224 | tf_op jit(solution)/shard_map/ppermute | solution.py:391
  20.2 2.0 %collective-permute-start.4 = (bf16[256,512]{1,0:T(8,128)(2,1)S(1)}, bf16[256,512]{1,0:T(8,128)(2,1)S(1)}, u32[]{:S(2)}, u32[]{:S(2)}) collective-permute-start(bf16[256,512]{1,0:T(8,128)(2,1)S(1)} %constant_dynamic-update-slice_fusion), channel_id=1, source_target_pairs={{0,16},{1,17},{2,18},{3,19},{4,20},{5,21},{6,22},{7,23},{8,24},{9,... | collective-permute-start | bytes 786440 | tf_op jit(solution)/shard_map/ppermute | solution.py:37
  22.7 1.9 %collective-permute-done.5 = bf16[128,512]{1,0:T(8,128)(2,1)S(1)} collective-permute-done((bf16[128,512]{1,0:T(8,128)(2,1)S(1)}, bf16[128,512]{1,0:T(8,128)(2,1)S(1)}, u32[]{:S(2)}, u32[]{:S(2)}) %collective-permute-start.5) | collective-permute-done | bytes 131104 | tf_op jit(solution)/shard_map/ppermute | solution.py:391
  24.6 3.2 %collective-permute-done.4 = bf16[256,512]{1,0:T(8,128)(2,1)S(1)} collective-permute-done((bf16[256,512]{1,0:T(8,128)(2,1)S(1)}, bf16[256,512]{1,0:T(8,128)(2,1)S(1)}, u32[]{:S(2)}, u32[]{:S(2)}) %collective-permute-start.4) | collective-permute-done | bytes 262176 | tf_op jit(solution)/shard_map/ppermute | solution.py:37
  28.4 1.5 %collective-permute-done.7.got_ref = bf16[512,512]{1,0:T(8,128)(2,1)S(1)} collective-permute-done((bf16[512,512]{1,0:T(8,128)(2,1)S(1)}, bf16[512,512]{1,0:T(8,128)(2,1)S(1)}, u32[]{:S(2)}, u32[]{:S(2)}) %collective-permute-start.7) | collective-permute-done | bytes 524320 | tf_op jit(solution)/shard_map/ppermute | solution.py:37
  29.9 2.5 %gate_up_first.1 = (bf16[256,512]{1,0:T(8,128)(2,1)S(1)}, bf16[256,512]{1,0:T(8,128)(2,1)S(1)}, bf16[256,512]{1,0:T(8,128)(2,1)S(1)}, bf16[256,512]{1,0:T(8,128)(2,1)S(1)}, bf16[1024,512]{1,0:T(8,128)(2,1)S(1)}) custom-call(bf16[512,512]{1,0:T(8,128)(2,1)S(1)} %constant_dynamic-update-slice_fusion.4.held_ref, ...), custom_call_target="tpu_custom_call" | custom-call | flops 1 | bytes 1 | tf_op jit(solution)/shard_map/gate_up_first/pallas_call | solution.py:358
  32.4 2.3 %gate_up_later.1 = (bf16[256,512]{1,0:T(8,128)(2,1)S(1)}, bf16[256,512]{1,0:T(8,128)(2,1)S(1)}, bf16[256,512]{1,0:T(8,128)(2,1)S(1)}, bf16[256,512]{1,0:T(8,128)(2,1)S(1)}) custom-call(bf16[1024,512]{1,0:T(8,128)(2,1)S(1)} %get-tuple-element.256.id_ref.rows_ref.refs_0_, bf16[1024,512]{1,0:T(8,128)(2,1)S(1)} %get-tuple-element.256.id_ref.rows_ref.refs_0_, ...), custom_call_target="tpu_custom_call" | custom-call | flops 1 | bytes 1 | tf_op jit(solution)/shard_map/gate_up_later/pallas_call | solution.py:358
  35.6 1.3 collective-permute-start.11
  37.0 1.2 collective-permute-start.8
  38.5 1.4 collective-permute-start.15
  39.9 1.4 act_grad_first.1
  41.4 1.3 act_grad_later.1
  42.7 2.1 %collective-permute-done.9 = bf16[256,512]{1,0:T(8,128)(2,1)S(1)} collective-permute-done((bf16[256,512]{1,0:T(8,128)(2,1)S(1)}, bf16[256,512]{1,0:T(8,128)(2,1)S(1)}, u32[]{:S(2)}, u32[]{:S(2)}) %collective-permute-start.9) | collective-permute-done | bytes 262176 | tf_op jit(solution)/shard_map/ppermute | solution.py:37
  45.0 1.3 collective-permute-start.12
  46.3 4.1 %collective-permute-done.16 = bf16[256,512]{1,0:T(8,128)(2,1)S(1)} collective-permute-done((bf16[256,512]{1,0:T(8,128)(2,1)S(1)}, bf16[256,512]{1,0:T(8,128)(2,1)S(1)}, u32[]{:S(2)}, u32[]{:S(2)}) %collective-permute-start.16) | collective-permute-done | bytes 262176 | tf_op jit(solution)/shard_map/ppermute | solution.py:37
  50.7 1.3 collective-permute-start.18
  52.0 0.9 collective-permute-done.14
  53.0 1.2 collective-permute-start.21
  54.2 1.8 %collective-permute-done.13 = bf16[256,512]{1,0:T(8,128)(2,1)S(1)} collective-permute-done((bf16[256,512]{1,0:T(8,128)(2,1)S(1)}, bf16[256,512]{1,0:T(8,128)(2,1)S(1)}, u32[]{:S(2)}, u32[]{:S(2)}) %collective-permute-start.13) | collective-permute-done | bytes 262176 | tf_op jit(solution)/shard_map/ppermute | solution.py:37
  56.0 2.5 %collective-permute-start.19 = (bf16[64,512]{1,0:T(8,128)(2,1)S(1)}, bf16[64,512]{1,0:T(8,128)(2,1)S(1)}, u32[]{:S(2)}, u32[]{:S(2)}) collective-permute-start(bf16[64,512]{1,0:T(8,128)(2,1)S(1)} %add_convert_fusion.17), channel_id=1, source_target_pairs={{0,4},{1,5},{2,6},{3,7},{4,0},{5,1},{6,2},{7,3},{8,12},{9,13},{10,... | collective-permute-start | bytes 196616 | tf_op jit(solution)/shard_map/ppermute | solution.py:37
  58.9 2.1 %collective-permute-done.21 = bf16[256,512]{1,0:T(8,128)(2,1)S(1)} collective-permute-done((bf16[256,512]{1,0:T(8,128)(2,1)S(1)}, bf16[256,512]{1,0:T(8,128)(2,1)S(1)}, u32[]{:S(2)}, u32[]{:S(2)}) %collective-permute-start.21) | collective-permute-done | bytes 262176 | tf_op jit(solution)/shard_map/ppermute | solution.py:37
  61.0 1.1 collective-permute-start.24
  62.1 2.6 %collective-permute-start.17 = (bf16[64,512]{1,0:T(8,128)(2,1)S(1)}, bf16[64,512]{1,0:T(8,128)(2,1)S(1)}, u32[]{:S(2)}, u32[]{:S(2)}) collective-permute-start(bf16[64,512]{1,0:T(8,128)(2,1)S(1)} %add_convert_fusion.16), channel_id=1, source_target_pairs={{0,4},{1,5},{2,6},{3,7},{4,0},{5,1},{6,2},{7,3},{8,12},{9,13},{10,... | collective-permute-start | bytes 196616 | tf_op jit(solution)/shard_map/ppermute | solution.py:37
  65.5 2.4 %collective-permute-start.22 = (bf16[64,512]{1,0:T(8,128)(2,1)S(1)}, bf16[64,512]{1,0:T(8,128)(2,1)S(1)}, u32[]{:S(2)}, u32[]{:S(2)}) collective-permute-start(bf16[64,512]{1,0:T(8,128)(2,1)S(1)} %add_convert_fusion.14), channel_id=1, source_target_pairs={{0,4},{1,5},{2,6},{3,7},{4,0},{5,1},{6,2},{7,3},{8,12},{9,13},{10,... | collective-permute-start | bytes 196616 | tf_op jit(solution)/shard_map/ppermute | solution.py:37
  68.6 1.0 collective-permute-start.29
  69.6 1.5 %collective-permute-start.28 = (bf16[64,512]{1,0:T(8,128)(2,1)S(1)}, bf16[64,512]{1,0:T(8,128)(2,1)S(1)}, u32[]{:S(2)}, u32[]{:S(2)}) collective-permute-start(bf16[64,512]{1,0:T(8,128)(2,1)S(1)} %add_convert_fusion.12), channel_id=1, source_target_pairs={{0,4},{1,5},{2,6},{3,7},{4,0},{5,1},{6,2},{7,3},{8,12},{9,13},{10,... | collective-permute-start | bytes 196616 | tf_op jit(solution)/shard_map/ppermute | solution.py:37
  71.2 3.3 %collective-permute-done.22 = bf16[64,512]{1,0:T(8,128)(2,1)S(1)} collective-permute-done((bf16[64,512]{1,0:T(8,128)(2,1)S(1)}, bf16[64,512]{1,0:T(8,128)(2,1)S(1)}, u32[]{:S(2)}, u32[]{:S(2)}) %collective-permute-start.22) | collective-permute-done | bytes 65568 | tf_op jit(solution)/shard_map/ppermute | solution.py:37
  74.6 3.3 %collective-permute-start.26 = (bf16[64,512]{1,0:T(8,128)(2,1)S(1)}, bf16[64,512]{1,0:T(8,128)(2,1)S(1)}, u32[]{:S(2)}, u32[]{:S(2)}) collective-permute-start(bf16[64,512]{1,0:T(8,128)(2,1)S(1)} %multiply_convert_fusion.5), channel_id=1, source_target_pairs={{0,4},{1,5},{2,6},{3,7},{4,0},{5,1},{6,2},{7,3},{8,12},{9,13},{10,... | collective-permute-start | bytes 196616 | tf_op jit(solution)/shard_map/ppermute | solution.py:37
  78.1 2.4 %collective-permute-start.33 = (bf16[64,512]{1,0:T(8,128)(2,1)S(1)}, bf16[64,512]{1,0:T(8,128)(2,1)S(1)}, u32[]{:S(2)}, u32[]{:S(2)}) collective-permute-start(bf16[64,512]{1,0:T(8,128)(2,1)S(1)} %get-tuple-element.208), channel_id=1, source_target_pairs={{0,4},{1,5},{2,6},{3,7},{4,0},{5,1},{6,2},{7,3},{8,12},{9,13},{10,... | collective-permute-start | bytes 196616 | tf_op jit(solution)/shard_map/ppermute | solution.py:37
  80.5 1.0 collective-permute-start.32
  81.5 3.9 %collective-permute-done.27 = bf16[64,512]{1,0:T(8,128)(2,1)S(1)} collective-permute-done((bf16[64,512]{1,0:T(8,128)(2,1)S(1)}, bf16[64,512]{1,0:T(8,128)(2,1)S(1)}, u32[]{:S(2)}, u32[]{:S(2)}) %collective-permute-start.27) | collective-permute-done | bytes 65568 | tf_op jit(solution)/shard_map/ppermute | solution.py:37
  85.4 0.9 collective-permute-start.31
  86.4 1.9 %collective-permute-start.30 = (bf16[128,512]{1,0:T(8,128)(2,1)S(1)}, bf16[128,512]{1,0:T(8,128)(2,1)S(1)}, u32[]{:S(2)}, u32[]{:S(2)}) collective-permute-start(bf16[128,512]{1,0:T(8,128)(2,1)S(1)} %constant_dynamic-update-slice_fusion.10), channel_id=1, source_target_pairs={{0,2},{1,3},{2,0},{3,1},{4,6},{5,7},{6,4},{7,5},{8,10},{9,11},{10,... | collective-permute-start | bytes 393224 | tf_op jit(solution)/shard_map/ppermute | solution.py:37
  88.3 1.3 collective-permute-start.38
  89.6 1.0 collective-permute-start.39
  92.5 1.5 collective-permute-start.35
  94.1 1.2 collective-permute-start.34
  95.8 1.9 %collective-permute-start.41 = (bf16[128,512]{1,0:T(8,128)(2,1)S(1)}, bf16[128,512]{1,0:T(8,128)(2,1)S(1)}, u32[]{:S(2)}, u32[]{:S(2)}) collective-permute-start(bf16[128,512]{1,0:T(8,128)(2,1)S(1)} %constant_dynamic-update-slice_fusion.22), channel_id=1, source_target_pairs={{0,2},{1,3},{2,0},{3,1},{4,6},{5,7},{6,4},{7,5},{8,10},{9,11},{10,... | collective-permute-start | bytes 393224 | tf_op jit(solution)/shard_map/ppermute | solution.py:37
  97.7 1.5 collective-permute-start.47
  99.2 1.7 %collective-permute-done.34.refs_1_ = bf16[256,512]{1,0:T(8,128)(2,1)S(1)} collective-permute-done((bf16[256,512]{1,0:T(8,128)(2,1)S(1)}, bf16[256,512]{1,0:T(8,128)(2,1)S(1)}, u32[]{:S(2)}, u32[]{:S(2)}) %collective-permute-start.34) | collective-permute-done | bytes 262176 | tf_op jit(solution)/shard_map/ppermute | solution.py:37
  100.9 1.3 collective-permute-start.46
  102.5 3.4 %out_rows.1 = (bf16[512,448]{1,0:T(8,128)(2,1)S(1)}, bf16[512,448]{1,0:T(8,128)(2,1)S(1)}) custom-call(bf16[1024,512]{1,0:T(8,128)(2,1)S(1)} %get-tuple-element.256.id_ref.rows_ref.refs_0_, bf16[4,448,512]{2,1,0:T(8,128)(2,1)S(1)} %bitcast.6, bf16[256,512]{1,0:T(8,128)(2,1)S(1)} %constant_dynamic-update-slice_fusion.18.refs_0_, ...), custom_call_target="tpu_custom_call" | custom-call | flops 1 | bytes 1 | tf_op jit(solution)/shard_map/out_rows/pallas_call | solution.py:358
  105.9 8.6 %collective-permute-start.40 = (bf16[512,448]{1,0:T(8,128)(2,1)S(1)}, bf16[512,448]{1,0:T(8,128)(2,1)S(1)}, u32[]{:S(2)}, u32[]{:S(2)}) collective-permute-start(bf16[512,448]{1,0:T(8,128)(2,1)S(1)} %get-tuple-element.231), channel_id=1, source_target_pairs={{0,8},{1,9},{2,10},{3,11},{4,12},{5,13},{6,14},{7,15},{8,0},{9,1},... | collective-permute-start | bytes 1376264 | tf_op jit(solution)/shard_map/ppermute | solution.py:37
  116.4 2.5 %token_gate_rows.1.refs_4_ = f32[1024,448]{1,0:T(8,128)S(1)} custom-call(bf16[1024,512]{1,0:T(8,128)(2,1)S(1)} %get-tuple-element.256.id_ref.rows_ref.refs_0_, bf16[4,448,512]{2,1,0:T(8,128)(2,1)S(1)} %copy-done, bf16[256,512]{1,0:T(8,128)(2,1)S(1)} %constant_dynamic-update-slice_fusion.26.refs_0_, bf16[256,512]{1,0:T(8,128)(2,1)S(1)} %collective-permute-done.46.refs_1_, ...), custom_call_target="tpu_custom_call" | custom-call | flops 1 | bytes 1 | tf_op jit(solution)/shard_map/token_gate_rows/pallas_call | solution.py:358
  119.0 3.8 %grad_gate.1 = bf16[4,448,512]{2,1,0:T(8,128)(2,1)} custom-call(bf16[1024,512]{1,0:T(8,128)(2,1)S(1)} %get-tuple-element.256.id_ref.rows_ref.refs_0_, bf16[1024,512]{1,0:T(8,128)(2,1)S(1)} %get-tuple-element.256.id_ref.rows_ref.refs_0_, bf16[256,512]{1,0:T(8,128)(2,1)S(1)} %constant_dynamic-update-slice_fusion.26.refs_0_, ...), custom_call_target="tpu_custom_call" | custom-call | flops 1 | bytes 1 | tf_op jit(solution)/shard_map/grad_gate/pallas_call | solution.py:358
  122.8 3.3 %token_rows.1 = (bf16[512,448]{1,0:T(8,128)(2,1)S(1)}, bf16[512,448]{1,0:T(8,128)(2,1)S(1)}) custom-call(bf16[1024,512]{1,0:T(8,128)(2,1)S(1)} %get-tuple-element.256.id_ref.rows_ref.refs_0_, bf16[4,448,512]{2,1,0:T(8,128)(2,1)S(1)} %copy-done.1, bf16[256,512]{1,0:T(8,128)(2,1)S(1)} %constant_dynamic-update-slice_fusion.30.refs_0_, ...), custom_call_target="tpu_custom_call" | custom-call | flops 1 | bytes 1 | tf_op jit(solution)/shard_map/token_rows/pallas_call | solution.py:358
  126.0 1.0 collective-permute-start.50
  127.1 1.4 collective-permute-done.50
  128.6 1.2 collective-permute-start.51
  129.8 4.2 %collective-permute-start.48 = (bf16[128,448]{1,0:T(8,128)(2,1)S(1)}, bf16[128,448]{1,0:T(8,128)(2,1)S(1)}, u32[]{:S(2)}, u32[]{:S(2)}) collective-permute-start(bf16[128,448]{1,0:T(8,128)(2,1)S(1)} %get-tuple-element.266), channel_id=1, source_target_pairs={{0,0},{1,1},{8,2},{9,3},{16,4},{17,5},{24,6},{25,7},{2,8},{3,9},{1... | collective-permute-start | bytes 344072 | tf_op jit(solution)/shard_map/ppermute | solution.py:144
  134.4 3.8 %grad_down.1 = bf16[4,448,512]{2,1,0:T(8,128)(2,1)} custom-call(bf16[1024,512]{1,0:T(8,128)(2,1)S(1)} %get-tuple-element.256.id_ref.rows_ref.refs_0_, bf16[1024,512]{1,0:T(8,128)(2,1)S(1)} %get-tuple-element.253.rows_ref, bf16[256,512]{1,0:T(8,128)(2,1)S(1)} %constant_dynamic-update-slice_fusion.18.refs_0_, ...), custom_call_target="tpu_custom_call" | custom-call | flops 1 | bytes 1 | tf_op jit(solution)/shard_map/grad_down/pallas_call | solution.py:358
  138.3 3.7 %collective-permute-start.53 = (bf16[128,448]{1,0:T(8,128)(2,1)S(1)}, bf16[128,448]{1,0:T(8,128)(2,1)S(1)}, u32[]{:S(2)}, u32[]{:S(2)}) collective-permute-start(bf16[128,448]{1,0:T(8,128)(2,1)S(1)} %get-tuple-element.263), channel_id=1, source_target_pairs={{17,0},{16,1},{25,2},{24,3},{1,4},{0,5},{9,6},{8,7},{19,8},{18,9},... | collective-permute-start | bytes 344072 | tf_op jit(solution)/shard_map/ppermute | solution.py:144
  142.0 3.2 %collective-permute-start.52 = (bf16[128,448]{1,0:T(8,128)(2,1)S(1)}, bf16[128,448]{1,0:T(8,128)(2,1)S(1)}, u32[]{:S(2)}, u32[]{:S(2)}) collective-permute-start(bf16[128,448]{1,0:T(8,128)(2,1)S(1)} %get-tuple-element.264), channel_id=1, source_target_pairs={{0,0},{1,1},{8,2},{9,3},{16,4},{17,5},{24,6},{25,7},{2,8},{3,9},{1... | collective-permute-start | bytes 344072 | tf_op jit(solution)/shard_map/ppermute | solution.py:144
  145.3 3.8 %grad_up.1 = bf16[4,448,512]{2,1,0:T(8,128)(2,1)} custom-call(bf16[1024,512]{1,0:T(8,128)(2,1)S(1)} %get-tuple-element.256.id_ref.rows_ref.refs_0_, bf16[1024,512]{1,0:T(8,128)(2,1)S(1)} %get-tuple-element.256.id_ref.rows_ref.refs_0_, bf16[256,512]{1,0:T(8,128)(2,1)S(1)} %constant_dynamic-update-slice_fusion.30.refs_0_, ...), custom_call_target="tpu_custom_call" | custom-call | flops 1 | bytes 1 | tf_op jit(solution)/shard_map/grad_up/pallas_call | solution.py:358
  150.0 1.3 collective-permute-done.52.mine_ref
  (139 shorter events, 12.6 us)
Async XLA Ops:
  0.6 29.3 %copy-start = (bf16[4,448,512]{2,1,0:T(8,128)(2,1)S(1)}, bf16[4,448,512]{2,1,0:T(8,128)(2,1)}, u32[]{:S(2)}) copy-start(bf16[4,448,512]{2,1,0:T(8,128)(2,1)} %w_ref.2) | copy-start | bytes 5505028
  2.6 4.6 %collective-permute-start = (bf16[128,512]{1,0:T(8,128)(2,1)}, bf16[128,512]{1,0:T(8,128)(2,1)S(1)}, u32[]{:S(2)}, u32[]{:S(2)}) collective-permute-start(bf16[128,512]{1,0:T(8,128)(2,1)} %get-tuple-element.134), channel_id=1, source_target_pairs={{0,16},{1,17},{2,18},{3,19},{4,20},{5,21},{6,22},{7,23},{8,24},{9,... | collective-permute-start | bytes 393224 | tf_op jit(solution)/shard_map/ppermute | solution.py:37
  5.7 8.1 %collective-permute-start.3 = (bf16[128,512]{1,0:T(8,128)(2,1)}, bf16[128,512]{1,0:T(8,128)(2,1)S(1)}, u32[]{:S(2)}, u32[]{:S(2)}) collective-permute-start(bf16[128,512]{1,0:T(8,128)(2,1)} %get-tuple-element.136), channel_id=1, source_target_pairs={{0,16},{1,17},{2,18},{3,19},{4,20},{5,21},{6,22},{7,23},{8,24},{9,... | collective-permute-start | bytes 393224 | tf_op jit(solution)/shard_map/ppermute | solution.py:37
  6.0 23.9 %copy-start.1 = (bf16[4,448,512]{2,1,0:T(8,128)(2,1)S(1)}, bf16[4,448,512]{2,1,0:T(8,128)(2,1)}, u32[]{:S(2)}) copy-start(bf16[4,448,512]{2,1,0:T(8,128)(2,1)} %w_ref.3) | copy-start | bytes 5505028
  8.1 12.0 %collective-permute-start.2 = (bf16[128,512]{1,0:T(8,128)(2,1)S(1)}, bf16[128,512]{1,0:T(8,128)(2,1)S(1)}, u32[]{:S(2)}, u32[]{:S(2)}) collective-permute-start(bf16[128,512]{1,0:T(8,128)(2,1)S(1)} %get-tuple-element.273), channel_id=1, source_target_pairs={{0,4},{1,5},{2,12},{3,13},{4,1},{5,0},{6,9},{7,8},{8,6},{9,7},{10,... | collective-permute-start | bytes 393224 | tf_op jit(solution)/shard_map/ppermute | solution.py:390
  10.7 9.4 %collective-permute-start.1 = (bf16[128,512]{1,0:T(8,128)(2,1)S(1)}, bf16[128,512]{1,0:T(8,128)(2,1)S(1)}, u32[]{:S(2)}, u32[]{:S(2)}) collective-permute-start(bf16[128,512]{1,0:T(8,128)(2,1)S(1)} %get-tuple-element.274), channel_id=1, source_target_pairs={{0,0},{1,1},{2,8},{3,9},{4,5},{5,4},{6,13},{7,12},{8,2},{9,3},{10,... | collective-permute-start | bytes 393224 | tf_op jit(solution)/shard_map/ppermute | solution.py:391
  14.7 8.0 %collective-permute-start.6 = (bf16[128,512]{1,0:T(8,128)(2,1)S(1)}, bf16[128,512]{1,0:T(8,128)(2,1)S(1)}, u32[]{:S(2)}, u32[]{:S(2)}) collective-permute-start(bf16[128,512]{1,0:T(8,128)(2,1)S(1)} %get-tuple-element.271), channel_id=1, source_target_pairs={{0,4},{1,5},{2,12},{3,13},{4,1},{5,0},{6,9},{7,8},{8,6},{9,7},{10,... | collective-permute-start | bytes 393224 | tf_op jit(solution)/shard_map/ppermute | solution.py:390
  17.4 7.2 %collective-permute-start.5 = (bf16[128,512]{1,0:T(8,128)(2,1)S(1)}, bf16[128,512]{1,0:T(8,128)(2,1)S(1)}, u32[]{:S(2)}, u32[]{:S(2)}) collective-permute-start(bf16[128,512]{1,0:T(8,128)(2,1)S(1)} %get-tuple-element.272), channel_id=1, source_target_pairs={{0,0},{1,1},{2,8},{3,9},{4,5},{5,4},{6,13},{7,12},{8,2},{9,3},{10,... | collective-permute-start | bytes 393224 | tf_op jit(solution)/shard_map/ppermute | solution.py:391
  20.2 7.6 %collective-permute-start.4 = (bf16[256,512]{1,0:T(8,128)(2,1)S(1)}, bf16[256,512]{1,0:T(8,128)(2,1)S(1)}, u32[]{:S(2)}, u32[]{:S(2)}) collective-permute-start(bf16[256,512]{1,0:T(8,128)(2,1)S(1)} %constant_dynamic-update-slice_fusion), channel_id=1, source_target_pairs={{0,16},{1,17},{2,18},{3,19},{4,20},{5,21},{6,22},{7,23},{8,24},{9,... | collective-permute-start | bytes 786440 | tf_op jit(solution)/shard_map/ppermute | solution.py:37
  27.9 2.0 %collective-permute-start.7 = (bf16[512,512]{1,0:T(8,128)(2,1)S(1)}, bf16[512,512]{1,0:T(8,128)(2,1)S(1)}, u32[]{:S(2)}, u32[]{:S(2)}) collective-permute-start(bf16[512,512]{1,0:T(8,128)(2,1)S(1)} %constant_dynamic-update-slice_fusion.4.held_ref), channel_id=1, source_target_pairs={{0,8},{1,9},{2,10},{3,11},{4,12},{5,13},{6,14},{7,15},{8,0},{9,1},... | collective-permute-start | bytes 1572872 | tf_op jit(solution)/shard_map/ppermute | solution.py:37
  28.0 7.5 %collective-permute-start.10 = (bf16[256,512]{1,0:T(8,128)(2,1)S(1)}, bf16[256,512]{1,0:T(8,128)(2,1)S(1)}, u32[]{:S(2)}, u32[]{:S(2)}) collective-permute-start(bf16[256,512]{1,0:T(8,128)(2,1)S(1)} %constant_dynamic-update-slice_fusion.2), channel_id=1, source_target_pairs={{0,16},{1,17},{2,18},{3,19},{4,20},{5,21},{6,22},{7,23},{8,24},{9,... | collective-permute-start | bytes 786440 | tf_op jit(solution)/shard_map/ppermute | solution.py:37
  32.4 7.5 %copy-start.2 = (bf16[4,512,448]{1,2,0:T(8,128)(2,1)S(1)}, bf16[4,512,448]{1,2,0:T(8,128)(2,1)}, u32[]{:S(2)}) copy-start(bf16[4,512,448]{1,2,0:T(8,128)(2,1)} %param.14) | copy-start | bytes 5505028
  35.6 4.3 %collective-permute-start.11 = (bf16[512,512]{1,0:T(8,128)(2,1)S(1)}, bf16[512,512]{1,0:T(8,128)(2,1)S(1)}, u32[]{:S(2)}, u32[]{:S(2)}) collective-permute-start(bf16[512,512]{1,0:T(8,128)(2,1)S(1)} %constant_dynamic-update-slice_fusion.6.held_ref), channel_id=1, source_target_pairs={{0,8},{1,9},{2,10},{3,11},{4,12},{5,13},{6,14},{7,15},{8,0},{9,1},... | collective-permute-start | bytes 1572872 | tf_op jit(solution)/shard_map/ppermute | solution.py:37
  36.9 7.9 %collective-permute-start.9 = (bf16[256,512]{1,0:T(8,128)(2,1)S(1)}, bf16[256,512]{1,0:T(8,128)(2,1)S(1)}, u32[]{:S(2)}, u32[]{:S(2)}) collective-permute-start(bf16[256,512]{1,0:T(8,128)(2,1)S(1)} %get-tuple-element.148), channel_id=1, source_target_pairs={{0,2},{1,3},{2,0},{3,1},{4,6},{5,7},{6,4},{7,5},{8,10},{9,11},{10,... | collective-permute-start | bytes 786440 | tf_op jit(solution)/shard_map/ppermute | solution.py:37
  37.0 8.0 %collective-permute-start.8 = (bf16[256,512]{1,0:T(8,128)(2,1)S(1)}, bf16[256,512]{1,0:T(8,128)(2,1)S(1)}, u32[]{:S(2)}, u32[]{:S(2)}) collective-permute-start(bf16[256,512]{1,0:T(8,128)(2,1)S(1)} %get-tuple-element.151), channel_id=1, source_target_pairs={{0,1},{1,0},{2,3},{3,2},{4,5},{5,4},{6,7},{7,6},{8,9},{9,8},{10,11... | collective-permute-start | bytes 786440 | tf_op jit(solution)/shard_map/ppermute | solution.py:37
  38.2 12.2 %collective-permute-start.16 = (bf16[256,512]{1,0:T(8,128)(2,1)S(1)}, bf16[256,512]{1,0:T(8,128)(2,1)S(1)}, u32[]{:S(2)}, u32[]{:S(2)}) collective-permute-start(bf16[256,512]{1,0:T(8,128)(2,1)S(1)} %get-tuple-element.169), channel_id=1, source_target_pairs={{0,2},{1,3},{2,0},{3,1},{4,6},{5,7},{6,4},{7,5},{8,10},{9,11},{10,... | collective-permute-start | bytes 786440 | tf_op jit(solution)/shard_map/ppermute | solution.py:37
  38.5 12.2 %collective-permute-start.15 = (bf16[256,512]{1,0:T(8,128)(2,1)S(1)}, bf16[256,512]{1,0:T(8,128)(2,1)S(1)}, u32[]{:S(2)}, u32[]{:S(2)}) collective-permute-start(bf16[256,512]{1,0:T(8,128)(2,1)S(1)} %get-tuple-element.167), channel_id=1, source_target_pairs={{0,1},{1,0},{2,3},{3,2},{4,5},{5,4},{6,7},{7,6},{8,9},{9,8},{10,11... | collective-permute-start | bytes 786440 | tf_op jit(solution)/shard_map/ppermute | solution.py:37
  41.3 14.8 %collective-permute-start.13 = (bf16[256,512]{1,0:T(8,128)(2,1)S(1)}, bf16[256,512]{1,0:T(8,128)(2,1)S(1)}, u32[]{:S(2)}, u32[]{:S(2)}) collective-permute-start(bf16[256,512]{1,0:T(8,128)(2,1)S(1)} %get-tuple-element.158), channel_id=1, source_target_pairs={{0,2},{1,3},{2,0},{3,1},{4,6},{5,7},{6,4},{7,5},{8,10},{9,11},{10,... | collective-permute-start | bytes 786440 | tf_op jit(solution)/shard_map/ppermute | solution.py:37
  44.8 8.1 %collective-permute-start.14 = (bf16[128,512]{1,0:T(8,128)(2,1)S(1)}, bf16[128,512]{1,0:T(8,128)(2,1)S(1)}, u32[]{:S(2)}, u32[]{:S(2)}) collective-permute-start(bf16[128,512]{1,0:T(8,128)(2,1)S(1)} %add_convert_fusion.11), channel_id=1, source_target_pairs={{0,1},{1,0},{2,3},{3,2},{4,5},{5,4},{6,7},{7,6},{8,9},{9,8},{10,11... | collective-permute-start | bytes 393224 | tf_op jit(solution)/shard_map/ppermute | solution.py:37
  45.0 13.8 %collective-permute-start.12 = (bf16[128,512]{1,0:T(8,128)(2,1)S(1)}, bf16[128,512]{1,0:T(8,128)(2,1)S(1)}, u32[]{:S(2)}, u32[]{:S(2)}) collective-permute-start(bf16[128,512]{1,0:T(8,128)(2,1)S(1)} %add_convert_fusion.10), channel_id=1, source_target_pairs={{0,2},{1,3},{2,0},{3,1},{4,6},{5,7},{6,4},{7,5},{8,10},{9,11},{10,... | collective-permute-start | bytes 393224 | tf_op jit(solution)/shard_map/ppermute | solution.py:37
  50.4 14.8 %copy-start.4 = (bf16[128,512]{1,0:T(8,128)(2,1)}, bf16[128,512]{1,0:T(8,128)(2,1)S(1)}, u32[]{:S(2)}) copy-start(bf16[128,512]{1,0:T(8,128)(2,1)S(1)} %slice.261) | copy-start | bytes 393220
  50.5 11.6 %collective-permute-start.20 = (bf16[128,512]{1,0:T(8,128)(2,1)S(1)}, bf16[128,512]{1,0:T(8,128)(2,1)S(1)}, u32[]{:S(2)}, u32[]{:S(2)}) collective-permute-start(bf16[128,512]{1,0:T(8,128)(2,1)S(1)} %add_convert_fusion.9), channel_id=1, source_target_pairs={{0,1},{1,0},{2,3},{3,2},{4,5},{5,4},{6,7},{7,6},{8,9},{9,8},{10,11... | collective-permute-start | bytes 393224 | tf_op jit(solution)/shard_map/ppermute | solution.py:37
  50.7 14.8 %collective-permute-start.18 = (bf16[128,512]{1,0:T(8,128)(2,1)S(1)}, bf16[128,512]{1,0:T(8,128)(2,1)S(1)}, u32[]{:S(2)}, u32[]{:S(2)}) collective-permute-start(bf16[128,512]{1,0:T(8,128)(2,1)S(1)} %add_convert_fusion.8), channel_id=1, source_target_pairs={{0,2},{1,3},{2,0},{3,1},{4,6},{5,7},{6,4},{7,5},{8,10},{9,11},{10,... | collective-permute-start | bytes 393224 | tf_op jit(solution)/shard_map/ppermute | solution.py:37
  53.0 7.9 %collective-permute-start.21 = (bf16[256,512]{1,0:T(8,128)(2,1)S(1)}, bf16[256,512]{1,0:T(8,128)(2,1)S(1)}, u32[]{:S(2)}, u32[]{:S(2)}) collective-permute-start(bf16[256,512]{1,0:T(8,128)(2,1)S(1)} %get-tuple-element.181), channel_id=1, source_target_pairs={{0,1},{1,0},{2,3},{3,2},{4,5},{5,4},{6,7},{7,6},{8,9},{9,8},{10,11... | collective-permute-start | bytes 786440 | tf_op jit(solution)/shard_map/ppermute | solution.py:37
  56.0 9.3 %collective-permute-start.19 = (bf16[64,512]{1,0:T(8,128)(2,1)S(1)}, bf16[64,512]{1,0:T(8,128)(2,1)S(1)}, u32[]{:S(2)}, u32[]{:S(2)}) collective-permute-start(bf16[64,512]{1,0:T(8,128)(2,1)S(1)} %add_convert_fusion.17), channel_id=1, source_target_pairs={{0,4},{1,5},{2,6},{3,7},{4,0},{5,1},{6,2},{7,3},{8,12},{9,13},{10,... | collective-permute-start | bytes 196616 | tf_op jit(solution)/shard_map/ppermute | solution.py:37
  61.0 8.6 %collective-permute-start.24 = (bf16[128,512]{1,0:T(8,128)(2,1)S(1)}, bf16[128,512]{1,0:T(8,128)(2,1)S(1)}, u32[]{:S(2)}, u32[]{:S(2)}) collective-permute-start(bf16[128,512]{1,0:T(8,128)(2,1)S(1)} %add_convert_fusion.6), channel_id=1, source_target_pairs={{0,2},{1,3},{2,0},{3,1},{4,6},{5,7},{6,4},{7,5},{8,10},{9,11},{10,... | collective-permute-start | bytes 393224 | tf_op jit(solution)/shard_map/ppermute | solution.py:37
  62.1 5.8 %collective-permute-start.17 = (bf16[64,512]{1,0:T(8,128)(2,1)S(1)}, bf16[64,512]{1,0:T(8,128)(2,1)S(1)}, u32[]{:S(2)}, u32[]{:S(2)}) collective-permute-start(bf16[64,512]{1,0:T(8,128)(2,1)S(1)} %add_convert_fusion.16), channel_id=1, source_target_pairs={{0,4},{1,5},{2,6},{3,7},{4,0},{5,1},{6,2},{7,3},{8,12},{9,13},{10,... | collective-permute-start | bytes 196616 | tf_op jit(solution)/shard_map/ppermute | solution.py:37
  64.7 3.8 %collective-permute-start.25 = (bf16[128,512]{1,0:T(8,128)(2,1)S(1)}, bf16[128,512]{1,0:T(8,128)(2,1)S(1)}, u32[]{:S(2)}, u32[]{:S(2)}) collective-permute-start(bf16[128,512]{1,0:T(8,128)(2,1)S(1)} %add_convert_fusion.7), channel_id=1, source_target_pairs={{0,1},{1,0},{2,3},{3,2},{4,5},{5,4},{6,7},{7,6},{8,9},{9,8},{10,11... | collective-permute-start | bytes 393224 | tf_op jit(solution)/shard_map/ppermute | solution.py:37
  65.3 5.8 %slice-start = ((bf16[128,512]{1,0:T(8,128)(2,1)}), bf16[64,512]{1,0:T(8,128)(2,1)S(1)}, s32[]{:S(2)}) async-start(bf16[128,512]{1,0:T(8,128)(2,1)} %copy-done.4), calls=%async_computation | async-start | bytes 131072 | tf_op jit(solution)/shard_map/slice | solution.py:99
  65.3 5.8 %collective-permute-start.23 = (bf16[64,512]{1,0:T(8,128)(2,1)S(1)}, bf16[64,512]{1,0:T(8,128)(2,1)S(1)}, u32[]{:S(2)}, u32[]{:S(2)}) collective-permute-start(bf16[64,512]{1,0:T(8,128)(2,1)S(1)} %add_convert_fusion.15), channel_id=1, source_target_pairs={{0,4},{1,5},{2,6},{3,7},{4,0},{5,1},{6,2},{7,3},{8,12},{9,13},{10,... | collective-permute-start | bytes 196616 | tf_op jit(solution)/shard_map/ppermute | solution.py:37
  65.5 9.0 %collective-permute-start.22 = (bf16[64,512]{1,0:T(8,128)(2,1)S(1)}, bf16[64,512]{1,0:T(8,128)(2,1)S(1)}, u32[]{:S(2)}, u32[]{:S(2)}) collective-permute-start(bf16[64,512]{1,0:T(8,128)(2,1)S(1)} %add_convert_fusion.14), channel_id=1, source_target_pairs={{0,4},{1,5},{2,6},{3,7},{4,0},{5,1},{6,2},{7,3},{8,12},{9,13},{10,... | collective-permute-start | bytes 196616 | tf_op jit(solution)/shard_map/ppermute | solution.py:37
  68.6 9.4 %collective-permute-start.29 = (bf16[64,512]{1,0:T(8,128)(2,1)S(1)}, bf16[64,512]{1,0:T(8,128)(2,1)S(1)}, u32[]{:S(2)}, u32[]{:S(2)}) collective-permute-start(bf16[64,512]{1,0:T(8,128)(2,1)S(1)} %add_convert_fusion.13), channel_id=1, source_target_pairs={{0,4},{1,5},{2,6},{3,7},{4,0},{5,1},{6,2},{7,3},{8,12},{9,13},{10,... | collective-permute-start | bytes 196616 | tf_op jit(solution)/shard_map/ppermute | solution.py:37
  69.6 10.9 %collective-permute-start.28 = (bf16[64,512]{1,0:T(8,128)(2,1)S(1)}, bf16[64,512]{1,0:T(8,128)(2,1)S(1)}, u32[]{:S(2)}, u32[]{:S(2)}) collective-permute-start(bf16[64,512]{1,0:T(8,128)(2,1)S(1)} %add_convert_fusion.12), channel_id=1, source_target_pairs={{0,4},{1,5},{2,6},{3,7},{4,0},{5,1},{6,2},{7,3},{8,12},{9,13},{10,... | collective-permute-start | bytes 196616 | tf_op jit(solution)/shard_map/ppermute | solution.py:37
  74.6 11.8 %collective-permute-start.26 = (bf16[64,512]{1,0:T(8,128)(2,1)S(1)}, bf16[64,512]{1,0:T(8,128)(2,1)S(1)}, u32[]{:S(2)}, u32[]{:S(2)}) collective-permute-start(bf16[64,512]{1,0:T(8,128)(2,1)S(1)} %multiply_convert_fusion.5), channel_id=1, source_target_pairs={{0,4},{1,5},{2,6},{3,7},{4,0},{5,1},{6,2},{7,3},{8,12},{9,13},{10,... | collective-permute-start | bytes 196616 | tf_op jit(solution)/shard_map/ppermute | solution.py:37
  77.9 7.5 %collective-permute-start.27 = (bf16[64,512]{1,0:T(8,128)(2,1)S(1)}, bf16[64,512]{1,0:T(8,128)(2,1)S(1)}, u32[]{:S(2)}, u32[]{:S(2)}) collective-permute-start(bf16[64,512]{1,0:T(8,128)(2,1)S(1)} %get-tuple-element.204), channel_id=1, source_target_pairs={{0,4},{1,5},{2,6},{3,7},{4,0},{5,1},{6,2},{7,3},{8,12},{9,13},{10,... | collective-permute-start | bytes 196616 | tf_op jit(solution)/shard_map/ppermute | solution.py:37
  78.1 11.5 %collective-permute-start.33 = (bf16[64,512]{1,0:T(8,128)(2,1)S(1)}, bf16[64,512]{1,0:T(8,128)(2,1)S(1)}, u32[]{:S(2)}, u32[]{:S(2)}) collective-permute-start(bf16[64,512]{1,0:T(8,128)(2,1)S(1)} %get-tuple-element.208), channel_id=1, source_target_pairs={{0,4},{1,5},{2,6},{3,7},{4,0},{5,1},{6,2},{7,3},{8,12},{9,13},{10,... | collective-permute-start | bytes 196616 | tf_op jit(solution)/shard_map/ppermute | solution.py:37
  80.5 10.1 %collective-permute-start.32 = (bf16[64,512]{1,0:T(8,128)(2,1)S(1)}, bf16[64,512]{1,0:T(8,128)(2,1)S(1)}, u32[]{:S(2)}, u32[]{:S(2)}) collective-permute-start(bf16[64,512]{1,0:T(8,128)(2,1)S(1)} %get-tuple-element.210), channel_id=1, source_target_pairs={{0,4},{1,5},{2,6},{3,7},{4,0},{5,1},{6,2},{7,3},{8,12},{9,13},{10,... | collective-permute-start | bytes 196616 | tf_op jit(solution)/shard_map/ppermute | solution.py:37
  85.4 6.1 %collective-permute-start.31 = (bf16[128,512]{1,0:T(8,128)(2,1)S(1)}, bf16[128,512]{1,0:T(8,128)(2,1)S(1)}, u32[]{:S(2)}, u32[]{:S(2)}) collective-permute-start(bf16[128,512]{1,0:T(8,128)(2,1)S(1)} %constant_dynamic-update-slice_fusion.8), channel_id=1, source_target_pairs={{0,1},{1,0},{2,3},{3,2},{4,5},{5,4},{6,7},{7,6},{8,9},{9,8},{10,11... | collective-permute-start | bytes 393224 | tf_op jit(solution)/shard_map/ppermute | solution.py:37
  86.4 6.1 %collective-permute-start.30 = (bf16[128,512]{1,0:T(8,128)(2,1)S(1)}, bf16[128,512]{1,0:T(8,128)(2,1)S(1)}, u32[]{:S(2)}, u32[]{:S(2)}) collective-permute-start(bf16[128,512]{1,0:T(8,128)(2,1)S(1)} %constant_dynamic-update-slice_fusion.10), channel_id=1, source_target_pairs={{0,2},{1,3},{2,0},{3,1},{4,6},{5,7},{6,4},{7,5},{8,10},{9,11},{10,... | collective-permute-start | bytes 393224 | tf_op jit(solution)/shard_map/ppermute | solution.py:37
  88.3 7.0 %collective-permute-start.38 = (bf16[64,512]{1,0:T(8,128)(2,1)S(1)}, bf16[64,512]{1,0:T(8,128)(2,1)S(1)}, u32[]{:S(2)}, u32[]{:S(2)}) collective-permute-start(bf16[64,512]{1,0:T(8,128)(2,1)S(1)} %get-tuple-element.220), channel_id=1, source_target_pairs={{0,4},{1,5},{2,6},{3,7},{4,0},{5,1},{6,2},{7,3},{8,12},{9,13},{10,... | collective-permute-start | bytes 196616 | tf_op jit(solution)/shard_map/ppermute | solution.py:37
  89.6 4.5 %collective-permute-start.39 = (bf16[64,512]{1,0:T(8,128)(2,1)S(1)}, bf16[64,512]{1,0:T(8,128)(2,1)S(1)}, u32[]{:S(2)}, u32[]{:S(2)}) collective-permute-start(bf16[64,512]{1,0:T(8,128)(2,1)S(1)} %get-tuple-element.218), channel_id=1, source_target_pairs={{0,4},{1,5},{2,6},{3,7},{4,0},{5,1},{6,2},{7,3},{8,12},{9,13},{10,... | collective-permute-start | bytes 196616 | tf_op jit(solution)/shard_map/ppermute | solution.py:37
  90.7 5.1 %collective-permute-start.37 = (bf16[128,512]{1,0:T(8,128)(2,1)S(1)}, bf16[128,512]{1,0:T(8,128)(2,1)S(1)}, u32[]{:S(2)}, u32[]{:S(2)}) collective-permute-start(bf16[128,512]{1,0:T(8,128)(2,1)S(1)} %constant_dynamic-update-slice_fusion.12), channel_id=1, source_target_pairs={{0,1},{1,0},{2,3},{3,2},{4,5},{5,4},{6,7},{7,6},{8,9},{9,8},{10,11... | collective-permute-start | bytes 393224 | tf_op jit(solution)/shard_map/ppermute | solution.py:37
  91.6 6.1 %collective-permute-start.36 = (bf16[128,512]{1,0:T(8,128)(2,1)S(1)}, bf16[128,512]{1,0:T(8,128)(2,1)S(1)}, u32[]{:S(2)}, u32[]{:S(2)}) collective-permute-start(bf16[128,512]{1,0:T(8,128)(2,1)S(1)} %constant_dynamic-update-slice_fusion.14), channel_id=1, source_target_pairs={{0,2},{1,3},{2,0},{3,1},{4,6},{5,7},{6,4},{7,5},{8,10},{9,11},{10,... | collective-permute-start | bytes 393224 | tf_op jit(solution)/shard_map/ppermute | solution.py:37
  92.5 10.0 %collective-permute-start.35 = (bf16[256,512]{1,0:T(8,128)(2,1)S(1)}, bf16[256,512]{1,0:T(8,128)(2,1)S(1)}, u32[]{:S(2)}, u32[]{:S(2)}) collective-permute-start(bf16[256,512]{1,0:T(8,128)(2,1)S(1)} %constant_dynamic-update-slice_fusion.16.refs_2_), channel_id=1, source_target_pairs={{0,2},{1,3},{2,0},{3,1},{4,6},{5,7},{6,4},{7,5},{8,10},{9,11},{10,... | collective-permute-start | bytes 786440 | tf_op jit(solution)/shard_map/ppermute | solution.py:37
  94.1 6.8 %collective-permute-start.34 = (bf16[256,512]{1,0:T(8,128)(2,1)S(1)}, bf16[256,512]{1,0:T(8,128)(2,1)S(1)}, u32[]{:S(2)}, u32[]{:S(2)}) collective-permute-start(bf16[256,512]{1,0:T(8,128)(2,1)S(1)} %constant_dynamic-update-slice_fusion.18.refs_0_), channel_id=1, source_target_pairs={{0,1},{1,0},{2,3},{3,2},{4,5},{5,4},{6,7},{7,6},{8,9},{9,8},{10,11... | collective-permute-start | bytes 786440 | tf_op jit(solution)/shard_map/ppermute | solution.py:37
  95.3 19.2 %collective-permute-start.42 = (bf16[128,512]{1,0:T(8,128)(2,1)S(1)}, bf16[128,512]{1,0:T(8,128)(2,1)S(1)}, u32[]{:S(2)}, u32[]{:S(2)}) collective-permute-start(bf16[128,512]{1,0:T(8,128)(2,1)S(1)} %constant_dynamic-update-slice_fusion.20), channel_id=1, source_target_pairs={{0,1},{1,0},{2,3},{3,2},{4,5},{5,4},{6,7},{7,6},{8,9},{9,8},{10,11... | collective-permute-start | bytes 393224 | tf_op jit(solution)/shard_map/ppermute | solution.py:37
  95.8 18.7 %collective-permute-start.41 = (bf16[128,512]{1,0:T(8,128)(2,1)S(1)}, bf16[128,512]{1,0:T(8,128)(2,1)S(1)}, u32[]{:S(2)}, u32[]{:S(2)}) collective-permute-start(bf16[128,512]{1,0:T(8,128)(2,1)S(1)} %constant_dynamic-update-slice_fusion.22), channel_id=1, source_target_pairs={{0,2},{1,3},{2,0},{3,1},{4,6},{5,7},{6,4},{7,5},{8,10},{9,11},{10,... | collective-permute-start | bytes 393224 | tf_op jit(solution)/shard_map/ppermute | solution.py:37
  97.7 18.8 %collective-permute-start.47 = (bf16[256,512]{1,0:T(8,128)(2,1)S(1)}, bf16[256,512]{1,0:T(8,128)(2,1)S(1)}, u32[]{:S(2)}, u32[]{:S(2)}) collective-permute-start(bf16[256,512]{1,0:T(8,128)(2,1)S(1)} %constant_dynamic-update-slice_fusion.24.refs_2_), channel_id=1, source_target_pairs={{0,2},{1,3},{2,0},{3,1},{4,6},{5,7},{6,4},{7,5},{8,10},{9,11},{10,... | collective-permute-start | bytes 786440 | tf_op jit(solution)/shard_map/ppermute | solution.py:37
  100.9 15.6 %collective-permute-start.46 = (bf16[256,512]{1,0:T(8,128)(2,1)S(1)}, bf16[256,512]{1,0:T(8,128)(2,1)S(1)}, u32[]{:S(2)}, u32[]{:S(2)}) collective-permute-start(bf16[256,512]{1,0:T(8,128)(2,1)S(1)} %constant_dynamic-update-slice_fusion.26.refs_0_), channel_id=1, source_target_pairs={{0,1},{1,0},{2,3},{3,2},{4,5},{5,4},{6,7},{7,6},{8,9},{9,8},{10,11... | collective-permute-start | bytes 786440 | tf_op jit(solution)/shard_map/ppermute | solution.py:37
  105.9 10.1 %collective-permute-start.40 = (bf16[512,448]{1,0:T(8,128)(2,1)S(1)}, bf16[512,448]{1,0:T(8,128)(2,1)S(1)}, u32[]{:S(2)}, u32[]{:S(2)}) collective-permute-start(bf16[512,448]{1,0:T(8,128)(2,1)S(1)} %get-tuple-element.231), channel_id=1, source_target_pairs={{0,8},{1,9},{2,10},{3,11},{4,12},{5,13},{6,14},{7,15},{8,0},{9,1},... | collective-permute-start | bytes 1376264 | tf_op jit(solution)/shard_map/ppermute | solution.py:37
  114.6 8.2 %collective-permute-start.44 = (bf16[256,512]{1,0:T(8,128)(2,1)S(1)}, bf16[256,512]{1,0:T(8,128)(2,1)S(1)}, u32[]{:S(2)}, u32[]{:S(2)}) collective-permute-start(bf16[256,512]{1,0:T(8,128)(2,1)S(1)} %constant_dynamic-update-slice_fusion.30.refs_0_), channel_id=1, source_target_pairs={{0,1},{1,0},{2,3},{3,2},{4,5},{5,4},{6,7},{7,6},{8,9},{9,8},{10,11... | collective-permute-start | bytes 786440 | tf_op jit(solution)/shard_map/ppermute | solution.py:37
  114.9 7.8 %collective-permute-start.45 = (bf16[256,512]{1,0:T(8,128)(2,1)S(1)}, bf16[256,512]{1,0:T(8,128)(2,1)S(1)}, u32[]{:S(2)}, u32[]{:S(2)}) collective-permute-start(bf16[256,512]{1,0:T(8,128)(2,1)S(1)} %constant_dynamic-update-slice_fusion.28.refs_2_), channel_id=1, source_target_pairs={{0,2},{1,3},{2,0},{3,1},{4,6},{5,7},{6,4},{7,5},{8,10},{9,11},{10,... | collective-permute-start | bytes 786440 | tf_op jit(solution)/shard_map/ppermute | solution.py:37
  116.1 10.9 %collective-permute-start.43 = (bf16[256,448]{1,0:T(8,128)(2,1)S(1)}, bf16[256,448]{1,0:T(8,128)(2,1)S(1)}, u32[]{:S(2)}, u32[]{:S(2)}) collective-permute-start(bf16[256,448]{1,0:T(8,128)(2,1)S(1)} %add_convert_fusion.1), channel_id=1, source_target_pairs={{0,16},{1,17},{2,18},{3,19},{4,20},{5,21},{6,22},{7,23},{8,24},{9,... | collective-permute-start | bytes 688136 | tf_op jit(solution)/shard_map/ppermute | solution.py:37
  126.0 2.5 %collective-permute-start.50 = (bf16[512,448]{1,0:T(8,128)(2,1)S(1)}, bf16[512,448]{1,0:T(8,128)(2,1)S(1)}, u32[]{:S(2)}, u32[]{:S(2)}) collective-permute-start(bf16[512,448]{1,0:T(8,128)(2,1)S(1)} %get-tuple-element.247), channel_id=1, source_target_pairs={{0,8},{1,9},{2,10},{3,11},{4,12},{5,13},{6,14},{7,15},{8,0},{9,1},... | collective-permute-start | bytes 1376264 | tf_op jit(solution)/shard_map/ppermute | solution.py:37
  128.6 9.6 %collective-permute-start.51 = (bf16[256,448]{1,0:T(8,128)(2,1)S(1)}, bf16[256,448]{1,0:T(8,128)(2,1)S(1)}, u32[]{:S(2)}, u32[]{:S(2)}) collective-permute-start(bf16[256,448]{1,0:T(8,128)(2,1)S(1)} %add_convert_fusion), channel_id=1, source_target_pairs={{0,16},{1,17},{2,18},{3,19},{4,20},{5,21},{6,22},{7,23},{8,24},{9,... | collective-permute-start | bytes 688136 | tf_op jit(solution)/shard_map/ppermute | solution.py:37
  129.8 19.3 %collective-permute-start.48 = (bf16[128,448]{1,0:T(8,128)(2,1)S(1)}, bf16[128,448]{1,0:T(8,128)(2,1)S(1)}, u32[]{:S(2)}, u32[]{:S(2)}) collective-permute-start(bf16[128,448]{1,0:T(8,128)(2,1)S(1)} %get-tuple-element.266), channel_id=1, source_target_pairs={{0,0},{1,1},{8,2},{9,3},{16,4},{17,5},{24,6},{25,7},{2,8},{3,9},{1... | collective-permute-start | bytes 344072 | tf_op jit(solution)/shard_map/ppermute | solution.py:144
  134.0 15.1 %collective-permute-start.49 = (bf16[128,448]{1,0:T(8,128)(2,1)S(1)}, bf16[128,448]{1,0:T(8,128)(2,1)S(1)}, u32[]{:S(2)}, u32[]{:S(2)}) collective-permute-start(bf16[128,448]{1,0:T(8,128)(2,1)S(1)} %get-tuple-element.265), channel_id=1, source_target_pairs={{17,0},{16,1},{25,2},{24,3},{1,4},{0,5},{9,6},{8,7},{19,8},{18,9},... | collective-permute-start | bytes 344072 | tf_op jit(solution)/shard_map/ppermute | solution.py:144
  138.3 11.6 %collective-permute-start.53 = (bf16[128,448]{1,0:T(8,128)(2,1)S(1)}, bf16[128,448]{1,0:T(8,128)(2,1)S(1)}, u32[]{:S(2)}, u32[]{:S(2)}) collective-permute-start(bf16[128,448]{1,0:T(8,128)(2,1)S(1)} %get-tuple-element.263), channel_id=1, source_target_pairs={{17,0},{16,1},{25,2},{24,3},{1,4},{0,5},{9,6},{8,7},{19,8},{18,9},... | collective-permute-start | bytes 344072 | tf_op jit(solution)/shard_map/ppermute | solution.py:144
  142.0 7.1 %copy-start.3 = (f32[128,1]{0,1:T(1,128)S(1)}, f32[128,1]{0,1:T(1,128)}, u32[]{:S(2)}) copy-start(f32[128,1]{0,1:T(1,128)} %param.10) | copy-start | bytes 1540
  142.0 9.3 %collective-permute-start.52 = (bf16[128,448]{1,0:T(8,128)(2,1)S(1)}, bf16[128,448]{1,0:T(8,128)(2,1)S(1)}, u32[]{:S(2)}, u32[]{:S(2)}) collective-permute-start(bf16[128,448]{1,0:T(8,128)(2,1)S(1)} %get-tuple-element.264), channel_id=1, source_target_pairs={{0,0},{1,1},{8,2},{9,3},{16,4},{17,5},{24,6},{25,7},{2,8},{3,9},{1... | collective-permute-start | bytes 344072 | tf_op jit(solution)/shard_map/ppermute | solution.py:144

commit v7 on v6

--- a/solution.py
+++ b/solution.py
@@ -362,7 +362,7 @@
             in_specs=in_specs or [full(a.shape) for a in args],
             out_specs=kw.get("out_specs") or jax.tree.map(lambda o: full(o.shape), out_shape),
             compiler_params=pltpu.CompilerParams(vmem_limit_bytes=kw.get("room", ROOM) << 20),
-            cost_estimate=pl.CostEstimate(flops=1, bytes_accessed=1, transcendentals=0),
+            cost_estimate=pl.CostEstimate(flops=10**9, bytes_accessed=2*10**6, transcendentals=0),
             name=name,
         )(*args)
 

time: 155 us -> 152 us (0.981); the launches traced: 152 us -> 151 us
  starting transfers between devices: 79.9 us -> 77.1 us
where the time goes in v7:
time: 152 us; the launch traced here: 151 us
  starting transfers between devices  77.1 us (51%)
  waiting for transfers between devices  35.3 us (23%)
  Pallas kernels  33.5 us (22%)
  other arithmetic  2.09 us (1%)
  local copies, waits for them, and re-layouts  1.97 us (1%)
    ppermute x46, starting transfers between devices, swap(): return lax.ppermute(block, AXES, pairs)  55.8 us
    pallas_call x14, Pallas kernels, call(): pl.pallas_call(body, out_shape=out_shape, grid=kw.get('grid', (1,)), in_s...  33.5 us
    ppermute x46, waiting for transfers between devices, swap(): return lax.ppermute(block, AXES, pairs)  30.2 us
    ppermute x4, starting transfers between devices, leave(): self.pieces[k] = lax.ppermute(piece, AXES, back)  10.2 us
    ppermute x2, starting transfers between devices, land(): return [lax.ppermute(near, AXES, column_pairs(0)), far]  5.8 us
    ppermute x2, starting transfers between devices, land(): far = lax.ppermute(far, AXES, column_pairs(1))  5.28 us
  transfers between devices with their start and end apart: 54, of which 22 were waited for; matrix products, arithmetic and copies ran while one was open for 2% of the time, Pallas kernels for 20%

profile of v7, /device:TPU:17, one launch (start us, length us, event | category | flops | bytes accessed | tf_op | source)
XLA Modules:
  0.0 151.2 jit_solution(2851739374335731474)
XLA Ops:
  0.6 1.9 %token_pieces.1 = (bf16[128,512]{1,0:T(8,128)(2,1)}, bf16[128,512]{1,0:T(8,128)(2,1)}) custom-call(s32[4]{0:T(128)} %hot_ref.1, s32[1,128]{1,0:T(1,128)} %bitcast.10, bf16[128,896]{1,0:T(8,128)(2,1)} %tokens_ref.1), custom_call_target="tpu_custom_call" | custom-call | flops 1000000000 | bytes 2000000 | tf_op jit(solution)/shard_map/token_pieces/pallas_call | solution.py:358
  2.5 1.2 collective-permute-start
  3.7 1.9 %cotangent_pieces.1 = (bf16[128,512]{1,0:T(8,128)(2,1)}, bf16[128,512]{1,0:T(8,128)(2,1)}) custom-call(f32[1,128]{1,0:T(1,128)} %bitcast.7, bf16[128,896]{1,0:T(8,128)(2,1)} %rows_ref.1), custom_call_target="tpu_custom_call" | custom-call | flops 1000000000 | bytes 2000000 | tf_op jit(solution)/shard_map/cotangent_pieces/pallas_call | solution.py:358
  5.9 1.2 collective-permute-done
  7.1 2.6 %collective-permute-start.2 = (bf16[128,512]{1,0:T(8,128)(2,1)S(1)}, bf16[128,512]{1,0:T(8,128)(2,1)S(1)}, u32[]{:S(2)}, u32[]{:S(2)}) collective-permute-start(bf16[128,512]{1,0:T(8,128)(2,1)S(1)} %get-tuple-element.273), channel_id=1, source_target_pairs={{0,4},{1,5},{2,12},{3,13},{4,1},{5,0},{6,9},{7,8},{8,6},{9,7},{10,... | collective-permute-start | bytes 393224 | tf_op jit(solution)/shard_map/ppermute | solution.py:390
  9.7 3.0 %collective-permute-start.1 = (bf16[128,512]{1,0:T(8,128)(2,1)S(1)}, bf16[128,512]{1,0:T(8,128)(2,1)S(1)}, u32[]{:S(2)}, u32[]{:S(2)}) collective-permute-start(bf16[128,512]{1,0:T(8,128)(2,1)S(1)} %get-tuple-element.274), channel_id=1, source_target_pairs={{0,0},{1,1},{2,8},{3,9},{4,5},{5,4},{6,13},{7,12},{8,2},{9,3},{10,... | collective-permute-start | bytes 393224 | tf_op jit(solution)/shard_map/ppermute | solution.py:391
  12.8 0.9 broadcast_select_fusion
  13.7 2.7 %collective-permute-start.6 = (bf16[128,512]{1,0:T(8,128)(2,1)S(1)}, bf16[128,512]{1,0:T(8,128)(2,1)S(1)}, u32[]{:S(2)}, u32[]{:S(2)}) collective-permute-start(bf16[128,512]{1,0:T(8,128)(2,1)S(1)} %get-tuple-element.271), channel_id=1, source_target_pairs={{0,4},{1,5},{2,12},{3,13},{4,1},{5,0},{6,9},{7,8},{8,6},{9,7},{10,... | collective-permute-start | bytes 393224 | tf_op jit(solution)/shard_map/ppermute | solution.py:390
  16.4 2.8 %collective-permute-start.5 = (bf16[128,512]{1,0:T(8,128)(2,1)S(1)}, bf16[128,512]{1,0:T(8,128)(2,1)S(1)}, u32[]{:S(2)}, u32[]{:S(2)}) collective-permute-start(bf16[128,512]{1,0:T(8,128)(2,1)S(1)} %get-tuple-element.272), channel_id=1, source_target_pairs={{0,0},{1,1},{2,8},{3,9},{4,5},{5,4},{6,13},{7,12},{8,2},{9,3},{10,... | collective-permute-start | bytes 393224 | tf_op jit(solution)/shard_map/ppermute | solution.py:391
  19.2 1.9 %collective-permute-start.4 = (bf16[256,512]{1,0:T(8,128)(2,1)S(1)}, bf16[256,512]{1,0:T(8,128)(2,1)S(1)}, u32[]{:S(2)}, u32[]{:S(2)}) collective-permute-start(bf16[256,512]{1,0:T(8,128)(2,1)S(1)} %constant_dynamic-update-slice_fusion), channel_id=1, source_target_pairs={{0,16},{1,17},{2,18},{3,19},{4,20},{5,21},{6,22},{7,23},{8,24},{9,... | collective-permute-start | bytes 786440 | tf_op jit(solution)/shard_map/ppermute | solution.py:37
  21.7 1.9 %collective-permute-done.5 = bf16[128,512]{1,0:T(8,128)(2,1)S(1)} collective-permute-done((bf16[128,512]{1,0:T(8,128)(2,1)S(1)}, bf16[128,512]{1,0:T(8,128)(2,1)S(1)}, u32[]{:S(2)}, u32[]{:S(2)}) %collective-permute-start.5) | collective-permute-done | bytes 131104 | tf_op jit(solution)/shard_map/ppermute | solution.py:391
  23.6 3.2 %collective-permute-done.4 = bf16[256,512]{1,0:T(8,128)(2,1)S(1)} collective-permute-done((bf16[256,512]{1,0:T(8,128)(2,1)S(1)}, bf16[256,512]{1,0:T(8,128)(2,1)S(1)}, u32[]{:S(2)}, u32[]{:S(2)}) %collective-permute-start.4) | collective-permute-done | bytes 262176 | tf_op jit(solution)/shard_map/ppermute | solution.py:37
  27.3 1.6 %collective-permute-done.7.got_ref = bf16[512,512]{1,0:T(8,128)(2,1)S(1)} collective-permute-done((bf16[512,512]{1,0:T(8,128)(2,1)S(1)}, bf16[512,512]{1,0:T(8,128)(2,1)S(1)}, u32[]{:S(2)}, u32[]{:S(2)}) %collective-permute-start.7) | collective-permute-done | bytes 524320 | tf_op jit(solution)/shard_map/ppermute | solution.py:37
  28.9 1.5 copy-done.1
  30.4 2.5 %gate_up_first.1 = (bf16[256,512]{1,0:T(8,128)(2,1)S(1)}, bf16[256,512]{1,0:T(8,128)(2,1)S(1)}, bf16[256,512]{1,0:T(8,128)(2,1)S(1)}, bf16[256,512]{1,0:T(8,128)(2,1)S(1)}, bf16[1024,512]{1,0:T(8,128)(2,1)S(1)}) custom-call(bf16[512,512]{1,0:T(8,128)(2,1)S(1)} %constant_dynamic-update-slice_fusion.4.held_ref, ...), custom_call_target="tpu_custom_call" | custom-call | flops 1000000000 | bytes 2000000 | tf_op jit(solution)/shard_map/gate_up_first/pallas_call | solution.py:358
  32.8 2.3 %gate_up_later.1 = (bf16[256,512]{1,0:T(8,128)(2,1)S(1)}, bf16[256,512]{1,0:T(8,128)(2,1)S(1)}, bf16[256,512]{1,0:T(8,128)(2,1)S(1)}, bf16[256,512]{1,0:T(8,128)(2,1)S(1)}) custom-call(bf16[1024,512]{1,0:T(8,128)(2,1)S(1)} %get-tuple-element.256.id_ref.rows_ref.refs_0_, bf16[1024,512]{1,0:T(8,128)(2,1)S(1)} %get-tuple-element.256.id_ref.rows_ref.refs_0_, ...), custom_call_target="tpu_custom_call" | custom-call | flops 1000000000 | bytes 2000000 | tf_op jit(solution)/shard_map/gate_up_later/pallas_call | solution.py:358
  35.9 1.2 collective-permute-start.8
  37.4 1.4 collective-permute-start.15
  38.8 1.4 act_grad_first.1
  40.3 1.3 act_grad_later.1
  41.6 2.1 %collective-permute-done.9 = bf16[256,512]{1,0:T(8,128)(2,1)S(1)} collective-permute-done((bf16[256,512]{1,0:T(8,128)(2,1)S(1)}, bf16[256,512]{1,0:T(8,128)(2,1)S(1)}, u32[]{:S(2)}, u32[]{:S(2)}) %collective-permute-start.9) | collective-permute-done | bytes 262176 | tf_op jit(solution)/shard_map/ppermute | solution.py:37
  43.9 1.3 collective-permute-start.12
  45.2 4.1 %collective-permute-done.16 = bf16[256,512]{1,0:T(8,128)(2,1)S(1)} collective-permute-done((bf16[256,512]{1,0:T(8,128)(2,1)S(1)}, bf16[256,512]{1,0:T(8,128)(2,1)S(1)}, u32[]{:S(2)}, u32[]{:S(2)}) %collective-permute-start.16) | collective-permute-done | bytes 262176 | tf_op jit(solution)/shard_map/ppermute | solution.py:37
  49.6 1.3 collective-permute-start.18
  50.9 0.9 collective-permute-done.14
  51.9 1.2 collective-permute-start.21
  53.2 1.8 %collective-permute-done.13 = bf16[256,512]{1,0:T(8,128)(2,1)S(1)} collective-permute-done((bf16[256,512]{1,0:T(8,128)(2,1)S(1)}, bf16[256,512]{1,0:T(8,128)(2,1)S(1)}, u32[]{:S(2)}, u32[]{:S(2)}) %collective-permute-start.13) | collective-permute-done | bytes 262176 | tf_op jit(solution)/shard_map/ppermute | solution.py:37
  55.0 2.5 %collective-permute-start.19 = (bf16[64,512]{1,0:T(8,128)(2,1)S(1)}, bf16[64,512]{1,0:T(8,128)(2,1)S(1)}, u32[]{:S(2)}, u32[]{:S(2)}) collective-permute-start(bf16[64,512]{1,0:T(8,128)(2,1)S(1)} %add_convert_fusion.17), channel_id=1, source_target_pairs={{0,4},{1,5},{2,6},{3,7},{4,0},{5,1},{6,2},{7,3},{8,12},{9,13},{10,... | collective-permute-start | bytes 196616 | tf_op jit(solution)/shard_map/ppermute | solution.py:37
  57.8 2.1 %collective-permute-done.21 = bf16[256,512]{1,0:T(8,128)(2,1)S(1)} collective-permute-done((bf16[256,512]{1,0:T(8,128)(2,1)S(1)}, bf16[256,512]{1,0:T(8,128)(2,1)S(1)}, u32[]{:S(2)}, u32[]{:S(2)}) %collective-permute-start.21) | collective-permute-done | bytes 262176 | tf_op jit(solution)/shard_map/ppermute | solution.py:37
  59.9 1.1 collective-permute-start.24
  61.1 2.6 %collective-permute-start.17 = (bf16[64,512]{1,0:T(8,128)(2,1)S(1)}, bf16[64,512]{1,0:T(8,128)(2,1)S(1)}, u32[]{:S(2)}, u32[]{:S(2)}) collective-permute-start(bf16[64,512]{1,0:T(8,128)(2,1)S(1)} %add_convert_fusion.16), channel_id=1, source_target_pairs={{0,4},{1,5},{2,6},{3,7},{4,0},{5,1},{6,2},{7,3},{8,12},{9,13},{10,... | collective-permute-start | bytes 196616 | tf_op jit(solution)/shard_map/ppermute | solution.py:37
  64.4 2.4 %collective-permute-start.22 = (bf16[64,512]{1,0:T(8,128)(2,1)S(1)}, bf16[64,512]{1,0:T(8,128)(2,1)S(1)}, u32[]{:S(2)}, u32[]{:S(2)}) collective-permute-start(bf16[64,512]{1,0:T(8,128)(2,1)S(1)} %add_convert_fusion.14), channel_id=1, source_target_pairs={{0,4},{1,5},{2,6},{3,7},{4,0},{5,1},{6,2},{7,3},{8,12},{9,13},{10,... | collective-permute-start | bytes 196616 | tf_op jit(solution)/shard_map/ppermute | solution.py:37
  67.6 0.9 collective-permute-start.29
  68.6 1.6 %collective-permute-start.28 = (bf16[64,512]{1,0:T(8,128)(2,1)S(1)}, bf16[64,512]{1,0:T(8,128)(2,1)S(1)}, u32[]{:S(2)}, u32[]{:S(2)}) collective-permute-start(bf16[64,512]{1,0:T(8,128)(2,1)S(1)} %add_convert_fusion.12), channel_id=1, source_target_pairs={{0,4},{1,5},{2,6},{3,7},{4,0},{5,1},{6,2},{7,3},{8,12},{9,13},{10,... | collective-permute-start | bytes 196616 | tf_op jit(solution)/shard_map/ppermute | solution.py:37
  70.2 3.5 %collective-permute-done.22 = bf16[64,512]{1,0:T(8,128)(2,1)S(1)} collective-permute-done((bf16[64,512]{1,0:T(8,128)(2,1)S(1)}, bf16[64,512]{1,0:T(8,128)(2,1)S(1)}, u32[]{:S(2)}, u32[]{:S(2)}) %collective-permute-start.22) | collective-permute-done | bytes 65568 | tf_op jit(solution)/shard_map/ppermute | solution.py:37
  73.7 3.2 %collective-permute-start.26 = (bf16[64,512]{1,0:T(8,128)(2,1)S(1)}, bf16[64,512]{1,0:T(8,128)(2,1)S(1)}, u32[]{:S(2)}, u32[]{:S(2)}) collective-permute-start(bf16[64,512]{1,0:T(8,128)(2,1)S(1)} %multiply_convert_fusion.5), channel_id=1, source_target_pairs={{0,4},{1,5},{2,6},{3,7},{4,0},{5,1},{6,2},{7,3},{8,12},{9,13},{10,... | collective-permute-start | bytes 196616 | tf_op jit(solution)/shard_map/ppermute | solution.py:37
  77.1 2.4 %collective-permute-start.33 = (bf16[64,512]{1,0:T(8,128)(2,1)S(1)}, bf16[64,512]{1,0:T(8,128)(2,1)S(1)}, u32[]{:S(2)}, u32[]{:S(2)}) collective-permute-start(bf16[64,512]{1,0:T(8,128)(2,1)S(1)} %get-tuple-element.208), channel_id=1, source_target_pairs={{0,4},{1,5},{2,6},{3,7},{4,0},{5,1},{6,2},{7,3},{8,12},{9,13},{10,... | collective-permute-start | bytes 196616 | tf_op jit(solution)/shard_map/ppermute | solution.py:37
  79.6 1.0 collective-permute-start.32
  80.6 3.9 %collective-permute-done.27 = bf16[64,512]{1,0:T(8,128)(2,1)S(1)} collective-permute-done((bf16[64,512]{1,0:T(8,128)(2,1)S(1)}, bf16[64,512]{1,0:T(8,128)(2,1)S(1)}, u32[]{:S(2)}, u32[]{:S(2)}) %collective-permute-start.27) | collective-permute-done | bytes 65568 | tf_op jit(solution)/shard_map/ppermute | solution.py:37
  85.3 1.8 %collective-permute-start.30 = (bf16[128,512]{1,0:T(8,128)(2,1)S(1)}, bf16[128,512]{1,0:T(8,128)(2,1)S(1)}, u32[]{:S(2)}, u32[]{:S(2)}) collective-permute-start(bf16[128,512]{1,0:T(8,128)(2,1)S(1)} %constant_dynamic-update-slice_fusion.10), channel_id=1, source_target_pairs={{0,2},{1,3},{2,0},{3,1},{4,6},{5,7},{6,4},{7,5},{8,10},{9,11},{10,... | collective-permute-start | bytes 393224 | tf_op jit(solution)/shard_map/ppermute | solution.py:37
  87.2 1.4 collective-permute-start.38
  88.6 1.1 collective-permute-start.39
  91.3 1.5 collective-permute-start.35
  93.0 1.1 collective-permute-start.34
  94.8 1.8 %collective-permute-start.41 = (bf16[128,512]{1,0:T(8,128)(2,1)S(1)}, bf16[128,512]{1,0:T(8,128)(2,1)S(1)}, u32[]{:S(2)}, u32[]{:S(2)}) collective-permute-start(bf16[128,512]{1,0:T(8,128)(2,1)S(1)} %constant_dynamic-update-slice_fusion.22), channel_id=1, source_target_pairs={{0,2},{1,3},{2,0},{3,1},{4,6},{5,7},{6,4},{7,5},{8,10},{9,11},{10,... | collective-permute-start | bytes 393224 | tf_op jit(solution)/shard_map/ppermute | solution.py:37
  96.6 1.5 collective-permute-start.47
  98.1 1.7 %collective-permute-done.34.refs_1_ = bf16[256,512]{1,0:T(8,128)(2,1)S(1)} collective-permute-done((bf16[256,512]{1,0:T(8,128)(2,1)S(1)}, bf16[256,512]{1,0:T(8,128)(2,1)S(1)}, u32[]{:S(2)}, u32[]{:S(2)}) %collective-permute-start.34) | collective-permute-done | bytes 262176 | tf_op jit(solution)/shard_map/ppermute | solution.py:37
  99.9 1.2 collective-permute-start.46
  101.4 3.4 %out_rows.1 = (bf16[512,448]{1,0:T(8,128)(2,1)S(1)}, bf16[512,448]{1,0:T(8,128)(2,1)S(1)}) custom-call(bf16[1024,512]{1,0:T(8,128)(2,1)S(1)} %get-tuple-element.256.id_ref.rows_ref.refs_0_, bf16[4,448,512]{2,1,0:T(8,128)(2,1)S(1)} %bitcast.6, bf16[256,512]{1,0:T(8,128)(2,1)S(1)} %constant_dynamic-update-slice_fusion.18.refs_0_, ...), custom_call_target="tpu_custom_call" | custom-call | flops 1000000000 | bytes 2000000 | tf_op jit(solution)/shard_map/out_rows/pallas_call | solution.py:358
  104.8 8.8 %collective-permute-start.40 = (bf16[512,448]{1,0:T(8,128)(2,1)S(1)}, bf16[512,448]{1,0:T(8,128)(2,1)S(1)}, u32[]{:S(2)}, u32[]{:S(2)}) collective-permute-start(bf16[512,448]{1,0:T(8,128)(2,1)S(1)} %get-tuple-element.231), channel_id=1, source_target_pairs={{0,8},{1,9},{2,10},{3,11},{4,12},{5,13},{6,14},{7,15},{8,0},{9,1},... | collective-permute-start | bytes 1376264 | tf_op jit(solution)/shard_map/ppermute | solution.py:37
  114.3 0.9 collective-permute-done.40
  115.4 2.5 %token_gate_rows.1.refs_4_ = f32[1024,448]{1,0:T(8,128)S(1)} custom-call(bf16[1024,512]{1,0:T(8,128)(2,1)S(1)} %get-tuple-element.256.id_ref.rows_ref.refs_0_, bf16[4,448,512]{2,1,0:T(8,128)(2,1)S(1)} %copy-done, bf16[256,512]{1,0:T(8,128)(2,1)S(1)} %constant_dynamic-update-slice_fusion.26.refs_0_, bf16[256,512]{1,0:T(8,128)(2,1)S(1)} %collective-permute-done.46.refs_1_, ...), custom_call_target="tpu_custom_call" | custom-call | flops 1000000000 | bytes 2000000 | tf_op jit(solution)/shard_map/token_gate_rows/pallas_call | solution.py:358
  117.9 3.8 %grad_gate.1 = bf16[4,448,512]{2,1,0:T(8,128)(2,1)} custom-call(bf16[1024,512]{1,0:T(8,128)(2,1)S(1)} %get-tuple-element.256.id_ref.rows_ref.refs_0_, bf16[1024,512]{1,0:T(8,128)(2,1)S(1)} %get-tuple-element.256.id_ref.rows_ref.refs_0_, bf16[256,512]{1,0:T(8,128)(2,1)S(1)} %constant_dynamic-update-slice_fusion.26.refs_0_, ...), custom_call_target="tpu_custom_call" | custom-call | flops 1000000000 | bytes 2000000 | tf_op jit(solution)/shard_map/grad_gate/pallas_call | solution.py:358
  121.9 3.3 %token_rows.1 = (bf16[512,448]{1,0:T(8,128)(2,1)S(1)}, bf16[512,448]{1,0:T(8,128)(2,1)S(1)}) custom-call(bf16[1024,512]{1,0:T(8,128)(2,1)S(1)} %get-tuple-element.256.id_ref.rows_ref.refs_0_, bf16[4,448,512]{2,1,0:T(8,128)(2,1)S(1)} %copy-done.2, bf16[256,512]{1,0:T(8,128)(2,1)S(1)} %constant_dynamic-update-slice_fusion.30.refs_0_, ...), custom_call_target="tpu_custom_call" | custom-call | flops 1000000000 | bytes 2000000 | tf_op jit(solution)/shard_map/token_rows/pallas_call | solution.py:358
  125.1 1.2 collective-permute-start.50
  126.5 1.4 collective-permute-done.50
  128.7 3.1 %collective-permute-start.48 = (bf16[128,448]{1,0:T(8,128)(2,1)S(1)}, bf16[128,448]{1,0:T(8,128)(2,1)S(1)}, u32[]{:S(2)}, u32[]{:S(2)}) collective-permute-start(bf16[128,448]{1,0:T(8,128)(2,1)S(1)} %get-tuple-element.266), channel_id=1, source_target_pairs={{0,0},{1,1},{8,2},{9,3},{16,4},{17,5},{24,6},{25,7},{2,8},{3,9},{1... | collective-permute-start | bytes 344072 | tf_op jit(solution)/shard_map/ppermute | solution.py:144
  131.9 1.3 collective-permute-start.49
  133.2 3.8 %grad_down.1 = bf16[4,448,512]{2,1,0:T(8,128)(2,1)} custom-call(bf16[1024,512]{1,0:T(8,128)(2,1)S(1)} %get-tuple-element.256.id_ref.rows_ref.refs_0_, bf16[1024,512]{1,0:T(8,128)(2,1)S(1)} %get-tuple-element.253.rows_ref, bf16[256,512]{1,0:T(8,128)(2,1)S(1)} %constant_dynamic-update-slice_fusion.18.refs_0_, ...), custom_call_target="tpu_custom_call" | custom-call | flops 1000000000 | bytes 2000000 | tf_op jit(solution)/shard_map/grad_down/pallas_call | solution.py:358
  137.1 4.9 %collective-permute-start.52 = (bf16[128,448]{1,0:T(8,128)(2,1)S(1)}, bf16[128,448]{1,0:T(8,128)(2,1)S(1)}, u32[]{:S(2)}, u32[]{:S(2)}) collective-permute-start(bf16[128,448]{1,0:T(8,128)(2,1)S(1)} %get-tuple-element.264), channel_id=1, source_target_pairs={{0,0},{1,1},{8,2},{9,3},{16,4},{17,5},{24,6},{25,7},{2,8},{3,9},{1... | collective-permute-start | bytes 344072 | tf_op jit(solution)/shard_map/ppermute | solution.py:144
  142.0 1.0 collective-permute-start.53
  143.0 3.8 %grad_up.1 = bf16[4,448,512]{2,1,0:T(8,128)(2,1)} custom-call(bf16[1024,512]{1,0:T(8,128)(2,1)S(1)} %get-tuple-element.256.id_ref.rows_ref.refs_0_, bf16[1024,512]{1,0:T(8,128)(2,1)S(1)} %get-tuple-element.256.id_ref.rows_ref.refs_0_, bf16[256,512]{1,0:T(8,128)(2,1)S(1)} %constant_dynamic-update-slice_fusion.30.refs_0_, ...), custom_call_target="tpu_custom_call" | custom-call | flops 1000000000 | bytes 2000000 | tf_op jit(solution)/shard_map/grad_up/pallas_call | solution.py:358
  146.8 0.9 join_output.1
  147.6 2.7 %collective-permute-done.53.other_ref = bf16[128,448]{1,0:T(8,128)(2,1)S(1)} collective-permute-done((bf16[128,448]{1,0:T(8,128)(2,1)S(1)}, bf16[128,448]{1,0:T(8,128)(2,1)S(1)}, u32[]{:S(2)}, u32[]{:S(2)}) %collective-permute-start.53) | collective-permute-done | bytes 114720 | tf_op jit(solution)/shard_map/ppermute | solution.py:144
  (143 shorter events, 11.8 us)
Async XLA Ops:
  2.5 4.6 %collective-permute-start = (bf16[128,512]{1,0:T(8,128)(2,1)}, bf16[128,512]{1,0:T(8,128)(2,1)S(1)}, u32[]{:S(2)}, u32[]{:S(2)}) collective-permute-start(bf16[128,512]{1,0:T(8,128)(2,1)} %get-tuple-element.134), channel_id=1, source_target_pairs={{0,16},{1,17},{2,18},{3,19},{4,20},{5,21},{6,22},{7,23},{8,24},{9,... | collective-permute-start | bytes 393224 | tf_op jit(solution)/shard_map/ppermute | solution.py:37
  3.7 3.4 %copy-start.6 = (bf16[128,512]{1,0:T(8,128)(2,1)S(1)}, bf16[128,512]{1,0:T(8,128)(2,1)}, u32[]{:S(2)}) copy-start(bf16[128,512]{1,0:T(8,128)(2,1)} %get-tuple-element.133) | copy-start | bytes 393220
  5.6 23.2 %copy-start = (bf16[4,448,512]{2,1,0:T(8,128)(2,1)S(1)}, bf16[4,448,512]{2,1,0:T(8,128)(2,1)}, u32[]{:S(2)}) copy-start(bf16[4,448,512]{2,1,0:T(8,128)(2,1)} %w_ref.2) | copy-start | bytes 5505028
  5.6 7.1 %collective-permute-start.3 = (bf16[128,512]{1,0:T(8,128)(2,1)}, bf16[128,512]{1,0:T(8,128)(2,1)S(1)}, u32[]{:S(2)}, u32[]{:S(2)}) collective-permute-start(bf16[128,512]{1,0:T(8,128)(2,1)} %get-tuple-element.136), channel_id=1, source_target_pairs={{0,16},{1,17},{2,18},{3,19},{4,20},{5,21},{6,22},{7,23},{8,24},{9,... | collective-permute-start | bytes 393224 | tf_op jit(solution)/shard_map/ppermute | solution.py:37
  7.1 12.0 %collective-permute-start.2 = (bf16[128,512]{1,0:T(8,128)(2,1)S(1)}, bf16[128,512]{1,0:T(8,128)(2,1)S(1)}, u32[]{:S(2)}, u32[]{:S(2)}) collective-permute-start(bf16[128,512]{1,0:T(8,128)(2,1)S(1)} %get-tuple-element.273), channel_id=1, source_target_pairs={{0,4},{1,5},{2,12},{3,13},{4,1},{5,0},{6,9},{7,8},{8,6},{9,7},{10,... | collective-permute-start | bytes 393224 | tf_op jit(solution)/shard_map/ppermute | solution.py:390
  9.7 9.4 %collective-permute-start.1 = (bf16[128,512]{1,0:T(8,128)(2,1)S(1)}, bf16[128,512]{1,0:T(8,128)(2,1)S(1)}, u32[]{:S(2)}, u32[]{:S(2)}) collective-permute-start(bf16[128,512]{1,0:T(8,128)(2,1)S(1)} %get-tuple-element.274), channel_id=1, source_target_pairs={{0,0},{1,1},{2,8},{3,9},{4,5},{5,4},{6,13},{7,12},{8,2},{9,3},{10,... | collective-permute-start | bytes 393224 | tf_op jit(solution)/shard_map/ppermute | solution.py:391
  13.7 8.0 %collective-permute-start.6 = (bf16[128,512]{1,0:T(8,128)(2,1)S(1)}, bf16[128,512]{1,0:T(8,128)(2,1)S(1)}, u32[]{:S(2)}, u32[]{:S(2)}) collective-permute-start(bf16[128,512]{1,0:T(8,128)(2,1)S(1)} %get-tuple-element.271), channel_id=1, source_target_pairs={{0,4},{1,5},{2,12},{3,13},{4,1},{5,0},{6,9},{7,8},{8,6},{9,7},{10,... | collective-permute-start | bytes 393224 | tf_op jit(solution)/shard_map/ppermute | solution.py:390
  16.4 7.2 %collective-permute-start.5 = (bf16[128,512]{1,0:T(8,128)(2,1)S(1)}, bf16[128,512]{1,0:T(8,128)(2,1)S(1)}, u32[]{:S(2)}, u32[]{:S(2)}) collective-permute-start(bf16[128,512]{1,0:T(8,128)(2,1)S(1)} %get-tuple-element.272), channel_id=1, source_target_pairs={{0,0},{1,1},{2,8},{3,9},{4,5},{5,4},{6,13},{7,12},{8,2},{9,3},{10,... | collective-permute-start | bytes 393224 | tf_op jit(solution)/shard_map/ppermute | solution.py:391
  19.2 7.6 %collective-permute-start.4 = (bf16[256,512]{1,0:T(8,128)(2,1)S(1)}, bf16[256,512]{1,0:T(8,128)(2,1)S(1)}, u32[]{:S(2)}, u32[]{:S(2)}) collective-permute-start(bf16[256,512]{1,0:T(8,128)(2,1)S(1)} %constant_dynamic-update-slice_fusion), channel_id=1, source_target_pairs={{0,16},{1,17},{2,18},{3,19},{4,20},{5,21},{6,22},{7,23},{8,24},{9,... | collective-permute-start | bytes 786440 | tf_op jit(solution)/shard_map/ppermute | solution.py:37
  26.9 2.0 %collective-permute-start.7 = (bf16[512,512]{1,0:T(8,128)(2,1)S(1)}, bf16[512,512]{1,0:T(8,128)(2,1)S(1)}, u32[]{:S(2)}, u32[]{:S(2)}) collective-permute-start(bf16[512,512]{1,0:T(8,128)(2,1)S(1)} %constant_dynamic-update-slice_fusion.4.held_ref), channel_id=1, source_target_pairs={{0,8},{1,9},{2,10},{3,11},{4,12},{5,13},{6,14},{7,15},{8,0},{9,1},... | collective-permute-start | bytes 1572872 | tf_op jit(solution)/shard_map/ppermute | solution.py:37
  27.0 8.1 %collective-permute-start.10 = (bf16[256,512]{1,0:T(8,128)(2,1)S(1)}, bf16[256,512]{1,0:T(8,128)(2,1)S(1)}, u32[]{:S(2)}, u32[]{:S(2)}) collective-permute-start(bf16[256,512]{1,0:T(8,128)(2,1)S(1)} %constant_dynamic-update-slice_fusion.2), channel_id=1, source_target_pairs={{0,16},{1,17},{2,18},{3,19},{4,20},{5,21},{6,22},{7,23},{8,24},{9,... | collective-permute-start | bytes 786440 | tf_op jit(solution)/shard_map/ppermute | solution.py:37
  28.9 1.5 copy-start.1
  32.8 6.0 %copy-start.3 = (bf16[4,512,448]{1,2,0:T(8,128)(2,1)S(1)}, bf16[4,512,448]{1,2,0:T(8,128)(2,1)}, u32[]{:S(2)}) copy-start(bf16[4,512,448]{1,2,0:T(8,128)(2,1)} %param.14) | copy-start | bytes 5505028
  35.2 3.6 %collective-permute-start.11 = (bf16[512,512]{1,0:T(8,128)(2,1)S(1)}, bf16[512,512]{1,0:T(8,128)(2,1)S(1)}, u32[]{:S(2)}, u32[]{:S(2)}) collective-permute-start(bf16[512,512]{1,0:T(8,128)(2,1)S(1)} %constant_dynamic-update-slice_fusion.6.held_ref), channel_id=1, source_target_pairs={{0,8},{1,9},{2,10},{3,11},{4,12},{5,13},{6,14},{7,15},{8,0},{9,1},... | collective-permute-start | bytes 1572872 | tf_op jit(solution)/shard_map/ppermute | solution.py:37
  35.9 7.9 %collective-permute-start.9 = (bf16[256,512]{1,0:T(8,128)(2,1)S(1)}, bf16[256,512]{1,0:T(8,128)(2,1)S(1)}, u32[]{:S(2)}, u32[]{:S(2)}) collective-permute-start(bf16[256,512]{1,0:T(8,128)(2,1)S(1)} %get-tuple-element.148), channel_id=1, source_target_pairs={{0,2},{1,3},{2,0},{3,1},{4,6},{5,7},{6,4},{7,5},{8,10},{9,11},{10,... | collective-permute-start | bytes 786440 | tf_op jit(solution)/shard_map/ppermute | solution.py:37
  35.9 8.0 %collective-permute-start.8 = (bf16[256,512]{1,0:T(8,128)(2,1)S(1)}, bf16[256,512]{1,0:T(8,128)(2,1)S(1)}, u32[]{:S(2)}, u32[]{:S(2)}) collective-permute-start(bf16[256,512]{1,0:T(8,128)(2,1)S(1)} %get-tuple-element.151), channel_id=1, source_target_pairs={{0,1},{1,0},{2,3},{3,2},{4,5},{5,4},{6,7},{7,6},{8,9},{9,8},{10,11... | collective-permute-start | bytes 786440 | tf_op jit(solution)/shard_map/ppermute | solution.py:37
  37.1 12.2 %collective-permute-start.16 = (bf16[256,512]{1,0:T(8,128)(2,1)S(1)}, bf16[256,512]{1,0:T(8,128)(2,1)S(1)}, u32[]{:S(2)}, u32[]{:S(2)}) collective-permute-start(bf16[256,512]{1,0:T(8,128)(2,1)S(1)} %get-tuple-element.169), channel_id=1, source_target_pairs={{0,2},{1,3},{2,0},{3,1},{4,6},{5,7},{6,4},{7,5},{8,10},{9,11},{10,... | collective-permute-start | bytes 786440 | tf_op jit(solution)/shard_map/ppermute | solution.py:37
  37.4 12.2 %collective-permute-start.15 = (bf16[256,512]{1,0:T(8,128)(2,1)S(1)}, bf16[256,512]{1,0:T(8,128)(2,1)S(1)}, u32[]{:S(2)}, u32[]{:S(2)}) collective-permute-start(bf16[256,512]{1,0:T(8,128)(2,1)S(1)} %get-tuple-element.167), channel_id=1, source_target_pairs={{0,1},{1,0},{2,3},{3,2},{4,5},{5,4},{6,7},{7,6},{8,9},{9,8},{10,11... | collective-permute-start | bytes 786440 | tf_op jit(solution)/shard_map/ppermute | solution.py:37
  40.2 14.8 %collective-permute-start.13 = (bf16[256,512]{1,0:T(8,128)(2,1)S(1)}, bf16[256,512]{1,0:T(8,128)(2,1)S(1)}, u32[]{:S(2)}, u32[]{:S(2)}) collective-permute-start(bf16[256,512]{1,0:T(8,128)(2,1)S(1)} %get-tuple-element.158), channel_id=1, source_target_pairs={{0,2},{1,3},{2,0},{3,1},{4,6},{5,7},{6,4},{7,5},{8,10},{9,11},{10,... | collective-permute-start | bytes 786440 | tf_op jit(solution)/shard_map/ppermute | solution.py:37
  43.8 8.1 %collective-permute-start.14 = (bf16[128,512]{1,0:T(8,128)(2,1)S(1)}, bf16[128,512]{1,0:T(8,128)(2,1)S(1)}, u32[]{:S(2)}, u32[]{:S(2)}) collective-permute-start(bf16[128,512]{1,0:T(8,128)(2,1)S(1)} %add_convert_fusion.11), channel_id=1, source_target_pairs={{0,1},{1,0},{2,3},{3,2},{4,5},{5,4},{6,7},{7,6},{8,9},{9,8},{10,11... | collective-permute-start | bytes 393224 | tf_op jit(solution)/shard_map/ppermute | solution.py:37
  43.9 13.9 %collective-permute-start.12 = (bf16[128,512]{1,0:T(8,128)(2,1)S(1)}, bf16[128,512]{1,0:T(8,128)(2,1)S(1)}, u32[]{:S(2)}, u32[]{:S(2)}) collective-permute-start(bf16[128,512]{1,0:T(8,128)(2,1)S(1)} %add_convert_fusion.10), channel_id=1, source_target_pairs={{0,2},{1,3},{2,0},{3,1},{4,6},{5,7},{6,4},{7,5},{8,10},{9,11},{10,... | collective-permute-start | bytes 393224 | tf_op jit(solution)/shard_map/ppermute | solution.py:37
  49.4 14.8 %copy-start.5 = (bf16[128,512]{1,0:T(8,128)(2,1)}, bf16[128,512]{1,0:T(8,128)(2,1)S(1)}, u32[]{:S(2)}) copy-start(bf16[128,512]{1,0:T(8,128)(2,1)S(1)} %slice.261) | copy-start | bytes 393220
  49.4 11.6 %collective-permute-start.20 = (bf16[128,512]{1,0:T(8,128)(2,1)S(1)}, bf16[128,512]{1,0:T(8,128)(2,1)S(1)}, u32[]{:S(2)}, u32[]{:S(2)}) collective-permute-start(bf16[128,512]{1,0:T(8,128)(2,1)S(1)} %add_convert_fusion.9), channel_id=1, source_target_pairs={{0,1},{1,0},{2,3},{3,2},{4,5},{5,4},{6,7},{7,6},{8,9},{9,8},{10,11... | collective-permute-start | bytes 393224 | tf_op jit(solution)/shard_map/ppermute | solution.py:37
  49.6 14.8 %collective-permute-start.18 = (bf16[128,512]{1,0:T(8,128)(2,1)S(1)}, bf16[128,512]{1,0:T(8,128)(2,1)S(1)}, u32[]{:S(2)}, u32[]{:S(2)}) collective-permute-start(bf16[128,512]{1,0:T(8,128)(2,1)S(1)} %add_convert_fusion.8), channel_id=1, source_target_pairs={{0,2},{1,3},{2,0},{3,1},{4,6},{5,7},{6,4},{7,5},{8,10},{9,11},{10,... | collective-permute-start | bytes 393224 | tf_op jit(solution)/shard_map/ppermute | solution.py:37
  51.9 8.0 %collective-permute-start.21 = (bf16[256,512]{1,0:T(8,128)(2,1)S(1)}, bf16[256,512]{1,0:T(8,128)(2,1)S(1)}, u32[]{:S(2)}, u32[]{:S(2)}) collective-permute-start(bf16[256,512]{1,0:T(8,128)(2,1)S(1)} %get-tuple-element.181), channel_id=1, source_target_pairs={{0,1},{1,0},{2,3},{3,2},{4,5},{5,4},{6,7},{7,6},{8,9},{9,8},{10,11... | collective-permute-start | bytes 786440 | tf_op jit(solution)/shard_map/ppermute | solution.py:37
  55.0 9.2 %collective-permute-start.19 = (bf16[64,512]{1,0:T(8,128)(2,1)S(1)}, bf16[64,512]{1,0:T(8,128)(2,1)S(1)}, u32[]{:S(2)}, u32[]{:S(2)}) collective-permute-start(bf16[64,512]{1,0:T(8,128)(2,1)S(1)} %add_convert_fusion.17), channel_id=1, source_target_pairs={{0,4},{1,5},{2,6},{3,7},{4,0},{5,1},{6,2},{7,3},{8,12},{9,13},{10,... | collective-permute-start | bytes 196616 | tf_op jit(solution)/shard_map/ppermute | solution.py:37
  59.9 8.6 %collective-permute-start.24 = (bf16[128,512]{1,0:T(8,128)(2,1)S(1)}, bf16[128,512]{1,0:T(8,128)(2,1)S(1)}, u32[]{:S(2)}, u32[]{:S(2)}) collective-permute-start(bf16[128,512]{1,0:T(8,128)(2,1)S(1)} %add_convert_fusion.6), channel_id=1, source_target_pairs={{0,2},{1,3},{2,0},{3,1},{4,6},{5,7},{6,4},{7,5},{8,10},{9,11},{10,... | collective-permute-start | bytes 393224 | tf_op jit(solution)/shard_map/ppermute | solution.py:37
  61.1 5.7 %collective-permute-start.17 = (bf16[64,512]{1,0:T(8,128)(2,1)S(1)}, bf16[64,512]{1,0:T(8,128)(2,1)S(1)}, u32[]{:S(2)}, u32[]{:S(2)}) collective-permute-start(bf16[64,512]{1,0:T(8,128)(2,1)S(1)} %add_convert_fusion.16), channel_id=1, source_target_pairs={{0,4},{1,5},{2,6},{3,7},{4,0},{5,1},{6,2},{7,3},{8,12},{9,13},{10,... | collective-permute-start | bytes 196616 | tf_op jit(solution)/shard_map/ppermute | solution.py:37
  63.7 3.8 %collective-permute-start.25 = (bf16[128,512]{1,0:T(8,128)(2,1)S(1)}, bf16[128,512]{1,0:T(8,128)(2,1)S(1)}, u32[]{:S(2)}, u32[]{:S(2)}) collective-permute-start(bf16[128,512]{1,0:T(8,128)(2,1)S(1)} %add_convert_fusion.7), channel_id=1, source_target_pairs={{0,1},{1,0},{2,3},{3,2},{4,5},{5,4},{6,7},{7,6},{8,9},{9,8},{10,11... | collective-permute-start | bytes 393224 | tf_op jit(solution)/shard_map/ppermute | solution.py:37
  64.2 5.9 %slice-start = ((bf16[128,512]{1,0:T(8,128)(2,1)}), bf16[64,512]{1,0:T(8,128)(2,1)S(1)}, s32[]{:S(2)}) async-start(bf16[128,512]{1,0:T(8,128)(2,1)} %copy-done.5), calls=%async_computation | async-start | bytes 131072 | tf_op jit(solution)/shard_map/slice | solution.py:99
  64.2 5.9 %collective-permute-start.23 = (bf16[64,512]{1,0:T(8,128)(2,1)S(1)}, bf16[64,512]{1,0:T(8,128)(2,1)S(1)}, u32[]{:S(2)}, u32[]{:S(2)}) collective-permute-start(bf16[64,512]{1,0:T(8,128)(2,1)S(1)} %add_convert_fusion.15), channel_id=1, source_target_pairs={{0,4},{1,5},{2,6},{3,7},{4,0},{5,1},{6,2},{7,3},{8,12},{9,13},{10,... | collective-permute-start | bytes 196616 | tf_op jit(solution)/shard_map/ppermute | solution.py:37
  64.4 9.2 %collective-permute-start.22 = (bf16[64,512]{1,0:T(8,128)(2,1)S(1)}, bf16[64,512]{1,0:T(8,128)(2,1)S(1)}, u32[]{:S(2)}, u32[]{:S(2)}) collective-permute-start(bf16[64,512]{1,0:T(8,128)(2,1)S(1)} %add_convert_fusion.14), channel_id=1, source_target_pairs={{0,4},{1,5},{2,6},{3,7},{4,0},{5,1},{6,2},{7,3},{8,12},{9,13},{10,... | collective-permute-start | bytes 196616 | tf_op jit(solution)/shard_map/ppermute | solution.py:37
  67.6 9.4 %collective-permute-start.29 = (bf16[64,512]{1,0:T(8,128)(2,1)S(1)}, bf16[64,512]{1,0:T(8,128)(2,1)S(1)}, u32[]{:S(2)}, u32[]{:S(2)}) collective-permute-start(bf16[64,512]{1,0:T(8,128)(2,1)S(1)} %add_convert_fusion.13), channel_id=1, source_target_pairs={{0,4},{1,5},{2,6},{3,7},{4,0},{5,1},{6,2},{7,3},{8,12},{9,13},{10,... | collective-permute-start | bytes 196616 | tf_op jit(solution)/shard_map/ppermute | solution.py:37
  68.6 10.9 %collective-permute-start.28 = (bf16[64,512]{1,0:T(8,128)(2,1)S(1)}, bf16[64,512]{1,0:T(8,128)(2,1)S(1)}, u32[]{:S(2)}, u32[]{:S(2)}) collective-permute-start(bf16[64,512]{1,0:T(8,128)(2,1)S(1)} %add_convert_fusion.12), channel_id=1, source_target_pairs={{0,4},{1,5},{2,6},{3,7},{4,0},{5,1},{6,2},{7,3},{8,12},{9,13},{10,... | collective-permute-start | bytes 196616 | tf_op jit(solution)/shard_map/ppermute | solution.py:37
  73.7 11.6 %collective-permute-start.26 = (bf16[64,512]{1,0:T(8,128)(2,1)S(1)}, bf16[64,512]{1,0:T(8,128)(2,1)S(1)}, u32[]{:S(2)}, u32[]{:S(2)}) collective-permute-start(bf16[64,512]{1,0:T(8,128)(2,1)S(1)} %multiply_convert_fusion.5), channel_id=1, source_target_pairs={{0,4},{1,5},{2,6},{3,7},{4,0},{5,1},{6,2},{7,3},{8,12},{9,13},{10,... | collective-permute-start | bytes 196616 | tf_op jit(solution)/shard_map/ppermute | solution.py:37
  76.9 7.5 %collective-permute-start.27 = (bf16[64,512]{1,0:T(8,128)(2,1)S(1)}, bf16[64,512]{1,0:T(8,128)(2,1)S(1)}, u32[]{:S(2)}, u32[]{:S(2)}) collective-permute-start(bf16[64,512]{1,0:T(8,128)(2,1)S(1)} %get-tuple-element.204), channel_id=1, source_target_pairs={{0,4},{1,5},{2,6},{3,7},{4,0},{5,1},{6,2},{7,3},{8,12},{9,13},{10,... | collective-permute-start | bytes 196616 | tf_op jit(solution)/shard_map/ppermute | solution.py:37
  77.1 11.5 %collective-permute-start.33 = (bf16[64,512]{1,0:T(8,128)(2,1)S(1)}, bf16[64,512]{1,0:T(8,128)(2,1)S(1)}, u32[]{:S(2)}, u32[]{:S(2)}) collective-permute-start(bf16[64,512]{1,0:T(8,128)(2,1)S(1)} %get-tuple-element.208), channel_id=1, source_target_pairs={{0,4},{1,5},{2,6},{3,7},{4,0},{5,1},{6,2},{7,3},{8,12},{9,13},{10,... | collective-permute-start | bytes 196616 | tf_op jit(solution)/shard_map/ppermute | solution.py:37
  79.6 10.1 %collective-permute-start.32 = (bf16[64,512]{1,0:T(8,128)(2,1)S(1)}, bf16[64,512]{1,0:T(8,128)(2,1)S(1)}, u32[]{:S(2)}, u32[]{:S(2)}) collective-permute-start(bf16[64,512]{1,0:T(8,128)(2,1)S(1)} %get-tuple-element.210), channel_id=1, source_target_pairs={{0,4},{1,5},{2,6},{3,7},{4,0},{5,1},{6,2},{7,3},{8,12},{9,13},{10,... | collective-permute-start | bytes 196616 | tf_op jit(solution)/shard_map/ppermute | solution.py:37
  84.4 6.1 %collective-permute-start.31 = (bf16[128,512]{1,0:T(8,128)(2,1)S(1)}, bf16[128,512]{1,0:T(8,128)(2,1)S(1)}, u32[]{:S(2)}, u32[]{:S(2)}) collective-permute-start(bf16[128,512]{1,0:T(8,128)(2,1)S(1)} %constant_dynamic-update-slice_fusion.8), channel_id=1, source_target_pairs={{0,1},{1,0},{2,3},{3,2},{4,5},{5,4},{6,7},{7,6},{8,9},{9,8},{10,11... | collective-permute-start | bytes 393224 | tf_op jit(solution)/shard_map/ppermute | solution.py:37
  85.3 6.0 %collective-permute-start.30 = (bf16[128,512]{1,0:T(8,128)(2,1)S(1)}, bf16[128,512]{1,0:T(8,128)(2,1)S(1)}, u32[]{:S(2)}, u32[]{:S(2)}) collective-permute-start(bf16[128,512]{1,0:T(8,128)(2,1)S(1)} %constant_dynamic-update-slice_fusion.10), channel_id=1, source_target_pairs={{0,2},{1,3},{2,0},{3,1},{4,6},{5,7},{6,4},{7,5},{8,10},{9,11},{10,... | collective-permute-start | bytes 393224 | tf_op jit(solution)/shard_map/ppermute | solution.py:37
  87.2 7.0 %collective-permute-start.38 = (bf16[64,512]{1,0:T(8,128)(2,1)S(1)}, bf16[64,512]{1,0:T(8,128)(2,1)S(1)}, u32[]{:S(2)}, u32[]{:S(2)}) collective-permute-start(bf16[64,512]{1,0:T(8,128)(2,1)S(1)} %get-tuple-element.220), channel_id=1, source_target_pairs={{0,4},{1,5},{2,6},{3,7},{4,0},{5,1},{6,2},{7,3},{8,12},{9,13},{10,... | collective-permute-start | bytes 196616 | tf_op jit(solution)/shard_map/ppermute | solution.py:37
  88.6 4.5 %collective-permute-start.39 = (bf16[64,512]{1,0:T(8,128)(2,1)S(1)}, bf16[64,512]{1,0:T(8,128)(2,1)S(1)}, u32[]{:S(2)}, u32[]{:S(2)}) collective-permute-start(bf16[64,512]{1,0:T(8,128)(2,1)S(1)} %get-tuple-element.218), channel_id=1, source_target_pairs={{0,4},{1,5},{2,6},{3,7},{4,0},{5,1},{6,2},{7,3},{8,12},{9,13},{10,... | collective-permute-start | bytes 196616 | tf_op jit(solution)/shard_map/ppermute | solution.py:37
  89.7 5.1 %collective-permute-start.37 = (bf16[128,512]{1,0:T(8,128)(2,1)S(1)}, bf16[128,512]{1,0:T(8,128)(2,1)S(1)}, u32[]{:S(2)}, u32[]{:S(2)}) collective-permute-start(bf16[128,512]{1,0:T(8,128)(2,1)S(1)} %constant_dynamic-update-slice_fusion.12), channel_id=1, source_target_pairs={{0,1},{1,0},{2,3},{3,2},{4,5},{5,4},{6,7},{7,6},{8,9},{9,8},{10,11... | collective-permute-start | bytes 393224 | tf_op jit(solution)/shard_map/ppermute | solution.py:37
  90.5 6.1 %collective-permute-start.36 = (bf16[128,512]{1,0:T(8,128)(2,1)S(1)}, bf16[128,512]{1,0:T(8,128)(2,1)S(1)}, u32[]{:S(2)}, u32[]{:S(2)}) collective-permute-start(bf16[128,512]{1,0:T(8,128)(2,1)S(1)} %constant_dynamic-update-slice_fusion.14), channel_id=1, source_target_pairs={{0,2},{1,3},{2,0},{3,1},{4,6},{5,7},{6,4},{7,5},{8,10},{9,11},{10,... | collective-permute-start | bytes 393224 | tf_op jit(solution)/shard_map/ppermute | solution.py:37
  91.3 10.0 %collective-permute-start.35 = (bf16[256,512]{1,0:T(8,128)(2,1)S(1)}, bf16[256,512]{1,0:T(8,128)(2,1)S(1)}, u32[]{:S(2)}, u32[]{:S(2)}) collective-permute-start(bf16[256,512]{1,0:T(8,128)(2,1)S(1)} %constant_dynamic-update-slice_fusion.16.refs_2_), channel_id=1, source_target_pairs={{0,2},{1,3},{2,0},{3,1},{4,6},{5,7},{6,4},{7,5},{8,10},{9,11},{10,... | collective-permute-start | bytes 786440 | tf_op jit(solution)/shard_map/ppermute | solution.py:37
  93.0 6.8 %collective-permute-start.34 = (bf16[256,512]{1,0:T(8,128)(2,1)S(1)}, bf16[256,512]{1,0:T(8,128)(2,1)S(1)}, u32[]{:S(2)}, u32[]{:S(2)}) collective-permute-start(bf16[256,512]{1,0:T(8,128)(2,1)S(1)} %constant_dynamic-update-slice_fusion.18.refs_0_), channel_id=1, source_target_pairs={{0,1},{1,0},{2,3},{3,2},{4,5},{5,4},{6,7},{7,6},{8,9},{9,8},{10,11... | collective-permute-start | bytes 786440 | tf_op jit(solution)/shard_map/ppermute | solution.py:37
  94.2 19.4 %collective-permute-start.42 = (bf16[128,512]{1,0:T(8,128)(2,1)S(1)}, bf16[128,512]{1,0:T(8,128)(2,1)S(1)}, u32[]{:S(2)}, u32[]{:S(2)}) collective-permute-start(bf16[128,512]{1,0:T(8,128)(2,1)S(1)} %constant_dynamic-update-slice_fusion.20), channel_id=1, source_target_pairs={{0,1},{1,0},{2,3},{3,2},{4,5},{5,4},{6,7},{7,6},{8,9},{9,8},{10,11... | collective-permute-start | bytes 393224 | tf_op jit(solution)/shard_map/ppermute | solution.py:37
  94.8 19.4 %collective-permute-start.41 = (bf16[128,512]{1,0:T(8,128)(2,1)S(1)}, bf16[128,512]{1,0:T(8,128)(2,1)S(1)}, u32[]{:S(2)}, u32[]{:S(2)}) collective-permute-start(bf16[128,512]{1,0:T(8,128)(2,1)S(1)} %constant_dynamic-update-slice_fusion.22), channel_id=1, source_target_pairs={{0,2},{1,3},{2,0},{3,1},{4,6},{5,7},{6,4},{7,5},{8,10},{9,11},{10,... | collective-permute-start | bytes 393224 | tf_op jit(solution)/shard_map/ppermute | solution.py:37
  96.6 18.7 %collective-permute-start.47 = (bf16[256,512]{1,0:T(8,128)(2,1)S(1)}, bf16[256,512]{1,0:T(8,128)(2,1)S(1)}, u32[]{:S(2)}, u32[]{:S(2)}) collective-permute-start(bf16[256,512]{1,0:T(8,128)(2,1)S(1)} %constant_dynamic-update-slice_fusion.24.refs_2_), channel_id=1, source_target_pairs={{0,2},{1,3},{2,0},{3,1},{4,6},{5,7},{6,4},{7,5},{8,10},{9,11},{10,... | collective-permute-start | bytes 786440 | tf_op jit(solution)/shard_map/ppermute | solution.py:37
  99.9 15.5 %collective-permute-start.46 = (bf16[256,512]{1,0:T(8,128)(2,1)S(1)}, bf16[256,512]{1,0:T(8,128)(2,1)S(1)}, u32[]{:S(2)}, u32[]{:S(2)}) collective-permute-start(bf16[256,512]{1,0:T(8,128)(2,1)S(1)} %constant_dynamic-update-slice_fusion.26.refs_0_), channel_id=1, source_target_pairs={{0,1},{1,0},{2,3},{3,2},{4,5},{5,4},{6,7},{7,6},{8,9},{9,8},{10,11... | collective-permute-start | bytes 786440 | tf_op jit(solution)/shard_map/ppermute | solution.py:37
  104.8 10.3 %collective-permute-start.40 = (bf16[512,448]{1,0:T(8,128)(2,1)S(1)}, bf16[512,448]{1,0:T(8,128)(2,1)S(1)}, u32[]{:S(2)}, u32[]{:S(2)}) collective-permute-start(bf16[512,448]{1,0:T(8,128)(2,1)S(1)} %get-tuple-element.231), channel_id=1, source_target_pairs={{0,8},{1,9},{2,10},{3,11},{4,12},{5,13},{6,14},{7,15},{8,0},{9,1},... | collective-permute-start | bytes 1376264 | tf_op jit(solution)/shard_map/ppermute | solution.py:37
  113.6 8.2 %collective-permute-start.45 = (bf16[256,512]{1,0:T(8,128)(2,1)S(1)}, bf16[256,512]{1,0:T(8,128)(2,1)S(1)}, u32[]{:S(2)}, u32[]{:S(2)}) collective-permute-start(bf16[256,512]{1,0:T(8,128)(2,1)S(1)} %constant_dynamic-update-slice_fusion.28.refs_2_), channel_id=1, source_target_pairs={{0,2},{1,3},{2,0},{3,1},{4,6},{5,7},{6,4},{7,5},{8,10},{9,11},{10,... | collective-permute-start | bytes 786440 | tf_op jit(solution)/shard_map/ppermute | solution.py:37
  114.2 7.7 %collective-permute-start.44 = (bf16[256,512]{1,0:T(8,128)(2,1)S(1)}, bf16[256,512]{1,0:T(8,128)(2,1)S(1)}, u32[]{:S(2)}, u32[]{:S(2)}) collective-permute-start(bf16[256,512]{1,0:T(8,128)(2,1)S(1)} %constant_dynamic-update-slice_fusion.30.refs_0_), channel_id=1, source_target_pairs={{0,1},{1,0},{2,3},{3,2},{4,5},{5,4},{6,7},{7,6},{8,9},{9,8},{10,11... | collective-permute-start | bytes 786440 | tf_op jit(solution)/shard_map/ppermute | solution.py:37
  115.2 11.1 %collective-permute-start.43 = (bf16[256,448]{1,0:T(8,128)(2,1)S(1)}, bf16[256,448]{1,0:T(8,128)(2,1)S(1)}, u32[]{:S(2)}, u32[]{:S(2)}) collective-permute-start(bf16[256,448]{1,0:T(8,128)(2,1)S(1)} %add_convert_fusion.1), channel_id=1, source_target_pairs={{0,16},{1,17},{2,18},{3,19},{4,20},{5,21},{6,22},{7,23},{8,24},{9,... | collective-permute-start | bytes 688136 | tf_op jit(solution)/shard_map/ppermute | solution.py:37
  117.9 4.0 %copy-start.2 = (bf16[4,448,512]{2,1,0:T(8,128)(2,1)S(1)}, bf16[4,448,512]{2,1,0:T(8,128)(2,1)}, u32[]{:S(2)}) copy-start(bf16[4,448,512]{2,1,0:T(8,128)(2,1)} %w_ref.3) | copy-start | bytes 5505028
  125.1 2.7 %collective-permute-start.50 = (bf16[512,448]{1,0:T(8,128)(2,1)S(1)}, bf16[512,448]{1,0:T(8,128)(2,1)S(1)}, u32[]{:S(2)}, u32[]{:S(2)}) collective-permute-start(bf16[512,448]{1,0:T(8,128)(2,1)S(1)} %get-tuple-element.247), channel_id=1, source_target_pairs={{0,8},{1,9},{2,10},{3,11},{4,12},{5,13},{6,14},{7,15},{8,0},{9,1},... | collective-permute-start | bytes 1376264 | tf_op jit(solution)/shard_map/ppermute | solution.py:37
  127.9 9.1 %collective-permute-start.51 = (bf16[256,448]{1,0:T(8,128)(2,1)S(1)}, bf16[256,448]{1,0:T(8,128)(2,1)S(1)}, u32[]{:S(2)}, u32[]{:S(2)}) collective-permute-start(bf16[256,448]{1,0:T(8,128)(2,1)S(1)} %add_convert_fusion), channel_id=1, source_target_pairs={{0,16},{1,17},{2,18},{3,19},{4,20},{5,21},{6,22},{7,23},{8,24},{9,... | collective-permute-start | bytes 688136 | tf_op jit(solution)/shard_map/ppermute | solution.py:37
  128.7 18.0 %collective-permute-start.48 = (bf16[128,448]{1,0:T(8,128)(2,1)S(1)}, bf16[128,448]{1,0:T(8,128)(2,1)S(1)}, u32[]{:S(2)}, u32[]{:S(2)}) collective-permute-start(bf16[128,448]{1,0:T(8,128)(2,1)S(1)} %get-tuple-element.266), channel_id=1, source_target_pairs={{0,0},{1,1},{8,2},{9,3},{16,4},{17,5},{24,6},{25,7},{2,8},{3,9},{1... | collective-permute-start | bytes 344072 | tf_op jit(solution)/shard_map/ppermute | solution.py:144
  131.9 14.9 %collective-permute-start.49 = (bf16[128,448]{1,0:T(8,128)(2,1)S(1)}, bf16[128,448]{1,0:T(8,128)(2,1)S(1)}, u32[]{:S(2)}, u32[]{:S(2)}) collective-permute-start(bf16[128,448]{1,0:T(8,128)(2,1)S(1)} %get-tuple-element.265), channel_id=1, source_target_pairs={{17,0},{16,1},{25,2},{24,3},{1,4},{0,5},{9,6},{8,7},{19,8},{18,9},... | collective-permute-start | bytes 344072 | tf_op jit(solution)/shard_map/ppermute | solution.py:144
  137.1 13.3 %collective-permute-start.52 = (bf16[128,448]{1,0:T(8,128)(2,1)S(1)}, bf16[128,448]{1,0:T(8,128)(2,1)S(1)}, u32[]{:S(2)}, u32[]{:S(2)}) collective-permute-start(bf16[128,448]{1,0:T(8,128)(2,1)S(1)} %get-tuple-element.264), channel_id=1, source_target_pairs={{0,0},{1,1},{8,2},{9,3},{16,4},{17,5},{24,6},{25,7},{2,8},{3,9},{1... | collective-permute-start | bytes 344072 | tf_op jit(solution)/shard_map/ppermute | solution.py:144
  142.0 4.8 %copy-start.4 = (f32[128,1]{0,1:T(1,128)S(1)}, f32[128,1]{0,1:T(1,128)}, u32[]{:S(2)}) copy-start(f32[128,1]{0,1:T(1,128)} %param.10) | copy-start | bytes 1540
  142.0 8.4 %collective-permute-start.53 = (bf16[128,448]{1,0:T(8,128)(2,1)S(1)}, bf16[128,448]{1,0:T(8,128)(2,1)S(1)}, u32[]{:S(2)}, u32[]{:S(2)}) collective-permute-start(bf16[128,448]{1,0:T(8,128)(2,1)S(1)} %get-tuple-element.263), channel_id=1, source_target_pairs={{17,0},{16,1},{25,2},{24,3},{1,4},{0,5},{9,6},{8,7},{19,8},{18,9},... | collective-permute-start | bytes 344072 | tf_op jit(solution)/shard_map/ppermute | solution.py:144

commit v8 on v7

--- a/solution.py
+++ b/solution.py
@@ -598,10 +598,10 @@
     (rows,) = line.begin(dz_rows)
     grad_down = line.end(grad(rows, act_pairs, "grad_down"))
     token.leave()
+    weights = (route_weights.reshape(1, tok),)
+    layer_output = line.end(joined(line.begin(*out.pieces), weights, "join_output"))
     (rows,) = line.begin(x_rows)
     grad_up = line.end(grad(rows, pairs, "grad_up"))
-    weights = (route_weights.reshape(1, tok),)
-    layer_output = line.end(joined(line.begin(*out.pieces), weights, "join_output"))
     grad_tokens = line.end(joined(line.begin(*token.pieces), (), "join_tokens"))
     return (layer_output, grad_tokens, grad_gate, grad_up, jnp.swapaxes(grad_down, 1, 2))
 

time: 152 us -> 152 us (level)
  no operation moved by 1% of the time
where the time goes in v8:
time: 152 us
  starting transfers between devices  77.1 us (51%)
  waiting for transfers between devices  35.8 us (24%)
  Pallas kernels  33.5 us (22%)
  other arithmetic  2.09 us (1%)
  local copies, waits for them, and re-layouts  1.97 us (1%)
    ppermute x46, starting transfers between devices, swap(): return lax.ppermute(block, AXES, pairs)  55.8 us
    pallas_call x14, Pallas kernels, call(): pl.pallas_call(body, out_shape=out_shape, grid=kw.get('grid', (1,)), in_s...  33.5 us
    ppermute x46, waiting for transfers between devices, swap(): return lax.ppermute(block, AXES, pairs)  30.2 us
    ppermute x4, starting transfers between devices, leave(): self.pieces[k] = lax.ppermute(piece, AXES, back)  10.2 us
    ppermute x2, starting transfers between devices, land(): return [lax.ppermute(near, AXES, column_pairs(0)), far]  5.8 us
    ppermute x2, starting transfers between devices, land(): far = lax.ppermute(far, AXES, column_pairs(1))  5.28 us
    ppermute x4, waiting for transfers between devices, leave(): self.pieces[k] = lax.ppermute(piece, AXES, back)  3.21 us
  transfers between devices with their start and end apart: 54, of which 22 were waited for; matrix products, arithmetic and copies ran while one was open for 2% of the time, Pallas kernels for 20%

profile of v8, /device:TPU:17, one launch (start us, length us, event | category | flops | bytes accessed | tf_op | source)
XLA Modules:
  0.0 151.7 jit_solution(11179325137837035710)
XLA Ops:
  0.6 1.9 %token_pieces.1 = (bf16[128,512]{1,0:T(8,128)(2,1)}, bf16[128,512]{1,0:T(8,128)(2,1)}) custom-call(s32[4]{0:T(128)} %hot_ref.1, s32[1,128]{1,0:T(1,128)} %bitcast.10, bf16[128,896]{1,0:T(8,128)(2,1)} %tokens_ref.1), custom_call_target="tpu_custom_call" | custom-call | flops 1000000000 | bytes 2000000 | tf_op jit(solution)/shard_map/token_pieces/pallas_call | solution.py:358
  2.5 1.2 collective-permute-start
  3.7 1.9 %cotangent_pieces.1 = (bf16[128,512]{1,0:T(8,128)(2,1)}, bf16[128,512]{1,0:T(8,128)(2,1)}) custom-call(f32[1,128]{1,0:T(1,128)} %bitcast.7, bf16[128,896]{1,0:T(8,128)(2,1)} %rows_ref.1), custom_call_target="tpu_custom_call" | custom-call | flops 1000000000 | bytes 2000000 | tf_op jit(solution)/shard_map/cotangent_pieces/pallas_call | solution.py:358
  5.9 1.2 collective-permute-done
  7.1 2.6 %collective-permute-start.2 = (bf16[128,512]{1,0:T(8,128)(2,1)S(1)}, bf16[128,512]{1,0:T(8,128)(2,1)S(1)}, u32[]{:S(2)}, u32[]{:S(2)}) collective-permute-start(bf16[128,512]{1,0:T(8,128)(2,1)S(1)} %get-tuple-element.273), channel_id=1, source_target_pairs={{0,4},{1,5},{2,12},{3,13},{4,1},{5,0},{6,9},{7,8},{8,6},{9,7},{10,... | collective-permute-start | bytes 393224 | tf_op jit(solution)/shard_map/ppermute | solution.py:390
  9.7 3.0 %collective-permute-start.1 = (bf16[128,512]{1,0:T(8,128)(2,1)S(1)}, bf16[128,512]{1,0:T(8,128)(2,1)S(1)}, u32[]{:S(2)}, u32[]{:S(2)}) collective-permute-start(bf16[128,512]{1,0:T(8,128)(2,1)S(1)} %get-tuple-element.274), channel_id=1, source_target_pairs={{0,0},{1,1},{2,8},{3,9},{4,5},{5,4},{6,13},{7,12},{8,2},{9,3},{10,... | collective-permute-start | bytes 393224 | tf_op jit(solution)/shard_map/ppermute | solution.py:391
  12.8 0.9 broadcast_select_fusion
  13.7 2.7 %collective-permute-start.6 = (bf16[128,512]{1,0:T(8,128)(2,1)S(1)}, bf16[128,512]{1,0:T(8,128)(2,1)S(1)}, u32[]{:S(2)}, u32[]{:S(2)}) collective-permute-start(bf16[128,512]{1,0:T(8,128)(2,1)S(1)} %get-tuple-element.271), channel_id=1, source_target_pairs={{0,4},{1,5},{2,12},{3,13},{4,1},{5,0},{6,9},{7,8},{8,6},{9,7},{10,... | collective-permute-start | bytes 393224 | tf_op jit(solution)/shard_map/ppermute | solution.py:390
  16.4 2.8 %collective-permute-start.5 = (bf16[128,512]{1,0:T(8,128)(2,1)S(1)}, bf16[128,512]{1,0:T(8,128)(2,1)S(1)}, u32[]{:S(2)}, u32[]{:S(2)}) collective-permute-start(bf16[128,512]{1,0:T(8,128)(2,1)S(1)} %get-tuple-element.272), channel_id=1, source_target_pairs={{0,0},{1,1},{2,8},{3,9},{4,5},{5,4},{6,13},{7,12},{8,2},{9,3},{10,... | collective-permute-start | bytes 393224 | tf_op jit(solution)/shard_map/ppermute | solution.py:391
  19.2 1.9 %collective-permute-start.4 = (bf16[256,512]{1,0:T(8,128)(2,1)S(1)}, bf16[256,512]{1,0:T(8,128)(2,1)S(1)}, u32[]{:S(2)}, u32[]{:S(2)}) collective-permute-start(bf16[256,512]{1,0:T(8,128)(2,1)S(1)} %constant_dynamic-update-slice_fusion), channel_id=1, source_target_pairs={{0,16},{1,17},{2,18},{3,19},{4,20},{5,21},{6,22},{7,23},{8,24},{9,... | collective-permute-start | bytes 786440 | tf_op jit(solution)/shard_map/ppermute | solution.py:37
  21.7 1.9 %collective-permute-done.5 = bf16[128,512]{1,0:T(8,128)(2,1)S(1)} collective-permute-done((bf16[128,512]{1,0:T(8,128)(2,1)S(1)}, bf16[128,512]{1,0:T(8,128)(2,1)S(1)}, u32[]{:S(2)}, u32[]{:S(2)}) %collective-permute-start.5) | collective-permute-done | bytes 131104 | tf_op jit(solution)/shard_map/ppermute | solution.py:391
  23.6 3.2 %collective-permute-done.4 = bf16[256,512]{1,0:T(8,128)(2,1)S(1)} collective-permute-done((bf16[256,512]{1,0:T(8,128)(2,1)S(1)}, bf16[256,512]{1,0:T(8,128)(2,1)S(1)}, u32[]{:S(2)}, u32[]{:S(2)}) %collective-permute-start.4) | collective-permute-done | bytes 262176 | tf_op jit(solution)/shard_map/ppermute | solution.py:37
  27.3 1.6 %collective-permute-done.7.got_ref = bf16[512,512]{1,0:T(8,128)(2,1)S(1)} collective-permute-done((bf16[512,512]{1,0:T(8,128)(2,1)S(1)}, bf16[512,512]{1,0:T(8,128)(2,1)S(1)}, u32[]{:S(2)}, u32[]{:S(2)}) %collective-permute-start.7) | collective-permute-done | bytes 524320 | tf_op jit(solution)/shard_map/ppermute | solution.py:37
  28.9 1.5 copy-done.1
  30.4 2.5 %gate_up_first.1 = (bf16[256,512]{1,0:T(8,128)(2,1)S(1)}, bf16[256,512]{1,0:T(8,128)(2,1)S(1)}, bf16[256,512]{1,0:T(8,128)(2,1)S(1)}, bf16[256,512]{1,0:T(8,128)(2,1)S(1)}, bf16[1024,512]{1,0:T(8,128)(2,1)S(1)}) custom-call(bf16[512,512]{1,0:T(8,128)(2,1)S(1)} %constant_dynamic-update-slice_fusion.4.held_ref, ...), custom_call_target="tpu_custom_call" | custom-call | flops 1000000000 | bytes 2000000 | tf_op jit(solution)/shard_map/gate_up_first/pallas_call | solution.py:358
  32.8 2.3 %gate_up_later.1 = (bf16[256,512]{1,0:T(8,128)(2,1)S(1)}, bf16[256,512]{1,0:T(8,128)(2,1)S(1)}, bf16[256,512]{1,0:T(8,128)(2,1)S(1)}, bf16[256,512]{1,0:T(8,128)(2,1)S(1)}) custom-call(bf16[1024,512]{1,0:T(8,128)(2,1)S(1)} %get-tuple-element.258.id_ref.rows_ref.refs_0_, bf16[1024,512]{1,0:T(8,128)(2,1)S(1)} %get-tuple-element.258.id_ref.rows_ref.refs_0_, ...), custom_call_target="tpu_custom_call" | custom-call | flops 1000000000 | bytes 2000000 | tf_op jit(solution)/shard_map/gate_up_later/pallas_call | solution.py:358
  35.9 1.2 collective-permute-start.8
  37.4 1.4 collective-permute-start.15
  38.8 1.4 act_grad_first.1
  40.3 1.3 act_grad_later.1
  41.6 2.1 %collective-permute-done.9 = bf16[256,512]{1,0:T(8,128)(2,1)S(1)} collective-permute-done((bf16[256,512]{1,0:T(8,128)(2,1)S(1)}, bf16[256,512]{1,0:T(8,128)(2,1)S(1)}, u32[]{:S(2)}, u32[]{:S(2)}) %collective-permute-start.9) | collective-permute-done | bytes 262176 | tf_op jit(solution)/shard_map/ppermute | solution.py:37
  43.9 1.3 collective-permute-start.12
  45.2 4.1 %collective-permute-done.16 = bf16[256,512]{1,0:T(8,128)(2,1)S(1)} collective-permute-done((bf16[256,512]{1,0:T(8,128)(2,1)S(1)}, bf16[256,512]{1,0:T(8,128)(2,1)S(1)}, u32[]{:S(2)}, u32[]{:S(2)}) %collective-permute-start.16) | collective-permute-done | bytes 262176 | tf_op jit(solution)/shard_map/ppermute | solution.py:37
  49.6 1.3 collective-permute-start.18
  50.9 0.9 collective-permute-done.14
  51.9 1.2 collective-permute-start.21
  53.2 1.8 %collective-permute-done.13 = bf16[256,512]{1,0:T(8,128)(2,1)S(1)} collective-permute-done((bf16[256,512]{1,0:T(8,128)(2,1)S(1)}, bf16[256,512]{1,0:T(8,128)(2,1)S(1)}, u32[]{:S(2)}, u32[]{:S(2)}) %collective-permute-start.13) | collective-permute-done | bytes 262176 | tf_op jit(solution)/shard_map/ppermute | solution.py:37
  55.0 2.5 %collective-permute-start.19 = (bf16[64,512]{1,0:T(8,128)(2,1)S(1)}, bf16[64,512]{1,0:T(8,128)(2,1)S(1)}, u32[]{:S(2)}, u32[]{:S(2)}) collective-permute-start(bf16[64,512]{1,0:T(8,128)(2,1)S(1)} %add_convert_fusion.17), channel_id=1, source_target_pairs={{0,4},{1,5},{2,6},{3,7},{4,0},{5,1},{6,2},{7,3},{8,12},{9,13},{10,... | collective-permute-start | bytes 196616 | tf_op jit(solution)/shard_map/ppermute | solution.py:37
  57.8 2.1 %collective-permute-done.21 = bf16[256,512]{1,0:T(8,128)(2,1)S(1)} collective-permute-done((bf16[256,512]{1,0:T(8,128)(2,1)S(1)}, bf16[256,512]{1,0:T(8,128)(2,1)S(1)}, u32[]{:S(2)}, u32[]{:S(2)}) %collective-permute-start.21) | collective-permute-done | bytes 262176 | tf_op jit(solution)/shard_map/ppermute | solution.py:37
  59.9 1.1 collective-permute-start.24
  61.1 2.6 %collective-permute-start.17 = (bf16[64,512]{1,0:T(8,128)(2,1)S(1)}, bf16[64,512]{1,0:T(8,128)(2,1)S(1)}, u32[]{:S(2)}, u32[]{:S(2)}) collective-permute-start(bf16[64,512]{1,0:T(8,128)(2,1)S(1)} %add_convert_fusion.16), channel_id=1, source_target_pairs={{0,4},{1,5},{2,6},{3,7},{4,0},{5,1},{6,2},{7,3},{8,12},{9,13},{10,... | collective-permute-start | bytes 196616 | tf_op jit(solution)/shard_map/ppermute | solution.py:37
  64.4 2.4 %collective-permute-start.22 = (bf16[64,512]{1,0:T(8,128)(2,1)S(1)}, bf16[64,512]{1,0:T(8,128)(2,1)S(1)}, u32[]{:S(2)}, u32[]{:S(2)}) collective-permute-start(bf16[64,512]{1,0:T(8,128)(2,1)S(1)} %add_convert_fusion.14), channel_id=1, source_target_pairs={{0,4},{1,5},{2,6},{3,7},{4,0},{5,1},{6,2},{7,3},{8,12},{9,13},{10,... | collective-permute-start | bytes 196616 | tf_op jit(solution)/shard_map/ppermute | solution.py:37
  67.6 0.9 collective-permute-start.29
  68.6 1.6 %collective-permute-start.28 = (bf16[64,512]{1,0:T(8,128)(2,1)S(1)}, bf16[64,512]{1,0:T(8,128)(2,1)S(1)}, u32[]{:S(2)}, u32[]{:S(2)}) collective-permute-start(bf16[64,512]{1,0:T(8,128)(2,1)S(1)} %add_convert_fusion.12), channel_id=1, source_target_pairs={{0,4},{1,5},{2,6},{3,7},{4,0},{5,1},{6,2},{7,3},{8,12},{9,13},{10,... | collective-permute-start | bytes 196616 | tf_op jit(solution)/shard_map/ppermute | solution.py:37
  70.2 3.5 %collective-permute-done.22 = bf16[64,512]{1,0:T(8,128)(2,1)S(1)} collective-permute-done((bf16[64,512]{1,0:T(8,128)(2,1)S(1)}, bf16[64,512]{1,0:T(8,128)(2,1)S(1)}, u32[]{:S(2)}, u32[]{:S(2)}) %collective-permute-start.22) | collective-permute-done | bytes 65568 | tf_op jit(solution)/shard_map/ppermute | solution.py:37
  73.7 3.2 %collective-permute-start.26 = (bf16[64,512]{1,0:T(8,128)(2,1)S(1)}, bf16[64,512]{1,0:T(8,128)(2,1)S(1)}, u32[]{:S(2)}, u32[]{:S(2)}) collective-permute-start(bf16[64,512]{1,0:T(8,128)(2,1)S(1)} %multiply_convert_fusion.5), channel_id=1, source_target_pairs={{0,4},{1,5},{2,6},{3,7},{4,0},{5,1},{6,2},{7,3},{8,12},{9,13},{10,... | collective-permute-start | bytes 196616 | tf_op jit(solution)/shard_map/ppermute | solution.py:37
  77.1 2.4 %collective-permute-start.33 = (bf16[64,512]{1,0:T(8,128)(2,1)S(1)}, bf16[64,512]{1,0:T(8,128)(2,1)S(1)}, u32[]{:S(2)}, u32[]{:S(2)}) collective-permute-start(bf16[64,512]{1,0:T(8,128)(2,1)S(1)} %get-tuple-element.208), channel_id=1, source_target_pairs={{0,4},{1,5},{2,6},{3,7},{4,0},{5,1},{6,2},{7,3},{8,12},{9,13},{10,... | collective-permute-start | bytes 196616 | tf_op jit(solution)/shard_map/ppermute | solution.py:37
  79.6 1.0 collective-permute-start.32
  80.6 3.9 %collective-permute-done.27 = bf16[64,512]{1,0:T(8,128)(2,1)S(1)} collective-permute-done((bf16[64,512]{1,0:T(8,128)(2,1)S(1)}, bf16[64,512]{1,0:T(8,128)(2,1)S(1)}, u32[]{:S(2)}, u32[]{:S(2)}) %collective-permute-start.27) | collective-permute-done | bytes 65568 | tf_op jit(solution)/shard_map/ppermute | solution.py:37
  85.3 1.8 %collective-permute-start.30 = (bf16[128,512]{1,0:T(8,128)(2,1)S(1)}, bf16[128,512]{1,0:T(8,128)(2,1)S(1)}, u32[]{:S(2)}, u32[]{:S(2)}) collective-permute-start(bf16[128,512]{1,0:T(8,128)(2,1)S(1)} %constant_dynamic-update-slice_fusion.10), channel_id=1, source_target_pairs={{0,2},{1,3},{2,0},{3,1},{4,6},{5,7},{6,4},{7,5},{8,10},{9,11},{10,... | collective-permute-start | bytes 393224 | tf_op jit(solution)/shard_map/ppermute | solution.py:37
  87.2 1.4 collective-permute-start.38
  88.6 1.1 collective-permute-start.39
  91.3 1.5 collective-permute-start.35
  93.0 1.1 collective-permute-start.34
  94.8 1.8 %collective-permute-start.41 = (bf16[128,512]{1,0:T(8,128)(2,1)S(1)}, bf16[128,512]{1,0:T(8,128)(2,1)S(1)}, u32[]{:S(2)}, u32[]{:S(2)}) collective-permute-start(bf16[128,512]{1,0:T(8,128)(2,1)S(1)} %constant_dynamic-update-slice_fusion.22), channel_id=1, source_target_pairs={{0,2},{1,3},{2,0},{3,1},{4,6},{5,7},{6,4},{7,5},{8,10},{9,11},{10,... | collective-permute-start | bytes 393224 | tf_op jit(solution)/shard_map/ppermute | solution.py:37
  96.6 1.5 collective-permute-start.47
  98.1 1.7 %collective-permute-done.34.refs_1_ = bf16[256,512]{1,0:T(8,128)(2,1)S(1)} collective-permute-done((bf16[256,512]{1,0:T(8,128)(2,1)S(1)}, bf16[256,512]{1,0:T(8,128)(2,1)S(1)}, u32[]{:S(2)}, u32[]{:S(2)}) %collective-permute-start.34) | collective-permute-done | bytes 262176 | tf_op jit(solution)/shard_map/ppermute | solution.py:37
  99.9 1.2 collective-permute-start.46
  101.4 3.4 %out_rows.1 = (bf16[512,448]{1,0:T(8,128)(2,1)S(1)}, bf16[512,448]{1,0:T(8,128)(2,1)S(1)}) custom-call(bf16[1024,512]{1,0:T(8,128)(2,1)S(1)} %get-tuple-element.258.id_ref.rows_ref.refs_0_, bf16[4,448,512]{2,1,0:T(8,128)(2,1)S(1)} %bitcast.6, bf16[256,512]{1,0:T(8,128)(2,1)S(1)} %constant_dynamic-update-slice_fusion.18.refs_0_, ...), custom_call_target="tpu_custom_call" | custom-call | flops 1000000000 | bytes 2000000 | tf_op jit(solution)/shard_map/out_rows/pallas_call | solution.py:358
  104.8 8.8 %collective-permute-start.40 = (bf16[512,448]{1,0:T(8,128)(2,1)S(1)}, bf16[512,448]{1,0:T(8,128)(2,1)S(1)}, u32[]{:S(2)}, u32[]{:S(2)}) collective-permute-start(bf16[512,448]{1,0:T(8,128)(2,1)S(1)} %get-tuple-element.231), channel_id=1, source_target_pairs={{0,8},{1,9},{2,10},{3,11},{4,12},{5,13},{6,14},{7,15},{8,0},{9,1},... | collective-permute-start | bytes 1376264 | tf_op jit(solution)/shard_map/ppermute | solution.py:37
  114.3 0.9 collective-permute-done.40
  115.4 2.5 %token_gate_rows.1.refs_4_ = f32[1024,448]{1,0:T(8,128)S(1)} custom-call(bf16[1024,512]{1,0:T(8,128)(2,1)S(1)} %get-tuple-element.258.id_ref.rows_ref.refs_0_, bf16[4,448,512]{2,1,0:T(8,128)(2,1)S(1)} %copy-done, bf16[256,512]{1,0:T(8,128)(2,1)S(1)} %constant_dynamic-update-slice_fusion.26.refs_0_, bf16[256,512]{1,0:T(8,128)(2,1)S(1)} %collective-permute-done.46.refs_1_, ...), custom_call_target="tpu_custom_call" | custom-call | flops 1000000000 | bytes 2000000 | tf_op jit(solution)/shard_map/token_gate_rows/pallas_call | solution.py:358
  117.9 3.8 %grad_gate.1 = bf16[4,448,512]{2,1,0:T(8,128)(2,1)} custom-call(bf16[1024,512]{1,0:T(8,128)(2,1)S(1)} %get-tuple-element.258.id_ref.rows_ref.refs_0_, bf16[1024,512]{1,0:T(8,128)(2,1)S(1)} %get-tuple-element.258.id_ref.rows_ref.refs_0_, bf16[256,512]{1,0:T(8,128)(2,1)S(1)} %constant_dynamic-update-slice_fusion.26.refs_0_, ...), custom_call_target="tpu_custom_call" | custom-call | flops 1000000000 | bytes 2000000 | tf_op jit(solution)/shard_map/grad_gate/pallas_call | solution.py:358
  121.9 3.3 %token_rows.1 = (bf16[512,448]{1,0:T(8,128)(2,1)S(1)}, bf16[512,448]{1,0:T(8,128)(2,1)S(1)}) custom-call(bf16[1024,512]{1,0:T(8,128)(2,1)S(1)} %get-tuple-element.258.id_ref.rows_ref.refs_0_, bf16[4,448,512]{2,1,0:T(8,128)(2,1)S(1)} %copy-done.2, bf16[256,512]{1,0:T(8,128)(2,1)S(1)} %constant_dynamic-update-slice_fusion.30.refs_0_, ...), custom_call_target="tpu_custom_call" | custom-call | flops 1000000000 | bytes 2000000 | tf_op jit(solution)/shard_map/token_rows/pallas_call | solution.py:358
  125.1 1.2 collective-permute-start.50
  126.5 1.4 collective-permute-done.50
  128.7 3.1 %collective-permute-start.48 = (bf16[128,448]{1,0:T(8,128)(2,1)S(1)}, bf16[128,448]{1,0:T(8,128)(2,1)S(1)}, u32[]{:S(2)}, u32[]{:S(2)}) collective-permute-start(bf16[128,448]{1,0:T(8,128)(2,1)S(1)} %get-tuple-element.266), channel_id=1, source_target_pairs={{0,0},{1,1},{8,2},{9,3},{16,4},{17,5},{24,6},{25,7},{2,8},{3,9},{1... | collective-permute-start | bytes 344072 | tf_op jit(solution)/shard_map/ppermute | solution.py:144
  131.9 1.3 collective-permute-start.49
  133.2 3.8 %grad_down.1 = bf16[4,448,512]{2,1,0:T(8,128)(2,1)} custom-call(bf16[1024,512]{1,0:T(8,128)(2,1)S(1)} %get-tuple-element.258.id_ref.rows_ref.refs_0_, bf16[1024,512]{1,0:T(8,128)(2,1)S(1)} %get-tuple-element.253.rows_ref, bf16[256,512]{1,0:T(8,128)(2,1)S(1)} %constant_dynamic-update-slice_fusion.18.refs_0_, ...), custom_call_target="tpu_custom_call" | custom-call | flops 1000000000 | bytes 2000000 | tf_op jit(solution)/shard_map/grad_down/pallas_call | solution.py:358
  137.1 4.8 %collective-permute-start.52 = (bf16[128,448]{1,0:T(8,128)(2,1)S(1)}, bf16[128,448]{1,0:T(8,128)(2,1)S(1)}, u32[]{:S(2)}, u32[]{:S(2)}) collective-permute-start(bf16[128,448]{1,0:T(8,128)(2,1)S(1)} %get-tuple-element.264), channel_id=1, source_target_pairs={{0,0},{1,1},{8,2},{9,3},{16,4},{17,5},{24,6},{25,7},{2,8},{3,9},{1... | collective-permute-start | bytes 344072 | tf_op jit(solution)/shard_map/ppermute | solution.py:144
  142.0 1.0 collective-permute-start.53
  143.0 0.9 join_output.1
  143.9 3.8 %grad_up.1 = bf16[4,448,512]{2,1,0:T(8,128)(2,1)} custom-call(bf16[1024,512]{1,0:T(8,128)(2,1)S(1)} %get-tuple-element.258.id_ref.rows_ref.refs_0_, bf16[1024,512]{1,0:T(8,128)(2,1)S(1)} %get-tuple-element.258.id_ref.rows_ref.refs_0_, bf16[256,512]{1,0:T(8,128)(2,1)S(1)} %constant_dynamic-update-slice_fusion.30.refs_0_, ...), custom_call_target="tpu_custom_call" | custom-call | flops 1000000000 | bytes 2000000 | tf_op jit(solution)/shard_map/grad_up/pallas_call | solution.py:358
  147.6 3.2 %collective-permute-done.53.other_ref = bf16[128,448]{1,0:T(8,128)(2,1)S(1)} collective-permute-done((bf16[128,448]{1,0:T(8,128)(2,1)S(1)}, bf16[128,448]{1,0:T(8,128)(2,1)S(1)}, u32[]{:S(2)}, u32[]{:S(2)}) %collective-permute-start.53) | collective-permute-done | bytes 114720 | tf_op jit(solution)/shard_map/ppermute | solution.py:144
  (143 shorter events, 11.8 us)
Async XLA Ops:
  2.5 4.6 %collective-permute-start = (bf16[128,512]{1,0:T(8,128)(2,1)}, bf16[128,512]{1,0:T(8,128)(2,1)S(1)}, u32[]{:S(2)}, u32[]{:S(2)}) collective-permute-start(bf16[128,512]{1,0:T(8,128)(2,1)} %get-tuple-element.134), channel_id=1, source_target_pairs={{0,16},{1,17},{2,18},{3,19},{4,20},{5,21},{6,22},{7,23},{8,24},{9,... | collective-permute-start | bytes 393224 | tf_op jit(solution)/shard_map/ppermute | solution.py:37
  3.7 3.4 %copy-start.6 = (bf16[128,512]{1,0:T(8,128)(2,1)S(1)}, bf16[128,512]{1,0:T(8,128)(2,1)}, u32[]{:S(2)}) copy-start(bf16[128,512]{1,0:T(8,128)(2,1)} %get-tuple-element.133) | copy-start | bytes 393220
  5.6 23.2 %copy-start = (bf16[4,448,512]{2,1,0:T(8,128)(2,1)S(1)}, bf16[4,448,512]{2,1,0:T(8,128)(2,1)}, u32[]{:S(2)}) copy-start(bf16[4,448,512]{2,1,0:T(8,128)(2,1)} %w_ref.2) | copy-start | bytes 5505028
  5.6 7.1 %collective-permute-start.3 = (bf16[128,512]{1,0:T(8,128)(2,1)}, bf16[128,512]{1,0:T(8,128)(2,1)S(1)}, u32[]{:S(2)}, u32[]{:S(2)}) collective-permute-start(bf16[128,512]{1,0:T(8,128)(2,1)} %get-tuple-element.136), channel_id=1, source_target_pairs={{0,16},{1,17},{2,18},{3,19},{4,20},{5,21},{6,22},{7,23},{8,24},{9,... | collective-permute-start | bytes 393224 | tf_op jit(solution)/shard_map/ppermute | solution.py:37
  7.1 12.0 %collective-permute-start.2 = (bf16[128,512]{1,0:T(8,128)(2,1)S(1)}, bf16[128,512]{1,0:T(8,128)(2,1)S(1)}, u32[]{:S(2)}, u32[]{:S(2)}) collective-permute-start(bf16[128,512]{1,0:T(8,128)(2,1)S(1)} %get-tuple-element.273), channel_id=1, source_target_pairs={{0,4},{1,5},{2,12},{3,13},{4,1},{5,0},{6,9},{7,8},{8,6},{9,7},{10,... | collective-permute-start | bytes 393224 | tf_op jit(solution)/shard_map/ppermute | solution.py:390
  9.7 9.4 %collective-permute-start.1 = (bf16[128,512]{1,0:T(8,128)(2,1)S(1)}, bf16[128,512]{1,0:T(8,128)(2,1)S(1)}, u32[]{:S(2)}, u32[]{:S(2)}) collective-permute-start(bf16[128,512]{1,0:T(8,128)(2,1)S(1)} %get-tuple-element.274), channel_id=1, source_target_pairs={{0,0},{1,1},{2,8},{3,9},{4,5},{5,4},{6,13},{7,12},{8,2},{9,3},{10,... | collective-permute-start | bytes 393224 | tf_op jit(solution)/shard_map/ppermute | solution.py:391
  13.7 8.0 %collective-permute-start.6 = (bf16[128,512]{1,0:T(8,128)(2,1)S(1)}, bf16[128,512]{1,0:T(8,128)(2,1)S(1)}, u32[]{:S(2)}, u32[]{:S(2)}) collective-permute-start(bf16[128,512]{1,0:T(8,128)(2,1)S(1)} %get-tuple-element.271), channel_id=1, source_target_pairs={{0,4},{1,5},{2,12},{3,13},{4,1},{5,0},{6,9},{7,8},{8,6},{9,7},{10,... | collective-permute-start | bytes 393224 | tf_op jit(solution)/shard_map/ppermute | solution.py:390
  16.4 7.2 %collective-permute-start.5 = (bf16[128,512]{1,0:T(8,128)(2,1)S(1)}, bf16[128,512]{1,0:T(8,128)(2,1)S(1)}, u32[]{:S(2)}, u32[]{:S(2)}) collective-permute-start(bf16[128,512]{1,0:T(8,128)(2,1)S(1)} %get-tuple-element.272), channel_id=1, source_target_pairs={{0,0},{1,1},{2,8},{3,9},{4,5},{5,4},{6,13},{7,12},{8,2},{9,3},{10,... | collective-permute-start | bytes 393224 | tf_op jit(solution)/shard_map/ppermute | solution.py:391
  19.2 7.6 %collective-permute-start.4 = (bf16[256,512]{1,0:T(8,128)(2,1)S(1)}, bf16[256,512]{1,0:T(8,128)(2,1)S(1)}, u32[]{:S(2)}, u32[]{:S(2)}) collective-permute-start(bf16[256,512]{1,0:T(8,128)(2,1)S(1)} %constant_dynamic-update-slice_fusion), channel_id=1, source_target_pairs={{0,16},{1,17},{2,18},{3,19},{4,20},{5,21},{6,22},{7,23},{8,24},{9,... | collective-permute-start | bytes 786440 | tf_op jit(solution)/shard_map/ppermute | solution.py:37
  26.9 2.0 %collective-permute-start.7 = (bf16[512,512]{1,0:T(8,128)(2,1)S(1)}, bf16[512,512]{1,0:T(8,128)(2,1)S(1)}, u32[]{:S(2)}, u32[]{:S(2)}) collective-permute-start(bf16[512,512]{1,0:T(8,128)(2,1)S(1)} %constant_dynamic-update-slice_fusion.4.held_ref), channel_id=1, source_target_pairs={{0,8},{1,9},{2,10},{3,11},{4,12},{5,13},{6,14},{7,15},{8,0},{9,1},... | collective-permute-start | bytes 1572872 | tf_op jit(solution)/shard_map/ppermute | solution.py:37
  27.0 8.1 %collective-permute-start.10 = (bf16[256,512]{1,0:T(8,128)(2,1)S(1)}, bf16[256,512]{1,0:T(8,128)(2,1)S(1)}, u32[]{:S(2)}, u32[]{:S(2)}) collective-permute-start(bf16[256,512]{1,0:T(8,128)(2,1)S(1)} %constant_dynamic-update-slice_fusion.2), channel_id=1, source_target_pairs={{0,16},{1,17},{2,18},{3,19},{4,20},{5,21},{6,22},{7,23},{8,24},{9,... | collective-permute-start | bytes 786440 | tf_op jit(solution)/shard_map/ppermute | solution.py:37
  28.9 1.5 copy-start.1
  32.8 6.0 %copy-start.3 = (bf16[4,512,448]{1,2,0:T(8,128)(2,1)S(1)}, bf16[4,512,448]{1,2,0:T(8,128)(2,1)}, u32[]{:S(2)}) copy-start(bf16[4,512,448]{1,2,0:T(8,128)(2,1)} %param.14) | copy-start | bytes 5505028
  35.2 3.6 %collective-permute-start.11 = (bf16[512,512]{1,0:T(8,128)(2,1)S(1)}, bf16[512,512]{1,0:T(8,128)(2,1)S(1)}, u32[]{:S(2)}, u32[]{:S(2)}) collective-permute-start(bf16[512,512]{1,0:T(8,128)(2,1)S(1)} %constant_dynamic-update-slice_fusion.6.held_ref), channel_id=1, source_target_pairs={{0,8},{1,9},{2,10},{3,11},{4,12},{5,13},{6,14},{7,15},{8,0},{9,1},... | collective-permute-start | bytes 1572872 | tf_op jit(solution)/shard_map/ppermute | solution.py:37
  35.9 7.9 %collective-permute-start.9 = (bf16[256,512]{1,0:T(8,128)(2,1)S(1)}, bf16[256,512]{1,0:T(8,128)(2,1)S(1)}, u32[]{:S(2)}, u32[]{:S(2)}) collective-permute-start(bf16[256,512]{1,0:T(8,128)(2,1)S(1)} %get-tuple-element.148), channel_id=1, source_target_pairs={{0,2},{1,3},{2,0},{3,1},{4,6},{5,7},{6,4},{7,5},{8,10},{9,11},{10,... | collective-permute-start | bytes 786440 | tf_op jit(solution)/shard_map/ppermute | solution.py:37
  35.9 8.0 %collective-permute-start.8 = (bf16[256,512]{1,0:T(8,128)(2,1)S(1)}, bf16[256,512]{1,0:T(8,128)(2,1)S(1)}, u32[]{:S(2)}, u32[]{:S(2)}) collective-permute-start(bf16[256,512]{1,0:T(8,128)(2,1)S(1)} %get-tuple-element.151), channel_id=1, source_target_pairs={{0,1},{1,0},{2,3},{3,2},{4,5},{5,4},{6,7},{7,6},{8,9},{9,8},{10,11... | collective-permute-start | bytes 786440 | tf_op jit(solution)/shard_map/ppermute | solution.py:37
  37.1 12.2 %collective-permute-start.16 = (bf16[256,512]{1,0:T(8,128)(2,1)S(1)}, bf16[256,512]{1,0:T(8,128)(2,1)S(1)}, u32[]{:S(2)}, u32[]{:S(2)}) collective-permute-start(bf16[256,512]{1,0:T(8,128)(2,1)S(1)} %get-tuple-element.169), channel_id=1, source_target_pairs={{0,2},{1,3},{2,0},{3,1},{4,6},{5,7},{6,4},{7,5},{8,10},{9,11},{10,... | collective-permute-start | bytes 786440 | tf_op jit(solution)/shard_map/ppermute | solution.py:37
  37.4 12.2 %collective-permute-start.15 = (bf16[256,512]{1,0:T(8,128)(2,1)S(1)}, bf16[256,512]{1,0:T(8,128)(2,1)S(1)}, u32[]{:S(2)}, u32[]{:S(2)}) collective-permute-start(bf16[256,512]{1,0:T(8,128)(2,1)S(1)} %get-tuple-element.167), channel_id=1, source_target_pairs={{0,1},{1,0},{2,3},{3,2},{4,5},{5,4},{6,7},{7,6},{8,9},{9,8},{10,11... | collective-permute-start | bytes 786440 | tf_op jit(solution)/shard_map/ppermute | solution.py:37
  40.2 14.8 %collective-permute-start.13 = (bf16[256,512]{1,0:T(8,128)(2,1)S(1)}, bf16[256,512]{1,0:T(8,128)(2,1)S(1)}, u32[]{:S(2)}, u32[]{:S(2)}) collective-permute-start(bf16[256,512]{1,0:T(8,128)(2,1)S(1)} %get-tuple-element.158), channel_id=1, source_target_pairs={{0,2},{1,3},{2,0},{3,1},{4,6},{5,7},{6,4},{7,5},{8,10},{9,11},{10,... | collective-permute-start | bytes 786440 | tf_op jit(solution)/shard_map/ppermute | solution.py:37
  43.8 8.1 %collective-permute-start.14 = (bf16[128,512]{1,0:T(8,128)(2,1)S(1)}, bf16[128,512]{1,0:T(8,128)(2,1)S(1)}, u32[]{:S(2)}, u32[]{:S(2)}) collective-permute-start(bf16[128,512]{1,0:T(8,128)(2,1)S(1)} %add_convert_fusion.11), channel_id=1, source_target_pairs={{0,1},{1,0},{2,3},{3,2},{4,5},{5,4},{6,7},{7,6},{8,9},{9,8},{10,11... | collective-permute-start | bytes 393224 | tf_op jit(solution)/shard_map/ppermute | solution.py:37
  43.9 13.9 %collective-permute-start.12 = (bf16[128,512]{1,0:T(8,128)(2,1)S(1)}, bf16[128,512]{1,0:T(8,128)(2,1)S(1)}, u32[]{:S(2)}, u32[]{:S(2)}) collective-permute-start(bf16[128,512]{1,0:T(8,128)(2,1)S(1)} %add_convert_fusion.10), channel_id=1, source_target_pairs={{0,2},{1,3},{2,0},{3,1},{4,6},{5,7},{6,4},{7,5},{8,10},{9,11},{10,... | collective-permute-start | bytes 393224 | tf_op jit(solution)/shard_map/ppermute | solution.py:37
  49.4 14.8 %copy-start.5 = (bf16[128,512]{1,0:T(8,128)(2,1)}, bf16[128,512]{1,0:T(8,128)(2,1)S(1)}, u32[]{:S(2)}) copy-start(bf16[128,512]{1,0:T(8,128)(2,1)S(1)} %slice.261) | copy-start | bytes 393220
  49.4 11.6 %collective-permute-start.20 = (bf16[128,512]{1,0:T(8,128)(2,1)S(1)}, bf16[128,512]{1,0:T(8,128)(2,1)S(1)}, u32[]{:S(2)}, u32[]{:S(2)}) collective-permute-start(bf16[128,512]{1,0:T(8,128)(2,1)S(1)} %add_convert_fusion.9), channel_id=1, source_target_pairs={{0,1},{1,0},{2,3},{3,2},{4,5},{5,4},{6,7},{7,6},{8,9},{9,8},{10,11... | collective-permute-start | bytes 393224 | tf_op jit(solution)/shard_map/ppermute | solution.py:37
  49.6 14.8 %collective-permute-start.18 = (bf16[128,512]{1,0:T(8,128)(2,1)S(1)}, bf16[128,512]{1,0:T(8,128)(2,1)S(1)}, u32[]{:S(2)}, u32[]{:S(2)}) collective-permute-start(bf16[128,512]{1,0:T(8,128)(2,1)S(1)} %add_convert_fusion.8), channel_id=1, source_target_pairs={{0,2},{1,3},{2,0},{3,1},{4,6},{5,7},{6,4},{7,5},{8,10},{9,11},{10,... | collective-permute-start | bytes 393224 | tf_op jit(solution)/shard_map/ppermute | solution.py:37
  51.9 8.0 %collective-permute-start.21 = (bf16[256,512]{1,0:T(8,128)(2,1)S(1)}, bf16[256,512]{1,0:T(8,128)(2,1)S(1)}, u32[]{:S(2)}, u32[]{:S(2)}) collective-permute-start(bf16[256,512]{1,0:T(8,128)(2,1)S(1)} %get-tuple-element.181), channel_id=1, source_target_pairs={{0,1},{1,0},{2,3},{3,2},{4,5},{5,4},{6,7},{7,6},{8,9},{9,8},{10,11... | collective-permute-start | bytes 786440 | tf_op jit(solution)/shard_map/ppermute | solution.py:37
  55.0 9.2 %collective-permute-start.19 = (bf16[64,512]{1,0:T(8,128)(2,1)S(1)}, bf16[64,512]{1,0:T(8,128)(2,1)S(1)}, u32[]{:S(2)}, u32[]{:S(2)}) collective-permute-start(bf16[64,512]{1,0:T(8,128)(2,1)S(1)} %add_convert_fusion.17), channel_id=1, source_target_pairs={{0,4},{1,5},{2,6},{3,7},{4,0},{5,1},{6,2},{7,3},{8,12},{9,13},{10,... | collective-permute-start | bytes 196616 | tf_op jit(solution)/shard_map/ppermute | solution.py:37
  59.9 8.6 %collective-permute-start.24 = (bf16[128,512]{1,0:T(8,128)(2,1)S(1)}, bf16[128,512]{1,0:T(8,128)(2,1)S(1)}, u32[]{:S(2)}, u32[]{:S(2)}) collective-permute-start(bf16[128,512]{1,0:T(8,128)(2,1)S(1)} %add_convert_fusion.6), channel_id=1, source_target_pairs={{0,2},{1,3},{2,0},{3,1},{4,6},{5,7},{6,4},{7,5},{8,10},{9,11},{10,... | collective-permute-start | bytes 393224 | tf_op jit(solution)/shard_map/ppermute | solution.py:37
  61.1 5.7 %collective-permute-start.17 = (bf16[64,512]{1,0:T(8,128)(2,1)S(1)}, bf16[64,512]{1,0:T(8,128)(2,1)S(1)}, u32[]{:S(2)}, u32[]{:S(2)}) collective-permute-start(bf16[64,512]{1,0:T(8,128)(2,1)S(1)} %add_convert_fusion.16), channel_id=1, source_target_pairs={{0,4},{1,5},{2,6},{3,7},{4,0},{5,1},{6,2},{7,3},{8,12},{9,13},{10,... | collective-permute-start | bytes 196616 | tf_op jit(solution)/shard_map/ppermute | solution.py:37
  63.7 3.8 %collective-permute-start.25 = (bf16[128,512]{1,0:T(8,128)(2,1)S(1)}, bf16[128,512]{1,0:T(8,128)(2,1)S(1)}, u32[]{:S(2)}, u32[]{:S(2)}) collective-permute-start(bf16[128,512]{1,0:T(8,128)(2,1)S(1)} %add_convert_fusion.7), channel_id=1, source_target_pairs={{0,1},{1,0},{2,3},{3,2},{4,5},{5,4},{6,7},{7,6},{8,9},{9,8},{10,11... | collective-permute-start | bytes 393224 | tf_op jit(solution)/shard_map/ppermute | solution.py:37
  64.2 5.9 %slice-start = ((bf16[128,512]{1,0:T(8,128)(2,1)}), bf16[64,512]{1,0:T(8,128)(2,1)S(1)}, s32[]{:S(2)}) async-start(bf16[128,512]{1,0:T(8,128)(2,1)} %copy-done.5), calls=%async_computation | async-start | bytes 131072 | tf_op jit(solution)/shard_map/slice | solution.py:99
  64.2 5.9 %collective-permute-start.23 = (bf16[64,512]{1,0:T(8,128)(2,1)S(1)}, bf16[64,512]{1,0:T(8,128)(2,1)S(1)}, u32[]{:S(2)}, u32[]{:S(2)}) collective-permute-start(bf16[64,512]{1,0:T(8,128)(2,1)S(1)} %add_convert_fusion.15), channel_id=1, source_target_pairs={{0,4},{1,5},{2,6},{3,7},{4,0},{5,1},{6,2},{7,3},{8,12},{9,13},{10,... | collective-permute-start | bytes 196616 | tf_op jit(solution)/shard_map/ppermute | solution.py:37
  64.4 9.2 %collective-permute-start.22 = (bf16[64,512]{1,0:T(8,128)(2,1)S(1)}, bf16[64,512]{1,0:T(8,128)(2,1)S(1)}, u32[]{:S(2)}, u32[]{:S(2)}) collective-permute-start(bf16[64,512]{1,0:T(8,128)(2,1)S(1)} %add_convert_fusion.14), channel_id=1, source_target_pairs={{0,4},{1,5},{2,6},{3,7},{4,0},{5,1},{6,2},{7,3},{8,12},{9,13},{10,... | collective-permute-start | bytes 196616 | tf_op jit(solution)/shard_map/ppermute | solution.py:37
  67.6 9.4 %collective-permute-start.29 = (bf16[64,512]{1,0:T(8,128)(2,1)S(1)}, bf16[64,512]{1,0:T(8,128)(2,1)S(1)}, u32[]{:S(2)}, u32[]{:S(2)}) collective-permute-start(bf16[64,512]{1,0:T(8,128)(2,1)S(1)} %add_convert_fusion.13), channel_id=1, source_target_pairs={{0,4},{1,5},{2,6},{3,7},{4,0},{5,1},{6,2},{7,3},{8,12},{9,13},{10,... | collective-permute-start | bytes 196616 | tf_op jit(solution)/shard_map/ppermute | solution.py:37
  68.6 10.9 %collective-permute-start.28 = (bf16[64,512]{1,0:T(8,128)(2,1)S(1)}, bf16[64,512]{1,0:T(8,128)(2,1)S(1)}, u32[]{:S(2)}, u32[]{:S(2)}) collective-permute-start(bf16[64,512]{1,0:T(8,128)(2,1)S(1)} %add_convert_fusion.12), channel_id=1, source_target_pairs={{0,4},{1,5},{2,6},{3,7},{4,0},{5,1},{6,2},{7,3},{8,12},{9,13},{10,... | collective-permute-start | bytes 196616 | tf_op jit(solution)/shard_map/ppermute | solution.py:37
  73.7 11.6 %collective-permute-start.26 = (bf16[64,512]{1,0:T(8,128)(2,1)S(1)}, bf16[64,512]{1,0:T(8,128)(2,1)S(1)}, u32[]{:S(2)}, u32[]{:S(2)}) collective-permute-start(bf16[64,512]{1,0:T(8,128)(2,1)S(1)} %multiply_convert_fusion.5), channel_id=1, source_target_pairs={{0,4},{1,5},{2,6},{3,7},{4,0},{5,1},{6,2},{7,3},{8,12},{9,13},{10,... | collective-permute-start | bytes 196616 | tf_op jit(solution)/shard_map/ppermute | solution.py:37
  76.9 7.5 %collective-permute-start.27 = (bf16[64,512]{1,0:T(8,128)(2,1)S(1)}, bf16[64,512]{1,0:T(8,128)(2,1)S(1)}, u32[]{:S(2)}, u32[]{:S(2)}) collective-permute-start(bf16[64,512]{1,0:T(8,128)(2,1)S(1)} %get-tuple-element.204), channel_id=1, source_target_pairs={{0,4},{1,5},{2,6},{3,7},{4,0},{5,1},{6,2},{7,3},{8,12},{9,13},{10,... | collective-permute-start | bytes 196616 | tf_op jit(solution)/shard_map/ppermute | solution.py:37
  77.1 11.5 %collective-permute-start.33 = (bf16[64,512]{1,0:T(8,128)(2,1)S(1)}, bf16[64,512]{1,0:T(8,128)(2,1)S(1)}, u32[]{:S(2)}, u32[]{:S(2)}) collective-permute-start(bf16[64,512]{1,0:T(8,128)(2,1)S(1)} %get-tuple-element.208), channel_id=1, source_target_pairs={{0,4},{1,5},{2,6},{3,7},{4,0},{5,1},{6,2},{7,3},{8,12},{9,13},{10,... | collective-permute-start | bytes 196616 | tf_op jit(solution)/shard_map/ppermute | solution.py:37
  79.6 10.1 %collective-permute-start.32 = (bf16[64,512]{1,0:T(8,128)(2,1)S(1)}, bf16[64,512]{1,0:T(8,128)(2,1)S(1)}, u32[]{:S(2)}, u32[]{:S(2)}) collective-permute-start(bf16[64,512]{1,0:T(8,128)(2,1)S(1)} %get-tuple-element.210), channel_id=1, source_target_pairs={{0,4},{1,5},{2,6},{3,7},{4,0},{5,1},{6,2},{7,3},{8,12},{9,13},{10,... | collective-permute-start | bytes 196616 | tf_op jit(solution)/shard_map/ppermute | solution.py:37
  84.4 6.1 %collective-permute-start.31 = (bf16[128,512]{1,0:T(8,128)(2,1)S(1)}, bf16[128,512]{1,0:T(8,128)(2,1)S(1)}, u32[]{:S(2)}, u32[]{:S(2)}) collective-permute-start(bf16[128,512]{1,0:T(8,128)(2,1)S(1)} %constant_dynamic-update-slice_fusion.8), channel_id=1, source_target_pairs={{0,1},{1,0},{2,3},{3,2},{4,5},{5,4},{6,7},{7,6},{8,9},{9,8},{10,11... | collective-permute-start | bytes 393224 | tf_op jit(solution)/shard_map/ppermute | solution.py:37
  85.3 6.0 %collective-permute-start.30 = (bf16[128,512]{1,0:T(8,128)(2,1)S(1)}, bf16[128,512]{1,0:T(8,128)(2,1)S(1)}, u32[]{:S(2)}, u32[]{:S(2)}) collective-permute-start(bf16[128,512]{1,0:T(8,128)(2,1)S(1)} %constant_dynamic-update-slice_fusion.10), channel_id=1, source_target_pairs={{0,2},{1,3},{2,0},{3,1},{4,6},{5,7},{6,4},{7,5},{8,10},{9,11},{10,... | collective-permute-start | bytes 393224 | tf_op jit(solution)/shard_map/ppermute | solution.py:37
  87.2 7.0 %collective-permute-start.38 = (bf16[64,512]{1,0:T(8,128)(2,1)S(1)}, bf16[64,512]{1,0:T(8,128)(2,1)S(1)}, u32[]{:S(2)}, u32[]{:S(2)}) collective-permute-start(bf16[64,512]{1,0:T(8,128)(2,1)S(1)} %get-tuple-element.220), channel_id=1, source_target_pairs={{0,4},{1,5},{2,6},{3,7},{4,0},{5,1},{6,2},{7,3},{8,12},{9,13},{10,... | collective-permute-start | bytes 196616 | tf_op jit(solution)/shard_map/ppermute | solution.py:37
  88.6 4.5 %collective-permute-start.39 = (bf16[64,512]{1,0:T(8,128)(2,1)S(1)}, bf16[64,512]{1,0:T(8,128)(2,1)S(1)}, u32[]{:S(2)}, u32[]{:S(2)}) collective-permute-start(bf16[64,512]{1,0:T(8,128)(2,1)S(1)} %get-tuple-element.218), channel_id=1, source_target_pairs={{0,4},{1,5},{2,6},{3,7},{4,0},{5,1},{6,2},{7,3},{8,12},{9,13},{10,... | collective-permute-start | bytes 196616 | tf_op jit(solution)/shard_map/ppermute | solution.py:37
  89.7 5.1 %collective-permute-start.37 = (bf16[128,512]{1,0:T(8,128)(2,1)S(1)}, bf16[128,512]{1,0:T(8,128)(2,1)S(1)}, u32[]{:S(2)}, u32[]{:S(2)}) collective-permute-start(bf16[128,512]{1,0:T(8,128)(2,1)S(1)} %constant_dynamic-update-slice_fusion.12), channel_id=1, source_target_pairs={{0,1},{1,0},{2,3},{3,2},{4,5},{5,4},{6,7},{7,6},{8,9},{9,8},{10,11... | collective-permute-start | bytes 393224 | tf_op jit(solution)/shard_map/ppermute | solution.py:37
  90.5 6.1 %collective-permute-start.36 = (bf16[128,512]{1,0:T(8,128)(2,1)S(1)}, bf16[128,512]{1,0:T(8,128)(2,1)S(1)}, u32[]{:S(2)}, u32[]{:S(2)}) collective-permute-start(bf16[128,512]{1,0:T(8,128)(2,1)S(1)} %constant_dynamic-update-slice_fusion.14), channel_id=1, source_target_pairs={{0,2},{1,3},{2,0},{3,1},{4,6},{5,7},{6,4},{7,5},{8,10},{9,11},{10,... | collective-permute-start | bytes 393224 | tf_op jit(solution)/shard_map/ppermute | solution.py:37
  91.3 10.0 %collective-permute-start.35 = (bf16[256,512]{1,0:T(8,128)(2,1)S(1)}, bf16[256,512]{1,0:T(8,128)(2,1)S(1)}, u32[]{:S(2)}, u32[]{:S(2)}) collective-permute-start(bf16[256,512]{1,0:T(8,128)(2,1)S(1)} %constant_dynamic-update-slice_fusion.16.refs_2_), channel_id=1, source_target_pairs={{0,2},{1,3},{2,0},{3,1},{4,6},{5,7},{6,4},{7,5},{8,10},{9,11},{10,... | collective-permute-start | bytes 786440 | tf_op jit(solution)/shard_map/ppermute | solution.py:37
  93.0 6.8 %collective-permute-start.34 = (bf16[256,512]{1,0:T(8,128)(2,1)S(1)}, bf16[256,512]{1,0:T(8,128)(2,1)S(1)}, u32[]{:S(2)}, u32[]{:S(2)}) collective-permute-start(bf16[256,512]{1,0:T(8,128)(2,1)S(1)} %constant_dynamic-update-slice_fusion.18.refs_0_), channel_id=1, source_target_pairs={{0,1},{1,0},{2,3},{3,2},{4,5},{5,4},{6,7},{7,6},{8,9},{9,8},{10,11... | collective-permute-start | bytes 786440 | tf_op jit(solution)/shard_map/ppermute | solution.py:37
  94.2 19.4 %collective-permute-start.42 = (bf16[128,512]{1,0:T(8,128)(2,1)S(1)}, bf16[128,512]{1,0:T(8,128)(2,1)S(1)}, u32[]{:S(2)}, u32[]{:S(2)}) collective-permute-start(bf16[128,512]{1,0:T(8,128)(2,1)S(1)} %constant_dynamic-update-slice_fusion.20), channel_id=1, source_target_pairs={{0,1},{1,0},{2,3},{3,2},{4,5},{5,4},{6,7},{7,6},{8,9},{9,8},{10,11... | collective-permute-start | bytes 393224 | tf_op jit(solution)/shard_map/ppermute | solution.py:37
  94.8 19.4 %collective-permute-start.41 = (bf16[128,512]{1,0:T(8,128)(2,1)S(1)}, bf16[128,512]{1,0:T(8,128)(2,1)S(1)}, u32[]{:S(2)}, u32[]{:S(2)}) collective-permute-start(bf16[128,512]{1,0:T(8,128)(2,1)S(1)} %constant_dynamic-update-slice_fusion.22), channel_id=1, source_target_pairs={{0,2},{1,3},{2,0},{3,1},{4,6},{5,7},{6,4},{7,5},{8,10},{9,11},{10,... | collective-permute-start | bytes 393224 | tf_op jit(solution)/shard_map/ppermute | solution.py:37
  96.6 18.7 %collective-permute-start.47 = (bf16[256,512]{1,0:T(8,128)(2,1)S(1)}, bf16[256,512]{1,0:T(8,128)(2,1)S(1)}, u32[]{:S(2)}, u32[]{:S(2)}) collective-permute-start(bf16[256,512]{1,0:T(8,128)(2,1)S(1)} %constant_dynamic-update-slice_fusion.24.refs_2_), channel_id=1, source_target_pairs={{0,2},{1,3},{2,0},{3,1},{4,6},{5,7},{6,4},{7,5},{8,10},{9,11},{10,... | collective-permute-start | bytes 786440 | tf_op jit(solution)/shard_map/ppermute | solution.py:37
  99.9 15.5 %collective-permute-start.46 = (bf16[256,512]{1,0:T(8,128)(2,1)S(1)}, bf16[256,512]{1,0:T(8,128)(2,1)S(1)}, u32[]{:S(2)}, u32[]{:S(2)}) collective-permute-start(bf16[256,512]{1,0:T(8,128)(2,1)S(1)} %constant_dynamic-update-slice_fusion.26.refs_0_), channel_id=1, source_target_pairs={{0,1},{1,0},{2,3},{3,2},{4,5},{5,4},{6,7},{7,6},{8,9},{9,8},{10,11... | collective-permute-start | bytes 786440 | tf_op jit(solution)/shard_map/ppermute | solution.py:37
  104.8 10.3 %collective-permute-start.40 = (bf16[512,448]{1,0:T(8,128)(2,1)S(1)}, bf16[512,448]{1,0:T(8,128)(2,1)S(1)}, u32[]{:S(2)}, u32[]{:S(2)}) collective-permute-start(bf16[512,448]{1,0:T(8,128)(2,1)S(1)} %get-tuple-element.231), channel_id=1, source_target_pairs={{0,8},{1,9},{2,10},{3,11},{4,12},{5,13},{6,14},{7,15},{8,0},{9,1},... | collective-permute-start | bytes 1376264 | tf_op jit(solution)/shard_map/ppermute | solution.py:37
  113.6 8.2 %collective-permute-start.45 = (bf16[256,512]{1,0:T(8,128)(2,1)S(1)}, bf16[256,512]{1,0:T(8,128)(2,1)S(1)}, u32[]{:S(2)}, u32[]{:S(2)}) collective-permute-start(bf16[256,512]{1,0:T(8,128)(2,1)S(1)} %constant_dynamic-update-slice_fusion.28.refs_2_), channel_id=1, source_target_pairs={{0,2},{1,3},{2,0},{3,1},{4,6},{5,7},{6,4},{7,5},{8,10},{9,11},{10,... | collective-permute-start | bytes 786440 | tf_op jit(solution)/shard_map/ppermute | solution.py:37
  114.2 7.7 %collective-permute-start.44 = (bf16[256,512]{1,0:T(8,128)(2,1)S(1)}, bf16[256,512]{1,0:T(8,128)(2,1)S(1)}, u32[]{:S(2)}, u32[]{:S(2)}) collective-permute-start(bf16[256,512]{1,0:T(8,128)(2,1)S(1)} %constant_dynamic-update-slice_fusion.30.refs_0_), channel_id=1, source_target_pairs={{0,1},{1,0},{2,3},{3,2},{4,5},{5,4},{6,7},{7,6},{8,9},{9,8},{10,11... | collective-permute-start | bytes 786440 | tf_op jit(solution)/shard_map/ppermute | solution.py:37
  115.2 11.1 %collective-permute-start.43 = (bf16[256,448]{1,0:T(8,128)(2,1)S(1)}, bf16[256,448]{1,0:T(8,128)(2,1)S(1)}, u32[]{:S(2)}, u32[]{:S(2)}) collective-permute-start(bf16[256,448]{1,0:T(8,128)(2,1)S(1)} %add_convert_fusion.1), channel_id=1, source_target_pairs={{0,16},{1,17},{2,18},{3,19},{4,20},{5,21},{6,22},{7,23},{8,24},{9,... | collective-permute-start | bytes 688136 | tf_op jit(solution)/shard_map/ppermute | solution.py:37
  117.9 4.0 %copy-start.2 = (bf16[4,448,512]{2,1,0:T(8,128)(2,1)S(1)}, bf16[4,448,512]{2,1,0:T(8,128)(2,1)}, u32[]{:S(2)}) copy-start(bf16[4,448,512]{2,1,0:T(8,128)(2,1)} %w_ref.3) | copy-start | bytes 5505028
  125.1 2.7 %collective-permute-start.50 = (bf16[512,448]{1,0:T(8,128)(2,1)S(1)}, bf16[512,448]{1,0:T(8,128)(2,1)S(1)}, u32[]{:S(2)}, u32[]{:S(2)}) collective-permute-start(bf16[512,448]{1,0:T(8,128)(2,1)S(1)} %get-tuple-element.247), channel_id=1, source_target_pairs={{0,8},{1,9},{2,10},{3,11},{4,12},{5,13},{6,14},{7,15},{8,0},{9,1},... | collective-permute-start | bytes 1376264 | tf_op jit(solution)/shard_map/ppermute | solution.py:37
  127.9 9.1 %collective-permute-start.51 = (bf16[256,448]{1,0:T(8,128)(2,1)S(1)}, bf16[256,448]{1,0:T(8,128)(2,1)S(1)}, u32[]{:S(2)}, u32[]{:S(2)}) collective-permute-start(bf16[256,448]{1,0:T(8,128)(2,1)S(1)} %add_convert_fusion), channel_id=1, source_target_pairs={{0,16},{1,17},{2,18},{3,19},{4,20},{5,21},{6,22},{7,23},{8,24},{9,... | collective-permute-start | bytes 688136 | tf_op jit(solution)/shard_map/ppermute | solution.py:37
  128.7 13.2 %collective-permute-start.48 = (bf16[128,448]{1,0:T(8,128)(2,1)S(1)}, bf16[128,448]{1,0:T(8,128)(2,1)S(1)}, u32[]{:S(2)}, u32[]{:S(2)}) collective-permute-start(bf16[128,448]{1,0:T(8,128)(2,1)S(1)} %get-tuple-element.266), channel_id=1, source_target_pairs={{0,0},{1,1},{8,2},{9,3},{16,4},{17,5},{24,6},{25,7},{2,8},{3,9},{1... | collective-permute-start | bytes 344072 | tf_op jit(solution)/shard_map/ppermute | solution.py:144
  131.9 10.1 %collective-permute-start.49 = (bf16[128,448]{1,0:T(8,128)(2,1)S(1)}, bf16[128,448]{1,0:T(8,128)(2,1)S(1)}, u32[]{:S(2)}, u32[]{:S(2)}) collective-permute-start(bf16[128,448]{1,0:T(8,128)(2,1)S(1)} %get-tuple-element.265), channel_id=1, source_target_pairs={{17,0},{16,1},{25,2},{24,3},{1,4},{0,5},{9,6},{8,7},{19,8},{18,9},... | collective-permute-start | bytes 344072 | tf_op jit(solution)/shard_map/ppermute | solution.py:144
  133.2 9.8 %copy-start.4 = (f32[128,1]{0,1:T(1,128)S(1)}, f32[128,1]{0,1:T(1,128)}, u32[]{:S(2)}) copy-start(f32[128,1]{0,1:T(1,128)} %param.10) | copy-start | bytes 1540
  137.1 13.7 %collective-permute-start.52 = (bf16[128,448]{1,0:T(8,128)(2,1)S(1)}, bf16[128,448]{1,0:T(8,128)(2,1)S(1)}, u32[]{:S(2)}, u32[]{:S(2)}) collective-permute-start(bf16[128,448]{1,0:T(8,128)(2,1)S(1)} %get-tuple-element.264), channel_id=1, source_target_pairs={{0,0},{1,1},{8,2},{9,3},{16,4},{17,5},{24,6},{25,7},{2,8},{3,9},{1... | collective-permute-start | bytes 344072 | tf_op jit(solution)/shard_map/ppermute | solution.py:144
  142.0 8.9 %collective-permute-start.53 = (bf16[128,448]{1,0:T(8,128)(2,1)S(1)}, bf16[128,448]{1,0:T(8,128)(2,1)S(1)}, u32[]{:S(2)}, u32[]{:S(2)}) collective-permute-start(bf16[128,448]{1,0:T(8,128)(2,1)S(1)} %get-tuple-element.263), channel_id=1, source_target_pairs={{17,0},{16,1},{25,2},{24,3},{1,4},{0,5},{9,6},{8,7},{19,8},{18,9},... | collective-permute-start | bytes 344072 | tf_op jit(solution)/shard_map/ppermute | solution.py:144
